TPU v7x, 32 devices: a whole 2x2x4 slice. The times are simulated.
32 devices in a mesh: tm: 16 (over z, y, core), space: 2 (over x).
Axes of the slice: x: 2, y: 2, z: 4, core: 2. Of those that a mesh axis runs over, the one named last changes fastest.
Arguments:
- c_points: float32 [32, 3, 64, 512], P('tm', None, 'space'), may hold values from -0.45 to 1.3, as said below
Outputs:
- updated: float32 [32, 3, 64, 512], P('tm', None, 'space')
- coarse_residual: float32 [32, 3, 2, 32, 512], P(None, None, 'space', 'tm')
Inputs may be any that keep to these rules, and one draw needn't show every extreme that they name: `c_points`: the first field (height) lies in 0.7 to 1.3, the other two (momenta) in -0.45 to 0.45.
All inputs are finite; a program needn't handle non-finite values.
Results may differ from a plain program's by a relative error of at most 0.000028.
Values sent between devices are 32-bit elements; how exact they have to be, the bound alone decides.
No kernel may reach another device: no remote copies, remote signals or barrier semaphores. Data moves between devices by JAX's collectives and lax.ppermute only.
A program may use at most 64 MiB of HBM per device.

v0:
```python
import jax
import jax.numpy as jnp
from jax import lax
from jax.sharding import PartitionSpec as P

FACTOR = 8


gravity = 1.0
half_ratio = 0.1


def padded(block, sides, width):
    for axis, dim in sides:
        count = lax.axis_size(axis)
        forward = [(i, i + 1) for i in range(count - 1)]
        forward.append((count - 1, 0))
        backward = [(target, source) for source, target in forward]
        low = lax.ppermute(
            lax.slice_in_dim(block, block.shape[dim] - width, None, axis=dim), axis, forward
        )
        high = lax.ppermute(lax.slice_in_dim(block, 0, width, axis=dim), axis, backward)
        block = jnp.concatenate([low, block, high], axis=dim)
    return block


def from_behind(block, axis, distance):
    devices = range(lax.axis_size(axis))
    route = [(i - distance, i) for i in devices if i - distance in devices]
    return lax.ppermute(block, axis, route)


def column_flux(state):
    height = state[..., 0, :, :]
    east_flow = state[..., 1, :, :]
    north_flow = state[..., 2, :, :]
    velocity = east_flow / height
    return jnp.stack(
        [east_flow, east_flow * velocity + 0.5 * gravity * height * height, north_flow * velocity],
        axis=-3,
    )


def row_flux(state):
    height = state[..., 0, :, :]
    east_flow = state[..., 1, :, :]
    north_flow = state[..., 2, :, :]
    velocity = north_flow / height
    return jnp.stack(
        [north_flow, east_flow * velocity, north_flow * velocity + 0.5 * gravity * height * height],
        axis=-3,
    )


def flux_step(extended):
    center = extended[..., 1:-1, :]
    upper_row = extended[..., 2:, :]
    lower_row = extended[..., :-2, :]
    right_cells = jnp.roll(center, -1, axis=-1)
    left_cells = jnp.roll(center, 1, axis=-1)
    average = 0.25 * (upper_row + lower_row + right_cells + left_cells)
    return (
        average
        - half_ratio * (column_flux(right_cells) - column_flux(left_cells))
        - half_ratio * (row_flux(upper_row) - row_flux(lower_row))
    )


def propagate(state):
    extended = padded(state, (("space", 2),), FACTOR)
    for step in range(FACTOR):
        extended = flux_step(extended)
    return extended


def on_device(c_points):
    leading = lax.axis_index("tm") == 0
    advanced = propagate(c_points)
    incoming = from_behind(advanced[-1], "tm", 1)
    opening = jnp.where(leading, c_points[0], incoming)
    updated = jnp.concatenate([opening[None], advanced[:-1]], axis=0)
    pushed = propagate(updated)
    residual = pushed - advanced
    coarse = lax.all_to_all(residual, "tm", split_axis=2, concat_axis=0, tiled=True)
    return (updated, coarse[:, :, None])


def solution(mesh):
    in_specs = (P("tm", None, "space", None),)
    out_specs = (P("tm", None, "space", None), P(None, None, "space", "tm", None))
    return jax.shard_map(
        on_device, mesh=mesh, in_specs=in_specs, out_specs=out_specs, check_vma=False
    )
```

profile of v0, /device:TPU:0, one launch (start us, length us, event | category | flops | bytes accessed | tf_op | source)
XLA Modules:
  0.0 70.0 jit_solution(7068001876295104290)
XLA Ops:
  0.6 1.0 %fusion.388 = (f32[2,3,8,512]{3,2,1,0:T(8,128)S(1)}, f32[2,3,8,512]{3,2,1,0:T(8,128)S(1)}) fusion(f32[2,3,32,512]{3,2,1,0:T(8,128)} %param.1), kind=kLoop, calls=%fused_computation.767 | loop fusion | bytes 393216 | tf_op jit(solution)/shard_map/slice | solution.py:22
  1.6 3.0 %collective-permute-start = (f32[2,3,8,512]{3,2,1,0:T(8,128)S(1)}, f32[2,3,8,512]{3,2,1,0:T(8,128)S(1)}, u32[]{:S(2)}, u32[]{:S(2)}) collective-permute-start(f32[2,3,8,512]{3,2,1,0:T(8,128)S(1)} %get-tuple-element.233), channel_id=1, source_target_pairs={{0,1},{1,0},{2,3},{3,2},{4,5},{5,4},{6,7},{7,6},{8,9},{9,8},{10,11... | collective-permute-start | bytes 294920 | tf_op jit(solution)/shard_map/ppermute | solution.py:19
  4.7 3.4 %collective-permute-done = f32[2,3,8,512]{3,2,1,0:T(8,128)S(1)} collective-permute-done((f32[2,3,8,512]{3,2,1,0:T(8,128)S(1)}, f32[2,3,8,512]{3,2,1,0:T(8,128)S(1)}, u32[]{:S(2)}, u32[]{:S(2)}) %collective-permute-start) | collective-permute-done | bytes 98336 | tf_op jit(solution)/shard_map/ppermute | solution.py:19
  8.2 1.4 %collective-permute-done.1 = f32[2,3,8,512]{3,2,1,0:T(8,128)S(1)} collective-permute-done((f32[2,3,8,512]{3,2,1,0:T(8,128)S(1)}, f32[2,3,8,512]{3,2,1,0:T(8,128)S(1)}, u32[]{:S(2)}, u32[]{:S(2)}) %collective-permute-start.1) | collective-permute-done | bytes 98336 | tf_op jit(solution)/shard_map/ppermute | solution.py:22
  10.6 0.6 fusion.28
  11.4 0.3 fusion.359
  12.3 0.6 fusion.23
  14.0 0.6 fusion.18
  15.5 0.5 fusion.80
  17.0 0.5 fusion.75
  18.5 0.5 fusion.70
  19.9 0.5 fusion.65
  21.3 0.4 fusion.107
  21.7 1.5 %collective-permute-start.2 = (f32[3,32,512]{2,1,0:T(8,128)S(1)}, f32[3,32,512]{2,1,0:T(8,128)S(1)}, u32[]{:S(2)}, u32[]{:S(2)}) collective-permute-start(f32[3,32,512]{2,1,0:T(8,128)S(1)} %get-tuple-element.230), channel_id=1, source_target_pairs={{0,2},{2,4},{4,6},{6,8},{8,10},{10,12},{12,14},{14,16},{16,18},{18... | collective-permute-start | bytes 589832 | tf_op jit(solution)/shard_map/ppermute | solution.py:30
  23.2 0.9 %collective-permute-done.2 = f32[3,32,512]{2,1,0:T(8,128)S(1)} collective-permute-done((f32[3,32,512]{2,1,0:T(8,128)S(1)}, f32[3,32,512]{2,1,0:T(8,128)S(1)}, u32[]{:S(2)}, u32[]{:S(2)}) %collective-permute-start.2) | collective-permute-done | bytes 196640 | tf_op jit(solution)/shard_map/ppermute | solution.py:30
  24.1 1.8 %collective-permute-start.3 = (f32[2,3,8,512]{3,2,1,0:T(8,128)S(1)}, f32[2,3,8,512]{3,2,1,0:T(8,128)S(1)}, u32[]{:S(2)}, u32[]{:S(2)}) collective-permute-start(f32[2,3,8,512]{3,2,1,0:T(8,128)S(1)} %get-tuple-element.228), channel_id=1, source_target_pairs={{0,1},{1,0},{2,3},{3,2},{4,5},{5,4},{6,7},{7,6},{8,9},{9,8},{10,11... | collective-permute-start | bytes 294920 | tf_op jit(solution)/shard_map/ppermute | solution.py:19
  25.9 0.3 collective-permute-start.4
  26.2 2.6 %collective-permute-done.3 = f32[2,3,8,512]{3,2,1,0:T(8,128)S(1)} collective-permute-done((f32[2,3,8,512]{3,2,1,0:T(8,128)S(1)}, f32[2,3,8,512]{3,2,1,0:T(8,128)S(1)}, u32[]{:S(2)}, u32[]{:S(2)}) %collective-permute-start.3) | collective-permute-done | bytes 98336 | tf_op jit(solution)/shard_map/ppermute | solution.py:19
  28.8 1.7 %collective-permute-done.4 = f32[2,3,8,512]{3,2,1,0:T(8,128)S(1)} collective-permute-done((f32[2,3,8,512]{3,2,1,0:T(8,128)S(1)}, f32[2,3,8,512]{3,2,1,0:T(8,128)S(1)}, u32[]{:S(2)}, u32[]{:S(2)}) %collective-permute-start.4) | collective-permute-done | bytes 98336 | tf_op jit(solution)/shard_map/ppermute | solution.py:22
  31.7 0.6 fusion.13
  33.4 0.6 fusion.8
  35.1 0.6 fusion.3
  36.6 0.5 fusion.60
  38.1 0.5 fusion.55
  39.6 0.5 fusion.50
  41.0 0.5 fusion.45
  42.4 0.4 fusion.102
  42.8 1.1 %copy.443 = f32[2,3,32,512]{3,1,0,2:T(4,128)} copy(f32[2,3,32,512]{3,2,1,0:T(8,128)S(1)} %fusion.102) | data formatting | bytes 786432 | tf_op jit(solution)/shard_map/sub | solution.py:83
  43.9 10.6 %all-to-all-start = ((f32[2,3,32,512]{3,1,0,2:T(4,128)}), f32[2,3,32,512]{3,1,0,2:T(4,128)S(1)}, u32[]{:S(2)}, u32[]{:S(2)}) async-start(f32[2,3,32,512]{3,1,0,2:T(4,128)} %copy.443), calls=%async_computation | async-start | bytes 1048576 | tf_op jit(solution)/shard_map/all_to_all | solution.py:84
  54.5 0.8 %pad_maximum_fusion.33 = f32[2,3,32,512]{3,2,1,0:T(8,128)} fusion(f32[1,3,32,512]{3,2,1,0:T(8,128)S(1)} %get-tuple-element.231, f32[1,3,32,512]{3,2,1,0:T(8,128)S(1)} %fusion.185), kind=kLoop, calls=%fused_computation.191 | loop fusion | flops 98304 | bytes 786432 | tf_op jit(solution)/shard_map/concatenate | solution.py:81
  55.2 13.7 %all-to-all-done = f32[2,3,32,512]{3,1,0,2:T(4,128)S(1)} async-done(((f32[2,3,32,512]{3,1,0,2:T(4,128)}), f32[2,3,32,512]{3,1,0,2:T(4,128)S(1)}, u32[]{:S(2)}, u32[]{:S(2)}) %all-to-all-start) | async-done | bytes 393248 | tf_op jit(solution)/shard_map/all_to_all | solution.py:84
  68.9 1.1 %copy.444 = f32[16,2,3,2,512]{4,3,2,1,0:T(2,128)} copy(f32[16,2,3,2,512]{4,2,1,3,0:T(4,128)S(1)} %bitcast.12) | data formatting | bytes 786432 | tf_op jit(solution)/shard_map/all_to_all | solution.py:84
  (120 shorter events, 15.8 us)
Async XLA Ops:
  0.6 7.5 %copy-start = (f32[2,3,32,512]{3,2,1,0:T(8,128)S(1)}, f32[2,3,32,512]{3,2,1,0:T(8,128)}, u32[]{:S(2)}) copy-start(f32[2,3,32,512]{3,2,1,0:T(8,128)} %param.1) | copy-start | bytes 1179652
  1.6 6.5 %collective-permute-start = (f32[2,3,8,512]{3,2,1,0:T(8,128)S(1)}, f32[2,3,8,512]{3,2,1,0:T(8,128)S(1)}, u32[]{:S(2)}, u32[]{:S(2)}) collective-permute-start(f32[2,3,8,512]{3,2,1,0:T(8,128)S(1)} %get-tuple-element.233), channel_id=1, source_target_pairs={{0,1},{1,0},{2,3},{3,2},{4,5},{5,4},{6,7},{7,6},{8,9},{9,8},{10,11... | collective-permute-start | bytes 294920 | tf_op jit(solution)/shard_map/ppermute | solution.py:19
  4.7 4.9 %collective-permute-start.1 = (f32[2,3,8,512]{3,2,1,0:T(8,128)S(1)}, f32[2,3,8,512]{3,2,1,0:T(8,128)S(1)}, u32[]{:S(2)}, u32[]{:S(2)}) collective-permute-start(f32[2,3,8,512]{3,2,1,0:T(8,128)S(1)} %get-tuple-element.232), channel_id=1, source_target_pairs={{1,0},{0,1},{3,2},{2,3},{5,4},{4,5},{7,6},{6,7},{9,8},{8,9},{11,10... | collective-permute-start | bytes 294920 | tf_op jit(solution)/shard_map/ppermute | solution.py:22
  21.7 2.4 %collective-permute-start.2 = (f32[3,32,512]{2,1,0:T(8,128)S(1)}, f32[3,32,512]{2,1,0:T(8,128)S(1)}, u32[]{:S(2)}, u32[]{:S(2)}) collective-permute-start(f32[3,32,512]{2,1,0:T(8,128)S(1)} %get-tuple-element.230), channel_id=1, source_target_pairs={{0,2},{2,4},{4,6},{6,8},{8,10},{10,12},{12,14},{14,16},{16,18},{18... | collective-permute-start | bytes 589832 | tf_op jit(solution)/shard_map/ppermute | solution.py:30
  24.1 4.7 %collective-permute-start.3 = (f32[2,3,8,512]{3,2,1,0:T(8,128)S(1)}, f32[2,3,8,512]{3,2,1,0:T(8,128)S(1)}, u32[]{:S(2)}, u32[]{:S(2)}) collective-permute-start(f32[2,3,8,512]{3,2,1,0:T(8,128)S(1)} %get-tuple-element.228), channel_id=1, source_target_pairs={{0,1},{1,0},{2,3},{3,2},{4,5},{5,4},{6,7},{7,6},{8,9},{9,8},{10,11... | collective-permute-start | bytes 294920 | tf_op jit(solution)/shard_map/ppermute | solution.py:19
  25.9 4.6 %collective-permute-start.4 = (f32[2,3,8,512]{3,2,1,0:T(8,128)S(1)}, f32[2,3,8,512]{3,2,1,0:T(8,128)S(1)}, u32[]{:S(2)}, u32[]{:S(2)}) collective-permute-start(f32[2,3,8,512]{3,2,1,0:T(8,128)S(1)} %get-tuple-element.229), channel_id=1, source_target_pairs={{1,0},{0,1},{3,2},{2,3},{5,4},{4,5},{7,6},{6,7},{9,8},{8,9},{11,10... | collective-permute-start | bytes 294920 | tf_op jit(solution)/shard_map/ppermute | solution.py:22
  43.9 25.1 %all-to-all-start = ((f32[2,3,32,512]{3,1,0,2:T(4,128)}), f32[2,3,32,512]{3,1,0,2:T(4,128)S(1)}, u32[]{:S(2)}, u32[]{:S(2)}) async-start(f32[2,3,32,512]{3,1,0,2:T(4,128)} %copy.443), calls=%async_computation | async-start | bytes 1048576 | tf_op jit(solution)/shard_map/all_to_all | solution.py:84
where the time goes:
time: 70.2 us; the launch traced here: 70 us
  waiting for transfers between devices  23.6 us (34%)
  other arithmetic  19 us (27%)
  starting transfers between devices  17.2 us (25%)
  local copies, waits for them, and re-layouts  8.67 us (12%)
  between operations  1.4 us (2%)
    all_to_all x1, waiting for transfers between devices, on_device(): lax.all_to_all(residual, 'tm', split_axis=2, concat_axis=0, tiled=True)  13.7 us
    all_to_all x1, starting transfers between devices, on_device(): lax.all_to_all(residual, 'tm', split_axis=2, concat_axis=0, tiled=True)  10.6 us
    sub x15, other arithmetic, flux_step(): average - half_ratio * (column_flux(right_cells) - column_flux(left_cells))  7.43 us
    ppermute x2, waiting for transfers between devices, padded(): lax.ppermute(lax.slice_in_dim(block, block.shape[dim] - width, None, axis...  6 us
    ppermute x2, starting transfers between devices, padded(): lax.ppermute(lax.slice_in_dim(block, block.shape[dim] - width, None, axis...  4.81 us
    add x31, other arithmetic, column_flux(): east_flow * velocity + 0.5 * gravity * height * height  4.11 us
    mul x32, other arithmetic, column_flux(): north_flow * velocity  4.11 us
    slice x16, local copies, waits for them, and re-layouts, flux_step(): left_cells = jnp.roll(center, 1, axis=-1)  3.78 us
  transfers between devices with their start and end apart: 6, of which 6 were waited for; matrix products, arithmetic and copies ran while one was open for 1% of the time, Pallas kernels for 0%

commit v1 on v0

v1 whole, which is shorter than its diff:
```python
import functools

import jax
import jax.numpy as jnp
from jax import lax
from jax.experimental import pallas as pl
from jax.experimental.pallas import tpu as pltpu
from jax.sharding import PartitionSpec as P

FACTOR = 8
LANES = 128
SUB = 8

MOMENTUM = 0.4
PRESSURE = 0.08


def reciprocal(x):
    r = pl.reciprocal(x, approx=True)
    return r * (2.0 - x * r)


def row_terms(read, chunks, factor, lane):
    north, south, east, west = [], [], [], []
    for c in range(chunks):
        h, p, q = read(0, c), read(1, c), read(2, c)
        r = reciprocal(h)
        u = p * r
        pressure = h * h * factor
        a = p * u + pressure
        b = q * u
        d = q * (q * r) + pressure
        east.append((h - p, p - a, q - b))
        west.append((h + p, p + a, q + b))
        north.append((h - q, p - b, q - d))
        south.append((h + q, p + b, q + d))
    level = []
    for c in range(chunks):
        after, before = (c + 1) % chunks, (c - 1) % chunks
        fields = []
        for f in range(3):
            e = jnp.where(lane == 0, east[after][f], east[c][f])
            w = jnp.where(lane == LANES - 1, west[before][f], west[c][f])
            fields.append(pltpu.roll(e, LANES - 1, 1) + pltpu.roll(w, 1, 1))
        level.append(tuple(fields))
    return north, south, level


def step(src, dst, held, points, depth, chunks, factor):
    lane = lax.broadcasted_iota(jnp.int32, (SUB, LANES), 1)
    cells = [(f, c) for f in range(3) for c in range(chunks)]
    for k in range(points):
        partial = south_before = None
        for i in range(depth):
            north, south, level = row_terms(
                lambda f, c: src[k, f, i, c], chunks, factor, lane
            )
            for f, c in cells:
                if i == 0:
                    held[k, f, c] = pltpu.roll(north[c][f], SUB - 1, 0)
                else:
                    dst[k, f, i - 1, c] = partial[c][f] + north[c][f]
            if i == 0:
                partial = level
            else:
                partial = [
                    tuple(level[c][f] + south_before[c][f] for f in range(3)) for c in range(chunks)
                ]
            south_before = south
        for f, c in cells:
            dst[k, f, depth - 1, c] = partial[c][f] + held[k, f, c]
            dst[k, f, 0, c] = dst[k, f, 0, c] + pltpu.roll(south_before[c][f], 1, 0)


def fill(ext, points, chunks, pieces):
    for k in range(points):
        start = 0
        for piece in pieces[k]:
            rows = piece.shape[1]
            for f in range(3):
                for c in range(chunks):
                    ext[k, f, c, start : start + rows, :] = piece[f, :, c * LANES : (c + 1) * LANES]
            start += rows


def propagate(ext, state, held, points, chunks):
    depth = ext.shape[3] // SUB
    cells = [(k, f, c, i) for k in range(points) for f in range(3) for c in range(chunks) for i in range(depth)]
    for k, f, c, i in cells:
        value = ext.at[k, f, c][pl.ds(i, SUB, stride=depth), :]
        state[0, k, f, i, c] = value if f == 0 else MOMENTUM * value

    def two(_, factor):
        step(state.at[0], state.at[1], held, points, depth, chunks, factor)
        factor = factor * 0.25
        step(state.at[1], state.at[0], held, points, depth, chunks, factor)
        return factor * 0.25

    lax.fori_loop(0, FACTOR // 2, two, jnp.float32(PRESSURE))
    shrink = 0.25**FACTOR
    for k, f, c, i in cells:
        value = state[0, k, f, i, c] * (shrink if f == 0 else shrink / MOMENTUM)
        ext.at[k, f, c][pl.ds(i, SUB, stride=depth), :] = value


def advance_kernel(points, chunks, own, low, high, out, ext, state, held):
    fill(ext, points, chunks, [(low.at[k], own.at[k], high.at[k]) for k in range(points)])
    propagate(ext, state, held, points, chunks)
    rows = own.shape[2]
    for k in range(points):
        for f in range(3):
            for c in range(chunks):
                out[k, f, :, c * LANES : (c + 1) * LANES] = ext[k, f, c, FACTOR : FACTOR + rows, :]


def residual_kernel(points, chunks, own, low, high, advanced, out, ext, state, held):
    fill(ext, points, chunks, [(low.at[k], own.at[k], high.at[k]) for k in range(points)])
    propagate(ext, state, held, points, chunks)
    rows = own.shape[2]
    for k in range(points):
        for f in range(3):
            for c in range(chunks):
                span = slice(c * LANES, (c + 1) * LANES)
                out[k, f, :, span] = ext[k, f, c, FACTOR : FACTOR + rows, :] - advanced[k, f, :, span]


def call(kernel, own, *others):
    points, fields, rows, columns = own.shape
    chunks = columns // LANES
    extended = rows + 2 * FACTOR
    cost = pl.CostEstimate(
        flops=points * extended * columns * FACTOR * 45,
        bytes_accessed=4 * points * fields * extended * columns * 2,
        transcendentals=points * extended * columns * FACTOR,
    )
    return pl.pallas_call(
        functools.partial(kernel, points, chunks),
        out_shape=jax.ShapeDtypeStruct(own.shape, own.dtype),
        in_specs=[pl.BlockSpec(memory_space=pltpu.VMEM)] * (1 + len(others)),
        out_specs=pl.BlockSpec(memory_space=pltpu.VMEM),
        scratch_shapes=[
            pltpu.VMEM((points, fields, chunks, extended, LANES), jnp.float32),
            pltpu.VMEM((2, points, fields, extended // SUB, chunks, SUB, LANES), jnp.float32),
            pltpu.VMEM((points, fields, chunks, SUB, LANES), jnp.float32),
        ],
        compiler_params=pltpu.CompilerParams(vmem_limit_bytes=24 * 2**20),
        cost_estimate=cost,
    )(own, *others)


def halos(block):
    count = lax.axis_size("space")
    forward = [(i, (i + 1) % count) for i in range(count)]
    backward = [(target, source) for source, target in forward]
    last, first = block[..., -FACTOR:, :], block[..., :FACTOR, :]
    return lax.ppermute(last, "space", forward), lax.ppermute(first, "space", backward)


def from_behind(block, axis, distance):
    devices = range(lax.axis_size(axis))
    route = [(i - distance, i) for i in devices if i - distance in devices]
    return lax.ppermute(block, axis, route)


def on_device(c_points):
    leading = lax.axis_index("tm") == 0
    low, high = halos(c_points)
    advanced = call(advance_kernel, c_points, low, high)
    incoming = from_behind(advanced[-1], "tm", 1)
    opening = jnp.where(leading, c_points[0], incoming)
    updated = jnp.concatenate([opening[None], advanced[:-1]], axis=0)
    low, high = halos(updated)
    residual = call(residual_kernel, updated, low, high, advanced)
    coarse = lax.all_to_all(residual, "tm", split_axis=2, concat_axis=0, tiled=True)
    return (updated, coarse[:, :, None])


def solution(mesh):
    in_specs = (P("tm", None, "space", None),)
    out_specs = (P("tm", None, "space", None), P(None, None, "space", "tm", None))
    return jax.shard_map(
        on_device, mesh=mesh, in_specs=in_specs, out_specs=out_specs, check_vma=False
    )
```

time: 70.2 us -> 48.4 us (0.69)
  blocking collectives: 0 us -> 22.6 us
  other arithmetic: 19 us -> 0.07 us
  waiting for transfers between devices: 23.6 us -> 10.1 us
  starting transfers between devices: 17.2 us -> 6.47 us
  local copies, waits for them, and re-layouts: 8.67 us -> 2.3 us
  Pallas kernels: 0 us -> 5.88 us
    all_to_all x0 -> x1, blocking collectives: none -> 22.6 us  [on_device(): lax.all_to_all(residual, 'tm', split_axis=2, concat_axis=0, tiled=True)]
    all_to_all x1 -> x0, waiting for transfers between devices: 13.7 us -> none  [on_device(): lax.all_to_all(residual, 'tm', split_axis=2, concat_axis=0, tiled=True)]
    all_to_all x1 -> x0, starting transfers between devices: 10.6 us -> none  [on_device(): lax.all_to_all(residual, 'tm', split_axis=2, concat_axis=0, tiled=True)]
    sub x16 -> x0, other arithmetic: 7.85 us -> none  [the longest x15 7.43 us: flux_step(): average - half_ratio * (column_flux(right_cells) - column_flux(left_cells))]
    pallas_call x0 -> x2, Pallas kernels: none -> 5.88 us  [call(): pl.pallas_call(functools.partial(kernel, points, chunks), out_shape=jax.S...]
    slice x33 -> x1, local copies, waits for them, and re-layouts: 6.46 us -> 1 us  [halos(): last, first = (block[..., -FACTOR:, :], block[..., :FACTOR, :])]
    add x31 -> x0, other arithmetic: 4.11 us -> none  [column_flux(): east_flow * velocity + 0.5 * gravity * height * height]
    mul x32 -> x0, other arithmetic: 4.11 us -> none  [column_flux(): north_flow * velocity]
  transfers between devices with their start and end apart: 6 -> 5, of which waited for: 6 -> 5; matrix products, arithmetic and copies ran while one was open for 1% -> 0% of each run, Pallas kernels for 0% -> 0%
where the time goes in v1:
time: 48.4 us; the launch traced here: 48.2 us
  blocking collectives  22.6 us (47%)
  waiting for transfers between devices  10.1 us (21%)
  starting transfers between devices  6.47 us (13%)
  Pallas kernels  5.88 us (12%)
  local copies, waits for them, and re-layouts  2.3 us (5%)
  between operations  0.72 us (1%)
    all_to_all x1, blocking collectives, on_device(): lax.all_to_all(residual, 'tm', split_axis=2, concat_axis=0, tiled=True)  22.6 us
    ppermute x2, waiting for transfers between devices, halos(): lax.ppermute(last, 'space', forward)  5.96 us
    pallas_call x2, Pallas kernels, call(): pl.pallas_call(functools.partial(kernel, points, chunks), out_shape=jax.S...  5.88 us
    ppermute x2, starting transfers between devices, halos(): lax.ppermute(last, 'space', forward)  4.81 us
    ppermute x2, waiting for transfers between devices, halos(): lax.ppermute(first, 'space', backward)  3.15 us
    ppermute x1, starting transfers between devices, from_behind(): return lax.ppermute(block, axis, route)  1.3 us
    ppermute x1, waiting for transfers between devices, from_behind(): return lax.ppermute(block, axis, route)  1.04 us
    slice x1, local copies, waits for them, and re-layouts, halos(): last, first = (block[..., -FACTOR:, :], block[..., :FACTOR, :])  1 us
  transfers between devices with their start and end apart: 5, of which 5 were waited for; matrix products, arithmetic and copies ran while one was open for 0% of the time, Pallas kernels for 0%

profile of v1, /device:TPU:0, one launch (start us, length us, event | category | flops | bytes accessed | tf_op | source)
XLA Modules:
  0.0 48.2 jit_solution(3494731496669020730)
XLA Ops:
  0.6 0.0 copy-start.1
  0.6 1.0 %fusion.3 = (f32[2,3,8,512]{3,2,1,0:T(8,128)S(1)}, f32[2,3,8,512]{3,2,1,0:T(8,128)S(1)}) fusion(f32[2,3,32,512]{3,2,1,0:T(8,128)} %own.1), kind=kLoop, calls=%fused_computation.10 | loop fusion | bytes 393216 | tf_op jit(solution)/shard_map/slice | solution.py:155
  1.6 3.0 %collective-permute-start = (f32[2,3,8,512]{3,2,1,0:T(8,128)S(1)}, f32[2,3,8,512]{3,2,1,0:T(8,128)S(1)}, u32[]{:S(2)}, u32[]{:S(2)}) collective-permute-start(f32[2,3,8,512]{3,2,1,0:T(8,128)S(1)} %get-tuple-element.7), channel_id=1, source_target_pairs={{0,1},{1,0},{2,3},{3,2},{4,5},{5,4},{6,7},{7,6},{8,9},{9,8},{10,11... | collective-permute-start | bytes 294920 | tf_op jit(solution)/shard_map/ppermute | solution.py:156
  4.7 0.1 collective-permute-start.1
  4.7 3.4 %collective-permute-done.low = f32[2,3,8,512]{3,2,1,0:T(8,128)S(1)} collective-permute-done((f32[2,3,8,512]{3,2,1,0:T(8,128)S(1)}, f32[2,3,8,512]{3,2,1,0:T(8,128)S(1)}, u32[]{:S(2)}, u32[]{:S(2)}) %collective-permute-start) | collective-permute-done | bytes 98336 | tf_op jit(solution)/shard_map/ppermute | solution.py:156
  8.1 1.4 %collective-permute-done.1.high = f32[2,3,8,512]{3,2,1,0:T(8,128)S(1)} collective-permute-done((f32[2,3,8,512]{3,2,1,0:T(8,128)S(1)}, f32[2,3,8,512]{3,2,1,0:T(8,128)S(1)}, u32[]{:S(2)}, u32[]{:S(2)}) %collective-permute-start.1) | collective-permute-done | bytes 98336 | tf_op jit(solution)/shard_map/ppermute | solution.py:156
  9.6 0.0 copy-done.1
  9.6 2.9 %shard_map.30.advanced = f32[2,3,32,512]{3,2,1,0:T(8,128)S(1)} custom-call(f32[2,3,32,512]{3,2,1,0:T(8,128)S(1)} %copy-done.1, f32[2,3,8,512]{3,2,1,0:T(8,128)S(1)} %collective-permute-done.low, f32[2,3,8,512]{3,2,1,0:T(8,128)S(1)} %collective-permute-done.1.high), custom_call_target="tpu_custom_call" | custom-call | flops 17694720 | bytes 1179648 | tf_op jit(solution)/shard_map/pallas_call | solution.py:136
  12.5 1.3 %collective-permute-start.2 = (f32[3,32,512]{2,1,0:T(8,128)S(1)}, f32[3,32,512]{2,1,0:T(8,128)S(1)}, u32[]{:S(2)}, u32[]{:S(2)}) collective-permute-start(f32[3,32,512]{2,1,0:T(8,128)S(1)} %get-tuple-element.4), channel_id=1, source_target_pairs={{0,2},{2,4},{4,6},{6,8},{8,10},{10,12},{12,14},{14,16},{16,18},{18... | collective-permute-start | bytes 589832 | tf_op jit(solution)/shard_map/ppermute | solution.py:162
  13.8 1.0 %collective-permute-done.2 = f32[3,32,512]{2,1,0:T(8,128)S(1)} collective-permute-done((f32[3,32,512]{2,1,0:T(8,128)S(1)}, f32[3,32,512]{2,1,0:T(8,128)S(1)}, u32[]{:S(2)}, u32[]{:S(2)}) %collective-permute-start.2) | collective-permute-done | bytes 196640 | tf_op jit(solution)/shard_map/ppermute | solution.py:162
  14.9 1.8 %collective-permute-start.3 = (f32[2,3,8,512]{3,2,1,0:T(8,128)S(1)}, f32[2,3,8,512]{3,2,1,0:T(8,128)S(1)}, u32[]{:S(2)}, u32[]{:S(2)}) collective-permute-start(f32[2,3,8,512]{3,2,1,0:T(8,128)S(1)} %get-tuple-element.3), channel_id=1, source_target_pairs={{0,1},{1,0},{2,3},{3,2},{4,5},{5,4},{6,7},{7,6},{8,9},{9,8},{10,11... | collective-permute-start | bytes 294920 | tf_op jit(solution)/shard_map/ppermute | solution.py:156
  16.7 0.3 collective-permute-start.4
  17.1 0.0 copy-start
  17.1 2.5 %collective-permute-done.3.low = f32[2,3,8,512]{3,2,1,0:T(8,128)S(1)} collective-permute-done((f32[2,3,8,512]{3,2,1,0:T(8,128)S(1)}, f32[2,3,8,512]{3,2,1,0:T(8,128)S(1)}, u32[]{:S(2)}, u32[]{:S(2)}) %collective-permute-start.3) | collective-permute-done | bytes 98336 | tf_op jit(solution)/shard_map/ppermute | solution.py:156
  19.6 1.7 %collective-permute-done.4.high = f32[2,3,8,512]{3,2,1,0:T(8,128)S(1)} collective-permute-done((f32[2,3,8,512]{3,2,1,0:T(8,128)S(1)}, f32[2,3,8,512]{3,2,1,0:T(8,128)S(1)}, u32[]{:S(2)}, u32[]{:S(2)}) %collective-permute-start.4) | collective-permute-done | bytes 98336 | tf_op jit(solution)/shard_map/ppermute | solution.py:156
  21.4 2.9 %shard_map.31 = f32[2,3,32,512]{3,2,1,0:T(8,128)S(1)} custom-call(f32[2,3,32,512]{3,2,1,0:T(8,128)S(1)} %pad_maximum_fusion.own, f32[2,3,8,512]{3,2,1,0:T(8,128)S(1)} %collective-permute-done.3.low, f32[2,3,8,512]{3,2,1,0:T(8,128)S(1)} %collective-permute-done.4.high, f32[2,3,32,512]{3,2,1,0:T(8,128)S(1)} %shard_map.30.advanced), custom_call_target="tpu_custom_call" | custom-call | flops 17694720 | bytes 1179648 | tf_op jit(solution)/shard_map/pallas_call | solution.py:136
  24.3 0.0 copy-done
  24.3 0.3 copy.6
  24.6 22.6 %all_to_all.15 = f32[2,3,32,512]{3,0,1,2:T(2,128)S(1)} all-to-all(f32[2,3,32,512]{3,0,1,2:T(2,128)S(1)} %copy.6), channel_id=1, replica_groups=mesh['tm'=16,'space'=2] {'tm'}, dimensions={2} | all-to-all | bytes 786432 | tf_op jit(solution)/shard_map/all_to_all | solution.py:174
  47.2 0.9 %copy.7 = f32[16,2,3,2,512]{4,3,2,1,0:T(2,128)} copy(f32[16,2,3,2,512]{4,1,2,3,0:T(2,128)S(1)} %bitcast.12) | data formatting | bytes 786432 | tf_op jit(solution)/shard_map/all_to_all | solution.py:174
  (4 shorter events, 0.1 us)
Async XLA Ops:
  0.6 8.9 %copy-start.1 = (f32[2,3,32,512]{3,2,1,0:T(8,128)S(1)}, f32[2,3,32,512]{3,2,1,0:T(8,128)}, u32[]{:S(2)}) copy-start(f32[2,3,32,512]{3,2,1,0:T(8,128)} %own.1) | copy-start | bytes 1179652
  1.6 6.5 %collective-permute-start = (f32[2,3,8,512]{3,2,1,0:T(8,128)S(1)}, f32[2,3,8,512]{3,2,1,0:T(8,128)S(1)}, u32[]{:S(2)}, u32[]{:S(2)}) collective-permute-start(f32[2,3,8,512]{3,2,1,0:T(8,128)S(1)} %get-tuple-element.7), channel_id=1, source_target_pairs={{0,1},{1,0},{2,3},{3,2},{4,5},{5,4},{6,7},{7,6},{8,9},{9,8},{10,11... | collective-permute-start | bytes 294920 | tf_op jit(solution)/shard_map/ppermute | solution.py:156
  4.7 4.9 %collective-permute-start.1 = (f32[2,3,8,512]{3,2,1,0:T(8,128)S(1)}, f32[2,3,8,512]{3,2,1,0:T(8,128)S(1)}, u32[]{:S(2)}, u32[]{:S(2)}) collective-permute-start(f32[2,3,8,512]{3,2,1,0:T(8,128)S(1)} %get-tuple-element.6), channel_id=1, source_target_pairs={{1,0},{0,1},{3,2},{2,3},{5,4},{4,5},{7,6},{6,7},{9,8},{8,9},{11,10... | collective-permute-start | bytes 294920 | tf_op jit(solution)/shard_map/ppermute | solution.py:156
  12.5 2.4 %collective-permute-start.2 = (f32[3,32,512]{2,1,0:T(8,128)S(1)}, f32[3,32,512]{2,1,0:T(8,128)S(1)}, u32[]{:S(2)}, u32[]{:S(2)}) collective-permute-start(f32[3,32,512]{2,1,0:T(8,128)S(1)} %get-tuple-element.4), channel_id=1, source_target_pairs={{0,2},{2,4},{4,6},{6,8},{8,10},{10,12},{12,14},{14,16},{16,18},{18... | collective-permute-start | bytes 589832 | tf_op jit(solution)/shard_map/ppermute | solution.py:162
  14.9 4.7 %collective-permute-start.3 = (f32[2,3,8,512]{3,2,1,0:T(8,128)S(1)}, f32[2,3,8,512]{3,2,1,0:T(8,128)S(1)}, u32[]{:S(2)}, u32[]{:S(2)}) collective-permute-start(f32[2,3,8,512]{3,2,1,0:T(8,128)S(1)} %get-tuple-element.3), channel_id=1, source_target_pairs={{0,1},{1,0},{2,3},{3,2},{4,5},{5,4},{6,7},{7,6},{8,9},{9,8},{10,11... | collective-permute-start | bytes 294920 | tf_op jit(solution)/shard_map/ppermute | solution.py:156
  16.7 4.6 %collective-permute-start.4 = (f32[2,3,8,512]{3,2,1,0:T(8,128)S(1)}, f32[2,3,8,512]{3,2,1,0:T(8,128)S(1)}, u32[]{:S(2)}, u32[]{:S(2)}) collective-permute-start(f32[2,3,8,512]{3,2,1,0:T(8,128)S(1)} %get-tuple-element.2), channel_id=1, source_target_pairs={{1,0},{0,1},{3,2},{2,3},{5,4},{4,5},{7,6},{6,7},{9,8},{8,9},{11,10... | collective-permute-start | bytes 294920 | tf_op jit(solution)/shard_map/ppermute | solution.py:156
  17.1 7.3 %copy-start = (f32[2,3,32,512]{3,2,1,0:T(8,128)}, f32[2,3,32,512]{3,2,1,0:T(8,128)S(1)}, u32[]{:S(2)}) copy-start(f32[2,3,32,512]{3,2,1,0:T(8,128)S(1)} %pad_maximum_fusion.own) | copy-start | bytes 1179652

commit v2 on v1

--- a/solution.py
+++ b/solution.py
@@ -103,76 +103,176 @@
         ext.at[k, f, c][pl.ds(i, SUB, stride=depth), :] = value
 
 
-def advance_kernel(points, chunks, own, low, high, out, ext, state, held):
-    fill(ext, points, chunks, [(low.at[k], own.at[k], high.at[k]) for k in range(points)])
+def edges_of(block):
+    return jnp.stack([block[..., -FACTOR:, :], block[..., :FACTOR, :]])
+
+
+def spans(chunks):
+    return [slice(c * LANES, (c + 1) * LANES) for c in range(chunks)]
+
+
+def advance_kernel(points, chunks, own, halo, out, last, near, far, ext, state, held):
+    fill(ext, points, chunks, [(halo.at[0, k], own.at[k], halo.at[1, k]) for k in range(points)])
     propagate(ext, state, held, points, chunks)
     rows = own.shape[2]
     for k in range(points):
+        target, edge = (last, far) if k == points - 1 else (out.at[k], near.at[:, k])
         for f in range(3):
-            for c in range(chunks):
-                out[k, f, :, c * LANES : (c + 1) * LANES] = ext[k, f, c, FACTOR : FACTOR + rows, :]
-
-
-def residual_kernel(points, chunks, own, low, high, advanced, out, ext, state, held):
-    fill(ext, points, chunks, [(low.at[k], own.at[k], high.at[k]) for k in range(points)])
+            for c, span in enumerate(spans(chunks)):
+                target[f, :, span] = ext[k, f, c, FACTOR : FACTOR + rows, :]
+                edge[0, f, :, span] = ext[k, f, c, rows : FACTOR + rows, :]
+                edge[1, f, :, span] = ext[k, f, c, FACTOR : 2 * FACTOR, :]
+
+
+def residual_kernel(
+    points, chunks, groups, start, start_halo, incoming, incoming_halo, advanced, near, last, *rest
+):
+    messages, (ext, state, held, packed) = rest[:-4], rest[-4:]
+    me = lax.axis_index("tm")
+
+    @pl.when(me == 0)
+    def _():
+        fill(ext, 1, chunks, [(start_halo.at[0, 0], start.at[0], start_halo.at[1, 0])])
+
+    @pl.when(me > 0)
+    def _():
+        fill(ext, 1, chunks, [(incoming_halo.at[0], incoming, incoming_halo.at[1])])
+
+    fill(
+        ext.at[pl.ds(1, points - 1)],
+        points - 1,
+        chunks,
+        [(near.at[0, k], advanced.at[k], near.at[1, k]) for k in range(points - 1)],
+    )
     propagate(ext, state, held, points, chunks)
-    rows = own.shape[2]
-    for k in range(points):
+    rows = last.shape[1]
+    share = rows // groups
+    for k in range(points):
+        before = last if k == points - 1 else advanced.at[k]
         for f in range(3):
-            for c in range(chunks):
-                span = slice(c * LANES, (c + 1) * LANES)
-                out[k, f, :, span] = ext[k, f, c, FACTOR : FACTOR + rows, :] - advanced[k, f, :, span]
-
-
-def call(kernel, own, *others):
-    points, fields, rows, columns = own.shape
+            for c, span in enumerate(spans(chunks)):
+                value = ext[k, f, c, FACTOR : FACTOR + rows, :] - before[f, :, span]
+                ext[k, f, c, FACTOR : FACTOR + rows, :] = value
+                for g in range(groups):
+                    base = FACTOR + g * share
+                    packed[g, k, f, :, span] = ext[k, f, c, base : base + share, :]
+    for d, message in enumerate(messages):
+        message[...] = packed[target_of(me, d, groups)]
+
+
+def target_of(i, d, count):
+    return i ^ d if count & (count - 1) == 0 else (i + d) % count
+
+
+def source_of(i, d, count):
+    return i ^ d if count & (count - 1) == 0 else (i - d) % count
+
+
+def gather_kernel(points, groups, *refs):
+    messages, out, sems = refs[:-2], refs[-2], refs[-1]
+    me = lax.axis_index("tm")
+    copies = []
+    for d, message in enumerate(messages):
+        place = source_of(me, d, groups) * points
+        copies.append(
+            pltpu.make_async_copy(message, out.at[pl.ds(place, points), :, 0], sems.at[d])
+        )
+    for copy in copies:
+        copy.start()
+    for copy in copies:
+        copy.wait()
+
+
+VMEM = pl.BlockSpec(memory_space=pltpu.VMEM)
+
+
+def call(kernel, shapes, points, rows, columns, operands, extra=()):
     chunks = columns // LANES
     extended = rows + 2 * FACTOR
     cost = pl.CostEstimate(
         flops=points * extended * columns * FACTOR * 45,
-        bytes_accessed=4 * points * fields * extended * columns * 2,
+        bytes_accessed=4 * points * 3 * extended * columns * 2,
         transcendentals=points * extended * columns * FACTOR,
     )
     return pl.pallas_call(
         functools.partial(kernel, points, chunks),
-        out_shape=jax.ShapeDtypeStruct(own.shape, own.dtype),
-        in_specs=[pl.BlockSpec(memory_space=pltpu.VMEM)] * (1 + len(others)),
-        out_specs=pl.BlockSpec(memory_space=pltpu.VMEM),
+        out_shape=[jax.ShapeDtypeStruct(shape, jnp.float32) for shape in shapes],
+        in_specs=[VMEM] * len(operands),
+        out_specs=[VMEM] * len(shapes),
         scratch_shapes=[
-            pltpu.VMEM((points, fields, chunks, extended, LANES), jnp.float32),
-            pltpu.VMEM((2, points, fields, extended // SUB, chunks, SUB, LANES), jnp.float32),
-            pltpu.VMEM((points, fields, chunks, SUB, LANES), jnp.float32),
+            pltpu.VMEM((points, 3, chunks, extended, LANES), jnp.float32),
+            pltpu.VMEM((2, points, 3, extended // SUB, chunks, SUB, LANES), jnp.float32),
+            pltpu.VMEM((points, 3, chunks, SUB, LANES), jnp.float32),
+            *extra,
         ],
         compiler_params=pltpu.CompilerParams(vmem_limit_bytes=24 * 2**20),
         cost_estimate=cost,
-    )(own, *others)
-
-
-def halos(block):
-    count = lax.axis_size("space")
-    forward = [(i, (i + 1) % count) for i in range(count)]
-    backward = [(target, source) for source, target in forward]
-    last, first = block[..., -FACTOR:, :], block[..., :FACTOR, :]
-    return lax.ppermute(last, "space", forward), lax.ppermute(first, "space", backward)
-
-
-def from_behind(block, axis, distance):
-    devices = range(lax.axis_size(axis))
-    route = [(i - distance, i) for i in devices if i - distance in devices]
-    return lax.ppermute(block, axis, route)
+    )(*operands)
+
+
+def exchange(edges, shift):
+    groups, strips = lax.axis_size("tm"), lax.axis_size("space")
+
+    def route(move):
+        return [
+            (t * strips + s, (t + shift) * strips + (s + move) % strips)
+            for t in range(groups - shift)
+            for s in range(strips)
+        ]
+
+    both = ("tm", "space")
+    if strips == 2:
+        return lax.ppermute(edges, both, route(1))
+    return jnp.stack(
+        [lax.ppermute(edges[0], both, route(1)), lax.ppermute(edges[1], both, route(-1))]
+    )
 
 
 def on_device(c_points):
-    leading = lax.axis_index("tm") == 0
-    low, high = halos(c_points)
-    advanced = call(advance_kernel, c_points, low, high)
-    incoming = from_behind(advanced[-1], "tm", 1)
-    opening = jnp.where(leading, c_points[0], incoming)
-    updated = jnp.concatenate([opening[None], advanced[:-1]], axis=0)
-    low, high = halos(updated)
-    residual = call(residual_kernel, updated, low, high, advanced)
-    coarse = lax.all_to_all(residual, "tm", split_axis=2, concat_axis=0, tiled=True)
-    return (updated, coarse[:, :, None])
+    points, fields, rows, columns = c_points.shape
+    groups = lax.axis_size("tm")
+    share = rows // groups
+    start_halo = exchange(edges_of(c_points), 0)
+    advanced, last, near, far = call(
+        advance_kernel,
+        [
+            (points - 1, fields, rows, columns),
+            (fields, rows, columns),
+            (2, points - 1, fields, FACTOR, columns),
+            (2, fields, FACTOR, columns),
+        ],
+        points,
+        rows,
+        columns,
+        (c_points, start_halo),
+    )
+    incoming_halo = exchange(far, 1)
+    incoming = lax.ppermute(last, "tm", [(i, i + 1) for i in range(groups - 1)])
+    near = exchange(near, 0)
+    opening = jnp.where(lax.axis_index("tm") == 0, c_points[0], incoming)
+    updated = jnp.concatenate([opening[None], advanced], axis=0)
+    packet = (points, fields, share, columns)
+    messages = call(
+        lambda p, c, *refs: residual_kernel(p, c, groups, *refs),
+        [packet] * groups,
+        points,
+        rows,
+        columns,
+        (c_points, start_halo, incoming, incoming_halo, advanced, near, last),
+        extra=[pltpu.VMEM((groups, *packet), jnp.float32)],
+    )
+    arrived = [messages[0]]
+    for d in range(1, groups):
+        route = [(i, target_of(i, d, groups)) for i in range(groups)]
+        arrived.append(lax.ppermute(messages[d], "tm", route))
+    coarse = pl.pallas_call(
+        functools.partial(gather_kernel, points, groups),
+        out_shape=jax.ShapeDtypeStruct((groups * points, fields, 1, share, columns), jnp.float32),
+        in_specs=[VMEM] * groups,
+        out_specs=pl.BlockSpec(memory_space=pl.ANY),
+        scratch_shapes=[pltpu.SemaphoreType.DMA((groups,))],
+    )(*arrived)
+    return (updated, coarse)
 
 
 def solution(mesh):

time: 48.4 us -> 56.5 us (1.17)
  starting transfers between devices: 6.47 us -> 31 us
  blocking collectives: 22.6 us -> 0 us
  waiting for transfers between devices: 10.1 us -> 13.5 us
  Pallas kernels: 5.88 us -> 7.88 us
  other arithmetic: 0.07 us -> 0.82 us
    ppermute x5 -> x19, starting transfers between devices: 6.47 us -> 31 us  [the longest x15 20.6 us: on_device(): arrived.append(lax.ppermute(messages[d], 'tm', route))]
    all_to_all x1 -> x0, blocking collectives: 22.6 us -> none  [on_device(): lax.all_to_all(residual, 'tm', split_axis=2, concat_axis=0, tiled=True)]
    ppermute x5 -> x19, waiting for transfers between devices: 10.1 us -> 13.5 us  [the longest x3 9.74 us: exchange(): return lax.ppermute(edges, both, route(1))]
    pallas_call x2 -> x3, Pallas kernels: 5.88 us -> 7.88 us  [the longest x2 6.07 us: call(): pl.pallas_call(functools.partial(kernel, points, chunks), out_shape=[jax....]
    unnamed x4 -> x34, local copies, waits for them, and re-layouts: 0.01 us -> 1.23 us
    another operation x0 -> x1, local copies, waits for them, and re-layouts: none -> 1.01 us  [edges_of(): return jnp.stack([block[..., -FACTOR:, :], block[..., :FACTOR, :]])]
    slice x1 -> x0, local copies, waits for them, and re-layouts: 1 us -> none  [halos(): last, first = (block[..., -FACTOR:, :], block[..., :FACTOR, :])]
    all_to_all x1 -> x0, local copies, waits for them, and re-layouts: 0.95 us -> none  [on_device(): lax.all_to_all(residual, 'tm', split_axis=2, concat_axis=0, tiled=True)]
  transfers between devices with their start and end apart: 5 -> 19, of which waited for: 5 -> 6; matrix products, arithmetic and copies ran while one was open for 0% -> 1% of each run, Pallas kernels for 0% -> 0%
where the time goes in v2:
time: 56.5 us; the launch traced here: 56.3 us
  starting transfers between devices  31 us (55%)
  waiting for transfers between devices  13.5 us (24%)
  Pallas kernels  7.88 us (14%)
  local copies, waits for them, and re-layouts  2.24 us (4%)
  between operations  0.85 us (2%)
  other arithmetic  0.82 us (1%)
    ppermute x15, starting transfers between devices, on_device(): arrived.append(lax.ppermute(messages[d], 'tm', route))  20.6 us
    ppermute x3, waiting for transfers between devices, exchange(): return lax.ppermute(edges, both, route(1))  9.74 us
    ppermute x3, starting transfers between devices, exchange(): return lax.ppermute(edges, both, route(1))  9.1 us
    pallas_call x2, Pallas kernels, call(): pl.pallas_call(functools.partial(kernel, points, chunks), out_shape=[jax....  6.07 us
    ppermute x15, waiting for transfers between devices, on_device(): arrived.append(lax.ppermute(messages[d], 'tm', route))  3.71 us
    pallas_call x1, Pallas kernels, on_device(): pl.pallas_call(functools.partial(gather_kernel, points, groups), out_shap...  1.81 us
    ppermute x1, starting transfers between devices, on_device(): incoming = lax.ppermute(last, 'tm', [(i, i + 1) for i in range(groups - 1)])  1.3 us
    unnamed x34, local copies, waits for them, and re-layouts  1.23 us
  transfers between devices with their start and end apart: 19, of which 6 were waited for; matrix products, arithmetic and copies ran while one was open for 1% of the time, Pallas kernels for 0%

profile of v2, /device:TPU:0, one launch (start us, length us, event | category | flops | bytes accessed | tf_op | source)
XLA Modules:
  0.0 56.3 jit_solution(15856680043550212084)
XLA Ops:
  0.6 1.0 %slice_bitcast_fusion.1 = (f32[1,2,3,8,512]{4,3,2,1,0:T(8,128)S(1)}, f32[1,2,3,8,512]{4,3,2,1,0:T(8,128)S(1)}) fusion(f32[2,3,32,512]{3,2,1,0:T(8,128)} %refs_0_.1), kind=kLoop, calls=%fused_computation.5 | loop fusion | bytes 393216 | tf_op jit(solution)/shard_map/stack | solution.py:107
  1.7 3.0 %collective-permute-start = (f32[2,2,3,8,512]{4,3,2,1,0:T(8,128)S(1)}, f32[2,2,3,8,512]{4,3,2,1,0:T(8,128)S(1)}, u32[]{:S(2)}, u32[]{:S(2)}) collective-permute-start(f32[2,2,3,8,512]{4,3,2,1,0:T(8,128)S(1)} %pad_maximum_fusion.1), channel_id=1, source_target_pairs={{0,1},{1,0},{2,3},{3,2},{4,5},{5,4},{6,7},{7,6},{8,9},{9,8},{10,11... | collective-permute-start | bytes 589832 | tf_op jit(solution)/shard_map/ppermute | solution.py:225
  4.7 4.9 %collective-permute-done.halo.refs_1_ = f32[2,2,3,8,512]{4,3,2,1,0:T(8,128)S(1)} collective-permute-done((f32[2,2,3,8,512]{4,3,2,1,0:T(8,128)S(1)}, f32[2,2,3,8,512]{4,3,2,1,0:T(8,128)S(1)}, u32[]{:S(2)}, u32[]{:S(2)}) %collective-permute-start) | collective-permute-done | bytes 196640 | tf_op jit(solution)/shard_map/ppermute | solution.py:225
  9.6 2.9 %shard_map.30 = (f32[1,3,32,512]{3,2,1,0:T(8,128)S(1)}, f32[3,32,512]{2,1,0:T(8,128)S(1)}, f32[2,1,3,8,512]{4,3,2,1,0:T(8,128)S(1)}, f32[2,3,8,512]{3,2,1,0:T(8,128)S(1)}) custom-call(f32[2,3,32,512]{3,2,1,0:T(8,128)S(1)} %copy-done, f32[2,2,3,8,512]{4,3,2,1,0:T(8,128)S(1)} %collective-permute-done.halo.refs_1_), custom_call_target="tpu_custom_call" | custom-call | flops 17694720 | bytes 1179648 | tf_op jit(solution)/shard_map/pallas_call | solution.py:197
  12.5 1.3 %collective-permute-start.1 = (f32[3,32,512]{2,1,0:T(8,128)S(1)}, f32[3,32,512]{2,1,0:T(8,128)S(1)}, u32[]{:S(2)}, u32[]{:S(2)}) collective-permute-start(f32[3,32,512]{2,1,0:T(8,128)S(1)} %get-tuple-element.22.refs_6_), channel_id=1, source_target_pairs={{0,2},{2,4},{4,6},{6,8},{8,10},{10,12},{12,14},{14,16},{16,18},{18... | collective-permute-start | bytes 589832 | tf_op jit(solution)/shard_map/ppermute | solution.py:250
  13.8 5.5 %collective-permute-start.2 = (f32[2,3,8,512]{3,2,1,0:T(8,128)S(1)}, f32[2,3,8,512]{3,2,1,0:T(8,128)S(1)}, u32[]{:S(2)}, u32[]{:S(2)}) collective-permute-start(f32[2,3,8,512]{3,2,1,0:T(8,128)S(1)} %get-tuple-element.24), channel_id=1, source_target_pairs={{0,3},{1,2},{2,5},{3,4},{4,7},{5,6},{6,9},{7,8},{8,11},{9,10},{10,... | collective-permute-start | bytes 294920 | tf_op jit(solution)/shard_map/ppermute | solution.py:225
  19.3 0.6 %collective-permute-start.3 = (f32[2,1,3,8,512]{4,3,2,1,0:T(8,128)S(1)}, f32[2,1,3,8,512]{4,3,2,1,0:T(8,128)S(1)}, u32[]{:S(2)}, u32[]{:S(2)}) collective-permute-start(f32[2,1,3,8,512]{4,3,2,1,0:T(8,128)S(1)} %get-tuple-element.25), channel_id=1, source_target_pairs={{0,1},{1,0},{2,3},{3,2},{4,5},{5,4},{6,7},{7,6},{8,9},{9,8},{10,11... | collective-permute-start | bytes 294920 | tf_op jit(solution)/shard_map/ppermute | solution.py:225
  19.9 2.5 %collective-permute-done.2.refs_3_ = f32[2,3,8,512]{3,2,1,0:T(8,128)S(1)} collective-permute-done((f32[2,3,8,512]{3,2,1,0:T(8,128)S(1)}, f32[2,3,8,512]{3,2,1,0:T(8,128)S(1)}, u32[]{:S(2)}, u32[]{:S(2)}) %collective-permute-start.2) | collective-permute-done | bytes 98336 | tf_op jit(solution)/shard_map/ppermute | solution.py:225
  22.5 2.3 %collective-permute-done.3.refs_5_ = f32[2,1,3,8,512]{4,3,2,1,0:T(8,128)S(1)} collective-permute-done((f32[2,1,3,8,512]{4,3,2,1,0:T(8,128)S(1)}, f32[2,1,3,8,512]{4,3,2,1,0:T(8,128)S(1)}, u32[]{:S(2)}, u32[]{:S(2)}) %collective-permute-start.3) | collective-permute-done | bytes 98336 | tf_op jit(solution)/shard_map/ppermute | solution.py:225
  24.8 0.0 collective-permute-done.1.refs_2_
  24.8 3.1 %shard_map.31 = (f32[2,3,2,512]{3,2,1,0:T(2,128)S(1)}, f32[2,3,2,512]{3,2,1,0:T(2,128)S(1)}, f32[2,3,2,512]{3,2,1,0:T(2,128)S(1)}, f32[2,3,2,512]{3,2,1,0:T(2,12...) custom-call(f32[2,3,32,512]{3,2,1,0:T(8,128)S(1)} %copy-done, ...), custom_call_target="tpu_custom_call" | custom-call | flops 17694720 | bytes 1179648 | tf_op jit(solution)/shard_map/pallas_call | solution.py:197
  27.9 0.6 %copy-done.1 = f32[2,3,2,512]{3,2,1,0:T(2,128)} copy-done((f32[2,3,2,512]{3,2,1,0:T(2,128)}, f32[2,3,2,512]{3,2,1,0:T(2,128)S(1)}, u32[]{:S(2)}) %copy-start.1) | copy-done | bytes 24600
  28.5 1.4 %collective-permute-start.10 = (f32[2,3,2,512]{3,2,1,0:T(2,128)S(1)}, f32[2,3,2,512]{3,2,1,0:T(2,128)S(1)}, u32[]{:S(2)}, u32[]{:S(2)}) collective-permute-start(f32[2,3,2,512]{3,2,1,0:T(2,128)S(1)} %get-tuple-element.33), channel_id=1, source_target_pairs={{0,14},{2,12},{4,10},{6,8},{8,6},{10,4},{12,2},{14,0},{16,30},{18,... | collective-permute-start | bytes 73736 | tf_op jit(solution)/shard_map/ppermute | solution.py:267
  29.9 1.2 %collective-permute-start.11 = (f32[2,3,2,512]{3,2,1,0:T(2,128)S(1)}, f32[2,3,2,512]{3,2,1,0:T(2,128)S(1)}, u32[]{:S(2)}, u32[]{:S(2)}) collective-permute-start(f32[2,3,2,512]{3,2,1,0:T(2,128)S(1)} %get-tuple-element.34), channel_id=1, source_target_pairs={{0,16},{2,18},{4,20},{6,22},{8,24},{10,26},{12,28},{14,30},{16,0},... | collective-permute-start | bytes 73736 | tf_op jit(solution)/shard_map/ppermute | solution.py:267
  31.1 2.4 %collective-permute-start.12 = (f32[2,3,2,512]{3,2,1,0:T(2,128)S(1)}, f32[2,3,2,512]{3,2,1,0:T(2,128)S(1)}, u32[]{:S(2)}, u32[]{:S(2)}) collective-permute-start(f32[2,3,2,512]{3,2,1,0:T(2,128)S(1)} %get-tuple-element.35), channel_id=1, source_target_pairs={{0,18},{2,16},{4,22},{6,20},{8,26},{10,24},{12,30},{14,28},{16,2},... | collective-permute-start | bytes 73736 | tf_op jit(solution)/shard_map/ppermute | solution.py:267
  33.5 2.5 %collective-permute-start.13 = (f32[2,3,2,512]{3,2,1,0:T(2,128)S(1)}, f32[2,3,2,512]{3,2,1,0:T(2,128)S(1)}, u32[]{:S(2)}, u32[]{:S(2)}) collective-permute-start(f32[2,3,2,512]{3,2,1,0:T(2,128)S(1)} %get-tuple-element.36), channel_id=1, source_target_pairs={{0,20},{2,22},{4,16},{6,18},{8,28},{10,30},{12,24},{14,26},{16,4},... | collective-permute-start | bytes 73736 | tf_op jit(solution)/shard_map/ppermute | solution.py:267
  36.0 0.2 collective-permute-start.14
  36.1 2.5 %collective-permute-start.15 = (f32[2,3,2,512]{3,2,1,0:T(2,128)S(1)}, f32[2,3,2,512]{3,2,1,0:T(2,128)S(1)}, u32[]{:S(2)}, u32[]{:S(2)}) collective-permute-start(f32[2,3,2,512]{3,2,1,0:T(2,128)S(1)} %get-tuple-element.38), channel_id=1, source_target_pairs={{0,24},{2,26},{4,28},{6,30},{8,16},{10,18},{12,20},{14,22},{16,8},... | collective-permute-start | bytes 73736 | tf_op jit(solution)/shard_map/ppermute | solution.py:267
  38.6 2.0 %collective-permute-start.16 = (f32[2,3,2,512]{3,2,1,0:T(2,128)S(1)}, f32[2,3,2,512]{3,2,1,0:T(2,128)S(1)}, u32[]{:S(2)}, u32[]{:S(2)}) collective-permute-start(f32[2,3,2,512]{3,2,1,0:T(2,128)S(1)} %get-tuple-element.39), channel_id=1, source_target_pairs={{0,26},{2,24},{4,30},{6,28},{8,18},{10,16},{12,22},{14,20},{16,10}... | collective-permute-start | bytes 73736 | tf_op jit(solution)/shard_map/ppermute | solution.py:267
  40.6 2.4 %collective-permute-start.17 = (f32[2,3,2,512]{3,2,1,0:T(2,128)S(1)}, f32[2,3,2,512]{3,2,1,0:T(2,128)S(1)}, u32[]{:S(2)}, u32[]{:S(2)}) collective-permute-start(f32[2,3,2,512]{3,2,1,0:T(2,128)S(1)} %get-tuple-element.40), channel_id=1, source_target_pairs={{0,28},{2,30},{4,24},{6,26},{8,20},{10,22},{12,16},{14,18},{16,12}... | collective-permute-start | bytes 73736 | tf_op jit(solution)/shard_map/ppermute | solution.py:267
  42.9 1.2 %collective-permute-start.18 = (f32[2,3,2,512]{3,2,1,0:T(2,128)S(1)}, f32[2,3,2,512]{3,2,1,0:T(2,128)S(1)}, u32[]{:S(2)}, u32[]{:S(2)}) collective-permute-start(f32[2,3,2,512]{3,2,1,0:T(2,128)S(1)} %get-tuple-element.41), channel_id=1, source_target_pairs={{0,30},{2,28},{4,26},{6,24},{8,22},{10,20},{12,18},{14,16},{16,14}... | collective-permute-start | bytes 73736 | tf_op jit(solution)/shard_map/ppermute | solution.py:267
  44.1 1.3 %collective-permute-start.4 = (f32[2,3,2,512]{3,2,1,0:T(2,128)S(1)}, f32[2,3,2,512]{3,2,1,0:T(2,128)S(1)}, u32[]{:S(2)}, u32[]{:S(2)}) collective-permute-start(f32[2,3,2,512]{3,2,1,0:T(2,128)S(1)} %get-tuple-element.27), channel_id=1, source_target_pairs={{0,2},{2,0},{4,6},{6,4},{8,10},{10,8},{12,14},{14,12},{16,18},{18,... | collective-permute-start | bytes 73736 | tf_op jit(solution)/shard_map/ppermute | solution.py:267
  45.5 0.5 collective-permute-start.5
  46.1 1.4 %collective-permute-start.6 = (f32[2,3,2,512]{3,2,1,0:T(2,128)S(1)}, f32[2,3,2,512]{3,2,1,0:T(2,128)S(1)}, u32[]{:S(2)}, u32[]{:S(2)}) collective-permute-start(f32[2,3,2,512]{3,2,1,0:T(2,128)S(1)} %get-tuple-element.29), channel_id=1, source_target_pairs={{0,6},{2,4},{4,2},{6,0},{8,14},{10,12},{12,10},{14,8},{16,22},{18,... | collective-permute-start | bytes 73736 | tf_op jit(solution)/shard_map/ppermute | solution.py:267
  47.4 1.5 %collective-permute-done.18.refs_15_ = f32[2,3,2,512]{3,2,1,0:T(2,128)S(1)} collective-permute-done((f32[2,3,2,512]{3,2,1,0:T(2,128)S(1)}, f32[2,3,2,512]{3,2,1,0:T(2,128)S(1)}, u32[]{:S(2)}, u32[]{:S(2)}) %collective-permute-start.18) | collective-permute-done | bytes 24608 | tf_op jit(solution)/shard_map/ppermute | solution.py:267
  48.9 0.2 collective-permute-start.8
  49.1 1.7 %collective-permute-start.9 = (f32[2,3,2,512]{3,2,1,0:T(2,128)S(1)}, f32[2,3,2,512]{3,2,1,0:T(2,128)S(1)}, u32[]{:S(2)}, u32[]{:S(2)}) collective-permute-start(f32[2,3,2,512]{3,2,1,0:T(2,128)S(1)} %get-tuple-element.32), channel_id=1, source_target_pairs={{0,12},{2,14},{4,8},{6,10},{8,4},{10,6},{12,0},{14,2},{16,28},{18,... | collective-permute-start | bytes 73736 | tf_op jit(solution)/shard_map/ppermute | solution.py:267
  50.8 0.8 %pad_maximum_fusion = f32[2,3,32,512]{3,2,1,0:T(8,128)} fusion(f32[1,3,32,512]{3,2,1,0:T(8,128)S(1)} %get-tuple-element.23.refs_4_, f32[1,3,32,512]{3,2,1,0:T(8,128)S(1)} %fusion), kind=kLoop, calls=%fused_computation | loop fusion | flops 98304 | bytes 786432 | tf_op jit(solution)/shard_map/concatenate | solution.py:253
  51.7 0.5 collective-permute-done.8.refs_5_
  52.2 1.7 %collective-permute-done.9.refs_6_ = f32[2,3,2,512]{3,2,1,0:T(2,128)S(1)} collective-permute-done((f32[2,3,2,512]{3,2,1,0:T(2,128)S(1)}, f32[2,3,2,512]{3,2,1,0:T(2,128)S(1)}, u32[]{:S(2)}, u32[]{:S(2)}) %collective-permute-start.9) | collective-permute-done | bytes 24608 | tf_op jit(solution)/shard_map/ppermute | solution.py:267
  53.9 0.6 %copy-done.16 = f32[2,3,2,512]{3,2,1,0:T(2,128)} copy-done((f32[2,3,2,512]{3,2,1,0:T(2,128)}, f32[2,3,2,512]{3,2,1,0:T(2,128)S(1)}, u32[]{:S(2)}) %copy-start.16) | copy-done | bytes 24600
  54.5 1.8 %shard_map.32 = f32[32,3,1,2,512]{4,3,2,1,0:T(2,128)} custom-call(f32[2,3,2,512]{3,2,1,0:T(2,128)} %copy-done.1, f32[2,3,2,512]{3,2,1,0:T(2,128)} %copy-done.11, f32[2,3,2,512]{3,2,1,0:T(2,128)} %copy-done.12, f32[2,3,2,512]{3,2,1,0:T(2,128)} %copy-done.13, f32[2,3,2,512]{3,2,1,0:T(2,128)} %copy-done.14, f32[2,3,2,512]{3,2,1,0:T(2,128)} %copy-done.15, ...), custom_call_target="tpu_custom_call" | custom-call | tf_op jit(solution)/shard_map/pallas_call | solution.py:268
  (47 shorter events, 0.1 us)
Async XLA Ops:
  0.6 8.9 %copy-start = (f32[2,3,32,512]{3,2,1,0:T(8,128)S(1)}, f32[2,3,32,512]{3,2,1,0:T(8,128)}, u32[]{:S(2)}) copy-start(f32[2,3,32,512]{3,2,1,0:T(8,128)} %refs_0_.1) | copy-start | bytes 1179652
  1.7 7.9 %collective-permute-start = (f32[2,2,3,8,512]{4,3,2,1,0:T(8,128)S(1)}, f32[2,2,3,8,512]{4,3,2,1,0:T(8,128)S(1)}, u32[]{:S(2)}, u32[]{:S(2)}) collective-permute-start(f32[2,2,3,8,512]{4,3,2,1,0:T(8,128)S(1)} %pad_maximum_fusion.1), channel_id=1, source_target_pairs={{0,1},{1,0},{2,3},{3,2},{4,5},{5,4},{6,7},{7,6},{8,9},{9,8},{10,11... | collective-permute-start | bytes 589832 | tf_op jit(solution)/shard_map/ppermute | solution.py:225
  12.5 12.3 %collective-permute-start.1 = (f32[3,32,512]{2,1,0:T(8,128)S(1)}, f32[3,32,512]{2,1,0:T(8,128)S(1)}, u32[]{:S(2)}, u32[]{:S(2)}) collective-permute-start(f32[3,32,512]{2,1,0:T(8,128)S(1)} %get-tuple-element.22.refs_6_), channel_id=1, source_target_pairs={{0,2},{2,4},{4,6},{6,8},{8,10},{10,12},{12,14},{14,16},{16,18},{18... | collective-permute-start | bytes 589832 | tf_op jit(solution)/shard_map/ppermute | solution.py:250
  13.8 8.6 %collective-permute-start.2 = (f32[2,3,8,512]{3,2,1,0:T(8,128)S(1)}, f32[2,3,8,512]{3,2,1,0:T(8,128)S(1)}, u32[]{:S(2)}, u32[]{:S(2)}) collective-permute-start(f32[2,3,8,512]{3,2,1,0:T(8,128)S(1)} %get-tuple-element.24), channel_id=1, source_target_pairs={{0,3},{1,2},{2,5},{3,4},{4,7},{5,6},{6,9},{7,8},{8,11},{9,10},{10,... | collective-permute-start | bytes 294920 | tf_op jit(solution)/shard_map/ppermute | solution.py:225
  19.3 5.4 %collective-permute-start.3 = (f32[2,1,3,8,512]{4,3,2,1,0:T(8,128)S(1)}, f32[2,1,3,8,512]{4,3,2,1,0:T(8,128)S(1)}, u32[]{:S(2)}, u32[]{:S(2)}) collective-permute-start(f32[2,1,3,8,512]{4,3,2,1,0:T(8,128)S(1)} %get-tuple-element.25), channel_id=1, source_target_pairs={{0,1},{1,0},{2,3},{3,2},{4,5},{5,4},{6,7},{7,6},{8,9},{9,8},{10,11... | collective-permute-start | bytes 294920 | tf_op jit(solution)/shard_map/ppermute | solution.py:225
  28.5 7.6 %collective-permute-start.10 = (f32[2,3,2,512]{3,2,1,0:T(2,128)S(1)}, f32[2,3,2,512]{3,2,1,0:T(2,128)S(1)}, u32[]{:S(2)}, u32[]{:S(2)}) collective-permute-start(f32[2,3,2,512]{3,2,1,0:T(2,128)S(1)} %get-tuple-element.33), channel_id=1, source_target_pairs={{0,14},{2,12},{4,10},{6,8},{8,6},{10,4},{12,2},{14,0},{16,30},{18,... | collective-permute-start | bytes 73736 | tf_op jit(solution)/shard_map/ppermute | solution.py:267
  29.9 8.7 %collective-permute-start.11 = (f32[2,3,2,512]{3,2,1,0:T(2,128)S(1)}, f32[2,3,2,512]{3,2,1,0:T(2,128)S(1)}, u32[]{:S(2)}, u32[]{:S(2)}) collective-permute-start(f32[2,3,2,512]{3,2,1,0:T(2,128)S(1)} %get-tuple-element.34), channel_id=1, source_target_pairs={{0,16},{2,18},{4,20},{6,22},{8,24},{10,26},{12,28},{14,30},{16,0},... | collective-permute-start | bytes 73736 | tf_op jit(solution)/shard_map/ppermute | solution.py:267
  31.1 9.5 %collective-permute-start.12 = (f32[2,3,2,512]{3,2,1,0:T(2,128)S(1)}, f32[2,3,2,512]{3,2,1,0:T(2,128)S(1)}, u32[]{:S(2)}, u32[]{:S(2)}) collective-permute-start(f32[2,3,2,512]{3,2,1,0:T(2,128)S(1)} %get-tuple-element.35), channel_id=1, source_target_pairs={{0,18},{2,16},{4,22},{6,20},{8,26},{10,24},{12,30},{14,28},{16,2},... | collective-permute-start | bytes 73736 | tf_op jit(solution)/shard_map/ppermute | solution.py:267
  33.5 9.5 %collective-permute-start.13 = (f32[2,3,2,512]{3,2,1,0:T(2,128)S(1)}, f32[2,3,2,512]{3,2,1,0:T(2,128)S(1)}, u32[]{:S(2)}, u32[]{:S(2)}) collective-permute-start(f32[2,3,2,512]{3,2,1,0:T(2,128)S(1)} %get-tuple-element.36), channel_id=1, source_target_pairs={{0,20},{2,22},{4,16},{6,18},{8,28},{10,30},{12,24},{14,26},{16,4},... | collective-permute-start | bytes 73736 | tf_op jit(solution)/shard_map/ppermute | solution.py:267
  36.0 8.2 %collective-permute-start.14 = (f32[2,3,2,512]{3,2,1,0:T(2,128)S(1)}, f32[2,3,2,512]{3,2,1,0:T(2,128)S(1)}, u32[]{:S(2)}, u32[]{:S(2)}) collective-permute-start(f32[2,3,2,512]{3,2,1,0:T(2,128)S(1)} %get-tuple-element.37), channel_id=1, source_target_pairs={{0,22},{2,20},{4,18},{6,16},{8,30},{10,28},{12,26},{14,24},{16,6},... | collective-permute-start | bytes 73736 | tf_op jit(solution)/shard_map/ppermute | solution.py:267
  36.1 9.3 %copy-start.2 = (f32[2,3,2,512]{3,2,1,0:T(2,128)}, f32[2,3,2,512]{3,2,1,0:T(2,128)S(1)}, u32[]{:S(2)}) copy-start(f32[2,3,2,512]{3,2,1,0:T(2,128)S(1)} %collective-permute-done.10.refs_7_) | copy-start | bytes 73732
  36.1 9.4 %collective-permute-start.15 = (f32[2,3,2,512]{3,2,1,0:T(2,128)S(1)}, f32[2,3,2,512]{3,2,1,0:T(2,128)S(1)}, u32[]{:S(2)}, u32[]{:S(2)}) collective-permute-start(f32[2,3,2,512]{3,2,1,0:T(2,128)S(1)} %get-tuple-element.38), channel_id=1, source_target_pairs={{0,24},{2,26},{4,28},{6,30},{8,16},{10,18},{12,20},{14,22},{16,8},... | collective-permute-start | bytes 73736 | tf_op jit(solution)/shard_map/ppermute | solution.py:267
  38.6 6.9 %copy-start.3 = (f32[2,3,2,512]{3,2,1,0:T(2,128)}, f32[2,3,2,512]{3,2,1,0:T(2,128)S(1)}, u32[]{:S(2)}) copy-start(f32[2,3,2,512]{3,2,1,0:T(2,128)S(1)} %collective-permute-done.11.refs_8_) | copy-start | bytes 73732
  38.6 7.4 %collective-permute-start.16 = (f32[2,3,2,512]{3,2,1,0:T(2,128)S(1)}, f32[2,3,2,512]{3,2,1,0:T(2,128)S(1)}, u32[]{:S(2)}, u32[]{:S(2)}) collective-permute-start(f32[2,3,2,512]{3,2,1,0:T(2,128)S(1)} %get-tuple-element.39), channel_id=1, source_target_pairs={{0,26},{2,24},{4,30},{6,28},{8,18},{10,16},{12,22},{14,20},{16,10}... | collective-permute-start | bytes 73736 | tf_op jit(solution)/shard_map/ppermute | solution.py:267
  40.6 4.9 %copy-start.4 = (f32[2,3,2,512]{3,2,1,0:T(2,128)}, f32[2,3,2,512]{3,2,1,0:T(2,128)S(1)}, u32[]{:S(2)}) copy-start(f32[2,3,2,512]{3,2,1,0:T(2,128)S(1)} %collective-permute-done.12.refs_9_) | copy-start | bytes 73732
  40.6 6.8 %collective-permute-start.17 = (f32[2,3,2,512]{3,2,1,0:T(2,128)S(1)}, f32[2,3,2,512]{3,2,1,0:T(2,128)S(1)}, u32[]{:S(2)}, u32[]{:S(2)}) collective-permute-start(f32[2,3,2,512]{3,2,1,0:T(2,128)S(1)} %get-tuple-element.40), channel_id=1, source_target_pairs={{0,28},{2,30},{4,24},{6,26},{8,20},{10,22},{12,16},{14,18},{16,12}... | collective-permute-start | bytes 73736 | tf_op jit(solution)/shard_map/ppermute | solution.py:267
  42.9 2.6 %copy-start.5 = (f32[2,3,2,512]{3,2,1,0:T(2,128)}, f32[2,3,2,512]{3,2,1,0:T(2,128)S(1)}, u32[]{:S(2)}) copy-start(f32[2,3,2,512]{3,2,1,0:T(2,128)S(1)} %collective-permute-done.13.refs_10_) | copy-start | bytes 73732
  42.9 6.0 %collective-permute-start.18 = (f32[2,3,2,512]{3,2,1,0:T(2,128)S(1)}, f32[2,3,2,512]{3,2,1,0:T(2,128)S(1)}, u32[]{:S(2)}, u32[]{:S(2)}) collective-permute-start(f32[2,3,2,512]{3,2,1,0:T(2,128)S(1)} %get-tuple-element.41), channel_id=1, source_target_pairs={{0,30},{2,28},{4,26},{6,24},{8,22},{10,20},{12,18},{14,16},{16,14}... | collective-permute-start | bytes 73736 | tf_op jit(solution)/shard_map/ppermute | solution.py:267
  44.1 5.0 %collective-permute-start.4 = (f32[2,3,2,512]{3,2,1,0:T(2,128)S(1)}, f32[2,3,2,512]{3,2,1,0:T(2,128)S(1)}, u32[]{:S(2)}, u32[]{:S(2)}) collective-permute-start(f32[2,3,2,512]{3,2,1,0:T(2,128)S(1)} %get-tuple-element.27), channel_id=1, source_target_pairs={{0,2},{2,0},{4,6},{6,4},{8,10},{10,8},{12,14},{14,12},{16,18},{18,... | collective-permute-start | bytes 73736 | tf_op jit(solution)/shard_map/ppermute | solution.py:267
  45.5 6.0 %copy-start.7 = (f32[2,3,2,512]{3,2,1,0:T(2,128)}, f32[2,3,2,512]{3,2,1,0:T(2,128)S(1)}, u32[]{:S(2)}) copy-start(f32[2,3,2,512]{3,2,1,0:T(2,128)S(1)} %collective-permute-done.15.refs_12_) | copy-start | bytes 73732
  45.5 6.1 %collective-permute-start.5 = (f32[2,3,2,512]{3,2,1,0:T(2,128)S(1)}, f32[2,3,2,512]{3,2,1,0:T(2,128)S(1)}, u32[]{:S(2)}, u32[]{:S(2)}) collective-permute-start(f32[2,3,2,512]{3,2,1,0:T(2,128)S(1)} %get-tuple-element.28), channel_id=1, source_target_pairs={{0,4},{2,6},{4,0},{6,2},{8,12},{10,14},{12,8},{14,10},{16,20},{18,... | collective-permute-start | bytes 73736 | tf_op jit(solution)/shard_map/ppermute | solution.py:267
  46.1 5.5 %copy-start.8 = (f32[2,3,2,512]{3,2,1,0:T(2,128)}, f32[2,3,2,512]{3,2,1,0:T(2,128)S(1)}, u32[]{:S(2)}) copy-start(f32[2,3,2,512]{3,2,1,0:T(2,128)S(1)} %collective-permute-done.16.refs_13_) | copy-start | bytes 73732
  46.1 5.6 %collective-permute-start.6 = (f32[2,3,2,512]{3,2,1,0:T(2,128)S(1)}, f32[2,3,2,512]{3,2,1,0:T(2,128)S(1)}, u32[]{:S(2)}, u32[]{:S(2)}) collective-permute-start(f32[2,3,2,512]{3,2,1,0:T(2,128)S(1)} %get-tuple-element.29), channel_id=1, source_target_pairs={{0,6},{2,4},{4,2},{6,0},{8,14},{10,12},{12,10},{14,8},{16,22},{18,... | collective-permute-start | bytes 73736 | tf_op jit(solution)/shard_map/ppermute | solution.py:267
  47.4 4.2 %copy-start.9 = (f32[2,3,2,512]{3,2,1,0:T(2,128)}, f32[2,3,2,512]{3,2,1,0:T(2,128)S(1)}, u32[]{:S(2)}) copy-start(f32[2,3,2,512]{3,2,1,0:T(2,128)S(1)} %collective-permute-done.17.refs_14_) | copy-start | bytes 73732
  47.4 4.2 %collective-permute-start.7 = (f32[2,3,2,512]{3,2,1,0:T(2,128)S(1)}, f32[2,3,2,512]{3,2,1,0:T(2,128)S(1)}, u32[]{:S(2)}, u32[]{:S(2)}) collective-permute-start(f32[2,3,2,512]{3,2,1,0:T(2,128)S(1)} %get-tuple-element.30), channel_id=1, source_target_pairs={{0,8},{2,10},{4,12},{6,14},{8,0},{10,2},{12,4},{14,6},{16,24},{18,... | collective-permute-start | bytes 73736 | tf_op jit(solution)/shard_map/ppermute | solution.py:267
  48.9 2.7 %copy-start.10 = (f32[2,3,2,512]{3,2,1,0:T(2,128)}, f32[2,3,2,512]{3,2,1,0:T(2,128)S(1)}, u32[]{:S(2)}) copy-start(f32[2,3,2,512]{3,2,1,0:T(2,128)S(1)} %collective-permute-done.18.refs_15_) | copy-start | bytes 73732
  48.9 3.3 %collective-permute-start.8 = (f32[2,3,2,512]{3,2,1,0:T(2,128)S(1)}, f32[2,3,2,512]{3,2,1,0:T(2,128)S(1)}, u32[]{:S(2)}, u32[]{:S(2)}) collective-permute-start(f32[2,3,2,512]{3,2,1,0:T(2,128)S(1)} %get-tuple-element.31), channel_id=1, source_target_pairs={{0,10},{2,8},{4,14},{6,12},{8,2},{10,0},{12,6},{14,4},{16,26},{18,... | collective-permute-start | bytes 73736 | tf_op jit(solution)/shard_map/ppermute | solution.py:267
  49.1 2.5 %copy-start.11 = (f32[2,3,2,512]{3,2,1,0:T(2,128)}, f32[2,3,2,512]{3,2,1,0:T(2,128)S(1)}, u32[]{:S(2)}) copy-start(f32[2,3,2,512]{3,2,1,0:T(2,128)S(1)} %collective-permute-done.4.refs_1_) | copy-start | bytes 73732
  49.1 4.7 %collective-permute-start.9 = (f32[2,3,2,512]{3,2,1,0:T(2,128)S(1)}, f32[2,3,2,512]{3,2,1,0:T(2,128)S(1)}, u32[]{:S(2)}, u32[]{:S(2)}) collective-permute-start(f32[2,3,2,512]{3,2,1,0:T(2,128)S(1)} %get-tuple-element.32), channel_id=1, source_target_pairs={{0,12},{2,14},{4,8},{6,10},{8,4},{10,6},{12,0},{14,2},{16,28},{18,... | collective-permute-start | bytes 73736 | tf_op jit(solution)/shard_map/ppermute | solution.py:267
  51.6 2.2 %copy-start.12 = (f32[2,3,2,512]{3,2,1,0:T(2,128)}, f32[2,3,2,512]{3,2,1,0:T(2,128)S(1)}, u32[]{:S(2)}) copy-start(f32[2,3,2,512]{3,2,1,0:T(2,128)S(1)} %collective-permute-done.5.refs_2_) | copy-start | bytes 73732
  51.6 2.2 %copy-start.13 = (f32[2,3,2,512]{3,2,1,0:T(2,128)}, f32[2,3,2,512]{3,2,1,0:T(2,128)S(1)}, u32[]{:S(2)}) copy-start(f32[2,3,2,512]{3,2,1,0:T(2,128)S(1)} %collective-permute-done.6.refs_3_) | copy-start | bytes 73732
  51.7 2.2 %copy-start.14 = (f32[2,3,2,512]{3,2,1,0:T(2,128)}, f32[2,3,2,512]{3,2,1,0:T(2,128)S(1)}, u32[]{:S(2)}) copy-start(f32[2,3,2,512]{3,2,1,0:T(2,128)S(1)} %collective-permute-done.7.refs_4_) | copy-start | bytes 73732
  (4 other events, 4.3 us)

commit v3 on v1

v3 whole, which is shorter than its diff:
```python
import functools

import jax
import jax.numpy as jnp
from jax import lax
from jax.experimental import pallas as pl
from jax.experimental.pallas import tpu as pltpu
from jax.sharding import PartitionSpec as P

FACTOR = 8
LANES = 128
SUB = 8

MOMENTUM = 0.4
PRESSURE = 0.08


def reciprocal(x):
    r = pl.reciprocal(x, approx=True)
    return r * (2.0 - x * r)


def row_terms(read, chunks, factor, lane):
    north, south, east, west = [], [], [], []
    for c in range(chunks):
        h, p, q = read(0, c), read(1, c), read(2, c)
        r = reciprocal(h)
        u = p * r
        pressure = h * h * factor
        a = p * u + pressure
        b = q * u
        d = q * (q * r) + pressure
        east.append((h - p, p - a, q - b))
        west.append((h + p, p + a, q + b))
        north.append((h - q, p - b, q - d))
        south.append((h + q, p + b, q + d))
    level = []
    for c in range(chunks):
        after, before = (c + 1) % chunks, (c - 1) % chunks
        fields = []
        for f in range(3):
            e = jnp.where(lane == 0, east[after][f], east[c][f])
            w = jnp.where(lane == LANES - 1, west[before][f], west[c][f])
            fields.append(pltpu.roll(e, LANES - 1, 1) + pltpu.roll(w, 1, 1))
        level.append(tuple(fields))
    return north, south, level


def step(src, dst, held, depth, chunks, factor):
    lane = lax.broadcasted_iota(jnp.int32, (SUB, LANES), 1)
    cells = [(f, c) for f in range(3) for c in range(chunks)]
    partial = south_before = None
    for i in range(depth):
        north, south, level = row_terms(lambda f, c: src[f, i, c], chunks, factor, lane)
        for f, c in cells:
            if i == 0:
                held[f, c] = pltpu.roll(north[c][f], SUB - 1, 0)
            else:
                dst[f, i - 1, c] = partial[c][f] + north[c][f]
        if i == 0:
            partial = level
        else:
            partial = [
                tuple(level[c][f] + south_before[c][f] for f in range(3)) for c in range(chunks)
            ]
        south_before = south
    for f, c in cells:
        dst[f, depth - 1, c] = partial[c][f] + held[f, c]
        dst[f, 0, c] = dst[f, 0, c] + pltpu.roll(south_before[c][f], 1, 0)


def spans(chunks):
    return [slice(c * LANES, (c + 1) * LANES) for c in range(chunks)]


def fill(ext, base, chunks, pieces):
    for piece in pieces:
        rows = piece.shape[1]
        for f in range(3):
            for c, span in enumerate(spans(chunks)):
                ext[f, c, base : base + rows, :] = piece[f, :, span]
        base += rows


def propagate(scratch, base, rows, chunks):
    ext, state, held = scratch
    depth = rows // SUB
    cells = [(f, c, i) for f in range(3) for c in range(chunks) for i in range(depth)]
    for f, c, i in cells:
        value = ext.at[f, c][pl.ds(base + i, SUB, stride=depth), :]
        state[0, f, i, c] = value if f == 0 else MOMENTUM * value

    def two(_, factor):
        step(state.at[0], state.at[1], held, depth, chunks, factor)
        factor = factor * 0.25
        step(state.at[1], state.at[0], held, depth, chunks, factor)
        return factor * 0.25

    lax.fori_loop(0, FACTOR // 2, two, jnp.float32(PRESSURE))
    shrink = 0.25**FACTOR
    for f, c, i in cells:
        value = state[0, f, i, c] * (shrink if f == 0 else shrink / MOMENTUM)
        ext.at[f, c][pl.ds(base + i, SUB, stride=depth), :] = value


def take(target, ext, rows, chunks):
    for f in range(3):
        for c, span in enumerate(spans(chunks)):
            target[f, :, span] = ext[f, c, 2 * FACTOR : 2 * FACTOR + rows, :]


def own_kernel(chunks, own, halo, advanced, pushed, *scratch):
    rows, ext = own.shape[2], scratch[0]
    for k in range(advanced.shape[0]):
        fill(ext, 0, chunks, [halo.at[0, k], own.at[k], halo.at[1, k]])
        propagate(scratch, 0, rows + 4 * FACTOR, chunks)
        take(advanced.at[k], ext, rows, chunks)
        propagate(scratch, FACTOR, rows + 2 * FACTOR, chunks)
        take(pushed.at[k], ext, rows, chunks)


def edge_kernel(
    chunks, groups, own, halo, behind, behind_halo, last_halo, advanced, pushed, updated, packed, *scratch
):
    points, _, rows, _ = own.shape
    share = rows // groups
    ext = scratch[0]

    def pack(k, difference):
        for f in range(3):
            for c, span in enumerate(spans(chunks)):
                ext[f, c, 2 * FACTOR : 2 * FACTOR + rows, :] = difference(
                    ext[f, c, 2 * FACTOR : 2 * FACTOR + rows, :], f, span
                )
                for g in range(groups):
                    start = 2 * FACTOR + g * share
                    packed[g, k, f, :, span] = ext[f, c, start : start + share, :]

    fill(ext, 0, chunks, [behind_halo.at[0], behind, behind_halo.at[1]])
    propagate(scratch, 0, rows + 4 * FACTOR, chunks)

    @pl.when(lax.axis_index("tm") == 0)
    def _():
        fill(ext, 0, chunks, [halo.at[0, 0], own.at[0], halo.at[1, 0]])

    take(updated.at[0], ext, rows, chunks)
    for k in range(points - 1):
        updated[k + 1] = advanced[k]
    propagate(scratch, FACTOR, rows + 2 * FACTOR, chunks)
    pack(0, lambda value, f, span: value - advanced[0, f, :, span])
    for k in range(1, points - 1):
        pack(k, lambda _, f, span: pushed[k - 1, f, :, span] - advanced[k, f, :, span])
    fill(ext, FACTOR, chunks, [last_halo.at[0], own.at[points - 1], last_halo.at[1]])
    propagate(scratch, FACTOR, rows + 2 * FACTOR, chunks)
    pack(points - 1, lambda value, f, span: pushed[points - 2, f, :, span] - value)


VMEM = pl.BlockSpec(memory_space=pltpu.VMEM)


def call(kernel, shapes, work, rows, columns, operands):
    chunks = columns // LANES
    extended = rows + 4 * FACTOR
    cost = pl.CostEstimate(
        flops=work * extended * columns * FACTOR * 45,
        bytes_accessed=4 * work * 3 * extended * columns,
        transcendentals=work * extended * columns * FACTOR,
    )
    return pl.pallas_call(
        functools.partial(kernel, chunks),
        out_shape=[jax.ShapeDtypeStruct(shape, jnp.float32) for shape in shapes],
        in_specs=[VMEM] * len(operands),
        out_specs=[VMEM] * len(shapes),
        scratch_shapes=[
            pltpu.VMEM((3, chunks, extended, LANES), jnp.float32),
            pltpu.VMEM((2, 3, extended // SUB, chunks, SUB, LANES), jnp.float32),
            pltpu.VMEM((3, chunks, SUB, LANES), jnp.float32),
        ],
        compiler_params=pltpu.CompilerParams(vmem_limit_bytes=24 * 2**20),
        cost_estimate=cost,
    )(*operands)


def edges_of(block, width):
    return jnp.stack([block[..., -width:, :], block[..., :width, :]])


def route(shift, move):
    groups, strips = lax.axis_size("tm"), lax.axis_size("space")
    return [
        (t * strips + s, (t + shift) % groups * strips + (s + move) % strips)
        for t in range(groups)
        for s in range(strips)
    ]


def exchange(edges, shift):
    both = ("tm", "space")
    if lax.axis_size("space") == 2:
        return lax.ppermute(edges, both, route(shift, 1))
    return jnp.stack(
        [
            lax.ppermute(edges[0], both, route(shift, 1)),
            lax.ppermute(edges[1], both, route(shift, -1)),
        ]
    )


def on_device(c_points):
    points, fields, rows, columns = c_points.shape
    groups = lax.axis_size("tm")
    last = c_points[-1]
    halo = exchange(edges_of(c_points[:-1], 2 * FACTOR), 0)
    behind_halo = exchange(edges_of(last, 2 * FACTOR), 1)
    behind = lax.ppermute(last, ("tm", "space"), route(1, 0))
    last_halo = exchange(edges_of(last, FACTOR), 0)
    inner = (points - 1, fields, rows, columns)
    advanced, pushed = call(
        own_kernel, [inner, inner], 2 * (points - 1), rows, columns, (c_points, halo)
    )
    updated, packed = call(
        lambda chunks, *refs: edge_kernel(chunks, groups, *refs),
        [c_points.shape, (groups, points, fields, rows // groups, columns)],
        3,
        rows,
        columns,
        (c_points, halo, behind, behind_halo, last_halo, advanced, pushed),
    )
    coarse = lax.all_to_all(packed, "tm", split_axis=0, concat_axis=0, tiled=True)
    return (updated, coarse.reshape(groups * points, fields, 1, rows // groups, columns))


def solution(mesh):
    in_specs = (P("tm", None, "space", None),)
    out_specs = (P("tm", None, "space", None), P(None, None, "space", "tm", None))
    return jax.shard_map(
        on_device, mesh=mesh, in_specs=in_specs, out_specs=out_specs, check_vma=False
    )
```

time: 48.4 us -> 42 us (0.87)
  waiting for transfers between devices: 10.1 us -> 3.76 us
  Pallas kernels: 5.88 us -> 10.1 us
  blocking collectives: 22.6 us -> 19 us
  local copies, waits for them, and re-layouts: 2.3 us -> 1.79 us
    ppermute x5 -> x4, waiting for transfers between devices: 10.1 us -> 3.76 us  [the longest x3 3.76 us: exchange(): return lax.ppermute(edges, both, route(shift, 1))]
    pallas_call x2, Pallas kernels: 5.88 us -> 10.1 us  [call(): pl.pallas_call(functools.partial(kernel, chunks), out_shape=[jax.ShapeDty...]
    all_to_all x1, blocking collectives: 22.6 us -> 19 us  [on_device(): lax.all_to_all(packed, 'tm', split_axis=0, concat_axis=0, tiled=True)]
    another operation x0 -> x3, local copies, waits for them, and re-layouts: none -> 1.03 us  [edges_of(): return jnp.stack([block[..., -width:, :], block[..., :width, :]])]
    slice x1 -> x0, local copies, waits for them, and re-layouts: 1 us -> none  [halos(): last, first = (block[..., -FACTOR:, :], block[..., :FACTOR, :])]
    all_to_all x1 -> x0, local copies, waits for them, and re-layouts: 0.95 us -> none  [on_device(): lax.all_to_all(residual, 'tm', split_axis=2, concat_axis=0, tiled=True)]
    unnamed x4 -> x3, local copies, waits for them, and re-layouts: 0.01 us -> 0.75 us
    ppermute x5 -> x4, starting transfers between devices: 6.47 us -> 6.42 us  [the longest x3 6.37 us: exchange(): return lax.ppermute(edges, both, route(shift, 1))]
  transfers between devices with their start and end apart: 5 -> 4, of which waited for: 5 -> 2; matrix products, arithmetic and copies ran while one was open for 0% -> 0% of each run, Pallas kernels for 0% -> 9%
where the time goes in v3:
time: 42 us; the launch traced here: 41.8 us
  blocking collectives  19 us (45%)
  Pallas kernels  10.1 us (24%)
  starting transfers between devices  6.42 us (15%)
  waiting for transfers between devices  3.76 us (9%)
  local copies, waits for them, and re-layouts  1.79 us (4%)
  between operations  0.69 us (2%)
    all_to_all x1, blocking collectives, on_device(): lax.all_to_all(packed, 'tm', split_axis=0, concat_axis=0, tiled=True)  19 us
    pallas_call x2, Pallas kernels, call(): pl.pallas_call(functools.partial(kernel, chunks), out_shape=[jax.ShapeDty...  10.1 us
    ppermute x3, starting transfers between devices, exchange(): return lax.ppermute(edges, both, route(shift, 1))  6.37 us
    ppermute x3, waiting for transfers between devices, exchange(): return lax.ppermute(edges, both, route(shift, 1))  3.76 us
    another operation x3, local copies, waits for them, and re-layouts, edges_of(): return jnp.stack([block[..., -width:, :], block[..., :width, :]])  1.03 us
  transfers between devices with their start and end apart: 4, of which 2 were waited for; matrix products, arithmetic and copies ran while one was open for 0% of the time, Pallas kernels for 9%

profile of v3, /device:TPU:0, one launch (start us, length us, event | category | flops | bytes accessed | tf_op | source)
XLA Modules:
  0.0 41.8 jit_solution(6493847151751340533)
XLA Ops:
  0.6 0.0 copy-start
  0.6 1.0 %slice_bitcast_fusion.4 = (f32[1,1,3,16,512]{4,3,2,1,0:T(8,128)S(1)}, f32[1,1,3,16,512]{4,3,2,1,0:T(8,128)S(1)}) fusion(f32[2,3,32,512]{3,2,1,0:T(8,128)} %refs_0_.1), kind=kLoop, calls=%fused_computation.7 | loop fusion | bytes 393216 | tf_op jit(solution)/shard_map/stack | solution.py:185
  1.7 3.0 %collective-permute-start = (f32[2,1,3,16,512]{4,3,2,1,0:T(8,128)S(1)}, f32[2,1,3,16,512]{4,3,2,1,0:T(8,128)S(1)}, u32[]{:S(2)}, u32[]{:S(2)}) collective-permute-start(f32[2,1,3,16,512]{4,3,2,1,0:T(8,128)S(1)} %pad_maximum_fusion), channel_id=1, source_target_pairs={{0,1},{1,0},{2,3},{3,2},{4,5},{5,4},{6,7},{7,6},{8,9},{9,8},{10,11... | collective-permute-start | bytes 589832 | tf_op jit(solution)/shard_map/ppermute | solution.py:200
  4.7 0.0 copy-done
  4.7 0.1 collective-permute-start.1
  4.8 1.8 %collective-permute-start.2 = (f32[2,3,16,512]{3,2,1,0:T(8,128)S(1)}, f32[2,3,16,512]{3,2,1,0:T(8,128)S(1)}, u32[]{:S(2)}, u32[]{:S(2)}) collective-permute-start(f32[2,3,16,512]{3,2,1,0:T(8,128)S(1)} %pad_maximum_fusion.1), channel_id=1, source_target_pairs={{0,3},{1,2},{2,5},{3,4},{4,7},{5,6},{6,9},{7,8},{8,11},{9,10},{10,... | collective-permute-start | bytes 589832 | tf_op jit(solution)/shard_map/ppermute | solution.py:200
  6.6 1.6 %collective-permute-start.3 = (f32[2,3,8,512]{3,2,1,0:T(8,128)S(1)}, f32[2,3,8,512]{3,2,1,0:T(8,128)S(1)}, u32[]{:S(2)}, u32[]{:S(2)}) collective-permute-start(f32[2,3,8,512]{3,2,1,0:T(8,128)S(1)} %pad_maximum_fusion.2), channel_id=1, source_target_pairs={{0,1},{1,0},{2,3},{3,2},{4,5},{5,4},{6,7},{7,6},{8,9},{9,8},{10,11... | collective-permute-start | bytes 294920 | tf_op jit(solution)/shard_map/ppermute | solution.py:200
  8.2 2.1 %collective-permute-done.halo.refs_1_ = f32[2,1,3,16,512]{4,3,2,1,0:T(8,128)S(1)} collective-permute-done((f32[2,1,3,16,512]{4,3,2,1,0:T(8,128)S(1)}, f32[2,1,3,16,512]{4,3,2,1,0:T(8,128)S(1)}, u32[]{:S(2)}, u32[]{:S(2)}) %collective-permute-start) | collective-permute-done | bytes 196640 | tf_op jit(solution)/shard_map/ppermute | solution.py:200
  10.3 3.9 %shard_map.30 = (f32[1,3,32,512]{3,2,1,0:T(8,128)S(1)}, f32[1,3,32,512]{3,2,1,0:T(8,128)S(1)}) custom-call(f32[2,3,32,512]{3,2,1,0:T(8,128)S(1)} %copy-done, f32[2,1,3,16,512]{4,3,2,1,0:T(8,128)S(1)} %collective-permute-done.halo.refs_1_), custom_call_target="tpu_custom_call" | custom-call | flops 23592960 | bytes 786432 | tf_op jit(solution)/shard_map/pallas_call | solution.py:169
  14.2 1.7 %collective-permute-done.3.refs_4_ = f32[2,3,8,512]{3,2,1,0:T(8,128)S(1)} collective-permute-done((f32[2,3,8,512]{3,2,1,0:T(8,128)S(1)}, f32[2,3,8,512]{3,2,1,0:T(8,128)S(1)}, u32[]{:S(2)}, u32[]{:S(2)}) %collective-permute-start.3) | collective-permute-done | bytes 98336 | tf_op jit(solution)/shard_map/ppermute | solution.py:200
  15.9 0.0 collective-permute-done.2.refs_3_
  15.9 0.0 collective-permute-done.1.refs_2_
  15.9 6.2 %shard_map.31 = (f32[2,3,32,512]{3,2,1,0:T(8,128)}, f32[16,2,3,2,512]{4,3,2,1,0:T(2,128)S(1)}) custom-call(f32[2,3,32,512]{3,2,1,0:T(8,128)S(1)} %copy-done, f32[2,1,3,16,512]{4,3,2,1,0:T(8,128)S(1)} %collective-permute-done.halo.refs_1_, f32[3,32,512]{2,1,0:T(8,128)S(1)} %collective-permute-done.1.refs_2_, ...), custom_call_target="tpu_custom_call" | custom-call | flops 35389440 | bytes 1179648 | tf_op jit(solution)/shard_map/pallas_call | solution.py:169
  22.1 19.0 %all_to_all.5 = f32[16,2,3,2,512]{4,3,2,1,0:T(2,128)S(1)} all-to-all(f32[16,2,3,2,512]{4,3,2,1,0:T(2,128)S(1)} %get-tuple-element.9), channel_id=1, replica_groups=mesh['tm'=16,'space'=2] {'tm'}, dimensions={0} | all-to-all | bytes 786432 | tf_op jit(solution)/shard_map/all_to_all | solution.py:229
  41.0 0.7 %copy.5 = f32[32,3,1,2,512]{4,3,2,1,0:T(2,128)} copy(f32[32,3,1,2,512]{4,3,2,1,0:T(2,128)S(1)} %bitcast.17) | data formatting | bytes 786432
  (6 shorter events, 0.1 us)
Async XLA Ops:
  0.6 4.1 %copy-start = (f32[2,3,32,512]{3,2,1,0:T(8,128)S(1)}, f32[2,3,32,512]{3,2,1,0:T(8,128)}, u32[]{:S(2)}) copy-start(f32[2,3,32,512]{3,2,1,0:T(8,128)} %refs_0_.1) | copy-start | bytes 1179652
  1.7 8.6 %collective-permute-start = (f32[2,1,3,16,512]{4,3,2,1,0:T(8,128)S(1)}, f32[2,1,3,16,512]{4,3,2,1,0:T(8,128)S(1)}, u32[]{:S(2)}, u32[]{:S(2)}) collective-permute-start(f32[2,1,3,16,512]{4,3,2,1,0:T(8,128)S(1)} %pad_maximum_fusion), channel_id=1, source_target_pairs={{0,1},{1,0},{2,3},{3,2},{4,5},{5,4},{6,7},{7,6},{8,9},{9,8},{10,11... | collective-permute-start | bytes 589832 | tf_op jit(solution)/shard_map/ppermute | solution.py:200
  4.7 11.2 %collective-permute-start.1 = (f32[3,32,512]{2,1,0:T(8,128)S(1)}, f32[3,32,512]{2,1,0:T(8,128)S(1)}, u32[]{:S(2)}, u32[]{:S(2)}) collective-permute-start(f32[3,32,512]{2,1,0:T(8,128)S(1)} %slice_bitcast_fusion), channel_id=1, source_target_pairs={{0,2},{1,3},{2,4},{3,5},{4,6},{5,7},{6,8},{7,9},{8,10},{9,11},{10,... | collective-permute-start | bytes 589832 | tf_op jit(solution)/shard_map/ppermute | solution.py:215
  4.8 11.1 %collective-permute-start.2 = (f32[2,3,16,512]{3,2,1,0:T(8,128)S(1)}, f32[2,3,16,512]{3,2,1,0:T(8,128)S(1)}, u32[]{:S(2)}, u32[]{:S(2)}) collective-permute-start(f32[2,3,16,512]{3,2,1,0:T(8,128)S(1)} %pad_maximum_fusion.1), channel_id=1, source_target_pairs={{0,3},{1,2},{2,5},{3,4},{4,7},{5,6},{6,9},{7,8},{8,11},{9,10},{10,... | collective-permute-start | bytes 589832 | tf_op jit(solution)/shard_map/ppermute | solution.py:200
  6.6 9.3 %collective-permute-start.3 = (f32[2,3,8,512]{3,2,1,0:T(8,128)S(1)}, f32[2,3,8,512]{3,2,1,0:T(8,128)S(1)}, u32[]{:S(2)}, u32[]{:S(2)}) collective-permute-start(f32[2,3,8,512]{3,2,1,0:T(8,128)S(1)} %pad_maximum_fusion.2), channel_id=1, source_target_pairs={{0,1},{1,0},{2,3},{3,2},{4,5},{5,4},{6,7},{7,6},{8,9},{9,8},{10,11... | collective-permute-start | bytes 294920 | tf_op jit(solution)/shard_map/ppermute | solution.py:200

commit v4 on v3

v4 whole, which is shorter than its diff:
```python
import functools

import jax
import jax.numpy as jnp
from jax import lax
from jax.experimental import pallas as pl
from jax.experimental.pallas import tpu as pltpu
from jax.sharding import PartitionSpec as P

FACTOR = 8
LANES = 128
SUB = 8

MOMENTUM = 0.4
PRESSURE = 0.08


def reciprocal(x):
    r = pl.reciprocal(x, approx=True)
    return r * (2.0 - x * r)


def row_terms(read, chunks, factor, lane):
    north, south, east, west = [], [], [], []
    for c in range(chunks):
        h, p, q = read(0, c), read(1, c), read(2, c)
        r = reciprocal(h)
        u = p * r
        pressure = h * h * factor
        a = p * u + pressure
        b = q * u
        d = q * (q * r) + pressure
        east.append((h - p, p - a, q - b))
        west.append((h + p, p + a, q + b))
        north.append((h - q, p - b, q - d))
        south.append((h + q, p + b, q + d))
    level = []
    for c in range(chunks):
        after, before = (c + 1) % chunks, (c - 1) % chunks
        fields = []
        for f in range(3):
            e = jnp.where(lane == 0, east[after][f], east[c][f])
            w = jnp.where(lane == LANES - 1, west[before][f], west[c][f])
            fields.append(pltpu.roll(e, LANES - 1, 1) + pltpu.roll(w, 1, 1))
        level.append(tuple(fields))
    return north, south, level


def step(src, dst, held, first, depth, chunks, factor):
    lane = lax.broadcasted_iota(jnp.int32, (SUB, LANES), 1)
    cells = [(f, c) for f in range(3) for c in range(chunks)]
    partial = south_before = None
    for n in range(depth):
        i, before = (first + n) % depth, (first + n - 1) % depth
        north, south, level = row_terms(lambda f, c: src[f, i, c], chunks, factor, lane)
        if i == 0:
            wrapped = [tuple(pltpu.roll(t, SUB - 1, 0) for t in terms) for terms in north]
        else:
            wrapped = north
        for f, c in cells:
            if n == 0:
                held[f, c] = wrapped[c][f]
            else:
                dst[f, before, c] = partial[c][f] + wrapped[c][f]
        partial = level
        if n > 0:
            partial = [
                tuple(level[c][f] + south_before[c][f] for f in range(3)) for c in range(chunks)
            ]
        south_before = south
        if i == depth - 1:
            south_before = [tuple(pltpu.roll(t, 1, 0) for t in terms) for terms in south]
    last = (first - 1) % depth
    for f, c in cells:
        if depth == 1:
            dst[f, 0, c] = partial[c][f] + held[f, c] + south_before[c][f]
        else:
            dst[f, last, c] = partial[c][f] + held[f, c]
            dst[f, first, c] = dst[f, first, c] + south_before[c][f]


def spans(chunks):
    return [slice(c * LANES, (c + 1) * LANES) for c in range(chunks)]


class Rows:
    def __init__(self, count, chunks):
        self.depth, self.chunks = count // SUB, chunks
        self.pitch = self.depth | 1

    def cells(self):
        return [
            (f, c, i) for f in range(3) for c in range(self.chunks) for i in range(self.depth)
        ]

    def pieces(self, start, count):
        found, at = [], 0
        while at < count:
            block, offset = divmod(start + at, self.depth)
            length = min(count - at, self.depth - offset)
            found.append((at, block * self.pitch + offset, length))
            at += length
        return found

    def fill(self, ext, arrays):
        start = 0
        for array in arrays:
            rows = array.shape[1]
            for at, place, length in self.pieces(start, rows):
                for f in range(3):
                    for c, span in enumerate(spans(self.chunks)):
                        ext[f, c, place : place + length, :] = array[f, at : at + length, span]
            start += rows

    def load(self, ext, state):
        for f, c, i in self.cells():
            value = ext.at[f, c][pl.ds(i, SUB, stride=self.pitch), :]
            state[0, f, i, c] = value if f == 0 else MOMENTUM * value

    def store(self, ext, state, steps):
        shrink = 0.25**steps
        for f, c, i in self.cells():
            value = state[0, f, i, c] * (shrink if f == 0 else shrink / MOMENTUM)
            ext.at[f, c][pl.ds(i, SUB, stride=self.pitch), :] = value

    def propagate(self, state, held, steps):
        depth = self.depth

        def two(_, factor):
            step(state.at[0], state.at[1], held, 0, depth, self.chunks, factor)
            factor = factor * 0.25
            step(state.at[1], state.at[0], held, 1 % depth, depth, self.chunks, factor)
            return factor * 0.25

        lax.fori_loop(0, FACTOR // 2, two, jnp.float32(PRESSURE * 0.25**steps))

    def take(self, ext, start, count, use):
        for at, place, length in self.pieces(start, count):
            for f in range(3):
                for c, span in enumerate(spans(self.chunks)):
                    use(f, span, at, length, ext[f, c, place : place + length, :])


def put(target):
    def use(f, span, at, length, value):
        target[f, at : at + length, span] = value

    return use


def own_kernel(chunks, own, halo, advanced, pushed, ext, state, held):
    rows = own.shape[2]
    wide = Rows(rows + 4 * FACTOR, chunks)
    for k in range(advanced.shape[0]):
        wide.fill(ext, [halo.at[0, k], own.at[k], halo.at[1, k]])
        wide.load(ext, state)
        wide.propagate(state, held, 0)
        wide.store(ext, state, FACTOR)
        wide.take(ext, 2 * FACTOR, rows, put(advanced.at[k]))
        wide.propagate(state, held, FACTOR)
        wide.store(ext, state, 2 * FACTOR)
        wide.take(ext, 2 * FACTOR, rows, put(pushed.at[k]))


def last_kernel(chunks, own, halo, advanced, pushed, residual, ext, state, held):
    points, _, rows, _ = own.shape
    narrow = Rows(rows + 2 * FACTOR, chunks)
    narrow.fill(ext, [halo.at[0], own.at[points - 1], halo.at[1]])
    narrow.load(ext, state)
    narrow.propagate(state, held, 0)
    narrow.store(ext, state, FACTOR)

    def use(f, span, at, length, value):
        part = slice(at, at + length)
        residual[points - 2, f, part, span] = pushed[points - 2, f, part, span] - value

    narrow.take(ext, FACTOR, rows, use)
    for k in range(points - 2):
        residual[k] = pushed[k] - advanced[k + 1]


def first_kernel(
    chunks, groups, own, halo, behind, behind_halo, advanced, residual,
    updated, packed, ext, state, held, first, sems,
):
    points, _, rows, _ = own.shape
    share = rows // groups
    wide = Rows(rows + 4 * FACTOR, chunks)
    copies = [
        pltpu.make_async_copy(advanced, updated.at[pl.ds(1, points - 1)], sems.at[0]),
        pltpu.make_async_copy(first, updated.at[0], sems.at[1]),
    ]
    copies[0].start()
    wide.fill(ext, [behind_halo.at[0], behind, behind_halo.at[1]])
    wide.load(ext, state)
    wide.propagate(state, held, 0)
    wide.store(ext, state, FACTOR)
    wide.take(ext, 2 * FACTOR, rows, put(first))
    shrink = 0.25**FACTOR

    @pl.when(lax.axis_index("tm") == 0)
    def _():
        wide.fill(ext, [halo.at[0, 0], own.at[0], halo.at[1, 0]])
        wide.load(ext, state)
        for f, c, i in wide.cells():
            state[0, f, i, c] = state[0, f, i, c] * (1 / shrink)
        first[...] = own[0]

    copies[1].start()
    wide.propagate(state, held, FACTOR)
    wide.store(ext, state, 2 * FACTOR)
    for at, place, length in wide.pieces(2 * FACTOR, rows):
        for f in range(3):
            for c, span in enumerate(spans(chunks)):
                part = slice(place, place + length)
                ext[f, c, part, :] = ext[f, c, part, :] - advanced[0, f, at : at + length, span]
    for g in range(groups):
        for f in range(3):
            for c, span in enumerate(spans(chunks)):
                for at, place, length in wide.pieces(2 * FACTOR + g * share, share):
                    packed[g * points, f, 0, at : at + length, span] = ext[
                        f, c, place : place + length, :
                    ]
                for k in range(1, points):
                    packed[g * points + k, f, 0, :, span] = residual[
                        k - 1, f, g * share : (g + 1) * share, span
                    ]
    for copy in copies:
        copy.wait()


VMEM = pl.BlockSpec(memory_space=pltpu.VMEM)


def call(kernel, shapes, work, rows, columns, operands, out_specs=None, extra=()):
    chunks = columns // LANES
    extended = rows + 4 * FACTOR
    cost = pl.CostEstimate(
        flops=work * extended * columns * FACTOR * 45,
        bytes_accessed=4 * work * 3 * extended * columns,
        transcendentals=work * extended * columns * FACTOR,
    )
    return pl.pallas_call(
        functools.partial(kernel, chunks),
        out_shape=[jax.ShapeDtypeStruct(shape, jnp.float32) for shape in shapes],
        in_specs=[VMEM] * len(operands),
        out_specs=out_specs or [VMEM] * len(shapes),
        scratch_shapes=[
            pltpu.VMEM((3, chunks, extended + SUB, LANES), jnp.float32),
            pltpu.VMEM((2, 3, extended // SUB, chunks, SUB, LANES), jnp.float32),
            pltpu.VMEM((3, chunks, SUB, LANES), jnp.float32),
            *extra,
        ],
        compiler_params=pltpu.CompilerParams(vmem_limit_bytes=24 * 2**20),
        cost_estimate=cost,
    )(*operands)


def edges_of(block, width):
    return jnp.stack([block[..., -width:, :], block[..., :width, :]])


def route(shift, move):
    groups, strips = lax.axis_size("tm"), lax.axis_size("space")
    return [
        (t * strips + s, (t + shift) % groups * strips + (s + move) % strips)
        for t in range(groups)
        for s in range(strips)
    ]


def exchange(edges, shift):
    both = ("tm", "space")
    if lax.axis_size("space") == 2:
        return lax.ppermute(edges, both, route(shift, 1))
    return jnp.stack(
        [
            lax.ppermute(edges[0], both, route(shift, 1)),
            lax.ppermute(edges[1], both, route(shift, -1)),
        ]
    )


def on_device(c_points):
    points, fields, rows, columns = c_points.shape
    groups = lax.axis_size("tm")
    last = c_points[-1]
    halo = exchange(edges_of(c_points[:-1], 2 * FACTOR), 0)
    last_halo = exchange(edges_of(last, FACTOR), 0)
    behind_halo = exchange(edges_of(last, 2 * FACTOR), 1)
    behind = lax.ppermute(last, ("tm", "space"), route(1, 0))
    inner = (points - 1, fields, rows, columns)
    advanced, pushed = call(
        own_kernel, [inner, inner], 2 * (points - 1), rows, columns, (c_points, halo)
    )
    (residual,) = call(
        last_kernel, [inner], 1, rows, columns, (c_points, last_halo, advanced, pushed)
    )
    updated, packed = call(
        lambda chunks, *refs: first_kernel(chunks, groups, *refs),
        [c_points.shape, (groups * points, fields, 1, rows // groups, columns)],
        2,
        rows,
        columns,
        (c_points, halo, behind, behind_halo, advanced, residual),
        out_specs=[pl.BlockSpec(memory_space=pl.ANY), VMEM],
        extra=[pltpu.VMEM((fields, rows, columns), jnp.float32), pltpu.SemaphoreType.DMA((2,))],
    )
    return (updated, lax.all_to_all(packed, "tm", split_axis=0, concat_axis=0, tiled=True))


def solution(mesh):
    in_specs = (P("tm", None, "space", None),)
    out_specs = (P("tm", None, "space", None), P(None, None, "space", "tm", None))
    return jax.shard_map(
        on_device, mesh=mesh, in_specs=in_specs, out_specs=out_specs, check_vma=False
    )
```

time: 42 us -> 42.1 us (level)
    pallas_call x2 -> x3, Pallas kernels: 10.1 us -> 10.2 us  [call(): pl.pallas_call(functools.partial(kernel, chunks), out_shape=[jax.ShapeDty...]
  transfers between devices with their start and end apart: 4 -> 4, of which waited for: 2 -> 2; matrix products, arithmetic and copies ran while one was open for 0% -> 0% of each run, Pallas kernels for 9% -> 14%
where the time goes in v4:
time: 42.1 us; the launch traced here: 41.9 us
  blocking collectives  19 us (45%)
  Pallas kernels  10.2 us (24%)
  starting transfers between devices  6.42 us (15%)
  waiting for transfers between devices  3.63 us (9%)
  local copies, waits for them, and re-layouts  1.79 us (4%)
  between operations  0.72 us (2%)
    all_to_all x1, blocking collectives, on_device(): lax.all_to_all(packed, 'tm', split_axis=0, concat_axis=0, tiled=True)  19 us
    pallas_call x3, Pallas kernels, call(): pl.pallas_call(functools.partial(kernel, chunks), out_shape=[jax.ShapeDty...  10.2 us
    ppermute x3, starting transfers between devices, exchange(): return lax.ppermute(edges, both, route(shift, 1))  6.37 us
    ppermute x3, waiting for transfers between devices, exchange(): return lax.ppermute(edges, both, route(shift, 1))  3.63 us
    another operation x3, local copies, waits for them, and re-layouts, edges_of(): return jnp.stack([block[..., -width:, :], block[..., :width, :]])  1.03 us
  transfers between devices with their start and end apart: 4, of which 2 were waited for; matrix products, arithmetic and copies ran while one was open for 0% of the time, Pallas kernels for 14%

profile of v4, /device:TPU:0, one launch (start us, length us, event | category | flops | bytes accessed | tf_op | source)
XLA Modules:
  0.0 41.9 jit_solution(11590233803531276172)
XLA Ops:
  0.6 0.0 copy-start
  0.6 1.0 %slice_bitcast_fusion.4 = (f32[1,1,3,16,512]{4,3,2,1,0:T(8,128)S(1)}, f32[1,1,3,16,512]{4,3,2,1,0:T(8,128)S(1)}) fusion(f32[2,3,32,512]{3,2,1,0:T(8,128)} %refs_0_.1), kind=kLoop, calls=%fused_computation.7 | loop fusion | bytes 393216 | tf_op jit(solution)/shard_map/stack | solution.py:260
  1.7 3.0 %collective-permute-start = (f32[2,1,3,16,512]{4,3,2,1,0:T(8,128)S(1)}, f32[2,1,3,16,512]{4,3,2,1,0:T(8,128)S(1)}, u32[]{:S(2)}, u32[]{:S(2)}) collective-permute-start(f32[2,1,3,16,512]{4,3,2,1,0:T(8,128)S(1)} %pad_maximum_fusion), channel_id=1, source_target_pairs={{0,1},{1,0},{2,3},{3,2},{4,5},{5,4},{6,7},{7,6},{8,9},{9,8},{10,11... | collective-permute-start | bytes 589832 | tf_op jit(solution)/shard_map/ppermute | solution.py:275
  4.7 0.0 copy-done
  4.7 0.1 collective-permute-start.1
  4.8 1.8 %collective-permute-start.2 = (f32[2,3,16,512]{3,2,1,0:T(8,128)S(1)}, f32[2,3,16,512]{3,2,1,0:T(8,128)S(1)}, u32[]{:S(2)}, u32[]{:S(2)}) collective-permute-start(f32[2,3,16,512]{3,2,1,0:T(8,128)S(1)} %pad_maximum_fusion.1), channel_id=1, source_target_pairs={{0,3},{1,2},{2,5},{3,4},{4,7},{5,6},{6,9},{7,8},{8,11},{9,10},{10,... | collective-permute-start | bytes 589832 | tf_op jit(solution)/shard_map/ppermute | solution.py:275
  6.6 1.6 %collective-permute-start.3 = (f32[2,3,8,512]{3,2,1,0:T(8,128)S(1)}, f32[2,3,8,512]{3,2,1,0:T(8,128)S(1)}, u32[]{:S(2)}, u32[]{:S(2)}) collective-permute-start(f32[2,3,8,512]{3,2,1,0:T(8,128)S(1)} %pad_maximum_fusion.2), channel_id=1, source_target_pairs={{0,1},{1,0},{2,3},{3,2},{4,5},{5,4},{6,7},{7,6},{8,9},{9,8},{10,11... | collective-permute-start | bytes 294920 | tf_op jit(solution)/shard_map/ppermute | solution.py:275
  8.2 2.1 %collective-permute-done.halo.refs_1_ = f32[2,1,3,16,512]{4,3,2,1,0:T(8,128)S(1)} collective-permute-done((f32[2,1,3,16,512]{4,3,2,1,0:T(8,128)S(1)}, f32[2,1,3,16,512]{4,3,2,1,0:T(8,128)S(1)}, u32[]{:S(2)}, u32[]{:S(2)}) %collective-permute-start) | collective-permute-done | bytes 196640 | tf_op jit(solution)/shard_map/ppermute | solution.py:275
  10.3 4.1 %shard_map.30 = (f32[1,3,32,512]{3,2,1,0:T(8,128)S(1)}, f32[1,3,32,512]{3,2,1,0:T(8,128)S(1)}) custom-call(f32[2,3,32,512]{3,2,1,0:T(8,128)S(1)} %copy-done, f32[2,1,3,16,512]{4,3,2,1,0:T(8,128)S(1)} %collective-permute-done.halo.refs_1_), custom_call_target="tpu_custom_call" | custom-call | flops 23592960 | bytes 786432 | tf_op jit(solution)/shard_map/pallas_call | solution.py:243
  14.4 1.5 %collective-permute-done.3.halo = f32[2,3,8,512]{3,2,1,0:T(8,128)S(1)} collective-permute-done((f32[2,3,8,512]{3,2,1,0:T(8,128)S(1)}, f32[2,3,8,512]{3,2,1,0:T(8,128)S(1)}, u32[]{:S(2)}, u32[]{:S(2)}) %collective-permute-start.3) | collective-permute-done | bytes 98336 | tf_op jit(solution)/shard_map/ppermute | solution.py:275
  15.9 1.8 %shard_map.31.refs_5_ = f32[1,3,32,512]{3,2,1,0:T(8,128)S(1)} custom-call(f32[2,3,32,512]{3,2,1,0:T(8,128)S(1)} %copy-done, f32[2,3,8,512]{3,2,1,0:T(8,128)S(1)} %collective-permute-done.3.halo, f32[1,3,32,512]{3,2,1,0:T(8,128)S(1)} %get-tuple-element.6.advanced.refs_4_, f32[1,3,32,512]{3,2,1,0:T(8,128)S(1)} %get-tuple-element.7.pushed), custom_call_target="tpu_custom_call" | custom-call | flops 11796480 | bytes 393216 | tf_op jit(solution)/shard_map/pallas_call | solution.py:243
  17.7 0.0 collective-permute-done.2.refs_3_
  17.7 0.0 collective-permute-done.1.refs_2_
  17.7 4.4 %shard_map.32 = (f32[2,3,32,512]{3,2,1,0:T(8,128)}, f32[32,3,1,2,512]{4,3,2,1,0:T(2,128)S(1)}) custom-call(f32[2,3,32,512]{3,2,1,0:T(8,128)S(1)} %copy-done, f32[2,1,3,16,512]{4,3,2,1,0:T(8,128)S(1)} %collective-permute-done.halo.refs_1_, f32[3,32,512]{2,1,0:T(8,128)S(1)} %collective-permute-done.1.refs_2_, ...), custom_call_target="tpu_custom_call" | custom-call | flops 23592960 | bytes 786432 | tf_op jit(solution)/shard_map/pallas_call | solution.py:243
  22.1 19.0 %all_to_all.5 = f32[32,3,1,2,512]{4,3,2,1,0:T(2,128)S(1)} all-to-all(f32[32,3,1,2,512]{4,3,2,1,0:T(2,128)S(1)} %get-tuple-element.9), channel_id=1, replica_groups=mesh['tm'=16,'space'=2] {'tm'}, dimensions={0} | all-to-all | bytes 786432 | tf_op jit(solution)/shard_map/all_to_all | solution.py:309
  41.1 0.7 %copy.4 = f32[32,3,1,2,512]{4,3,2,1,0:T(2,128)} copy(f32[32,3,1,2,512]{4,3,2,1,0:T(2,128)S(1)} %all_to_all.5) | data formatting | bytes 786432
  (6 shorter events, 0.1 us)
Async XLA Ops:
  0.6 4.1 %copy-start = (f32[2,3,32,512]{3,2,1,0:T(8,128)S(1)}, f32[2,3,32,512]{3,2,1,0:T(8,128)}, u32[]{:S(2)}) copy-start(f32[2,3,32,512]{3,2,1,0:T(8,128)} %refs_0_.1) | copy-start | bytes 1179652
  1.7 8.6 %collective-permute-start = (f32[2,1,3,16,512]{4,3,2,1,0:T(8,128)S(1)}, f32[2,1,3,16,512]{4,3,2,1,0:T(8,128)S(1)}, u32[]{:S(2)}, u32[]{:S(2)}) collective-permute-start(f32[2,1,3,16,512]{4,3,2,1,0:T(8,128)S(1)} %pad_maximum_fusion), channel_id=1, source_target_pairs={{0,1},{1,0},{2,3},{3,2},{4,5},{5,4},{6,7},{7,6},{8,9},{9,8},{10,11... | collective-permute-start | bytes 589832 | tf_op jit(solution)/shard_map/ppermute | solution.py:275
  4.7 13.0 %collective-permute-start.1 = (f32[3,32,512]{2,1,0:T(8,128)S(1)}, f32[3,32,512]{2,1,0:T(8,128)S(1)}, u32[]{:S(2)}, u32[]{:S(2)}) collective-permute-start(f32[3,32,512]{2,1,0:T(8,128)S(1)} %slice_bitcast_fusion), channel_id=1, source_target_pairs={{0,2},{1,3},{2,4},{3,5},{4,6},{5,7},{6,8},{7,9},{8,10},{9,11},{10,... | collective-permute-start | bytes 589832 | tf_op jit(solution)/shard_map/ppermute | solution.py:291
  4.8 12.9 %collective-permute-start.2 = (f32[2,3,16,512]{3,2,1,0:T(8,128)S(1)}, f32[2,3,16,512]{3,2,1,0:T(8,128)S(1)}, u32[]{:S(2)}, u32[]{:S(2)}) collective-permute-start(f32[2,3,16,512]{3,2,1,0:T(8,128)S(1)} %pad_maximum_fusion.1), channel_id=1, source_target_pairs={{0,3},{1,2},{2,5},{3,4},{4,7},{5,6},{6,9},{7,8},{8,11},{9,10},{10,... | collective-permute-start | bytes 589832 | tf_op jit(solution)/shard_map/ppermute | solution.py:275
  6.6 9.3 %collective-permute-start.3 = (f32[2,3,8,512]{3,2,1,0:T(8,128)S(1)}, f32[2,3,8,512]{3,2,1,0:T(8,128)S(1)}, u32[]{:S(2)}, u32[]{:S(2)}) collective-permute-start(f32[2,3,8,512]{3,2,1,0:T(8,128)S(1)} %pad_maximum_fusion.2), channel_id=1, source_target_pairs={{0,1},{1,0},{2,3},{3,2},{4,5},{5,4},{6,7},{7,6},{8,9},{9,8},{10,11... | collective-permute-start | bytes 294920 | tf_op jit(solution)/shard_map/ppermute | solution.py:275

commit v5 on v4

--- a/solution.py
+++ b/solution.py
@@ -287,7 +287,8 @@
     last = c_points[-1]
     halo = exchange(edges_of(c_points[:-1], 2 * FACTOR), 0)
     last_halo = exchange(edges_of(last, FACTOR), 0)
-    behind_halo = exchange(edges_of(last, 2 * FACTOR), 1)
+    halo, last_edges = lax.optimization_barrier((halo, edges_of(last, 2 * FACTOR)))
+    behind_halo = exchange(last_edges, 1)
     behind = lax.ppermute(last, ("tm", "space"), route(1, 0))
     inner = (points - 1, fields, rows, columns)
     advanced, pushed = call(

time: 42.1 us -> 44.2 us (1.050)
  waiting for transfers between devices: 3.63 us -> 7.56 us
  starting transfers between devices: 6.42 us -> 4.87 us
    ppermute x3, waiting for transfers between devices: 3.63 us -> 7.56 us  [exchange(): return lax.ppermute(edges, both, route(shift, 1))]
    ppermute x3, starting transfers between devices: 6.37 us -> 4.81 us  [exchange(): return lax.ppermute(edges, both, route(shift, 1))]
  transfers between devices with their start and end apart: 4 -> 4, of which waited for: 2 -> 2; matrix products, arithmetic and copies ran while one was open for 0% -> 0% of each run, Pallas kernels for 14% -> 13%
where the time goes in v5:
time: 44.2 us; the launch traced here: 44 us
  blocking collectives  18.7 us (42%)
  Pallas kernels  10.2 us (23%)
  waiting for transfers between devices  7.56 us (17%)
  starting transfers between devices  4.87 us (11%)
  local copies, waits for them, and re-layouts  1.8 us (4%)
  between operations  0.73 us (2%)
    all_to_all x1, blocking collectives, on_device(): lax.all_to_all(packed, 'tm', split_axis=0, concat_axis=0, tiled=True)  18.7 us
    pallas_call x3, Pallas kernels, call(): pl.pallas_call(functools.partial(kernel, chunks), out_shape=[jax.ShapeDty...  10.2 us
    ppermute x3, waiting for transfers between devices, exchange(): return lax.ppermute(edges, both, route(shift, 1))  7.56 us
    ppermute x3, starting transfers between devices, exchange(): return lax.ppermute(edges, both, route(shift, 1))  4.81 us
    another operation x3, local copies, waits for them, and re-layouts, edges_of(): return jnp.stack([block[..., -width:, :], block[..., :width, :]])  1.03 us
  transfers between devices with their start and end apart: 4, of which 2 were waited for; matrix products, arithmetic and copies ran while one was open for 0% of the time, Pallas kernels for 13%

profile of v5, /device:TPU:0, one launch (start us, length us, event | category | flops | bytes accessed | tf_op | source)
XLA Modules:
  0.0 44.0 jit_solution(12476602347531919708)
XLA Ops:
  0.6 0.0 copy-start
  0.6 1.0 %slice_bitcast_fusion.4 = (f32[1,1,3,16,512]{4,3,2,1,0:T(8,128)S(1)}, f32[1,1,3,16,512]{4,3,2,1,0:T(8,128)S(1)}) fusion(f32[2,3,32,512]{3,2,1,0:T(8,128)} %refs_0_.1), kind=kLoop, calls=%fused_computation.7 | loop fusion | bytes 393216 | tf_op jit(solution)/shard_map/stack | solution.py:260
  1.7 3.0 %collective-permute-start = (f32[2,1,3,16,512]{4,3,2,1,0:T(8,128)S(1)}, f32[2,1,3,16,512]{4,3,2,1,0:T(8,128)S(1)}, u32[]{:S(2)}, u32[]{:S(2)}) collective-permute-start(f32[2,1,3,16,512]{4,3,2,1,0:T(8,128)S(1)} %pad_maximum_fusion), channel_id=1, source_target_pairs={{0,1},{1,0},{2,3},{3,2},{4,5},{5,4},{6,7},{7,6},{8,9},{9,8},{10,11... | collective-permute-start | bytes 589832 | tf_op jit(solution)/shard_map/ppermute | solution.py:275
  4.7 0.0 copy-done
  4.7 0.1 collective-permute-start.1
  4.8 4.8 %collective-permute-done.halo.refs_1_ = f32[2,1,3,16,512]{4,3,2,1,0:T(8,128)S(1)} collective-permute-done((f32[2,1,3,16,512]{4,3,2,1,0:T(8,128)S(1)}, f32[2,1,3,16,512]{4,3,2,1,0:T(8,128)S(1)}, u32[]{:S(2)}, u32[]{:S(2)}) %collective-permute-start) | collective-permute-done | bytes 196640 | tf_op jit(solution)/shard_map/ppermute | solution.py:275
  9.6 0.3 collective-permute-start.2
  9.9 1.5 %collective-permute-start.3 = (f32[2,3,8,512]{3,2,1,0:T(8,128)S(1)}, f32[2,3,8,512]{3,2,1,0:T(8,128)S(1)}, u32[]{:S(2)}, u32[]{:S(2)}) collective-permute-start(f32[2,3,8,512]{3,2,1,0:T(8,128)S(1)} %pad_maximum_fusion.2), channel_id=1, source_target_pairs={{0,1},{1,0},{2,3},{3,2},{4,5},{5,4},{6,7},{7,6},{8,9},{9,8},{10,11... | collective-permute-start | bytes 294920 | tf_op jit(solution)/shard_map/ppermute | solution.py:275
  11.4 4.1 %shard_map.30 = (f32[1,3,32,512]{3,2,1,0:T(8,128)S(1)}, f32[1,3,32,512]{3,2,1,0:T(8,128)S(1)}) custom-call(f32[2,3,32,512]{3,2,1,0:T(8,128)S(1)} %copy-done, f32[2,1,3,16,512]{4,3,2,1,0:T(8,128)S(1)} %collective-permute-done.halo.refs_1_), custom_call_target="tpu_custom_call" | custom-call | flops 23592960 | bytes 786432 | tf_op jit(solution)/shard_map/pallas_call | solution.py:243
  15.5 2.8 %collective-permute-done.3.halo = f32[2,3,8,512]{3,2,1,0:T(8,128)S(1)} collective-permute-done((f32[2,3,8,512]{3,2,1,0:T(8,128)S(1)}, f32[2,3,8,512]{3,2,1,0:T(8,128)S(1)}, u32[]{:S(2)}, u32[]{:S(2)}) %collective-permute-start.3) | collective-permute-done | bytes 98336 | tf_op jit(solution)/shard_map/ppermute | solution.py:275
  18.3 1.8 %shard_map.31.refs_5_ = f32[1,3,32,512]{3,2,1,0:T(8,128)S(1)} custom-call(f32[2,3,32,512]{3,2,1,0:T(8,128)S(1)} %copy-done, f32[2,3,8,512]{3,2,1,0:T(8,128)S(1)} %collective-permute-done.3.halo, f32[1,3,32,512]{3,2,1,0:T(8,128)S(1)} %get-tuple-element.10.advanced.refs_4_, f32[1,3,32,512]{3,2,1,0:T(8,128)S(1)} %get-tuple-element.11.pushed), custom_call_target="tpu_custom_call" | custom-call | flops 11796480 | bytes 393216 | tf_op jit(solution)/shard_map/pallas_call | solution.py:243
  20.1 0.0 collective-permute-done.1.refs_2_
  20.1 0.0 collective-permute-done.2.refs_3_
  20.1 4.4 %shard_map.32 = (f32[2,3,32,512]{3,2,1,0:T(8,128)}, f32[32,3,1,2,512]{4,3,2,1,0:T(2,128)S(1)}) custom-call(f32[2,3,32,512]{3,2,1,0:T(8,128)S(1)} %copy-done, f32[2,1,3,16,512]{4,3,2,1,0:T(8,128)S(1)} %collective-permute-done.halo.refs_1_, f32[3,32,512]{2,1,0:T(8,128)S(1)} %collective-permute-done.1.refs_2_, ...), custom_call_target="tpu_custom_call" | custom-call | flops 23592960 | bytes 786432 | tf_op jit(solution)/shard_map/pallas_call | solution.py:243
  24.5 18.7 %all_to_all.5 = f32[32,3,1,2,512]{4,3,2,1,0:T(2,128)S(1)} all-to-all(f32[32,3,1,2,512]{4,3,2,1,0:T(2,128)S(1)} %get-tuple-element.13), channel_id=1, replica_groups=mesh['tm'=16,'space'=2] {'tm'}, dimensions={0} | all-to-all | bytes 786432 | tf_op jit(solution)/shard_map/all_to_all | solution.py:310
  43.2 0.7 %copy.4 = f32[32,3,1,2,512]{4,3,2,1,0:T(2,128)} copy(f32[32,3,1,2,512]{4,3,2,1,0:T(2,128)S(1)} %all_to_all.5) | data formatting | bytes 786432
  (6 shorter events, 0.1 us)
Async XLA Ops:
  0.6 4.1 %copy-start = (f32[2,3,32,512]{3,2,1,0:T(8,128)S(1)}, f32[2,3,32,512]{3,2,1,0:T(8,128)}, u32[]{:S(2)}) copy-start(f32[2,3,32,512]{3,2,1,0:T(8,128)} %refs_0_.1) | copy-start | bytes 1179652
  1.7 7.9 %collective-permute-start = (f32[2,1,3,16,512]{4,3,2,1,0:T(8,128)S(1)}, f32[2,1,3,16,512]{4,3,2,1,0:T(8,128)S(1)}, u32[]{:S(2)}, u32[]{:S(2)}) collective-permute-start(f32[2,1,3,16,512]{4,3,2,1,0:T(8,128)S(1)} %pad_maximum_fusion), channel_id=1, source_target_pairs={{0,1},{1,0},{2,3},{3,2},{4,5},{5,4},{6,7},{7,6},{8,9},{9,8},{10,11... | collective-permute-start | bytes 589832 | tf_op jit(solution)/shard_map/ppermute | solution.py:275
  4.7 15.4 %collective-permute-start.1 = (f32[3,32,512]{2,1,0:T(8,128)S(1)}, f32[3,32,512]{2,1,0:T(8,128)S(1)}, u32[]{:S(2)}, u32[]{:S(2)}) collective-permute-start(f32[3,32,512]{2,1,0:T(8,128)S(1)} %slice_bitcast_fusion), channel_id=1, source_target_pairs={{0,2},{1,3},{2,4},{3,5},{4,6},{5,7},{6,8},{7,9},{8,10},{9,11},{10,... | collective-permute-start | bytes 589832 | tf_op jit(solution)/shard_map/ppermute | solution.py:292
  9.6 10.5 %collective-permute-start.2 = (f32[2,3,16,512]{3,2,1,0:T(8,128)S(1)}, f32[2,3,16,512]{3,2,1,0:T(8,128)S(1)}, u32[]{:S(2)}, u32[]{:S(2)}) collective-permute-start(f32[2,3,16,512]{3,2,1,0:T(8,128)S(1)} %pad_maximum_fusion.1), channel_id=1, source_target_pairs={{0,3},{1,2},{2,5},{3,4},{4,7},{5,6},{6,9},{7,8},{8,11},{9,10},{10,... | collective-permute-start | bytes 589832 | tf_op jit(solution)/shard_map/ppermute | solution.py:275
  9.9 8.4 %collective-permute-start.3 = (f32[2,3,8,512]{3,2,1,0:T(8,128)S(1)}, f32[2,3,8,512]{3,2,1,0:T(8,128)S(1)}, u32[]{:S(2)}, u32[]{:S(2)}) collective-permute-start(f32[2,3,8,512]{3,2,1,0:T(8,128)S(1)} %pad_maximum_fusion.2), channel_id=1, source_target_pairs={{0,1},{1,0},{2,3},{3,2},{4,5},{5,4},{6,7},{7,6},{8,9},{9,8},{10,11... | collective-permute-start | bytes 294920 | tf_op jit(solution)/shard_map/ppermute | solution.py:275

commit v6 on v5

--- a/solution.py
+++ b/solution.py
@@ -148,10 +148,38 @@
     return use
 
 
-def own_kernel(chunks, own, halo, advanced, pushed, ext, state, held):
+def pack(ext, layout, start, rows, groups, packed, k):
+    share = rows // groups
+    for g in range(groups):
+        for at, place, length in layout.pieces(start + g * share, share):
+            for f in range(3):
+                for c, span in enumerate(spans(layout.chunks)):
+                    packed[g, k, f, 0, at : at + length, span] = ext[f, c, place : place + length, :]
+
+
+def subtract(ext, layout, start, rows, difference):
+    for at, place, length in layout.pieces(start, rows):
+        for f in range(3):
+            for c, span in enumerate(spans(layout.chunks)):
+                part = slice(place, place + length)
+                ext[f, c, part, :] = difference(ext[f, c, part, :], f, slice(at, at + length), span)
+
+
+def last_kernel(chunks, own, halo, advanced, ext, state, held):
+    points, _, rows, _ = own.shape
+    narrow = Rows(rows + 2 * FACTOR, chunks)
+    narrow.fill(ext, [halo.at[0], own.at[points - 1], halo.at[1]])
+    narrow.load(ext, state)
+    narrow.propagate(state, held, 0)
+    narrow.store(ext, state, FACTOR)
+    narrow.take(ext, FACTOR, rows, put(advanced))
+
+
+def own_kernel(chunks, groups, own, halo, last, advanced, packed, ext, state, held):
     rows = own.shape[2]
     wide = Rows(rows + 4 * FACTOR, chunks)
-    for k in range(advanced.shape[0]):
+    following = last
+    for k in reversed(range(advanced.shape[0])):
         wide.fill(ext, [halo.at[0, k], own.at[k], halo.at[1, k]])
         wide.load(ext, state)
         wide.propagate(state, held, 0)
@@ -159,32 +187,18 @@
         wide.take(ext, 2 * FACTOR, rows, put(advanced.at[k]))
         wide.propagate(state, held, FACTOR)
         wide.store(ext, state, 2 * FACTOR)
-        wide.take(ext, 2 * FACTOR, rows, put(pushed.at[k]))
-
-
-def last_kernel(chunks, own, halo, advanced, pushed, residual, ext, state, held):
-    points, _, rows, _ = own.shape
-    narrow = Rows(rows + 2 * FACTOR, chunks)
-    narrow.fill(ext, [halo.at[0], own.at[points - 1], halo.at[1]])
-    narrow.load(ext, state)
-    narrow.propagate(state, held, 0)
-    narrow.store(ext, state, FACTOR)
-
-    def use(f, span, at, length, value):
-        part = slice(at, at + length)
-        residual[points - 2, f, part, span] = pushed[points - 2, f, part, span] - value
-
-    narrow.take(ext, FACTOR, rows, use)
-    for k in range(points - 2):
-        residual[k] = pushed[k] - advanced[k + 1]
+        subtract(
+            ext, wide, 2 * FACTOR, rows, lambda v, f, part, span: v - following[f, part, span]
+        )
+        pack(ext, wide, 2 * FACTOR, rows, groups, packed, k)
+        following = advanced.at[k]
 
 
 def first_kernel(
-    chunks, groups, own, halo, behind, behind_halo, advanced, residual,
+    chunks, groups, own, halo, behind, behind_halo, advanced,
     updated, packed, ext, state, held, first, sems,
 ):
     points, _, rows, _ = own.shape
-    share = rows // groups
     wide = Rows(rows + 4 * FACTOR, chunks)
     copies = [
         pltpu.make_async_copy(advanced, updated.at[pl.ds(1, points - 1)], sems.at[0]),
@@ -209,22 +223,20 @@
     copies[1].start()
     wide.propagate(state, held, FACTOR)
     wide.store(ext, state, 2 * FACTOR)
-    for at, place, length in wide.pieces(2 * FACTOR, rows):
-        for f in range(3):
-            for c, span in enumerate(spans(chunks)):
-                part = slice(place, place + length)
-                ext[f, c, part, :] = ext[f, c, part, :] - advanced[0, f, at : at + length, span]
-    for g in range(groups):
-        for f in range(3):
-            for c, span in enumerate(spans(chunks)):
-                for at, place, length in wide.pieces(2 * FACTOR + g * share, share):
-                    packed[g * points, f, 0, at : at + length, span] = ext[
-                        f, c, place : place + length, :
-                    ]
-                for k in range(1, points):
-                    packed[g * points + k, f, 0, :, span] = residual[
-                        k - 1, f, g * share : (g + 1) * share, span
-                    ]
+    subtract(ext, wide, 2 * FACTOR, rows, lambda v, f, part, span: v - advanced[0, f, part, span])
+    pack(ext, wide, 2 * FACTOR, rows, groups, packed, 0)
+    for copy in copies:
+        copy.wait()
+
+
+def join_kernel(opening, others, out, sems):
+    inner = others.shape[1]
+    copies = [
+        pltpu.make_async_copy(others, out.at[:, pl.ds(1, inner)], sems.at[0]),
+        pltpu.make_async_copy(opening, out.at[:, pl.ds(0, 1)], sems.at[1]),
+    ]
+    for copy in copies:
+        copy.start()
     for copy in copies:
         copy.wait()
 
@@ -285,29 +297,44 @@
     points, fields, rows, columns = c_points.shape
     groups = lax.axis_size("tm")
     last = c_points[-1]
+    last_halo = exchange(edges_of(last, FACTOR), 0)
     halo = exchange(edges_of(c_points[:-1], 2 * FACTOR), 0)
-    last_halo = exchange(edges_of(last, FACTOR), 0)
-    halo, last_edges = lax.optimization_barrier((halo, edges_of(last, 2 * FACTOR)))
+    halo, last_edges, last = lax.optimization_barrier((halo, edges_of(last, 2 * FACTOR), last))
     behind_halo = exchange(last_edges, 1)
     behind = lax.ppermute(last, ("tm", "space"), route(1, 0))
     inner = (points - 1, fields, rows, columns)
-    advanced, pushed = call(
-        own_kernel, [inner, inner], 2 * (points - 1), rows, columns, (c_points, halo)
-    )
-    (residual,) = call(
-        last_kernel, [inner], 1, rows, columns, (c_points, last_halo, advanced, pushed)
-    )
+    packet = (fields, 1, rows // groups, columns)
+    (advanced_last,) = call(
+        last_kernel, [last.shape], 1, rows, columns, (c_points, last_halo)
+    )
+    advanced, packed = call(
+        lambda chunks, *refs: own_kernel(chunks, groups, *refs),
+        [inner, (groups, points - 1, *packet)],
+        2 * (points - 1),
+        rows,
+        columns,
+        (c_points, halo, advanced_last),
+    )
+    others = lax.all_to_all(packed, "tm", split_axis=0, concat_axis=0, tiled=True)
     updated, packed = call(
         lambda chunks, *refs: first_kernel(chunks, groups, *refs),
-        [c_points.shape, (groups * points, fields, 1, rows // groups, columns)],
+        [c_points.shape, (groups, 1, *packet)],
         2,
         rows,
         columns,
-        (c_points, halo, behind, behind_halo, advanced, residual),
+        (c_points, halo, behind, behind_halo, advanced),
         out_specs=[pl.BlockSpec(memory_space=pl.ANY), VMEM],
         extra=[pltpu.VMEM((fields, rows, columns), jnp.float32), pltpu.SemaphoreType.DMA((2,))],
     )
-    return (updated, lax.all_to_all(packed, "tm", split_axis=0, concat_axis=0, tiled=True))
+    opening = lax.all_to_all(packed, "tm", split_axis=0, concat_axis=0, tiled=True)
+    coarse = pl.pallas_call(
+        join_kernel,
+        out_shape=jax.ShapeDtypeStruct((groups, points, *packet), jnp.float32),
+        in_specs=[VMEM] * 2,
+        out_specs=pl.BlockSpec(memory_space=pl.ANY),
+        scratch_shapes=[pltpu.SemaphoreType.DMA((2,))],
+    )(opening, others)
+    return (updated, coarse.reshape(groups * points, *packet))
 
 
 def solution(mesh):

time: 44.2 us -> 55.5 us (1.26)
  waiting for transfers between devices: 7.56 us -> 16 us
  starting transfers between devices: 4.87 us -> 12.4 us
  blocking collectives: 18.7 us -> 12.3 us
  Pallas kernels: 10.2 us -> 12.7 us
  local copies, waits for them, and re-layouts: 1.8 us -> 1.05 us
    ppermute x1, waiting for transfers between devices: 0.01 us -> 8.04 us  [on_device(): behind = lax.ppermute(last, ('tm', 'space'), route(1, 0))]
    all_to_all x1, blocking collectives: 18.7 us -> 12.3 us  [on_device(): lax.all_to_all(packed, 'tm', split_axis=0, concat_axis=0, tiled=True)]
    all_to_all x0 -> x1, starting transfers between devices: none -> 6.27 us  [on_device(): lax.all_to_all(packed, 'tm', split_axis=0, concat_axis=0, tiled=True)]
    pallas_call x0 -> x1, Pallas kernels: none -> 1.78 us  [on_device(): pl.pallas_call(join_kernel, out_shape=jax.ShapeDtypeStruct((groups, point...]
    another operation x3, local copies, waits for them, and re-layouts: 1.03 us -> 0.04 us  [edges_of(): return jnp.stack([block[..., -width:, :], block[..., :width, :]])]
    squeeze x1, local copies, waits for them, and re-layouts: 0.01 us -> 1 us  [on_device(): last = c_points[-1]]
    ppermute x3, starting transfers between devices: 4.81 us -> 5.74 us  [exchange(): return lax.ppermute(edges, both, route(shift, 1))]
    unnamed x3 -> x4, local copies, waits for them, and re-layouts: 0.75 us -> 0.01 us
  transfers between devices with their start and end apart: 4 -> 5, of which waited for: 2 -> 4; matrix products, arithmetic and copies ran while one was open for 0% -> 0% of each run, Pallas kernels for 13% -> 11%
where the time goes in v6:
time: 55.5 us; the launch traced here: 55.2 us
  waiting for transfers between devices  16 us (29%)
  Pallas kernels  12.7 us (23%)
  starting transfers between devices  12.4 us (22%)
  blocking collectives  12.3 us (22%)
  local copies, waits for them, and re-layouts  1.05 us (2%)
  between operations  0.72 us (1%)
    all_to_all x1, blocking collectives, on_device(): lax.all_to_all(packed, 'tm', split_axis=0, concat_axis=0, tiled=True)  12.3 us
    pallas_call x3, Pallas kernels, call(): pl.pallas_call(functools.partial(kernel, chunks), out_shape=[jax.ShapeDty...  10.9 us
    ppermute x1, waiting for transfers between devices, on_device(): behind = lax.ppermute(last, ('tm', 'space'), route(1, 0))  8.04 us
    ppermute x3, waiting for transfers between devices, exchange(): return lax.ppermute(edges, both, route(shift, 1))  8 us
    all_to_all x1, starting transfers between devices, on_device(): lax.all_to_all(packed, 'tm', split_axis=0, concat_axis=0, tiled=True)  6.27 us
    ppermute x3, starting transfers between devices, exchange(): return lax.ppermute(edges, both, route(shift, 1))  5.74 us
    pallas_call x1, Pallas kernels, on_device(): pl.pallas_call(join_kernel, out_shape=jax.ShapeDtypeStruct((groups, point...  1.78 us
  transfers between devices with their start and end apart: 5, of which 4 were waited for; matrix products, arithmetic and copies ran while one was open for 0% of the time, Pallas kernels for 11%

profile of v6, /device:TPU:0, one launch (start us, length us, event | category | flops | bytes accessed | tf_op | source)
XLA Modules:
  0.0 55.2 jit_solution(5750376840881093232)
XLA Ops:
  0.6 0.0 copy-start
  0.6 1.0 %slice_bitcast_fusion = f32[3,32,512]{2,1,0:T(8,128)S(1)} fusion(f32[2,3,32,512]{3,2,1,0:T(8,128)} %refs_0_.3), kind=kLoop, calls=%fused_computation.2 | loop fusion | bytes 393216 | tf_op jit(solution)/shard_map/squeeze | solution.py:299
  1.7 3.0 %collective-permute-start.3 = (f32[2,3,8,512]{3,2,1,0:T(8,128)S(1)}, f32[2,3,8,512]{3,2,1,0:T(8,128)S(1)}, u32[]{:S(2)}, u32[]{:S(2)}) collective-permute-start(f32[2,3,8,512]{3,2,1,0:T(8,128)S(1)} %pad_maximum_fusion.2), channel_id=1, source_target_pairs={{0,1},{1,0},{2,3},{3,2},{4,5},{5,4},{6,7},{7,6},{8,9},{9,8},{10,11... | collective-permute-start | bytes 294920 | tf_op jit(solution)/shard_map/ppermute | solution.py:287
  4.7 0.0 copy-done
  4.7 0.1 collective-permute-start
  4.9 3.2 %collective-permute-done.3.halo = f32[2,3,8,512]{3,2,1,0:T(8,128)S(1)} collective-permute-done((f32[2,3,8,512]{3,2,1,0:T(8,128)S(1)}, f32[2,3,8,512]{3,2,1,0:T(8,128)S(1)}, u32[]{:S(2)}, u32[]{:S(2)}) %collective-permute-start.3) | collective-permute-done | bytes 98336 | tf_op jit(solution)/shard_map/ppermute | solution.py:287
  8.1 1.8 %shard_map.30.refs_2_ = f32[3,32,512]{2,1,0:T(8,128)S(1)} custom-call(f32[2,3,32,512]{3,2,1,0:T(8,128)S(1)} %copy-done, f32[2,3,8,512]{3,2,1,0:T(8,128)S(1)} %collective-permute-done.3.halo), custom_call_target="tpu_custom_call" | custom-call | flops 11796480 | bytes 393216 | tf_op jit(solution)/shard_map/pallas_call | solution.py:255
  9.8 1.8 %collective-permute-done.refs_1_ = f32[2,1,3,16,512]{4,3,2,1,0:T(8,128)S(1)} collective-permute-done((f32[2,1,3,16,512]{4,3,2,1,0:T(8,128)S(1)}, f32[2,1,3,16,512]{4,3,2,1,0:T(8,128)S(1)}, u32[]{:S(2)}, u32[]{:S(2)}) %collective-permute-start) | collective-permute-done | bytes 196640 | tf_op jit(solution)/shard_map/ppermute | solution.py:287
  11.7 4.8 %shard_map.31 = (f32[1,3,32,512]{3,2,1,0:T(8,128)S(1)}, f32[16,1,3,1,2,512]{5,4,3,2,1,0:T(2,128)}) custom-call(f32[2,3,32,512]{3,2,1,0:T(8,128)S(1)} %copy-done, f32[2,1,3,16,512]{4,3,2,1,0:T(8,128)S(1)} %collective-permute-done.refs_1_, f32[3,32,512]{2,1,0:T(8,128)S(1)} %shard_map.30.refs_2_), custom_call_target="tpu_custom_call" | custom-call | flops 23592960 | bytes 786432 | tf_op jit(solution)/shard_map/pallas_call | solution.py:255
  16.5 6.3 %all-to-all-start.1 = ((f32[16,1,3,1,2,512]{5,4,3,2,1,0:T(2,128)}), f32[16,1,3,1,2,512]{5,4,3,2,1,0:T(2,128)S(1)}, u32[]{:S(2)}, u32[]{:S(2)}) async-start(f32[16,1,3,1,2,512]{5,4,3,2,1,0:T(2,128)} %get-tuple-element.15), calls=%async_computation.1 | async-start | bytes 393216 | tf_op jit(solution)/shard_map/all_to_all | solution.py:318
  22.8 0.4 collective-permute-start.1
  23.2 2.6 %collective-permute-start.2 = (f32[2,3,16,512]{3,2,1,0:T(8,128)S(1)}, f32[2,3,16,512]{3,2,1,0:T(8,128)S(1)}, u32[]{:S(2)}, u32[]{:S(2)}) collective-permute-start(f32[2,3,16,512]{3,2,1,0:T(8,128)S(1)} %pad_maximum_fusion.1), channel_id=1, source_target_pairs={{0,3},{1,2},{2,5},{3,4},{4,7},{5,6},{6,9},{7,8},{8,11},{9,10},{10,... | collective-permute-start | bytes 589832 | tf_op jit(solution)/shard_map/ppermute | solution.py:287
  25.8 8.0 %collective-permute-done.1.refs_2_ = f32[3,32,512]{2,1,0:T(8,128)S(1)} collective-permute-done((f32[3,32,512]{2,1,0:T(8,128)S(1)}, f32[3,32,512]{2,1,0:T(8,128)S(1)}, u32[]{:S(2)}, u32[]{:S(2)}) %collective-permute-start.1) | collective-permute-done | bytes 196640 | tf_op jit(solution)/shard_map/ppermute | solution.py:304
  33.9 3.0 %collective-permute-done.2.refs_3_ = f32[2,3,16,512]{3,2,1,0:T(8,128)S(1)} collective-permute-done((f32[2,3,16,512]{3,2,1,0:T(8,128)S(1)}, f32[2,3,16,512]{3,2,1,0:T(8,128)S(1)}, u32[]{:S(2)}, u32[]{:S(2)}) %collective-permute-start.2) | collective-permute-done | bytes 196640 | tf_op jit(solution)/shard_map/ppermute | solution.py:287
  36.8 4.3 %shard_map.32 = (f32[2,3,32,512]{3,2,1,0:T(8,128)}, f32[16,1,3,1,2,512]{5,4,3,2,1,0:T(2,128)S(1)}) custom-call(f32[2,3,32,512]{3,2,1,0:T(8,128)S(1)} %copy-done, f32[2,1,3,16,512]{4,3,2,1,0:T(8,128)S(1)} %collective-permute-done.refs_1_, f32[3,32,512]{2,1,0:T(8,128)S(1)} %collective-permute-done.1.refs_2_, ...), custom_call_target="tpu_custom_call" | custom-call | flops 23592960 | bytes 786432 | tf_op jit(solution)/shard_map/pallas_call | solution.py:255
  41.1 0.0 all-to-all-done.1.others
  41.1 0.0 copy-start.1
  41.1 12.3 %all_to_all.10.opening = f32[16,1,3,1,2,512]{5,4,3,2,1,0:T(2,128)} all-to-all(f32[16,1,3,1,2,512]{5,4,3,2,1,0:T(2,128)S(1)} %get-tuple-element.14), channel_id=1, replica_groups=mesh['tm'=16,'space'=2] {'tm'}, dimensions={0} | all-to-all | bytes 393216 | tf_op jit(solution)/shard_map/all_to_all | solution.py:329
  53.4 0.0 copy-done.1
  53.4 1.8 %shard_map.33 = f32[16,2,3,1,2,512]{5,4,3,2,1,0:T(2,128)} custom-call(f32[16,1,3,1,2,512]{5,4,3,2,1,0:T(2,128)} %all_to_all.10.opening, f32[16,1,3,1,2,512]{5,4,3,2,1,0:T(2,128)} %copy-done.1), custom_call_target="tpu_custom_call" | custom-call | tf_op jit(solution)/shard_map/pallas_call | solution.py:330
  (6 shorter events, 0.1 us)
Async XLA Ops:
  0.6 4.1 %copy-start = (f32[2,3,32,512]{3,2,1,0:T(8,128)S(1)}, f32[2,3,32,512]{3,2,1,0:T(8,128)}, u32[]{:S(2)}) copy-start(f32[2,3,32,512]{3,2,1,0:T(8,128)} %refs_0_.3) | copy-start | bytes 1179652
  1.7 6.4 %collective-permute-start.3 = (f32[2,3,8,512]{3,2,1,0:T(8,128)S(1)}, f32[2,3,8,512]{3,2,1,0:T(8,128)S(1)}, u32[]{:S(2)}, u32[]{:S(2)}) collective-permute-start(f32[2,3,8,512]{3,2,1,0:T(8,128)S(1)} %pad_maximum_fusion.2), channel_id=1, source_target_pairs={{0,1},{1,0},{2,3},{3,2},{4,5},{5,4},{6,7},{7,6},{8,9},{9,8},{10,11... | collective-permute-start | bytes 294920 | tf_op jit(solution)/shard_map/ppermute | solution.py:287
  4.7 7.0 %collective-permute-start = (f32[2,1,3,16,512]{4,3,2,1,0:T(8,128)S(1)}, f32[2,1,3,16,512]{4,3,2,1,0:T(8,128)S(1)}, u32[]{:S(2)}, u32[]{:S(2)}) collective-permute-start(f32[2,1,3,16,512]{4,3,2,1,0:T(8,128)S(1)} %pad_maximum_fusion), channel_id=1, source_target_pairs={{0,1},{1,0},{2,3},{3,2},{4,5},{5,4},{6,7},{7,6},{8,9},{9,8},{10,11... | collective-permute-start | bytes 589832 | tf_op jit(solution)/shard_map/ppermute | solution.py:287
  16.5 24.6 %all-to-all-start.1 = ((f32[16,1,3,1,2,512]{5,4,3,2,1,0:T(2,128)}), f32[16,1,3,1,2,512]{5,4,3,2,1,0:T(2,128)S(1)}, u32[]{:S(2)}, u32[]{:S(2)}) async-start(f32[16,1,3,1,2,512]{5,4,3,2,1,0:T(2,128)} %get-tuple-element.15), calls=%async_computation.1 | async-start | bytes 393216 | tf_op jit(solution)/shard_map/all_to_all | solution.py:318
  22.8 11.1 %collective-permute-start.1 = (f32[3,32,512]{2,1,0:T(8,128)S(1)}, f32[3,32,512]{2,1,0:T(8,128)S(1)}, u32[]{:S(2)}, u32[]{:S(2)}) collective-permute-start(f32[3,32,512]{2,1,0:T(8,128)S(1)} %slice_bitcast_fusion), channel_id=1, source_target_pairs={{0,2},{1,3},{2,4},{3,5},{4,6},{5,7},{6,8},{7,9},{8,10},{9,11},{10,... | collective-permute-start | bytes 589832 | tf_op jit(solution)/shard_map/ppermute | solution.py:304
  23.2 13.6 %collective-permute-start.2 = (f32[2,3,16,512]{3,2,1,0:T(8,128)S(1)}, f32[2,3,16,512]{3,2,1,0:T(8,128)S(1)}, u32[]{:S(2)}, u32[]{:S(2)}) collective-permute-start(f32[2,3,16,512]{3,2,1,0:T(8,128)S(1)} %pad_maximum_fusion.1), channel_id=1, source_target_pairs={{0,3},{1,2},{2,5},{3,4},{4,7},{5,6},{6,9},{7,8},{8,11},{9,10},{10,... | collective-permute-start | bytes 589832 | tf_op jit(solution)/shard_map/ppermute | solution.py:287
  41.1 12.3 %copy-start.1 = (f32[16,1,3,1,2,512]{5,4,3,2,1,0:T(2,128)}, f32[16,1,3,1,2,512]{5,4,3,2,1,0:T(2,128)S(1)}, u32[]{:S(2)}) copy-start(f32[16,1,3,1,2,512]{5,4,3,2,1,0:T(2,128)S(1)} %all-to-all-done.1.others) | copy-start | bytes 589828

commit v7 on v4

--- a/solution.py
+++ b/solution.py
@@ -148,91 +148,49 @@
     return use
 
 
-def own_kernel(chunks, own, halo, advanced, pushed, ext, state, held):
+def chain_kernel(chunks, point, own, halo, advanced, pushed, ext, state, held):
     rows = own.shape[2]
     wide = Rows(rows + 4 * FACTOR, chunks)
-    for k in range(advanced.shape[0]):
-        wide.fill(ext, [halo.at[0, k], own.at[k], halo.at[1, k]])
-        wide.load(ext, state)
-        wide.propagate(state, held, 0)
-        wide.store(ext, state, FACTOR)
-        wide.take(ext, 2 * FACTOR, rows, put(advanced.at[k]))
-        wide.propagate(state, held, FACTOR)
-        wide.store(ext, state, 2 * FACTOR)
-        wide.take(ext, 2 * FACTOR, rows, put(pushed.at[k]))
-
-
-def last_kernel(chunks, own, halo, advanced, pushed, residual, ext, state, held):
-    points, _, rows, _ = own.shape
-    narrow = Rows(rows + 2 * FACTOR, chunks)
-    narrow.fill(ext, [halo.at[0], own.at[points - 1], halo.at[1]])
-    narrow.load(ext, state)
-    narrow.propagate(state, held, 0)
-    narrow.store(ext, state, FACTOR)
-
-    def use(f, span, at, length, value):
-        part = slice(at, at + length)
-        residual[points - 2, f, part, span] = pushed[points - 2, f, part, span] - value
-
-    narrow.take(ext, FACTOR, rows, use)
-    for k in range(points - 2):
-        residual[k] = pushed[k] - advanced[k + 1]
-
-
-def first_kernel(
-    chunks, groups, own, halo, behind, behind_halo, advanced, residual,
-    updated, packed, ext, state, held, first, sems,
-):
-    points, _, rows, _ = own.shape
-    share = rows // groups
-    wide = Rows(rows + 4 * FACTOR, chunks)
-    copies = [
-        pltpu.make_async_copy(advanced, updated.at[pl.ds(1, points - 1)], sems.at[0]),
-        pltpu.make_async_copy(first, updated.at[0], sems.at[1]),
-    ]
-    copies[0].start()
-    wide.fill(ext, [behind_halo.at[0], behind, behind_halo.at[1]])
+    wide.fill(ext, [halo.at[0], own.at[point], halo.at[1]])
     wide.load(ext, state)
     wide.propagate(state, held, 0)
     wide.store(ext, state, FACTOR)
-    wide.take(ext, 2 * FACTOR, rows, put(first))
-    shrink = 0.25**FACTOR
-
-    @pl.when(lax.axis_index("tm") == 0)
-    def _():
-        wide.fill(ext, [halo.at[0, 0], own.at[0], halo.at[1, 0]])
-        wide.load(ext, state)
-        for f, c, i in wide.cells():
-            state[0, f, i, c] = state[0, f, i, c] * (1 / shrink)
-        first[...] = own[0]
-
-    copies[1].start()
+    wide.take(ext, 2 * FACTOR, rows, put(advanced))
     wide.propagate(state, held, FACTOR)
     wide.store(ext, state, 2 * FACTOR)
-    for at, place, length in wide.pieces(2 * FACTOR, rows):
-        for f in range(3):
-            for c, span in enumerate(spans(chunks)):
-                part = slice(place, place + length)
-                ext[f, c, part, :] = ext[f, c, part, :] - advanced[0, f, at : at + length, span]
-    for g in range(groups):
-        for f in range(3):
-            for c, span in enumerate(spans(chunks)):
-                for at, place, length in wide.pieces(2 * FACTOR + g * share, share):
-                    packed[g * points, f, 0, at : at + length, span] = ext[
-                        f, c, place : place + length, :
-                    ]
-                for k in range(1, points):
-                    packed[g * points + k, f, 0, :, span] = residual[
-                        k - 1, f, g * share : (g + 1) * share, span
-                    ]
-    for copy in copies:
-        copy.wait()
+    wide.take(ext, 2 * FACTOR, rows, put(pushed))
+
+
+def pack_kernel(points, groups, pair, *refs):
+    following, pushed, outs = refs[:points], refs[points : 2 * points], refs[2 * points : -1]
+    difference = refs[-1]
+    me = lax.axis_index("tm")
+    rows = difference.shape[2]
+    share = rows // groups
+    for k in range(points):
+        difference[k] = pushed[k][...] - following[k][...]
+
+    @pl.when(me == groups - 1)
+    def _():
+        first = following[points - 1]
+        difference[points - 1] = first[...] - first[...]
+
+    def sort(side):
+        for g in range(groups):
+            target = outs[(g % pair) ^ side]
+            part = slice(g * share, (g + 1) * share)
+            for k in range(points):
+                for f in range(3):
+                    target[g // pair, k, f, 0] = difference[k, f, part, :]
+
+    for side in range(pair):
+        pl.when(me % pair == side)(functools.partial(sort, side))
 
 
 VMEM = pl.BlockSpec(memory_space=pltpu.VMEM)
 
 
-def call(kernel, shapes, work, rows, columns, operands, out_specs=None, extra=()):
+def call(kernel, shapes, work, rows, columns, operands):
     chunks = columns // LANES
     extended = rows + 4 * FACTOR
     cost = pl.CostEstimate(
@@ -244,16 +202,28 @@
         functools.partial(kernel, chunks),
         out_shape=[jax.ShapeDtypeStruct(shape, jnp.float32) for shape in shapes],
         in_specs=[VMEM] * len(operands),
-        out_specs=out_specs or [VMEM] * len(shapes),
+        out_specs=[VMEM] * len(shapes),
         scratch_shapes=[
             pltpu.VMEM((3, chunks, extended + SUB, LANES), jnp.float32),
             pltpu.VMEM((2, 3, extended // SUB, chunks, SUB, LANES), jnp.float32),
             pltpu.VMEM((3, chunks, SUB, LANES), jnp.float32),
-            *extra,
         ],
         compiler_params=pltpu.CompilerParams(vmem_limit_bytes=24 * 2**20),
         cost_estimate=cost,
     )(*operands)
+
+
+def chain(point, c_points, halo):
+    _, fields, rows, columns = c_points.shape
+    shape = (fields, rows, columns)
+    return call(
+        lambda chunks, *refs: chain_kernel(chunks, point, *refs),
+        [shape, shape],
+        2,
+        rows,
+        columns,
+        (c_points, halo),
+    )
 
 
 def edges_of(block, width):
@@ -281,32 +251,49 @@
     )
 
 
+def pack(following, pushed, groups, pair):
+    points, (fields, rows, columns) = len(pushed), pushed[0].shape
+    packet = (groups // pair, points, fields, 1, rows // groups, columns)
+    size = 4 * points * fields * rows * columns
+    return pl.pallas_call(
+        functools.partial(pack_kernel, points, groups, pair),
+        out_shape=[jax.ShapeDtypeStruct(packet, jnp.float32)] * pair,
+        in_specs=[VMEM] * (2 * points),
+        out_specs=[VMEM] * pair,
+        scratch_shapes=[pltpu.VMEM((points, fields, rows, columns), jnp.float32)],
+        compiler_params=pltpu.CompilerParams(vmem_limit_bytes=24 * 2**20),
+        cost_estimate=pl.CostEstimate(flops=size, bytes_accessed=3 * size, transcendentals=0),
+    )(*following, *pushed)
+
+
 def on_device(c_points):
-    points, fields, rows, columns = c_points.shape
+    points = c_points.shape[0]
     groups = lax.axis_size("tm")
-    last = c_points[-1]
-    halo = exchange(edges_of(c_points[:-1], 2 * FACTOR), 0)
-    last_halo = exchange(edges_of(last, FACTOR), 0)
-    behind_halo = exchange(edges_of(last, 2 * FACTOR), 1)
-    behind = lax.ppermute(last, ("tm", "space"), route(1, 0))
-    inner = (points - 1, fields, rows, columns)
-    advanced, pushed = call(
-        own_kernel, [inner, inner], 2 * (points - 1), rows, columns, (c_points, halo)
-    )
-    (residual,) = call(
-        last_kernel, [inner], 1, rows, columns, (c_points, last_halo, advanced, pushed)
-    )
-    updated, packed = call(
-        lambda chunks, *refs: first_kernel(chunks, groups, *refs),
-        [c_points.shape, (groups * points, fields, 1, rows // groups, columns)],
-        2,
-        rows,
-        columns,
-        (c_points, halo, behind, behind_halo, advanced, residual),
-        out_specs=[pl.BlockSpec(memory_space=pl.ANY), VMEM],
-        extra=[pltpu.VMEM((fields, rows, columns), jnp.float32), pltpu.SemaphoreType.DMA((2,))],
-    )
-    return (updated, lax.all_to_all(packed, "tm", split_axis=0, concat_axis=0, tiled=True))
+    me = lax.axis_index("tm")
+    pair = 2 if groups % 2 == 0 else 1
+    both = ("tm", "space")
+    halos = [exchange(edges_of(c_points[k], 2 * FACTOR), 0) for k in range(points)]
+    advanced, pushed = zip(*[chain(k, c_points, halos[k]) for k in range(points)])
+    next_first = lax.ppermute(advanced[0], both, route(-1, 0))
+    sides = pack([*advanced[1:], next_first], pushed, groups, pair)
+    if pair == 2:
+        other = lax.ppermute(sides[1], "tm", [(i, i ^ 1) for i in range(groups)])
+        even = jnp.where(me & 1 == 0, sides[0], other)
+        odd = jnp.where(me & 1 == 0, other, sides[0])
+        sides = [even, odd]
+    coarse = lax.all_to_all(
+        jnp.stack(sides, axis=1),
+        "tm",
+        split_axis=0,
+        concat_axis=0,
+        axis_index_groups=[list(range(side, groups, pair)) for side in range(pair)],
+        tiled=True,
+    )
+    coarse = coarse.reshape(groups * points, *coarse.shape[3:])
+    coarse = jnp.concatenate([coarse[-1:], coarse[:-1]], axis=0)
+    incoming = lax.ppermute(advanced[-1], both, route(1, 0))
+    opening = jnp.where(me == 0, c_points[0], incoming)
+    return (jnp.stack([opening, *advanced[:-1]]), coarse)
 
 
 def solution(mesh):

time: 42.1 us -> 45.1 us (1.071)
  blocking collectives: 19 us -> 0 us
  waiting for transfers between devices: 3.63 us -> 21 us
  starting transfers between devices: 6.42 us -> 10.9 us
  other arithmetic: 0.04 us -> 2.13 us
  Pallas kernels: 10.2 us -> 8.27 us
    all_to_all x1 -> x0, blocking collectives: 19 us -> none  [on_device(): lax.all_to_all(packed, 'tm', split_axis=0, concat_axis=0, tiled=True)]
    ppermute x1 -> x3, waiting for transfers between devices: 0.01 us -> 15.4 us  [the longest x1 13.9 us: on_device(): incoming = lax.ppermute(advanced[-1], both, route(1, 0))]
    all_to_all x0 -> x1, starting transfers between devices: none -> 5.02 us  [on_device(): lax.all_to_all(jnp.stack(sides, axis=1), 'tm', split_axis=0, concat_axis=...]
    ppermute x3 -> x2, starting transfers between devices: 6.37 us -> 3.09 us  [exchange(): return lax.ppermute(edges, both, route(shift, 1))]
    ppermute x1 -> x3, starting transfers between devices: 0.06 us -> 2.75 us  [the longest x1 2.6 us: on_device(): next_first = lax.ppermute(advanced[0], both, route(-1, 0))]
    pallas_call x3 -> x2, Pallas kernels: 10.2 us -> 8.14 us  [call(): pl.pallas_call(functools.partial(kernel, chunks), out_shape=[jax.ShapeDty...]
    ppermute x3 -> x2, waiting for transfers between devices: 3.63 us -> 5.63 us  [exchange(): return lax.ppermute(edges, both, route(shift, 1))]
    another operation x0 -> x5, other arithmetic: none -> 1.18 us  [the longest x2 0.8 us: on_device(): return (jnp.stack([opening, *advanced[:-1]]), coarse)]
  transfers between devices with their start and end apart: 4 -> 6, of which waited for: 2 -> 3; matrix products, arithmetic and copies ran while one was open for 0% -> 2% of each run, Pallas kernels for 14% -> 18%
where the time goes in v7:
time: 45.1 us; the launch traced here: 44.9 us
  waiting for transfers between devices  21 us (47%)
  starting transfers between devices  10.9 us (24%)
  Pallas kernels  8.27 us (18%)
  other arithmetic  2.13 us (5%)
  local copies, waits for them, and re-layouts  1.89 us (4%)
  between operations  0.75 us (2%)
    ppermute x1, waiting for transfers between devices, on_device(): incoming = lax.ppermute(advanced[-1], both, route(1, 0))  13.9 us
    pallas_call x2, Pallas kernels, call(): pl.pallas_call(functools.partial(kernel, chunks), out_shape=[jax.ShapeDty...  8.14 us
    ppermute x2, waiting for transfers between devices, exchange(): return lax.ppermute(edges, both, route(shift, 1))  5.63 us
    all_to_all x1, starting transfers between devices, on_device(): lax.all_to_all(jnp.stack(sides, axis=1), 'tm', split_axis=0, concat_axis=...  5.02 us
    ppermute x2, starting transfers between devices, exchange(): return lax.ppermute(edges, both, route(shift, 1))  3.09 us
    ppermute x1, starting transfers between devices, on_device(): next_first = lax.ppermute(advanced[0], both, route(-1, 0))  2.6 us
    ppermute x1, waiting for transfers between devices, on_device(): other = lax.ppermute(sides[1], 'tm', [(i, i ^ 1) for i in range(groups)])  1.42 us
    squeeze x1, local copies, waits for them, and re-layouts, on_device(): c_points[k]  1.05 us
  transfers between devices with their start and end apart: 6, of which 3 were waited for; matrix products, arithmetic and copies ran while one was open for 2% of the time, Pallas kernels for 18%

profile of v7, /device:TPU:0, one launch (start us, length us, event | category | flops | bytes accessed | tf_op | source)
XLA Modules:
  0.0 44.9 jit_solution(3888490162960203915)
XLA Ops:
  0.6 1.1 %slice_bitcast_fusion = (f32[3,32,512]{2,1,0:T(8,128)S(1)}, f32[3,32,512]{2,1,0:T(8,128)S(1)}) fusion(f32[2,3,32,512]{3,2,1,0:T(8,128)} %refs_0_.3), kind=kLoop, calls=%fused_computation.10 | loop fusion | bytes 786432 | tf_op jit(solution)/shard_map/squeeze | solution.py:275
  1.7 0.0 copy-start
  1.8 3.0 %collective-permute-start.2 = (f32[2,3,16,512]{3,2,1,0:T(8,128)S(1)}, f32[2,3,16,512]{3,2,1,0:T(8,128)S(1)}, u32[]{:S(2)}, u32[]{:S(2)}) collective-permute-start(f32[2,3,16,512]{3,2,1,0:T(8,128)S(1)} %pad_maximum_fusion.3), channel_id=1, source_target_pairs={{0,1},{1,0},{2,3},{3,2},{4,5},{5,4},{6,7},{7,6},{8,9},{9,8},{10,11... | collective-permute-start | bytes 589832 | tf_op jit(solution)/shard_map/ppermute | solution.py:245
  4.8 0.1 collective-permute-start
  4.9 5.6 %collective-permute-done.2.refs_1_ = f32[2,3,16,512]{3,2,1,0:T(8,128)S(1)} collective-permute-done((f32[2,3,16,512]{3,2,1,0:T(8,128)S(1)}, f32[2,3,16,512]{3,2,1,0:T(8,128)S(1)}, u32[]{:S(2)}, u32[]{:S(2)}) %collective-permute-start.2) | collective-permute-done | bytes 196640 | tf_op jit(solution)/shard_map/ppermute | solution.py:245
  10.5 0.0 copy-done
  10.5 4.1 %shard_map.31 = (f32[3,32,512]{2,1,0:T(8,128)S(1)}, f32[3,32,512]{2,1,0:T(8,128)S(1)}) custom-call(f32[2,3,32,512]{3,2,1,0:T(8,128)S(1)} %copy-done, f32[2,3,16,512]{3,2,1,0:T(8,128)S(1)} %collective-permute-done.2.refs_1_), custom_call_target="tpu_custom_call" | custom-call | flops 23592960 | bytes 786432 | tf_op jit(solution)/shard_map/pallas_call | solution.py:201
  14.6 2.6 %collective-permute-start.3 = (f32[3,32,512]{2,1,0:T(8,128)S(1)}, f32[3,32,512]{2,1,0:T(8,128)S(1)}, u32[]{:S(2)}, u32[]{:S(2)}) collective-permute-start(f32[3,32,512]{2,1,0:T(8,128)S(1)} %get-tuple-element.9), channel_id=1, source_target_pairs={{0,30},{1,31},{2,0},{3,1},{4,2},{5,3},{6,4},{7,5},{8,6},{9,7},{10,... | collective-permute-start | bytes 589832 | tf_op jit(solution)/shard_map/ppermute | solution.py:277
  17.2 0.0 collective-permute-done.refs_1_
  17.2 4.1 %shard_map.30 = (f32[3,32,512]{2,1,0:T(8,128)S(1)}, f32[3,32,512]{2,1,0:T(8,128)S(1)}) custom-call(f32[2,3,32,512]{3,2,1,0:T(8,128)S(1)} %copy-done, f32[2,3,16,512]{3,2,1,0:T(8,128)S(1)} %collective-permute-done.refs_1_), custom_call_target="tpu_custom_call" | custom-call | flops 23592960 | bytes 786432 | tf_op jit(solution)/shard_map/pallas_call | solution.py:201
  21.3 0.0 collective-permute-done.3.refs_1_
  21.3 0.1 shard_map.32
  21.4 0.1 collective-permute-start.4
  21.5 1.4 %collective-permute-done.4 = f32[8,2,3,1,2,512]{5,4,3,2,1,0:T(2,128)S(1)} collective-permute-done((f32[8,2,3,1,2,512]{5,4,3,2,1,0:T(2,128)S(1)}, f32[8,2,3,1,2,512]{5,4,3,2,1,0:T(2,128)S(1)}, u32[]{:S(2)}, u32[]{:S(2)}) %collective-permute-start.4) | collective-permute-done | bytes 196640 | tf_op jit(solution)/shard_map/ppermute | solution.py:280
  22.9 0.1 fusion.1
  23.0 0.1 fusion
  23.1 0.2 pad_maximum_fusion.1
  23.3 0.8 %copy.14 = f32[8,2,2,3,1,2,512]{6,5,3,2,4,1,0:T(2,128)} copy(f32[8,2,2,3,1,2,512]{6,5,3,2,0,4,1:T(2,128)S(1)} %pad_maximum_fusion.1) | data formatting | bytes 786432 | tf_op jit(solution)/shard_map/stack | solution.py:285
  24.1 5.0 %all-to-all-start = ((f32[8,2,2,3,1,2,512]{6,5,3,2,4,1,0:T(2,128)}), f32[8,2,2,3,1,2,512]{6,5,3,2,4,1,0:T(2,128)S(1)}, u32[]{:S(2)}, u32[]{:S(2)}) async-start(f32[8,2,2,3,1,2,512]{6,5,3,2,4,1,0:T(2,128)} %copy.14), calls=%async_computation | async-start | bytes 786432 | tf_op jit(solution)/shard_map/all_to_all | solution.py:284
  29.1 0.1 collective-permute-start.1
  29.2 13.9 %collective-permute-done.1 = f32[3,32,512]{2,1,0:T(8,128)S(1)} collective-permute-done((f32[3,32,512]{2,1,0:T(8,128)S(1)}, f32[3,32,512]{2,1,0:T(8,128)S(1)}, u32[]{:S(2)}, u32[]{:S(2)}) %collective-permute-start.1) | collective-permute-done | bytes 196640 | tf_op jit(solution)/shard_map/ppermute | solution.py:294
  43.1 0.8 %pad_maximum_fusion = f32[2,3,32,512]{3,2,1,0:T(8,128)} fusion(f32[1,3,32,512]{3,2,1,0:T(8,128)S(1)} %bitcast.34, f32[1,3,32,512]{3,2,1,0:T(8,128)S(1)} %select_bitcast_fusion), kind=kLoop, calls=%fused_computation | loop fusion | flops 98304 | bytes 786432 | tf_op jit(solution)/shard_map/stack | solution.py:296
  43.9 0.0 all-to-all-done
  44.0 0.9 %maximum_bitcast_fusion = f32[32,3,1,2,512]{4,3,2,1,0:T(2,128)} fusion(f32[31,3,1,2,512]{4,3,1,0,2:T(2,128)S(1)} %slice.38, f32[1,3,1,2,512]{4,3,1,0,2:T(2,128)S(1)} %slice.37), kind=kLoop, calls=%fused_computation.2 | loop fusion | flops 98304 | bytes 786432
  (6 shorter events, 0.1 us)
Async XLA Ops:
  1.7 8.8 %copy-start = (f32[2,3,32,512]{3,2,1,0:T(8,128)S(1)}, f32[2,3,32,512]{3,2,1,0:T(8,128)}, u32[]{:S(2)}) copy-start(f32[2,3,32,512]{3,2,1,0:T(8,128)} %refs_0_.3) | copy-start | bytes 1179652
  1.8 8.7 %collective-permute-start.2 = (f32[2,3,16,512]{3,2,1,0:T(8,128)S(1)}, f32[2,3,16,512]{3,2,1,0:T(8,128)S(1)}, u32[]{:S(2)}, u32[]{:S(2)}) collective-permute-start(f32[2,3,16,512]{3,2,1,0:T(8,128)S(1)} %pad_maximum_fusion.3), channel_id=1, source_target_pairs={{0,1},{1,0},{2,3},{3,2},{4,5},{5,4},{6,7},{7,6},{8,9},{9,8},{10,11... | collective-permute-start | bytes 589832 | tf_op jit(solution)/shard_map/ppermute | solution.py:245
  4.8 12.4 %collective-permute-start = (f32[2,3,16,512]{3,2,1,0:T(8,128)S(1)}, f32[2,3,16,512]{3,2,1,0:T(8,128)S(1)}, u32[]{:S(2)}, u32[]{:S(2)}) collective-permute-start(f32[2,3,16,512]{3,2,1,0:T(8,128)S(1)} %pad_maximum_fusion.2), channel_id=1, source_target_pairs={{0,1},{1,0},{2,3},{3,2},{4,5},{5,4},{6,7},{7,6},{8,9},{9,8},{10,11... | collective-permute-start | bytes 589832 | tf_op jit(solution)/shard_map/ppermute | solution.py:245
  14.6 6.7 %collective-permute-start.3 = (f32[3,32,512]{2,1,0:T(8,128)S(1)}, f32[3,32,512]{2,1,0:T(8,128)S(1)}, u32[]{:S(2)}, u32[]{:S(2)}) collective-permute-start(f32[3,32,512]{2,1,0:T(8,128)S(1)} %get-tuple-element.9), channel_id=1, source_target_pairs={{0,30},{1,31},{2,0},{3,1},{4,2},{5,3},{6,4},{7,5},{8,6},{9,7},{10,... | collective-permute-start | bytes 589832 | tf_op jit(solution)/shard_map/ppermute | solution.py:277
  21.4 1.5 %collective-permute-start.4 = (f32[8,2,3,1,2,512]{5,4,3,2,1,0:T(2,128)S(1)}, f32[8,2,3,1,2,512]{5,4,3,2,1,0:T(2,128)S(1)}, u32[]{:S(2)}, u32[]{:S(2)}) collective-permute-start(f32[8,2,3,1,2,512]{5,4,3,2,1,0:T(2,128)S(1)} %get-tuple-element.13), channel_id=1, source_target_pairs={{0,2},{2,0},{4,6},{6,4},{8,10},{10,8},{12,14},{14,12},{16,18},{18,... | collective-permute-start | bytes 589832 | tf_op jit(solution)/shard_map/ppermute | solution.py:280
  24.1 19.8 %all-to-all-start = ((f32[8,2,2,3,1,2,512]{6,5,3,2,4,1,0:T(2,128)}), f32[8,2,2,3,1,2,512]{6,5,3,2,4,1,0:T(2,128)S(1)}, u32[]{:S(2)}, u32[]{:S(2)}) async-start(f32[8,2,2,3,1,2,512]{6,5,3,2,4,1,0:T(2,128)} %copy.14), calls=%async_computation | async-start | bytes 786432 | tf_op jit(solution)/shard_map/all_to_all | solution.py:284
  29.1 14.0 %collective-permute-start.1 = (f32[3,32,512]{2,1,0:T(8,128)S(1)}, f32[3,32,512]{2,1,0:T(8,128)S(1)}, u32[]{:S(2)}, u32[]{:S(2)}) collective-permute-start(f32[3,32,512]{2,1,0:T(8,128)S(1)} %get-tuple-element.8.refs_0_), channel_id=1, source_target_pairs={{0,2},{1,3},{2,4},{3,5},{4,6},{5,7},{6,8},{7,9},{8,10},{9,11},{10,... | collective-permute-start | bytes 589832 | tf_op jit(solution)/shard_map/ppermute | solution.py:294

commit v8 on v7

--- a/solution.py
+++ b/solution.py
@@ -148,10 +148,10 @@
     return use
 
 
-def chain_kernel(chunks, point, own, halo, advanced, pushed, ext, state, held):
-    rows = own.shape[2]
+def behind_kernel(chunks, own, halo, advanced, pushed, ext, state, held):
+    rows = own.shape[1]
     wide = Rows(rows + 4 * FACTOR, chunks)
-    wide.fill(ext, [halo.at[0], own.at[point], halo.at[1]])
+    wide.fill(ext, [halo.at[0], own, halo.at[1]])
     wide.load(ext, state)
     wide.propagate(state, held, 0)
     wide.store(ext, state, FACTOR)
@@ -161,36 +161,53 @@
     wide.take(ext, 2 * FACTOR, rows, put(pushed))
 
 
-def pack_kernel(points, groups, pair, *refs):
-    following, pushed, outs = refs[:points], refs[points : 2 * points], refs[2 * points : -1]
-    difference = refs[-1]
-    me = lax.axis_index("tm")
+def own_kernel(chunks, own, halo, behind, advanced, pushed, updated, ext, state, held, sems):
+    inner, _, rows, _ = advanced.shape
+    wide = Rows(rows + 4 * FACTOR, chunks)
+    leading = lax.axis_index("tm") == 0
+    start = pltpu.make_async_copy(own.at[0], updated.at[0], sems.at[0])
+    opening = pltpu.make_async_copy(behind, updated.at[0], sems.at[0])
+    pl.when(leading)(start.start)
+    pl.when(jnp.logical_not(leading))(opening.start)
+    copies = []
+    for k in range(inner):
+        wide.fill(ext, [halo.at[0, k], own.at[k], halo.at[1, k]])
+        wide.load(ext, state)
+        wide.propagate(state, held, 0)
+        wide.store(ext, state, FACTOR)
+        wide.take(ext, 2 * FACTOR, rows, put(advanced.at[k]))
+        copies.append(pltpu.make_async_copy(advanced.at[k], updated.at[k + 1], sems.at[k + 1]))
+        copies[-1].start()
+        wide.propagate(state, held, FACTOR)
+        wide.store(ext, state, 2 * FACTOR)
+        wide.take(ext, 2 * FACTOR, rows, put(pushed.at[k]))
+    opening.wait()
+    for copy in copies:
+        copy.wait()
+
+
+def pack_kernel(points, groups, opening, advanced, pushed, following, packed, difference):
     rows = difference.shape[2]
     share = rows // groups
     for k in range(points):
-        difference[k] = pushed[k][...] - following[k][...]
-
-    @pl.when(me == groups - 1)
+        before = opening[...] if k == 0 else pushed[k - 1]
+        difference[k] = before - (following[...] if k == points - 1 else advanced[k])
+
+    @pl.when(lax.axis_index("tm") == 0)
     def _():
-        first = following[points - 1]
-        difference[points - 1] = first[...] - first[...]
-
-    def sort(side):
-        for g in range(groups):
-            target = outs[(g % pair) ^ side]
-            part = slice(g * share, (g + 1) * share)
-            for k in range(points):
-                for f in range(3):
-                    target[g // pair, k, f, 0] = difference[k, f, part, :]
-
-    for side in range(pair):
-        pl.when(me % pair == side)(functools.partial(sort, side))
+        difference[0] = advanced[0] - advanced[0]
+
+    for g in range(groups):
+        part = slice(g * share, (g + 1) * share)
+        for k in range(points):
+            for f in range(3):
+                packed[g * points + k, f, 0] = difference[k, f, part, :]
 
 
 VMEM = pl.BlockSpec(memory_space=pltpu.VMEM)
 
 
-def call(kernel, shapes, work, rows, columns, operands):
+def call(kernel, shapes, work, rows, columns, operands, out_specs=None, extra=()):
     chunks = columns // LANES
     extended = rows + 4 * FACTOR
     cost = pl.CostEstimate(
@@ -202,28 +219,16 @@
         functools.partial(kernel, chunks),
         out_shape=[jax.ShapeDtypeStruct(shape, jnp.float32) for shape in shapes],
         in_specs=[VMEM] * len(operands),
-        out_specs=[VMEM] * len(shapes),
+        out_specs=out_specs or [VMEM] * len(shapes),
         scratch_shapes=[
             pltpu.VMEM((3, chunks, extended + SUB, LANES), jnp.float32),
             pltpu.VMEM((2, 3, extended // SUB, chunks, SUB, LANES), jnp.float32),
             pltpu.VMEM((3, chunks, SUB, LANES), jnp.float32),
+            *extra,
         ],
         compiler_params=pltpu.CompilerParams(vmem_limit_bytes=24 * 2**20),
         cost_estimate=cost,
     )(*operands)
-
-
-def chain(point, c_points, halo):
-    _, fields, rows, columns = c_points.shape
-    shape = (fields, rows, columns)
-    return call(
-        lambda chunks, *refs: chain_kernel(chunks, point, *refs),
-        [shape, shape],
-        2,
-        rows,
-        columns,
-        (c_points, halo),
-    )
 
 
 def edges_of(block, width):
@@ -251,49 +256,46 @@
     )
 
 
-def pack(following, pushed, groups, pair):
-    points, (fields, rows, columns) = len(pushed), pushed[0].shape
-    packet = (groups // pair, points, fields, 1, rows // groups, columns)
-    size = 4 * points * fields * rows * columns
+def pack(opening, advanced, pushed, following, groups):
+    points, (fields, rows, columns) = pushed.shape[0] + 1, opening.shape
+    packet = (groups * points, fields, 1, rows // groups, columns)
+    size = points * fields * rows * columns
     return pl.pallas_call(
-        functools.partial(pack_kernel, points, groups, pair),
-        out_shape=[jax.ShapeDtypeStruct(packet, jnp.float32)] * pair,
-        in_specs=[VMEM] * (2 * points),
-        out_specs=[VMEM] * pair,
+        functools.partial(pack_kernel, points, groups),
+        out_shape=jax.ShapeDtypeStruct(packet, jnp.float32),
+        in_specs=[VMEM] * 4,
+        out_specs=VMEM,
         scratch_shapes=[pltpu.VMEM((points, fields, rows, columns), jnp.float32)],
         compiler_params=pltpu.CompilerParams(vmem_limit_bytes=24 * 2**20),
-        cost_estimate=pl.CostEstimate(flops=size, bytes_accessed=3 * size, transcendentals=0),
-    )(*following, *pushed)
+        cost_estimate=pl.CostEstimate(flops=size, bytes_accessed=12 * size, transcendentals=0),
+    )(opening, advanced, pushed, following)
 
 
 def on_device(c_points):
-    points = c_points.shape[0]
+    points, fields, rows, columns = c_points.shape
     groups = lax.axis_size("tm")
-    me = lax.axis_index("tm")
-    pair = 2 if groups % 2 == 0 else 1
     both = ("tm", "space")
-    halos = [exchange(edges_of(c_points[k], 2 * FACTOR), 0) for k in range(points)]
-    advanced, pushed = zip(*[chain(k, c_points, halos[k]) for k in range(points)])
-    next_first = lax.ppermute(advanced[0], both, route(-1, 0))
-    sides = pack([*advanced[1:], next_first], pushed, groups, pair)
-    if pair == 2:
-        other = lax.ppermute(sides[1], "tm", [(i, i ^ 1) for i in range(groups)])
-        even = jnp.where(me & 1 == 0, sides[0], other)
-        odd = jnp.where(me & 1 == 0, other, sides[0])
-        sides = [even, odd]
-    coarse = lax.all_to_all(
-        jnp.stack(sides, axis=1),
-        "tm",
-        split_axis=0,
-        concat_axis=0,
-        axis_index_groups=[list(range(side, groups, pair)) for side in range(pair)],
-        tiled=True,
-    )
-    coarse = coarse.reshape(groups * points, *coarse.shape[3:])
-    coarse = jnp.concatenate([coarse[-1:], coarse[:-1]], axis=0)
-    incoming = lax.ppermute(advanced[-1], both, route(1, 0))
-    opening = jnp.where(me == 0, c_points[0], incoming)
-    return (jnp.stack([opening, *advanced[:-1]]), coarse)
+    last = c_points[-1]
+    behind_halo = exchange(edges_of(last, 2 * FACTOR), 1)
+    behind = lax.ppermute(last, both, route(1, 0))
+    halo = exchange(edges_of(c_points[:-1], 2 * FACTOR), 0)
+    opening, first_pushed = call(
+        behind_kernel, [last.shape] * 2, 2, rows, columns, (behind, behind_halo)
+    )
+    following = lax.ppermute(opening, both, route(-1, 0))
+    inner = (points - 1, fields, rows, columns)
+    advanced, pushed, updated = call(
+        own_kernel,
+        [inner, inner, c_points.shape],
+        2 * (points - 1),
+        rows,
+        columns,
+        (c_points, halo, opening),
+        out_specs=[VMEM, VMEM, pl.BlockSpec(memory_space=pl.ANY)],
+        extra=[pltpu.SemaphoreType.DMA((points,))],
+    )
+    packed = pack(first_pushed, advanced, pushed, following, groups)
+    return (updated, lax.all_to_all(packed, "tm", split_axis=0, concat_axis=0, tiled=True))
 
 
 def solution(mesh):

time: 45.1 us -> 42 us (0.931)
  blocking collectives: 0 us -> 17 us
  waiting for transfers between devices: 21 us -> 7.47 us
  starting transfers between devices: 10.9 us -> 6.6 us
  other arithmetic: 2.13 us -> 0.03 us
    all_to_all x0 -> x1, blocking collectives: none -> 17 us  [on_device(): lax.all_to_all(packed, 'tm', split_axis=0, concat_axis=0, tiled=True)]
    ppermute x3 -> x2, waiting for transfers between devices: 15.4 us -> 3.89 us  [the longest x1 3.89 us: on_device(): behind = lax.ppermute(last, both, route(1, 0))]
    all_to_all x1 -> x0, starting transfers between devices: 5.02 us -> none  [on_device(): lax.all_to_all(jnp.stack(sides, axis=1), 'tm', split_axis=0, concat_axis=...]
    ppermute x2, waiting for transfers between devices: 5.63 us -> 3.58 us  [exchange(): return lax.ppermute(edges, both, route(shift, 1))]
    ppermute x2, starting transfers between devices: 3.09 us -> 4.38 us  [exchange(): return lax.ppermute(edges, both, route(shift, 1))]
    another operation x5 -> x0, other arithmetic: 1.18 us -> none  [the longest x2 0.8 us: on_device(): return (jnp.stack([opening, *advanced[:-1]]), coarse)]
    unnamed x1 -> x0, other arithmetic: 0.92 us -> none
    another operation x1 -> x0, local copies, waits for them, and re-layouts: 0.78 us -> none  [on_device(): jnp.stack(sides, axis=1)]
  transfers between devices with their start and end apart: 6 -> 4, of which waited for: 3 -> 2; matrix products, arithmetic and copies ran while one was open for 2% -> 0% of each run, Pallas kernels for 18% -> 19%
where the time goes in v8:
time: 42 us; the launch traced here: 41.9 us
  blocking collectives  17 us (40%)
  Pallas kernels  8.3 us (20%)
  waiting for transfers between devices  7.47 us (18%)
  starting transfers between devices  6.6 us (16%)
  local copies, waits for them, and re-layouts  1.72 us (4%)
  between operations  0.7 us (2%)
    all_to_all x1, blocking collectives, on_device(): lax.all_to_all(packed, 'tm', split_axis=0, concat_axis=0, tiled=True)  17 us
    pallas_call x2, Pallas kernels, call(): pl.pallas_call(functools.partial(kernel, chunks), out_shape=[jax.ShapeDty...  8.16 us
    ppermute x2, starting transfers between devices, exchange(): return lax.ppermute(edges, both, route(shift, 1))  4.38 us
    ppermute x1, waiting for transfers between devices, on_device(): behind = lax.ppermute(last, both, route(1, 0))  3.89 us
    ppermute x2, waiting for transfers between devices, exchange(): return lax.ppermute(edges, both, route(shift, 1))  3.58 us
    ppermute x1, starting transfers between devices, on_device(): following = lax.ppermute(opening, both, route(-1, 0))  1.72 us
    squeeze x1, local copies, waits for them, and re-layouts, on_device(): last = c_points[-1]  0.94 us
  transfers between devices with their start and end apart: 4, of which 2 were waited for; matrix products, arithmetic and copies ran while one was open for 0% of the time, Pallas kernels for 19%

profile of v8, /device:TPU:0, one launch (start us, length us, event | category | flops | bytes accessed | tf_op | source)
XLA Modules:
  0.0 41.9 jit_solution(14063252934018562628)
XLA Ops:
  0.6 0.9 %slice_bitcast_fusion = f32[3,32,512]{2,1,0:T(8,128)S(1)} fusion(f32[2,3,32,512]{3,2,1,0:T(8,128)} %own.1), kind=kLoop, calls=%fused_computation.2 | loop fusion | bytes 393216 | tf_op jit(solution)/shard_map/squeeze | solution.py:278
  1.6 0.0 copy-start
  1.6 0.5 %collective-permute-start.1 = (f32[3,32,512]{2,1,0:T(8,128)S(1)}, f32[3,32,512]{2,1,0:T(8,128)S(1)}, u32[]{:S(2)}, u32[]{:S(2)}) collective-permute-start(f32[3,32,512]{2,1,0:T(8,128)S(1)} %slice_bitcast_fusion), channel_id=1, source_target_pairs={{0,2},{1,3},{2,4},{3,5},{4,6},{5,7},{6,8},{7,9},{8,10},{9,11},{10,... | collective-permute-start | bytes 589832 | tf_op jit(solution)/shard_map/ppermute | solution.py:280
  2.1 3.8 %collective-permute-start.2 = (f32[2,3,16,512]{3,2,1,0:T(8,128)S(1)}, f32[2,3,16,512]{3,2,1,0:T(8,128)S(1)}, u32[]{:S(2)}, u32[]{:S(2)}) collective-permute-start(f32[2,3,16,512]{3,2,1,0:T(8,128)S(1)} %pad_maximum_fusion.1), channel_id=1, source_target_pairs={{0,3},{1,2},{2,5},{3,4},{4,7},{5,6},{6,9},{7,8},{8,11},{9,10},{10,... | collective-permute-start | bytes 589832 | tf_op jit(solution)/shard_map/ppermute | solution.py:250
  5.9 0.0 copy-done
  6.0 0.6 %collective-permute-start = (f32[2,1,3,16,512]{4,3,2,1,0:T(8,128)S(1)}, f32[2,1,3,16,512]{4,3,2,1,0:T(8,128)S(1)}, u32[]{:S(2)}, u32[]{:S(2)}) collective-permute-start(f32[2,1,3,16,512]{4,3,2,1,0:T(8,128)S(1)} %pad_maximum_fusion), channel_id=1, source_target_pairs={{0,1},{1,0},{2,3},{3,2},{4,5},{5,4},{6,7},{7,6},{8,9},{9,8},{10,11... | collective-permute-start | bytes 589832 | tf_op jit(solution)/shard_map/ppermute | solution.py:250
  6.6 3.9 %collective-permute-done.1.own = f32[3,32,512]{2,1,0:T(8,128)S(1)} collective-permute-done((f32[3,32,512]{2,1,0:T(8,128)S(1)}, f32[3,32,512]{2,1,0:T(8,128)S(1)}, u32[]{:S(2)}, u32[]{:S(2)}) %collective-permute-start.1) | collective-permute-done | bytes 196640 | tf_op jit(solution)/shard_map/ppermute | solution.py:280
  10.4 3.6 %collective-permute-done.2.halo = f32[2,3,16,512]{3,2,1,0:T(8,128)S(1)} collective-permute-done((f32[2,3,16,512]{3,2,1,0:T(8,128)S(1)}, f32[2,3,16,512]{3,2,1,0:T(8,128)S(1)}, u32[]{:S(2)}, u32[]{:S(2)}) %collective-permute-start.2) | collective-permute-done | bytes 196640 | tf_op jit(solution)/shard_map/ppermute | solution.py:250
  14.0 4.1 %shard_map.30 = (f32[3,32,512]{2,1,0:T(8,128)S(1)}, f32[3,32,512]{2,1,0:T(8,128)S(1)}) custom-call(f32[3,32,512]{2,1,0:T(8,128)S(1)} %collective-permute-done.1.own, f32[2,3,16,512]{3,2,1,0:T(8,128)S(1)} %collective-permute-done.2.halo), custom_call_target="tpu_custom_call" | custom-call | flops 23592960 | bytes 786432 | tf_op jit(solution)/shard_map/pallas_call | solution.py:218
  18.1 1.7 %collective-permute-start.3 = (f32[3,32,512]{2,1,0:T(8,128)S(1)}, f32[3,32,512]{2,1,0:T(8,128)S(1)}, u32[]{:S(2)}, u32[]{:S(2)}) collective-permute-start(f32[3,32,512]{2,1,0:T(8,128)S(1)} %get-tuple-element.7.behind), channel_id=1, source_target_pairs={{0,30},{1,31},{2,0},{3,1},{4,2},{5,3},{6,4},{7,5},{8,6},{9,7},{10,... | collective-permute-start | bytes 589832 | tf_op jit(solution)/shard_map/ppermute | solution.py:285
  19.8 0.0 collective-permute-done.halo
  19.8 4.1 %shard_map.31 = (f32[1,3,32,512]{3,2,1,0:T(8,128)S(1)}, f32[1,3,32,512]{3,2,1,0:T(8,128)S(1)}, f32[2,3,32,512]{3,2,1,0:T(8,128)}) custom-call(f32[2,3,32,512]{3,2,1,0:T(8,128)S(1)} %copy-done, f32[2,1,3,16,512]{4,3,2,1,0:T(8,128)S(1)} %collective-permute-done.halo, f32[3,32,512]{2,1,0:T(8,128)S(1)} %get-tuple-element.7.behind), custom_call_target="tpu_custom_call" | custom-call | flops 23592960 | bytes 786432 | tf_op jit(solution)/shard_map/pallas_call | solution.py:218
  23.9 0.0 collective-permute-done.3.following
  23.9 0.1 shard_map.32
  24.1 17.0 %all_to_all.5 = f32[32,3,1,2,512]{4,3,2,1,0:T(2,128)S(1)} all-to-all(f32[32,3,1,2,512]{4,3,2,1,0:T(2,128)S(1)} %shard_map.32), channel_id=1, replica_groups=mesh['tm'=16,'space'=2] {'tm'}, dimensions={0} | all-to-all | bytes 786432 | tf_op jit(solution)/shard_map/all_to_all | solution.py:298
  41.1 0.7 %copy.4 = f32[32,3,1,2,512]{4,3,2,1,0:T(2,128)} copy(f32[32,3,1,2,512]{4,3,2,1,0:T(2,128)S(1)} %all_to_all.5) | data formatting | bytes 786432
  (4 shorter events, 0.1 us)
Async XLA Ops:
  1.6 4.3 %copy-start = (f32[2,3,32,512]{3,2,1,0:T(8,128)S(1)}, f32[2,3,32,512]{3,2,1,0:T(8,128)}, u32[]{:S(2)}) copy-start(f32[2,3,32,512]{3,2,1,0:T(8,128)} %own.1) | copy-start | bytes 1179652
  1.6 8.9 %collective-permute-start.1 = (f32[3,32,512]{2,1,0:T(8,128)S(1)}, f32[3,32,512]{2,1,0:T(8,128)S(1)}, u32[]{:S(2)}, u32[]{:S(2)}) collective-permute-start(f32[3,32,512]{2,1,0:T(8,128)S(1)} %slice_bitcast_fusion), channel_id=1, source_target_pairs={{0,2},{1,3},{2,4},{3,5},{4,6},{5,7},{6,8},{7,9},{8,10},{9,11},{10,... | collective-permute-start | bytes 589832 | tf_op jit(solution)/shard_map/ppermute | solution.py:280
  2.1 11.9 %collective-permute-start.2 = (f32[2,3,16,512]{3,2,1,0:T(8,128)S(1)}, f32[2,3,16,512]{3,2,1,0:T(8,128)S(1)}, u32[]{:S(2)}, u32[]{:S(2)}) collective-permute-start(f32[2,3,16,512]{3,2,1,0:T(8,128)S(1)} %pad_maximum_fusion.1), channel_id=1, source_target_pairs={{0,3},{1,2},{2,5},{3,4},{4,7},{5,6},{6,9},{7,8},{8,11},{9,10},{10,... | collective-permute-start | bytes 589832 | tf_op jit(solution)/shard_map/ppermute | solution.py:250
  6.0 13.9 %collective-permute-start = (f32[2,1,3,16,512]{4,3,2,1,0:T(8,128)S(1)}, f32[2,1,3,16,512]{4,3,2,1,0:T(8,128)S(1)}, u32[]{:S(2)}, u32[]{:S(2)}) collective-permute-start(f32[2,1,3,16,512]{4,3,2,1,0:T(8,128)S(1)} %pad_maximum_fusion), channel_id=1, source_target_pairs={{0,1},{1,0},{2,3},{3,2},{4,5},{5,4},{6,7},{7,6},{8,9},{9,8},{10,11... | collective-permute-start | bytes 589832 | tf_op jit(solution)/shard_map/ppermute | solution.py:250
  18.1 5.8 %collective-permute-start.3 = (f32[3,32,512]{2,1,0:T(8,128)S(1)}, f32[3,32,512]{2,1,0:T(8,128)S(1)}, u32[]{:S(2)}, u32[]{:S(2)}) collective-permute-start(f32[3,32,512]{2,1,0:T(8,128)S(1)} %get-tuple-element.7.behind), channel_id=1, source_target_pairs={{0,30},{1,31},{2,0},{3,1},{4,2},{5,3},{6,4},{7,5},{8,6},{9,7},{10,... | collective-permute-start | bytes 589832 | tf_op jit(solution)/shard_map/ppermute | solution.py:285

commit v9 on v7

--- a/solution.py
+++ b/solution.py
@@ -161,30 +161,23 @@
     wide.take(ext, 2 * FACTOR, rows, put(pushed))
 
 
-def pack_kernel(points, groups, pair, *refs):
-    following, pushed, outs = refs[:points], refs[points : 2 * points], refs[2 * points : -1]
-    difference = refs[-1]
-    me = lax.axis_index("tm")
+def pack_kernel(points, groups, *refs):
+    following, pushed, (packed, difference) = refs[:points], refs[points:-2], refs[-2:]
     rows = difference.shape[2]
     share = rows // groups
     for k in range(points):
         difference[k] = pushed[k][...] - following[k][...]
 
-    @pl.when(me == groups - 1)
+    @pl.when(lax.axis_index("tm") == groups - 1)
     def _():
         first = following[points - 1]
         difference[points - 1] = first[...] - first[...]
 
-    def sort(side):
-        for g in range(groups):
-            target = outs[(g % pair) ^ side]
-            part = slice(g * share, (g + 1) * share)
-            for k in range(points):
-                for f in range(3):
-                    target[g // pair, k, f, 0] = difference[k, f, part, :]
-
-    for side in range(pair):
-        pl.when(me % pair == side)(functools.partial(sort, side))
+    for g in range(groups):
+        part = slice(g * share, (g + 1) * share)
+        for k in range(points):
+            for f in range(3):
+                packed[g * points + k, f, 0] = difference[k, f, part, :]
 
 
 VMEM = pl.BlockSpec(memory_space=pltpu.VMEM)
@@ -251,48 +244,32 @@
     )
 
 
-def pack(following, pushed, groups, pair):
+def pack(following, pushed, groups):
     points, (fields, rows, columns) = len(pushed), pushed[0].shape
-    packet = (groups // pair, points, fields, 1, rows // groups, columns)
-    size = 4 * points * fields * rows * columns
+    packet = (groups * points, fields, 1, rows // groups, columns)
+    size = points * fields * rows * columns
     return pl.pallas_call(
-        functools.partial(pack_kernel, points, groups, pair),
-        out_shape=[jax.ShapeDtypeStruct(packet, jnp.float32)] * pair,
+        functools.partial(pack_kernel, points, groups),
+        out_shape=jax.ShapeDtypeStruct(packet, jnp.float32),
         in_specs=[VMEM] * (2 * points),
-        out_specs=[VMEM] * pair,
+        out_specs=VMEM,
         scratch_shapes=[pltpu.VMEM((points, fields, rows, columns), jnp.float32)],
         compiler_params=pltpu.CompilerParams(vmem_limit_bytes=24 * 2**20),
-        cost_estimate=pl.CostEstimate(flops=size, bytes_accessed=3 * size, transcendentals=0),
+        cost_estimate=pl.CostEstimate(flops=size, bytes_accessed=12 * size, transcendentals=0),
     )(*following, *pushed)
 
 
 def on_device(c_points):
     points = c_points.shape[0]
     groups = lax.axis_size("tm")
-    me = lax.axis_index("tm")
-    pair = 2 if groups % 2 == 0 else 1
-    both = ("tm", "space")
     halos = [exchange(edges_of(c_points[k], 2 * FACTOR), 0) for k in range(points)]
     advanced, pushed = zip(*[chain(k, c_points, halos[k]) for k in range(points)])
-    next_first = lax.ppermute(advanced[0], both, route(-1, 0))
-    sides = pack([*advanced[1:], next_first], pushed, groups, pair)
-    if pair == 2:
-        other = lax.ppermute(sides[1], "tm", [(i, i ^ 1) for i in range(groups)])
-        even = jnp.where(me & 1 == 0, sides[0], other)
-        odd = jnp.where(me & 1 == 0, other, sides[0])
-        sides = [even, odd]
-    coarse = lax.all_to_all(
-        jnp.stack(sides, axis=1),
-        "tm",
-        split_axis=0,
-        concat_axis=0,
-        axis_index_groups=[list(range(side, groups, pair)) for side in range(pair)],
-        tiled=True,
-    )
-    coarse = coarse.reshape(groups * points, *coarse.shape[3:])
+    next_first = lax.ppermute(advanced[0], ("tm", "space"), route(-1, 0))
+    packed = pack([*advanced[1:], next_first], pushed, groups)
+    coarse = lax.all_to_all(packed, "tm", split_axis=0, concat_axis=0, tiled=True)
     coarse = jnp.concatenate([coarse[-1:], coarse[:-1]], axis=0)
-    incoming = lax.ppermute(advanced[-1], both, route(1, 0))
-    opening = jnp.where(me == 0, c_points[0], incoming)
+    incoming = lax.ppermute(advanced[-1], "tm", [(i, i + 1) for i in range(groups - 1)])
+    opening = jnp.where(lax.axis_index("tm") == 0, c_points[0], incoming)
     return (jnp.stack([opening, *advanced[:-1]]), coarse)
 
 

time: 45.1 us -> 41.2 us (0.914)
  the two profiles are of different devices: /device:TPU:0 before, /device:TPU:16 now
where the time goes in v9:
time: 41.2 us; the launch traced here: 41 us
  waiting for transfers between devices  16.8 us (41%)
  starting transfers between devices  11.6 us (28%)
  Pallas kernels  9 us (22%)
  other arithmetic  1.75 us (4%)
  local copies, waits for them, and re-layouts  1.12 us (3%)
  between operations  0.74 us (2%)
    ppermute x1, waiting for transfers between devices, on_device(): lax.ppermute(advanced[-1], 'tm', [(i, i + 1) for i in range(groups - 1)])  11.1 us
    pallas_call x2, Pallas kernels, call(): pl.pallas_call(functools.partial(kernel, chunks), out_shape=[jax.ShapeDty...  8.14 us
    all_to_all x1, starting transfers between devices, on_device(): lax.all_to_all(packed, 'tm', split_axis=0, concat_axis=0, tiled=True)  7.3 us
    ppermute x2, waiting for transfers between devices, exchange(): return lax.ppermute(edges, both, route(shift, 1))  5.68 us
    ppermute x2, starting transfers between devices, exchange(): return lax.ppermute(edges, both, route(shift, 1))  2.16 us
    ppermute x1, starting transfers between devices, on_device(): lax.ppermute(advanced[-1], 'tm', [(i, i + 1) for i in range(groups - 1)])  2.05 us
    squeeze x1, local copies, waits for them, and re-layouts, on_device(): c_points[k]  1.05 us
    concatenate x1, other arithmetic, on_device(): coarse = jnp.concatenate([coarse[-1:], coarse[:-1]], axis=0)  0.92 us
  transfers between devices with their start and end apart: 5, of which 2 were waited for; matrix products, arithmetic and copies ran while one was open for 2% of the time, Pallas kernels for 20%

profile of v9, /device:TPU:16, one launch (start us, length us, event | category | flops | bytes accessed | tf_op | source)
XLA Modules:
  0.0 41.0 jit_solution(2765644911494554328)
XLA Ops:
  0.6 1.1 %slice_bitcast_fusion = (f32[3,32,512]{2,1,0:T(8,128)S(1)}, f32[3,32,512]{2,1,0:T(8,128)S(1)}) fusion(f32[2,3,32,512]{3,2,1,0:T(8,128)} %refs_0_.3), kind=kLoop, calls=%fused_computation.5 | loop fusion | bytes 786432 | tf_op jit(solution)/shard_map/squeeze | solution.py:265
  1.7 0.0 copy-start
  1.8 1.6 %collective-permute-start.2 = (f32[2,3,16,512]{3,2,1,0:T(8,128)S(1)}, f32[2,3,16,512]{3,2,1,0:T(8,128)S(1)}, u32[]{:S(2)}, u32[]{:S(2)}) collective-permute-start(f32[2,3,16,512]{3,2,1,0:T(8,128)S(1)} %pad_maximum_fusion.3), channel_id=1, source_target_pairs={{0,1},{1,0},{2,3},{3,2},{4,5},{5,4},{6,7},{7,6},{8,9},{9,8},{10,11... | collective-permute-start | bytes 589832 | tf_op jit(solution)/shard_map/ppermute | solution.py:238
  3.3 0.6 %collective-permute-start = (f32[2,3,16,512]{3,2,1,0:T(8,128)S(1)}, f32[2,3,16,512]{3,2,1,0:T(8,128)S(1)}, u32[]{:S(2)}, u32[]{:S(2)}) collective-permute-start(f32[2,3,16,512]{3,2,1,0:T(8,128)S(1)} %pad_maximum_fusion.2), channel_id=1, source_target_pairs={{0,1},{1,0},{2,3},{3,2},{4,5},{5,4},{6,7},{7,6},{8,9},{9,8},{10,11... | collective-permute-start | bytes 589832 | tf_op jit(solution)/shard_map/ppermute | solution.py:238
  3.9 5.7 %collective-permute-done.2.refs_1_ = f32[2,3,16,512]{3,2,1,0:T(8,128)S(1)} collective-permute-done((f32[2,3,16,512]{3,2,1,0:T(8,128)S(1)}, f32[2,3,16,512]{3,2,1,0:T(8,128)S(1)}, u32[]{:S(2)}, u32[]{:S(2)}) %collective-permute-start.2) | collective-permute-done | bytes 196640 | tf_op jit(solution)/shard_map/ppermute | solution.py:238
  9.6 0.0 copy-done
  9.6 4.1 %shard_map.31 = (f32[3,32,512]{2,1,0:T(8,128)S(1)}, f32[3,32,512]{2,1,0:T(8,128)S(1)}) custom-call(f32[2,3,32,512]{3,2,1,0:T(8,128)S(1)} %copy-done, f32[2,3,16,512]{3,2,1,0:T(8,128)S(1)} %collective-permute-done.2.refs_1_), custom_call_target="tpu_custom_call" | custom-call | flops 23592960 | bytes 786432 | tf_op jit(solution)/shard_map/pallas_call | solution.py:194
  13.7 0.1 collective-permute-start.3
  13.8 0.0 collective-permute-done.refs_1_
  13.8 4.1 %shard_map.30 = (f32[3,32,512]{2,1,0:T(8,128)S(1)}, f32[3,32,512]{2,1,0:T(8,128)S(1)}) custom-call(f32[2,3,32,512]{3,2,1,0:T(8,128)S(1)} %copy-done, f32[2,3,16,512]{3,2,1,0:T(8,128)S(1)} %collective-permute-done.refs_1_), custom_call_target="tpu_custom_call" | custom-call | flops 23592960 | bytes 786432 | tf_op jit(solution)/shard_map/pallas_call | solution.py:194
  17.8 0.0 collective-permute-done.3.refs_1_
  17.9 0.9 %shard_map.32 = f32[32,3,1,2,512]{4,3,2,1,0:T(2,128)} custom-call(f32[3,32,512]{2,1,0:T(8,128)S(1)} %get-tuple-element.6.refs_0_, f32[3,32,512]{2,1,0:T(8,128)S(1)} %collective-permute-done.3.refs_1_, f32[3,32,512]{2,1,0:T(8,128)S(1)} %get-tuple-element.8.refs_2_, f32[3,32,512]{2,1,0:T(8,128)S(1)} %get-tuple-element.9.refs_3_), custom_call_target="tpu_custom_call" | custom-call | flops 98304 | bytes 1179648 | tf_op jit(solution)/shard_map/pallas_call | solution.py:251
  18.7 7.3 %all-to-all-start = ((f32[32,3,1,2,512]{4,3,2,1,0:T(2,128)}), f32[32,3,1,2,512]{4,3,2,1,0:T(2,128)S(1)}, u32[]{:S(2)}, u32[]{:S(2)}) async-start(f32[32,3,1,2,512]{4,3,2,1,0:T(2,128)} %shard_map.32), calls=%async_computation | async-start | bytes 786432 | tf_op jit(solution)/shard_map/all_to_all | solution.py:269
  26.0 2.0 %collective-permute-start.1 = (f32[3,32,512]{2,1,0:T(8,128)S(1)}, f32[3,32,512]{2,1,0:T(8,128)S(1)}, u32[]{:S(2)}, u32[]{:S(2)}) collective-permute-start(f32[3,32,512]{2,1,0:T(8,128)S(1)} %get-tuple-element.6.refs_0_), channel_id=1, source_target_pairs={{0,2},{2,4},{4,6},{6,8},{8,10},{10,12},{12,14},{14,16},{16,18},{18... | collective-permute-start | bytes 589832 | tf_op jit(solution)/shard_map/ppermute | solution.py:271
  28.1 11.1 %collective-permute-done.1 = f32[3,32,512]{2,1,0:T(8,128)S(1)} collective-permute-done((f32[3,32,512]{2,1,0:T(8,128)S(1)}, f32[3,32,512]{2,1,0:T(8,128)S(1)}, u32[]{:S(2)}, u32[]{:S(2)}) %collective-permute-start.1) | collective-permute-done | bytes 196640 | tf_op jit(solution)/shard_map/ppermute | solution.py:271
  39.2 0.8 %pad_maximum_fusion = f32[2,3,32,512]{3,2,1,0:T(8,128)} fusion(f32[1,3,32,512]{3,2,1,0:T(8,128)S(1)} %bitcast.17, f32[1,3,32,512]{3,2,1,0:T(8,128)S(1)} %select_bitcast_fusion), kind=kLoop, calls=%fused_computation | loop fusion | flops 98304 | bytes 786432 | tf_op jit(solution)/shard_map/stack | solution.py:273
  40.0 0.0 all-to-all-done
  40.1 0.9 %pad_maximum_fusion.1 = f32[32,3,1,2,512]{4,3,2,1,0:T(2,128)} fusion(f32[31,3,1,2,512]{4,3,2,1,0:T(2,128)S(1)} %slice.38, f32[1,3,1,2,512]{4,3,2,1,0:T(2,128)S(1)} %slice.37), kind=kLoop, calls=%fused_computation.1 | loop fusion | flops 98304 | bytes 786432 | tf_op jit(solution)/shard_map/concatenate | solution.py:270
  (6 shorter events, 0.1 us)
Async XLA Ops:
  1.7 7.9 %copy-start = (f32[2,3,32,512]{3,2,1,0:T(8,128)S(1)}, f32[2,3,32,512]{3,2,1,0:T(8,128)}, u32[]{:S(2)}) copy-start(f32[2,3,32,512]{3,2,1,0:T(8,128)} %refs_0_.3) | copy-start | bytes 1179652
  1.8 7.9 %collective-permute-start.2 = (f32[2,3,16,512]{3,2,1,0:T(8,128)S(1)}, f32[2,3,16,512]{3,2,1,0:T(8,128)S(1)}, u32[]{:S(2)}, u32[]{:S(2)}) collective-permute-start(f32[2,3,16,512]{3,2,1,0:T(8,128)S(1)} %pad_maximum_fusion.3), channel_id=1, source_target_pairs={{0,1},{1,0},{2,3},{3,2},{4,5},{5,4},{6,7},{7,6},{8,9},{9,8},{10,11... | collective-permute-start | bytes 589832 | tf_op jit(solution)/shard_map/ppermute | solution.py:238
  3.3 10.4 %collective-permute-start = (f32[2,3,16,512]{3,2,1,0:T(8,128)S(1)}, f32[2,3,16,512]{3,2,1,0:T(8,128)S(1)}, u32[]{:S(2)}, u32[]{:S(2)}) collective-permute-start(f32[2,3,16,512]{3,2,1,0:T(8,128)S(1)} %pad_maximum_fusion.2), channel_id=1, source_target_pairs={{0,1},{1,0},{2,3},{3,2},{4,5},{5,4},{6,7},{7,6},{8,9},{9,8},{10,11... | collective-permute-start | bytes 589832 | tf_op jit(solution)/shard_map/ppermute | solution.py:238
  13.7 4.2 %collective-permute-start.3 = (f32[3,32,512]{2,1,0:T(8,128)S(1)}, f32[3,32,512]{2,1,0:T(8,128)S(1)}, u32[]{:S(2)}, u32[]{:S(2)}) collective-permute-start(f32[3,32,512]{2,1,0:T(8,128)S(1)} %get-tuple-element.7), channel_id=1, source_target_pairs={{0,30},{1,31},{2,0},{3,1},{4,2},{5,3},{6,4},{7,5},{8,6},{9,7},{10,... | collective-permute-start | bytes 589832 | tf_op jit(solution)/shard_map/ppermute | solution.py:267
  18.7 21.3 %all-to-all-start = ((f32[32,3,1,2,512]{4,3,2,1,0:T(2,128)}), f32[32,3,1,2,512]{4,3,2,1,0:T(2,128)S(1)}, u32[]{:S(2)}, u32[]{:S(2)}) async-start(f32[32,3,1,2,512]{4,3,2,1,0:T(2,128)} %shard_map.32), calls=%async_computation | async-start | bytes 786432 | tf_op jit(solution)/shard_map/all_to_all | solution.py:269
  26.0 13.2 %collective-permute-start.1 = (f32[3,32,512]{2,1,0:T(8,128)S(1)}, f32[3,32,512]{2,1,0:T(8,128)S(1)}, u32[]{:S(2)}, u32[]{:S(2)}) collective-permute-start(f32[3,32,512]{2,1,0:T(8,128)S(1)} %get-tuple-element.6.refs_0_), channel_id=1, source_target_pairs={{0,2},{2,4},{4,6},{6,8},{8,10},{10,12},{12,14},{14,16},{16,18},{18... | collective-permute-start | bytes 589832 | tf_op jit(solution)/shard_map/ppermute | solution.py:271

commit v10 on v9

--- a/solution.py
+++ b/solution.py
@@ -161,9 +161,19 @@
     wide.take(ext, 2 * FACTOR, rows, put(pushed))
 
 
+def half_kernel(chunks, own, halo, advanced, ext, state, held):
+    rows = own.shape[1]
+    narrow = Rows(rows + 2 * FACTOR, chunks)
+    narrow.fill(ext, [halo.at[0], own, halo.at[1]])
+    narrow.load(ext, state)
+    narrow.propagate(state, held, 0)
+    narrow.store(ext, state, FACTOR)
+    narrow.take(ext, FACTOR, rows, put(advanced))
+
+
 def pack_kernel(points, groups, *refs):
     following, pushed, (packed, difference) = refs[:points], refs[points:-2], refs[-2:]
-    rows = difference.shape[2]
+    _, _, rows, columns = difference.shape
     share = rows // groups
     for k in range(points):
         difference[k] = pushed[k][...] - following[k][...]
@@ -177,7 +187,8 @@
         part = slice(g * share, (g + 1) * share)
         for k in range(points):
             for f in range(3):
-                packed[g * points + k, f, 0] = difference[k, f, part, :]
+                for span in spans(columns // LANES):
+                    packed[g * points + k, f, 0, :, span] = difference[k, f, part, span]
 
 
 VMEM = pl.BlockSpec(memory_space=pltpu.VMEM)
@@ -262,14 +273,19 @@
 def on_device(c_points):
     points = c_points.shape[0]
     groups = lax.axis_size("tm")
+    both = ("tm", "space")
+    last = c_points[-1]
     halos = [exchange(edges_of(c_points[k], 2 * FACTOR), 0) for k in range(points)]
+    behind = lax.ppermute(last, both, route(1, 0))
+    behind_halo = exchange(edges_of(last, FACTOR), 1)
     advanced, pushed = zip(*[chain(k, c_points, halos[k]) for k in range(points)])
-    next_first = lax.ppermute(advanced[0], ("tm", "space"), route(-1, 0))
+    next_first = lax.ppermute(advanced[0], both, route(-1, 0))
     packed = pack([*advanced[1:], next_first], pushed, groups)
     coarse = lax.all_to_all(packed, "tm", split_axis=0, concat_axis=0, tiled=True)
     coarse = jnp.concatenate([coarse[-1:], coarse[:-1]], axis=0)
-    incoming = lax.ppermute(advanced[-1], "tm", [(i, i + 1) for i in range(groups - 1)])
-    opening = jnp.where(lax.axis_index("tm") == 0, c_points[0], incoming)
+    behind, behind_halo, _ = lax.optimization_barrier((behind, behind_halo, packed))
+    (before,) = call(half_kernel, [last.shape], 1, *last.shape[1:], (behind, behind_halo))
+    opening = jnp.where(lax.axis_index("tm") == 0, c_points[0], before)
     return (jnp.stack([opening, *advanced[:-1]]), coarse)
 
 

time: 41.2 us -> 46.1 us (1.12)
  the two profiles are of different devices: /device:TPU:16 before, /device:TPU:0 now
where the time goes in v10:
time: 46.1 us; the launch traced here: 45.8 us
  waiting for transfers between devices  18.2 us (39%)
  starting transfers between devices  13.1 us (28%)
  Pallas kernels  10.9 us (24%)
  other arithmetic  1.76 us (4%)
  local copies, waits for them, and re-layouts  1.13 us (2%)
  between operations  0.74 us (2%)
    ppermute x3, waiting for transfers between devices, exchange(): return lax.ppermute(edges, both, route(shift, 1))  18.2 us
    pallas_call x3, Pallas kernels, call(): pl.pallas_call(functools.partial(kernel, chunks), out_shape=[jax.ShapeDty...  9.91 us
    all_to_all x1, starting transfers between devices, on_device(): lax.all_to_all(packed, 'tm', split_axis=0, concat_axis=0, tiled=True)  5.83 us
    ppermute x3, starting transfers between devices, exchange(): return lax.ppermute(edges, both, route(shift, 1))  4.64 us
    ppermute x1, starting transfers between devices, on_device(): next_first = lax.ppermute(advanced[0], both, route(-1, 0))  2.6 us
    squeeze x1, local copies, waits for them, and re-layouts, on_device(): last = c_points[-1]  1.05 us
    pallas_call x1, Pallas kernels, pack(): pl.pallas_call(functools.partial(pack_kernel, points, groups), out_shape=...  1 us
  transfers between devices with their start and end apart: 6, of which 2 were waited for; matrix products, arithmetic and copies ran while one was open for 2% of the time, Pallas kernels for 24%

profile of v10, /device:TPU:0, one launch (start us, length us, event | category | flops | bytes accessed | tf_op | source)
XLA Modules:
  0.0 45.8 jit_solution(2459158495406732454)
XLA Ops:
  0.6 1.1 %slice_bitcast_fusion = (f32[3,32,512]{2,1,0:T(8,128)S(1)}, f32[3,32,512]{2,1,0:T(8,128)S(1)}) fusion(f32[2,3,32,512]{3,2,1,0:T(8,128)} %refs_0_.3), kind=kLoop, calls=%fused_computation.5 | loop fusion | bytes 786432 | tf_op jit(solution)/shard_map/squeeze | solution.py:277
  1.7 0.0 copy-start
  1.8 3.0 %collective-permute-start.3 = (f32[2,3,16,512]{3,2,1,0:T(8,128)S(1)}, f32[2,3,16,512]{3,2,1,0:T(8,128)S(1)}, u32[]{:S(2)}, u32[]{:S(2)}) collective-permute-start(f32[2,3,16,512]{3,2,1,0:T(8,128)S(1)} %pad_maximum_fusion.3), channel_id=1, source_target_pairs={{0,1},{1,0},{2,3},{3,2},{4,5},{5,4},{6,7},{7,6},{8,9},{9,8},{10,11... | collective-permute-start | bytes 589832 | tf_op jit(solution)/shard_map/ppermute | solution.py:249
  4.8 0.1 collective-permute-start.2
  4.9 5.6 %collective-permute-done.3.refs_1_ = f32[2,3,16,512]{3,2,1,0:T(8,128)S(1)} collective-permute-done((f32[2,3,16,512]{3,2,1,0:T(8,128)S(1)}, f32[2,3,16,512]{3,2,1,0:T(8,128)S(1)}, u32[]{:S(2)}, u32[]{:S(2)}) %collective-permute-start.3) | collective-permute-done | bytes 196640 | tf_op jit(solution)/shard_map/ppermute | solution.py:249
  10.5 0.0 copy-done
  10.5 4.1 %shard_map.31 = (f32[3,32,512]{2,1,0:T(8,128)S(1)}, f32[3,32,512]{2,1,0:T(8,128)S(1)}) custom-call(f32[2,3,32,512]{3,2,1,0:T(8,128)S(1)} %copy-done, f32[2,3,16,512]{3,2,1,0:T(8,128)S(1)} %collective-permute-done.3.refs_1_), custom_call_target="tpu_custom_call" | custom-call | flops 23592960 | bytes 786432 | tf_op jit(solution)/shard_map/pallas_call | solution.py:205
  14.6 2.6 %collective-permute-start.4 = (f32[3,32,512]{2,1,0:T(8,128)S(1)}, f32[3,32,512]{2,1,0:T(8,128)S(1)}, u32[]{:S(2)}, u32[]{:S(2)}) collective-permute-start(f32[3,32,512]{2,1,0:T(8,128)S(1)} %get-tuple-element.9), channel_id=1, source_target_pairs={{0,30},{1,31},{2,0},{3,1},{4,2},{5,3},{6,4},{7,5},{8,6},{9,7},{10,... | collective-permute-start | bytes 589832 | tf_op jit(solution)/shard_map/ppermute | solution.py:282
  17.2 0.0 collective-permute-start
  17.2 0.0 collective-permute-done.2.refs_1_
  17.2 4.1 %shard_map.30 = (f32[3,32,512]{2,1,0:T(8,128)S(1)}, f32[3,32,512]{2,1,0:T(8,128)S(1)}) custom-call(f32[2,3,32,512]{3,2,1,0:T(8,128)S(1)} %copy-done, f32[2,3,16,512]{3,2,1,0:T(8,128)S(1)} %collective-permute-done.2.refs_1_), custom_call_target="tpu_custom_call" | custom-call | flops 23592960 | bytes 786432 | tf_op jit(solution)/shard_map/pallas_call | solution.py:205
  21.3 0.0 collective-permute-done.4.refs_1_
  21.3 1.0 %shard_map.32 = f32[32,3,1,2,512]{4,3,2,1,0:T(2,128)} custom-call(f32[3,32,512]{2,1,0:T(8,128)S(1)} %get-tuple-element.8.refs_0_, f32[3,32,512]{2,1,0:T(8,128)S(1)} %collective-permute-done.4.refs_1_, f32[3,32,512]{2,1,0:T(8,128)S(1)} %get-tuple-element.10.refs_2_, f32[3,32,512]{2,1,0:T(8,128)S(1)} %get-tuple-element.11.refs_3_), custom_call_target="tpu_custom_call" | custom-call | flops 98304 | bytes 1179648 | tf_op jit(solution)/shard_map/pallas_call | solution.py:262
  22.3 5.8 %all-to-all-start = ((f32[32,3,1,2,512]{4,3,2,1,0:T(2,128)}), f32[32,3,1,2,512]{4,3,2,1,0:T(2,128)S(1)}, u32[]{:S(2)}, u32[]{:S(2)}) async-start(f32[32,3,1,2,512]{4,3,2,1,0:T(2,128)} %shard_map.32), calls=%async_computation | async-start | bytes 786432 | tf_op jit(solution)/shard_map/all_to_all | solution.py:284
  28.1 1.6 %collective-permute-start.1 = (f32[2,3,8,512]{3,2,1,0:T(8,128)S(1)}, f32[2,3,8,512]{3,2,1,0:T(8,128)S(1)}, u32[]{:S(2)}, u32[]{:S(2)}) collective-permute-start(f32[2,3,8,512]{3,2,1,0:T(8,128)S(1)} %pad_maximum_fusion.4), channel_id=1, source_target_pairs={{0,3},{1,2},{2,5},{3,4},{4,7},{5,6},{6,9},{7,8},{8,11},{9,10},{10,... | collective-permute-start | bytes 294920 | tf_op jit(solution)/shard_map/ppermute | solution.py:249
  29.7 12.6 %collective-permute-done.1.halo = f32[2,3,8,512]{3,2,1,0:T(8,128)S(1)} collective-permute-done((f32[2,3,8,512]{3,2,1,0:T(8,128)S(1)}, f32[2,3,8,512]{3,2,1,0:T(8,128)S(1)}, u32[]{:S(2)}, u32[]{:S(2)}) %collective-permute-start.1) | collective-permute-done | bytes 98336 | tf_op jit(solution)/shard_map/ppermute | solution.py:249
  42.3 0.0 collective-permute-done.own
  42.3 1.8 %shard_map.33 = f32[3,32,512]{2,1,0:T(8,128)S(1)} custom-call(f32[3,32,512]{2,1,0:T(8,128)S(1)} %collective-permute-done.own, f32[2,3,8,512]{3,2,1,0:T(8,128)S(1)} %collective-permute-done.1.halo), custom_call_target="tpu_custom_call" | custom-call | flops 11796480 | bytes 393216 | tf_op jit(solution)/shard_map/pallas_call | solution.py:205
  44.1 0.8 %pad_maximum_fusion = f32[2,3,32,512]{3,2,1,0:T(8,128)} fusion(f32[1,3,32,512]{3,2,1,0:T(8,128)S(1)} %bitcast.21, f32[1,3,32,512]{3,2,1,0:T(8,128)S(1)} %select_bitcast_fusion), kind=kLoop, calls=%fused_computation | loop fusion | flops 98304 | bytes 786432 | tf_op jit(solution)/shard_map/stack | solution.py:289
  44.9 0.0 all-to-all-done
  44.9 0.9 %pad_maximum_fusion.1 = f32[32,3,1,2,512]{4,3,2,1,0:T(2,128)} fusion(f32[31,3,1,2,512]{4,3,2,1,0:T(2,128)S(1)} %slice.49, f32[1,3,1,2,512]{4,3,2,1,0:T(2,128)S(1)} %slice.48), kind=kLoop, calls=%fused_computation.1 | loop fusion | flops 98304 | bytes 786432 | tf_op jit(solution)/shard_map/concatenate | solution.py:285
  (8 shorter events, 0.1 us)
Async XLA Ops:
  1.7 8.8 %copy-start = (f32[2,3,32,512]{3,2,1,0:T(8,128)S(1)}, f32[2,3,32,512]{3,2,1,0:T(8,128)}, u32[]{:S(2)}) copy-start(f32[2,3,32,512]{3,2,1,0:T(8,128)} %refs_0_.3) | copy-start | bytes 1179652
  1.8 8.7 %collective-permute-start.3 = (f32[2,3,16,512]{3,2,1,0:T(8,128)S(1)}, f32[2,3,16,512]{3,2,1,0:T(8,128)S(1)}, u32[]{:S(2)}, u32[]{:S(2)}) collective-permute-start(f32[2,3,16,512]{3,2,1,0:T(8,128)S(1)} %pad_maximum_fusion.3), channel_id=1, source_target_pairs={{0,1},{1,0},{2,3},{3,2},{4,5},{5,4},{6,7},{7,6},{8,9},{9,8},{10,11... | collective-permute-start | bytes 589832 | tf_op jit(solution)/shard_map/ppermute | solution.py:249
  4.8 12.4 %collective-permute-start.2 = (f32[2,3,16,512]{3,2,1,0:T(8,128)S(1)}, f32[2,3,16,512]{3,2,1,0:T(8,128)S(1)}, u32[]{:S(2)}, u32[]{:S(2)}) collective-permute-start(f32[2,3,16,512]{3,2,1,0:T(8,128)S(1)} %pad_maximum_fusion.2), channel_id=1, source_target_pairs={{0,1},{1,0},{2,3},{3,2},{4,5},{5,4},{6,7},{7,6},{8,9},{9,8},{10,11... | collective-permute-start | bytes 589832 | tf_op jit(solution)/shard_map/ppermute | solution.py:249
  14.6 6.7 %collective-permute-start.4 = (f32[3,32,512]{2,1,0:T(8,128)S(1)}, f32[3,32,512]{2,1,0:T(8,128)S(1)}, u32[]{:S(2)}, u32[]{:S(2)}) collective-permute-start(f32[3,32,512]{2,1,0:T(8,128)S(1)} %get-tuple-element.9), channel_id=1, source_target_pairs={{0,30},{1,31},{2,0},{3,1},{4,2},{5,3},{6,4},{7,5},{8,6},{9,7},{10,... | collective-permute-start | bytes 589832 | tf_op jit(solution)/shard_map/ppermute | solution.py:282
  17.2 25.1 %collective-permute-start = (f32[3,32,512]{2,1,0:T(8,128)S(1)}, f32[3,32,512]{2,1,0:T(8,128)S(1)}, u32[]{:S(2)}, u32[]{:S(2)}) collective-permute-start(f32[3,32,512]{2,1,0:T(8,128)S(1)} %get-tuple-element.14), channel_id=1, source_target_pairs={{0,2},{1,3},{2,4},{3,5},{4,6},{5,7},{6,8},{7,9},{8,10},{9,11},{10,... | collective-permute-start | bytes 589832 | tf_op jit(solution)/shard_map/ppermute | solution.py:279
  22.3 22.6 %all-to-all-start = ((f32[32,3,1,2,512]{4,3,2,1,0:T(2,128)}), f32[32,3,1,2,512]{4,3,2,1,0:T(2,128)S(1)}, u32[]{:S(2)}, u32[]{:S(2)}) async-start(f32[32,3,1,2,512]{4,3,2,1,0:T(2,128)} %shard_map.32), calls=%async_computation | async-start | bytes 786432 | tf_op jit(solution)/shard_map/all_to_all | solution.py:284
  28.1 14.1 %collective-permute-start.1 = (f32[2,3,8,512]{3,2,1,0:T(8,128)S(1)}, f32[2,3,8,512]{3,2,1,0:T(8,128)S(1)}, u32[]{:S(2)}, u32[]{:S(2)}) collective-permute-start(f32[2,3,8,512]{3,2,1,0:T(8,128)S(1)} %pad_maximum_fusion.4), channel_id=1, source_target_pairs={{0,3},{1,2},{2,5},{3,4},{4,7},{5,6},{6,9},{7,8},{8,11},{9,10},{10,... | collective-permute-start | bytes 294920 | tf_op jit(solution)/shard_map/ppermute | solution.py:249

commit v11 on v9

v11 whole, which is shorter than its diff:
```python
import functools

import jax
import jax.numpy as jnp
from jax import lax
from jax.experimental import pallas as pl
from jax.experimental.pallas import tpu as pltpu
from jax.sharding import PartitionSpec as P

FACTOR = 8
LANES = 128
SUB = 8

MOMENTUM = 0.4
PRESSURE = 0.08


def reciprocal(x):
    r = pl.reciprocal(x, approx=True)
    return r * (2.0 - x * r)


def cell_terms(h, p, q, factor):
    r = reciprocal(h)
    u = p * r
    pressure = h * h * factor
    a = p * u + pressure
    b = q * u
    d = q * (q * r) + pressure
    return (h - q, p - b, q - d), (h + q, p + b, q + d), (h - p, p - a, q - b), (h + p, p + a, q + b)


def added(x, y):
    return y if x is None else [a + b for a, b in zip(x, y)]


def step(src, dst, first, depth, chunks, factor):
    lane = lax.broadcasted_iota(jnp.int32, (SUB, LANES), 1)
    fields, last = range(3), chunks - 1
    below = [None] * chunks

    def from_east(mine, after):
        return [pltpu.roll(jnp.where(lane == 0, a, m), LANES - 1, 1) for m, a in zip(mine, after)]

    def from_west(mine, before):
        return [pltpu.roll(jnp.where(lane == last_lane, b, m), 1, 1) for m, b in zip(mine, before)]

    last_lane = LANES - 1
    for n in range(depth):
        i, before = (first + n) % depth, (first + n - 1) % depth

        def keep(c, total):
            for f in fields:
                dst[f, i, c] = dst[f, i, c] + total[f] if n == depth - 1 else total[f]

        to_west, to_east, total = [None] * chunks, [None] * chunks, below
        below = [None] * chunks
        for c in range(chunks):
            to_south, to_north, to_west[c], to_east[c] = cell_terms(
                src[0, i, c], src[1, i, c], src[2, i, c], factor
            )
            if i == 0:
                to_south = [pltpu.roll(t, SUB - 1, 0) for t in to_south]
            if i == depth - 1:
                to_north = [pltpu.roll(t, 1, 0) for t in to_north]
            for f in fields:
                dst[f, before, c] = to_south[f] if n == 0 else dst[f, before, c] + to_south[f]
            below[c] = to_north
            if c > 0:
                total[c] = added(total[c], from_west(to_east[c], to_east[c - 1]))
                total[c - 1] = added(total[c - 1], from_east(to_west[c - 1], to_west[c]))
                if c > 1:
                    keep(c - 1, total[c - 1])
        total[0] = added(total[0], from_west(to_east[0], to_east[last]))
        total[last] = added(total[last], from_east(to_west[last], to_west[0]))
        for c in sorted({0, last}):
            keep(c, total[c])
    for c in range(chunks):
        for f in fields:
            dst[f, first, c] = dst[f, first, c] + below[c][f]


def spans(chunks):
    return [slice(c * LANES, (c + 1) * LANES) for c in range(chunks)]


class Rows:
    def __init__(self, count, chunks):
        self.depth, self.chunks = count // SUB, chunks
        self.pitch = self.depth | 1

    def cells(self):
        return [
            (f, c, i) for f in range(3) for c in range(self.chunks) for i in range(self.depth)
        ]

    def pieces(self, start, count):
        found, at = [], 0
        while at < count:
            block, offset = divmod(start + at, self.depth)
            length = min(count - at, self.depth - offset)
            found.append((at, block * self.pitch + offset, length))
            at += length
        return found

    def fill(self, ext, arrays):
        start = 0
        for array in arrays:
            rows = array.shape[1]
            for at, place, length in self.pieces(start, rows):
                for f in range(3):
                    for c, span in enumerate(spans(self.chunks)):
                        ext[f, c, place : place + length, :] = array[f, at : at + length, span]
            start += rows

    def load(self, ext, state):
        for f, c, i in self.cells():
            value = ext.at[f, c][pl.ds(i, SUB, stride=self.pitch), :]
            state[0, f, i, c] = value if f == 0 else MOMENTUM * value

    def store(self, ext, state, steps):
        shrink = 0.25**steps
        for f, c, i in self.cells():
            value = state[0, f, i, c] * (shrink if f == 0 else shrink / MOMENTUM)
            ext.at[f, c][pl.ds(i, SUB, stride=self.pitch), :] = value

    def propagate(self, state, steps):
        depth = self.depth

        def two(_, factor):
            step(state.at[0], state.at[1], 0, depth, self.chunks, factor)
            factor = factor * 0.25
            step(state.at[1], state.at[0], 1 % depth, depth, self.chunks, factor)
            return factor * 0.25

        lax.fori_loop(0, FACTOR // 2, two, jnp.float32(PRESSURE * 0.25**steps))

    def take(self, ext, start, count, use):
        for at, place, length in self.pieces(start, count):
            for f in range(3):
                for c, span in enumerate(spans(self.chunks)):
                    use(f, span, at, length, ext[f, c, place : place + length, :])


def put(target):
    def use(f, span, at, length, value):
        target[f, at : at + length, span] = value

    return use


def chain_kernel(chunks, point, own, halo, advanced, pushed, ext, state):
    rows = own.shape[2]
    wide = Rows(rows + 4 * FACTOR, chunks)
    wide.fill(ext, [halo.at[0], own.at[point], halo.at[1]])
    wide.load(ext, state)
    wide.propagate(state, 0)
    wide.store(ext, state, FACTOR)
    wide.take(ext, 2 * FACTOR, rows, put(advanced))
    wide.propagate(state, FACTOR)
    wide.store(ext, state, 2 * FACTOR)
    wide.take(ext, 2 * FACTOR, rows, put(pushed))


VMEM = pl.BlockSpec(memory_space=pltpu.VMEM)


def call(kernel, shapes, work, rows, columns, operands):
    chunks = columns // LANES
    extended = rows + 4 * FACTOR
    cost = pl.CostEstimate(
        flops=work * extended * columns * FACTOR * 45,
        bytes_accessed=4 * work * 3 * extended * columns,
        transcendentals=work * extended * columns * FACTOR,
    )
    return pl.pallas_call(
        functools.partial(kernel, chunks),
        out_shape=[jax.ShapeDtypeStruct(shape, jnp.float32) for shape in shapes],
        in_specs=[VMEM] * len(operands),
        out_specs=[VMEM] * len(shapes),
        scratch_shapes=[
            pltpu.VMEM((3, chunks, extended + SUB, LANES), jnp.float32),
            pltpu.VMEM((2, 3, extended // SUB, chunks, SUB, LANES), jnp.float32),
        ],
        compiler_params=pltpu.CompilerParams(vmem_limit_bytes=24 * 2**20),
        cost_estimate=cost,
    )(*operands)


def chain(point, c_points, halo):
    _, fields, rows, columns = c_points.shape
    shape = (fields, rows, columns)
    return call(
        lambda chunks, *refs: chain_kernel(chunks, point, *refs),
        [shape, shape],
        2,
        rows,
        columns,
        (c_points, halo),
    )


def edges_of(block, width):
    return jnp.stack([block[..., -width:, :], block[..., :width, :]])


def route(shift, move):
    groups, strips = lax.axis_size("tm"), lax.axis_size("space")
    return [
        (t * strips + s, (t + shift) % groups * strips + (s + move) % strips)
        for t in range(groups)
        for s in range(strips)
    ]


def exchange(edges, shift):
    both = ("tm", "space")
    if lax.axis_size("space") == 2:
        return lax.ppermute(edges, both, route(shift, 1))
    return jnp.stack(
        [
            lax.ppermute(edges[0], both, route(shift, 1)),
            lax.ppermute(edges[1], both, route(shift, -1)),
        ]
    )


def on_device(c_points):
    points = c_points.shape[0]
    groups = lax.axis_size("tm")
    halos = [exchange(edges_of(c_points[k], 2 * FACTOR), 0) for k in range(points)]
    advanced, pushed = zip(*[chain(k, c_points, halos[k]) for k in range(points)])
    next_first = lax.ppermute(advanced[0], ("tm", "space"), route(-1, 0))
    me = lax.axis_index("tm")
    wrapped = jnp.where(me == groups - 1, next_first, pushed[-1])
    residual = jnp.stack(
        [after - now for after, now in zip([*pushed[:-1], wrapped], [*advanced[1:], next_first])]
    )
    points, fields, rows, columns = c_points.shape
    shares = residual.reshape(points, fields, groups, rows // groups, columns)
    packed = shares.transpose(2, 0, 1, 3, 4).reshape(-1, fields, 1, rows // groups, columns)
    coarse = lax.all_to_all(packed, "tm", split_axis=0, concat_axis=0, tiled=True)
    coarse = jnp.concatenate([coarse[-1:], coarse[:-1]], axis=0)
    incoming = lax.ppermute(advanced[-1], "tm", [(i, i + 1) for i in range(groups - 1)])
    opening = jnp.where(me == 0, c_points[0], incoming)
    return (jnp.stack([opening, *advanced[:-1]]), coarse)


def solution(mesh):
    in_specs = (P("tm", None, "space", None),)
    out_specs = (P("tm", None, "space", None), P(None, None, "space", "tm", None))
    return jax.shard_map(
        on_device, mesh=mesh, in_specs=in_specs, out_specs=out_specs, check_vma=False
    )
```

time: 41.2 us -> 41.4 us (level)
  local copies, waits for them, and re-layouts: 1.12 us -> 2.11 us
  Pallas kernels: 9 us -> 8.08 us
    pallas_call x1 -> x0, Pallas kernels: 0.87 us -> none  [pack(): pl.pallas_call(functools.partial(pack_kernel, points, groups), out_shape=...]
    transpose x0 -> x1, local copies, waits for them, and re-layouts: none -> 0.77 us  [on_device(): shares.transpose(2, 0, 1, 3, 4)]
where the time goes in v11:
time: 41.4 us; the launch traced here: 41.2 us
  waiting for transfers between devices  16.8 us (41%)
  starting transfers between devices  11.4 us (28%)
  Pallas kernels  8.08 us (20%)
  local copies, waits for them, and re-layouts  2.11 us (5%)
  other arithmetic  2 us (5%)
  between operations  0.77 us (2%)
    ppermute x1, waiting for transfers between devices, on_device(): lax.ppermute(advanced[-1], 'tm', [(i, i + 1) for i in range(groups - 1)])  11.1 us
    pallas_call x2, Pallas kernels, call(): pl.pallas_call(functools.partial(kernel, chunks), out_shape=[jax.ShapeDty...  8.08 us
    all_to_all x1, starting transfers between devices, on_device(): lax.all_to_all(packed, 'tm', split_axis=0, concat_axis=0, tiled=True)  7.15 us
    ppermute x2, waiting for transfers between devices, exchange(): return lax.ppermute(edges, both, route(shift, 1))  5.68 us
    ppermute x2, starting transfers between devices, exchange(): return lax.ppermute(edges, both, route(shift, 1))  2.16 us
    ppermute x1, starting transfers between devices, on_device(): lax.ppermute(advanced[-1], 'tm', [(i, i + 1) for i in range(groups - 1)])  2.05 us
    squeeze x1, local copies, waits for them, and re-layouts, on_device(): c_points[k]  1.05 us
    concatenate x1, other arithmetic, on_device(): coarse = jnp.concatenate([coarse[-1:], coarse[:-1]], axis=0)  0.92 us
  transfers between devices with their start and end apart: 5, of which 2 were waited for; matrix products, arithmetic and copies ran while one was open for 2% of the time, Pallas kernels for 20%

profile of v11, /device:TPU:16, one launch (start us, length us, event | category | flops | bytes accessed | tf_op | source)
XLA Modules:
  0.0 41.2 jit_solution(9505663368760682626)
XLA Ops:
  0.6 1.1 %slice_bitcast_fusion = (f32[3,32,512]{2,1,0:T(8,128)S(1)}, f32[3,32,512]{2,1,0:T(8,128)S(1)}) fusion(f32[2,3,32,512]{3,2,1,0:T(8,128)} %refs_0_.3), kind=kLoop, calls=%fused_computation.7 | loop fusion | bytes 786432 | tf_op jit(solution)/shard_map/squeeze | solution.py:231
  1.7 0.0 copy-start
  1.8 1.6 %collective-permute-start.2 = (f32[2,3,16,512]{3,2,1,0:T(8,128)S(1)}, f32[2,3,16,512]{3,2,1,0:T(8,128)S(1)}, u32[]{:S(2)}, u32[]{:S(2)}) collective-permute-start(f32[2,3,16,512]{3,2,1,0:T(8,128)S(1)} %pad_maximum_fusion.3), channel_id=1, source_target_pairs={{0,1},{1,0},{2,3},{3,2},{4,5},{5,4},{6,7},{7,6},{8,9},{9,8},{10,11... | collective-permute-start | bytes 589832 | tf_op jit(solution)/shard_map/ppermute | solution.py:219
  3.3 0.6 %collective-permute-start = (f32[2,3,16,512]{3,2,1,0:T(8,128)S(1)}, f32[2,3,16,512]{3,2,1,0:T(8,128)S(1)}, u32[]{:S(2)}, u32[]{:S(2)}) collective-permute-start(f32[2,3,16,512]{3,2,1,0:T(8,128)S(1)} %pad_maximum_fusion.2), channel_id=1, source_target_pairs={{0,1},{1,0},{2,3},{3,2},{4,5},{5,4},{6,7},{7,6},{8,9},{9,8},{10,11... | collective-permute-start | bytes 589832 | tf_op jit(solution)/shard_map/ppermute | solution.py:219
  3.9 5.7 %collective-permute-done.2.refs_1_ = f32[2,3,16,512]{3,2,1,0:T(8,128)S(1)} collective-permute-done((f32[2,3,16,512]{3,2,1,0:T(8,128)S(1)}, f32[2,3,16,512]{3,2,1,0:T(8,128)S(1)}, u32[]{:S(2)}, u32[]{:S(2)}) %collective-permute-start.2) | collective-permute-done | bytes 196640 | tf_op jit(solution)/shard_map/ppermute | solution.py:219
  9.6 0.0 copy-done
  9.6 4.0 %shard_map.31 = (f32[3,32,512]{2,1,0:T(8,128)S(1)}, f32[3,32,512]{2,1,0:T(8,128)S(1)}) custom-call(f32[2,3,32,512]{3,2,1,0:T(8,128)S(1)} %copy-done, f32[2,3,16,512]{3,2,1,0:T(8,128)S(1)} %collective-permute-done.2.refs_1_), custom_call_target="tpu_custom_call" | custom-call | flops 23592960 | bytes 786432 | tf_op jit(solution)/shard_map/pallas_call | solution.py:176
  13.7 0.1 collective-permute-start.3
  13.7 0.0 collective-permute-done.refs_1_
  13.7 4.0 %shard_map.30 = (f32[3,32,512]{2,1,0:T(8,128)S(1)}, f32[3,32,512]{2,1,0:T(8,128)S(1)}) custom-call(f32[2,3,32,512]{3,2,1,0:T(8,128)S(1)} %copy-done, f32[2,3,16,512]{3,2,1,0:T(8,128)S(1)} %collective-permute-done.refs_1_), custom_call_target="tpu_custom_call" | custom-call | flops 23592960 | bytes 786432 | tf_op jit(solution)/shard_map/pallas_call | solution.py:176
  17.8 0.1 stack.45
  17.9 0.0 collective-permute-done.3
  18.0 0.1 stack.46
  18.1 0.2 maximum_bitcast_fusion
  18.3 0.8 %copy.3 = f32[16,2,3,2,512]{4,3,2,1,0:T(2,128)} copy(f32[16,2,3,2,512]{4,3,0,2,1:T(2,128)S(1)} %maximum_bitcast_fusion) | data formatting | bytes 786432 | tf_op jit(solution)/shard_map/transpose | solution.py:241
  19.1 7.1 %all-to-all-start = ((f32[32,3,1,2,512]{4,3,2,1,0:T(2,128)}), f32[32,3,1,2,512]{4,3,2,1,0:T(2,128)S(1)}, u32[]{:S(2)}, u32[]{:S(2)}) async-start(f32[32,3,1,2,512]{4,3,2,1,0:T(2,128)} %bitcast.9), calls=%async_computation | async-start | bytes 786432 | tf_op jit(solution)/shard_map/all_to_all | solution.py:242
  26.2 2.0 %collective-permute-start.1 = (f32[3,32,512]{2,1,0:T(8,128)S(1)}, f32[3,32,512]{2,1,0:T(8,128)S(1)}, u32[]{:S(2)}, u32[]{:S(2)}) collective-permute-start(f32[3,32,512]{2,1,0:T(8,128)S(1)} %get-tuple-element.6), channel_id=1, source_target_pairs={{0,2},{2,4},{4,6},{6,8},{8,10},{10,12},{12,14},{14,16},{16,18},{18... | collective-permute-start | bytes 589832 | tf_op jit(solution)/shard_map/ppermute | solution.py:244
  28.3 11.1 %collective-permute-done.1 = f32[3,32,512]{2,1,0:T(8,128)S(1)} collective-permute-done((f32[3,32,512]{2,1,0:T(8,128)S(1)}, f32[3,32,512]{2,1,0:T(8,128)S(1)}, u32[]{:S(2)}, u32[]{:S(2)}) %collective-permute-start.1) | collective-permute-done | bytes 196640 | tf_op jit(solution)/shard_map/ppermute | solution.py:244
  39.5 0.8 %pad_maximum_fusion = f32[2,3,32,512]{3,2,1,0:T(8,128)} fusion(f32[1,3,32,512]{3,2,1,0:T(8,128)S(1)} %bitcast.20, f32[1,3,32,512]{3,2,1,0:T(8,128)S(1)} %select_bitcast_fusion), kind=kLoop, calls=%fused_computation | loop fusion | flops 98304 | bytes 786432 | tf_op jit(solution)/shard_map/stack | solution.py:246
  40.2 0.0 all-to-all-done
  40.3 0.9 %pad_maximum_fusion.1 = f32[32,3,1,2,512]{4,3,2,1,0:T(2,128)} fusion(f32[31,3,1,2,512]{4,3,2,1,0:T(2,128)S(1)} %slice.38, f32[1,3,1,2,512]{4,3,2,1,0:T(2,128)S(1)} %slice.37), kind=kLoop, calls=%fused_computation.2 | loop fusion | flops 98304 | bytes 786432 | tf_op jit(solution)/shard_map/concatenate | solution.py:243
  (8 shorter events, 0.2 us)
Async XLA Ops:
  1.7 7.9 %copy-start = (f32[2,3,32,512]{3,2,1,0:T(8,128)S(1)}, f32[2,3,32,512]{3,2,1,0:T(8,128)}, u32[]{:S(2)}) copy-start(f32[2,3,32,512]{3,2,1,0:T(8,128)} %refs_0_.3) | copy-start | bytes 1179652
  1.8 7.9 %collective-permute-start.2 = (f32[2,3,16,512]{3,2,1,0:T(8,128)S(1)}, f32[2,3,16,512]{3,2,1,0:T(8,128)S(1)}, u32[]{:S(2)}, u32[]{:S(2)}) collective-permute-start(f32[2,3,16,512]{3,2,1,0:T(8,128)S(1)} %pad_maximum_fusion.3), channel_id=1, source_target_pairs={{0,1},{1,0},{2,3},{3,2},{4,5},{5,4},{6,7},{7,6},{8,9},{9,8},{10,11... | collective-permute-start | bytes 589832 | tf_op jit(solution)/shard_map/ppermute | solution.py:219
  3.3 10.4 %collective-permute-start = (f32[2,3,16,512]{3,2,1,0:T(8,128)S(1)}, f32[2,3,16,512]{3,2,1,0:T(8,128)S(1)}, u32[]{:S(2)}, u32[]{:S(2)}) collective-permute-start(f32[2,3,16,512]{3,2,1,0:T(8,128)S(1)} %pad_maximum_fusion.2), channel_id=1, source_target_pairs={{0,1},{1,0},{2,3},{3,2},{4,5},{5,4},{6,7},{7,6},{8,9},{9,8},{10,11... | collective-permute-start | bytes 589832 | tf_op jit(solution)/shard_map/ppermute | solution.py:219
  13.7 4.3 %collective-permute-start.3 = (f32[3,32,512]{2,1,0:T(8,128)S(1)}, f32[3,32,512]{2,1,0:T(8,128)S(1)}, u32[]{:S(2)}, u32[]{:S(2)}) collective-permute-start(f32[3,32,512]{2,1,0:T(8,128)S(1)} %get-tuple-element.7), channel_id=1, source_target_pairs={{0,30},{1,31},{2,0},{3,1},{4,2},{5,3},{6,4},{7,5},{8,6},{9,7},{10,... | collective-permute-start | bytes 589832 | tf_op jit(solution)/shard_map/ppermute | solution.py:233
  19.1 21.1 %all-to-all-start = ((f32[32,3,1,2,512]{4,3,2,1,0:T(2,128)}), f32[32,3,1,2,512]{4,3,2,1,0:T(2,128)S(1)}, u32[]{:S(2)}, u32[]{:S(2)}) async-start(f32[32,3,1,2,512]{4,3,2,1,0:T(2,128)} %bitcast.9), calls=%async_computation | async-start | bytes 786432 | tf_op jit(solution)/shard_map/all_to_all | solution.py:242
  26.2 13.2 %collective-permute-start.1 = (f32[3,32,512]{2,1,0:T(8,128)S(1)}, f32[3,32,512]{2,1,0:T(8,128)S(1)}, u32[]{:S(2)}, u32[]{:S(2)}) collective-permute-start(f32[3,32,512]{2,1,0:T(8,128)S(1)} %get-tuple-element.6), channel_id=1, source_target_pairs={{0,2},{2,4},{4,6},{6,8},{8,10},{10,12},{12,14},{14,16},{16,18},{18... | collective-permute-start | bytes 589832 | tf_op jit(solution)/shard_map/ppermute | solution.py:244

commit v12 on v9

--- a/solution.py
+++ b/solution.py
@@ -177,7 +177,7 @@
         part = slice(g * share, (g + 1) * share)
         for k in range(points):
             for f in range(3):
-                packed[g * points + k, f, 0] = difference[k, f, part, :]
+                packed[(groups - 1 - g) * points + k, f, 0] = difference[k, f, part, :]
 
 
 VMEM = pl.BlockSpec(memory_space=pltpu.VMEM)
@@ -266,7 +266,11 @@
     advanced, pushed = zip(*[chain(k, c_points, halos[k]) for k in range(points)])
     next_first = lax.ppermute(advanced[0], ("tm", "space"), route(-1, 0))
     packed = pack([*advanced[1:], next_first], pushed, groups)
-    coarse = lax.all_to_all(packed, "tm", split_axis=0, concat_axis=0, tiled=True)
+    members = [list(reversed(range(groups)))]
+    coarse = lax.all_to_all(
+        packed, "tm", split_axis=0, concat_axis=0, axis_index_groups=members, tiled=True
+    )
+    coarse = coarse.reshape(groups, points, *coarse.shape[1:])[::-1].reshape(coarse.shape)
     coarse = jnp.concatenate([coarse[-1:], coarse[:-1]], axis=0)
     incoming = lax.ppermute(advanced[-1], "tm", [(i, i + 1) for i in range(groups - 1)])
     opening = jnp.where(lax.axis_index("tm") == 0, c_points[0], incoming)

time: 41.2 us -> 41 us (level)
  no operation moved by 1% of the time
where the time goes in v12:
time: 41 us; the launch traced here: 40.7 us
  waiting for transfers between devices  16.8 us (41%)
  starting transfers between devices  11.2 us (27%)
  Pallas kernels  9 us (22%)
  other arithmetic  1.75 us (4%)
  local copies, waits for them, and re-layouts  1.14 us (3%)
  between operations  0.74 us (2%)
    ppermute x1, waiting for transfers between devices, on_device(): lax.ppermute(advanced[-1], 'tm', [(i, i + 1) for i in range(groups - 1)])  11.2 us
    pallas_call x2, Pallas kernels, call(): pl.pallas_call(functools.partial(kernel, chunks), out_shape=[jax.ShapeDty...  8.14 us
    all_to_all x1, starting transfers between devices, on_device(): lax.all_to_all(packed, 'tm', split_axis=0, concat_axis=0, axis_index_grou...  7.05 us
    ppermute x2, waiting for transfers between devices, exchange(): return lax.ppermute(edges, both, route(shift, 1))  5.68 us
    ppermute x2, starting transfers between devices, exchange(): return lax.ppermute(edges, both, route(shift, 1))  2.16 us
    ppermute x1, starting transfers between devices, on_device(): lax.ppermute(advanced[-1], 'tm', [(i, i + 1) for i in range(groups - 1)])  1.98 us
    squeeze x1, local copies, waits for them, and re-layouts, on_device(): c_points[k]  1.05 us
    concatenate x1, other arithmetic, on_device(): coarse = jnp.concatenate([coarse[-1:], coarse[:-1]], axis=0)  0.92 us
  transfers between devices with their start and end apart: 5, of which 2 were waited for; matrix products, arithmetic and copies ran while one was open for 2% of the time, Pallas kernels for 20%

profile of v12, /device:TPU:16, one launch (start us, length us, event | category | flops | bytes accessed | tf_op | source)
XLA Modules:
  0.0 40.7 jit_solution(10801767771512837546)
XLA Ops:
  0.6 1.1 %slice_bitcast_fusion = (f32[3,32,512]{2,1,0:T(8,128)S(1)}, f32[3,32,512]{2,1,0:T(8,128)S(1)}) fusion(f32[2,3,32,512]{3,2,1,0:T(8,128)} %refs_0_.3), kind=kLoop, calls=%fused_computation.5 | loop fusion | bytes 786432 | tf_op jit(solution)/shard_map/squeeze | solution.py:265
  1.7 0.0 copy-start
  1.8 1.6 %collective-permute-start.2 = (f32[2,3,16,512]{3,2,1,0:T(8,128)S(1)}, f32[2,3,16,512]{3,2,1,0:T(8,128)S(1)}, u32[]{:S(2)}, u32[]{:S(2)}) collective-permute-start(f32[2,3,16,512]{3,2,1,0:T(8,128)S(1)} %pad_maximum_fusion.3), channel_id=1, source_target_pairs={{0,1},{1,0},{2,3},{3,2},{4,5},{5,4},{6,7},{7,6},{8,9},{9,8},{10,11... | collective-permute-start | bytes 589832 | tf_op jit(solution)/shard_map/ppermute | solution.py:238
  3.3 0.6 %collective-permute-start = (f32[2,3,16,512]{3,2,1,0:T(8,128)S(1)}, f32[2,3,16,512]{3,2,1,0:T(8,128)S(1)}, u32[]{:S(2)}, u32[]{:S(2)}) collective-permute-start(f32[2,3,16,512]{3,2,1,0:T(8,128)S(1)} %pad_maximum_fusion.2), channel_id=1, source_target_pairs={{0,1},{1,0},{2,3},{3,2},{4,5},{5,4},{6,7},{7,6},{8,9},{9,8},{10,11... | collective-permute-start | bytes 589832 | tf_op jit(solution)/shard_map/ppermute | solution.py:238
  3.9 5.7 %collective-permute-done.2.refs_1_ = f32[2,3,16,512]{3,2,1,0:T(8,128)S(1)} collective-permute-done((f32[2,3,16,512]{3,2,1,0:T(8,128)S(1)}, f32[2,3,16,512]{3,2,1,0:T(8,128)S(1)}, u32[]{:S(2)}, u32[]{:S(2)}) %collective-permute-start.2) | collective-permute-done | bytes 196640 | tf_op jit(solution)/shard_map/ppermute | solution.py:238
  9.6 0.0 copy-done
  9.6 4.1 %shard_map.31 = (f32[3,32,512]{2,1,0:T(8,128)S(1)}, f32[3,32,512]{2,1,0:T(8,128)S(1)}) custom-call(f32[2,3,32,512]{3,2,1,0:T(8,128)S(1)} %copy-done, f32[2,3,16,512]{3,2,1,0:T(8,128)S(1)} %collective-permute-done.2.refs_1_), custom_call_target="tpu_custom_call" | custom-call | flops 23592960 | bytes 786432 | tf_op jit(solution)/shard_map/pallas_call | solution.py:194
  13.7 0.1 collective-permute-start.3
  13.8 0.0 collective-permute-done.refs_1_
  13.8 4.1 %shard_map.30 = (f32[3,32,512]{2,1,0:T(8,128)S(1)}, f32[3,32,512]{2,1,0:T(8,128)S(1)}) custom-call(f32[2,3,32,512]{3,2,1,0:T(8,128)S(1)} %copy-done, f32[2,3,16,512]{3,2,1,0:T(8,128)S(1)} %collective-permute-done.refs_1_), custom_call_target="tpu_custom_call" | custom-call | flops 23592960 | bytes 786432 | tf_op jit(solution)/shard_map/pallas_call | solution.py:194
  17.8 0.0 collective-permute-done.3.refs_1_
  17.9 0.9 %shard_map.32 = f32[32,3,1,2,512]{4,3,2,1,0:T(2,128)} custom-call(f32[3,32,512]{2,1,0:T(8,128)S(1)} %get-tuple-element.6.refs_0_, f32[3,32,512]{2,1,0:T(8,128)S(1)} %collective-permute-done.3.refs_1_, f32[3,32,512]{2,1,0:T(8,128)S(1)} %get-tuple-element.8.refs_2_, f32[3,32,512]{2,1,0:T(8,128)S(1)} %get-tuple-element.9.refs_3_), custom_call_target="tpu_custom_call" | custom-call | flops 98304 | bytes 1179648 | tf_op jit(solution)/shard_map/pallas_call | solution.py:251
  18.7 7.1 %all-to-all-start = ((f32[32,3,1,2,512]{4,3,2,1,0:T(2,128)}), f32[32,3,1,2,512]{4,3,2,1,0:T(2,128)S(1)}, u32[]{:S(2)}, u32[]{:S(2)}) async-start(f32[32,3,1,2,512]{4,3,2,1,0:T(2,128)} %shard_map.32), calls=%async_computation | async-start | bytes 786432 | tf_op jit(solution)/shard_map/all_to_all | solution.py:270
  25.8 2.0 %collective-permute-start.1 = (f32[3,32,512]{2,1,0:T(8,128)S(1)}, f32[3,32,512]{2,1,0:T(8,128)S(1)}, u32[]{:S(2)}, u32[]{:S(2)}) collective-permute-start(f32[3,32,512]{2,1,0:T(8,128)S(1)} %get-tuple-element.6.refs_0_), channel_id=1, source_target_pairs={{0,2},{2,4},{4,6},{6,8},{8,10},{10,12},{12,14},{14,16},{16,18},{18... | collective-permute-start | bytes 589832 | tf_op jit(solution)/shard_map/ppermute | solution.py:275
  27.8 11.2 %collective-permute-done.1 = f32[3,32,512]{2,1,0:T(8,128)S(1)} collective-permute-done((f32[3,32,512]{2,1,0:T(8,128)S(1)}, f32[3,32,512]{2,1,0:T(8,128)S(1)}, u32[]{:S(2)}, u32[]{:S(2)}) %collective-permute-start.1) | collective-permute-done | bytes 196640 | tf_op jit(solution)/shard_map/ppermute | solution.py:275
  39.0 0.8 %pad_maximum_fusion = f32[2,3,32,512]{3,2,1,0:T(8,128)} fusion(f32[1,3,32,512]{3,2,1,0:T(8,128)S(1)} %bitcast.19, f32[1,3,32,512]{3,2,1,0:T(8,128)S(1)} %select_bitcast_fusion), kind=kLoop, calls=%fused_computation | loop fusion | flops 98304 | bytes 786432 | tf_op jit(solution)/shard_map/stack | solution.py:277
  39.7 0.0 all-to-all-done
  39.8 0.9 %pad_maximum_fusion.1 = f32[32,3,1,2,512]{4,3,2,1,0:T(2,128)} fusion(f32[31,3,1,2,512]{4,3,2,1,0:T(2,128)S(1)} %slice.38, f32[1,3,1,2,512]{4,3,2,1,0:T(2,128)S(1)} %slice.37), kind=kLoop, calls=%fused_computation.1 | loop fusion | flops 98304 | bytes 786432 | tf_op jit(solution)/shard_map/concatenate | solution.py:274
  (7 shorter events, 0.1 us)
Async XLA Ops:
  1.7 7.9 %copy-start = (f32[2,3,32,512]{3,2,1,0:T(8,128)S(1)}, f32[2,3,32,512]{3,2,1,0:T(8,128)}, u32[]{:S(2)}) copy-start(f32[2,3,32,512]{3,2,1,0:T(8,128)} %refs_0_.3) | copy-start | bytes 1179652
  1.8 7.9 %collective-permute-start.2 = (f32[2,3,16,512]{3,2,1,0:T(8,128)S(1)}, f32[2,3,16,512]{3,2,1,0:T(8,128)S(1)}, u32[]{:S(2)}, u32[]{:S(2)}) collective-permute-start(f32[2,3,16,512]{3,2,1,0:T(8,128)S(1)} %pad_maximum_fusion.3), channel_id=1, source_target_pairs={{0,1},{1,0},{2,3},{3,2},{4,5},{5,4},{6,7},{7,6},{8,9},{9,8},{10,11... | collective-permute-start | bytes 589832 | tf_op jit(solution)/shard_map/ppermute | solution.py:238
  3.3 10.4 %collective-permute-start = (f32[2,3,16,512]{3,2,1,0:T(8,128)S(1)}, f32[2,3,16,512]{3,2,1,0:T(8,128)S(1)}, u32[]{:S(2)}, u32[]{:S(2)}) collective-permute-start(f32[2,3,16,512]{3,2,1,0:T(8,128)S(1)} %pad_maximum_fusion.2), channel_id=1, source_target_pairs={{0,1},{1,0},{2,3},{3,2},{4,5},{5,4},{6,7},{7,6},{8,9},{9,8},{10,11... | collective-permute-start | bytes 589832 | tf_op jit(solution)/shard_map/ppermute | solution.py:238
  13.7 4.2 %collective-permute-start.3 = (f32[3,32,512]{2,1,0:T(8,128)S(1)}, f32[3,32,512]{2,1,0:T(8,128)S(1)}, u32[]{:S(2)}, u32[]{:S(2)}) collective-permute-start(f32[3,32,512]{2,1,0:T(8,128)S(1)} %get-tuple-element.7), channel_id=1, source_target_pairs={{0,30},{1,31},{2,0},{3,1},{4,2},{5,3},{6,4},{7,5},{8,6},{9,7},{10,... | collective-permute-start | bytes 589832 | tf_op jit(solution)/shard_map/ppermute | solution.py:267
  18.7 21.0 %all-to-all-start = ((f32[32,3,1,2,512]{4,3,2,1,0:T(2,128)}), f32[32,3,1,2,512]{4,3,2,1,0:T(2,128)S(1)}, u32[]{:S(2)}, u32[]{:S(2)}) async-start(f32[32,3,1,2,512]{4,3,2,1,0:T(2,128)} %shard_map.32), calls=%async_computation | async-start | bytes 786432 | tf_op jit(solution)/shard_map/all_to_all | solution.py:270
  25.8 13.1 %collective-permute-start.1 = (f32[3,32,512]{2,1,0:T(8,128)S(1)}, f32[3,32,512]{2,1,0:T(8,128)S(1)}, u32[]{:S(2)}, u32[]{:S(2)}) collective-permute-start(f32[3,32,512]{2,1,0:T(8,128)S(1)} %get-tuple-element.6.refs_0_), channel_id=1, source_target_pairs={{0,2},{2,4},{4,6},{6,8},{8,10},{10,12},{12,14},{14,16},{16,18},{18... | collective-permute-start | bytes 589832 | tf_op jit(solution)/shard_map/ppermute | solution.py:275

commit v13 on v12

--- a/solution.py
+++ b/solution.py
@@ -161,6 +161,26 @@
     wide.take(ext, 2 * FACTOR, rows, put(pushed))
 
 
+def head_kernel(chunks, point, own, halo, advanced, carried, ext, state, held):
+    rows = own.shape[2]
+    wide = Rows(rows + 4 * FACTOR, chunks)
+    wide.fill(ext, [halo.at[0], own.at[point], halo.at[1]])
+    wide.load(ext, state)
+    wide.propagate(state, held, 0)
+    wide.store(ext, state, FACTOR)
+    wide.take(ext, 2 * FACTOR, rows, put(advanced))
+    carried[...] = state[0]
+
+
+def finish_kernel(chunks, carried, pushed, ext, state, held):
+    rows = pushed.shape[1]
+    wide = Rows(rows + 4 * FACTOR, chunks)
+    state[0] = carried[...]
+    wide.propagate(state, held, FACTOR)
+    wide.store(ext, state, 2 * FACTOR)
+    wide.take(ext, 2 * FACTOR, rows, put(pushed))
+
+
 def pack_kernel(points, groups, *refs):
     following, pushed, (packed, difference) = refs[:points], refs[points:-2], refs[-2:]
     rows = difference.shape[2]
@@ -177,7 +197,7 @@
         part = slice(g * share, (g + 1) * share)
         for k in range(points):
             for f in range(3):
-                packed[(groups - 1 - g) * points + k, f, 0] = difference[k, f, part, :]
+                packed[(g - groups // 2) % groups * points + k, f, 0] = difference[k, f, part, :]
 
 
 VMEM = pl.BlockSpec(memory_space=pltpu.VMEM)
@@ -219,6 +239,24 @@
     )
 
 
+def head(point, c_points, halo):
+    _, fields, rows, columns = c_points.shape
+    vectors = (fields, (rows + 4 * FACTOR) // SUB, columns // LANES, SUB, LANES)
+    return call(
+        lambda chunks, *refs: head_kernel(chunks, point, *refs),
+        [(fields, rows, columns), vectors],
+        1,
+        rows,
+        columns,
+        (c_points, halo),
+    )
+
+
+def finish(carried, shape):
+    _, rows, columns = shape
+    return call(finish_kernel, [shape], 1, rows, columns, (carried,))[0]
+
+
 def edges_of(block, width):
     return jnp.stack([block[..., -width:, :], block[..., :width, :]])
 
@@ -263,15 +301,18 @@
     points = c_points.shape[0]
     groups = lax.axis_size("tm")
     halos = [exchange(edges_of(c_points[k], 2 * FACTOR), 0) for k in range(points)]
-    advanced, pushed = zip(*[chain(k, c_points, halos[k]) for k in range(points)])
+    first, carried = head(0, c_points, halos[0])
+    ends = [(first, finish(carried, first.shape))]
+    ends += [chain(k, c_points, halos[k]) for k in range(1, points)]
+    advanced, pushed = zip(*ends)
     next_first = lax.ppermute(advanced[0], ("tm", "space"), route(-1, 0))
     packed = pack([*advanced[1:], next_first], pushed, groups)
-    members = [list(reversed(range(groups)))]
+    members = [[(groups // 2 + g) % groups for g in range(groups)]]
     coarse = lax.all_to_all(
         packed, "tm", split_axis=0, concat_axis=0, axis_index_groups=members, tiled=True
     )
-    coarse = coarse.reshape(groups, points, *coarse.shape[1:])[::-1].reshape(coarse.shape)
-    coarse = jnp.concatenate([coarse[-1:], coarse[:-1]], axis=0)
+    split = (groups - groups // 2) * points - 1
+    coarse = jnp.concatenate([coarse[split:], coarse[:split]], axis=0)
     incoming = lax.ppermute(advanced[-1], "tm", [(i, i + 1) for i in range(groups - 1)])
     opening = jnp.where(lax.axis_index("tm") == 0, c_points[0], incoming)
     return (jnp.stack([opening, *advanced[:-1]]), coarse)

time: 41 us -> 39.4 us (0.961)
  starting transfers between devices: 11.2 us -> 8.55 us
  waiting for transfers between devices: 16.8 us -> 17.9 us
    all_to_all x1, starting transfers between devices: 7.05 us -> 4.03 us  [on_device(): lax.all_to_all(packed, 'tm', split_axis=0, concat_axis=0, axis_index_grou...]
    ppermute x1, waiting for transfers between devices: 11.2 us -> 12.2 us  [on_device(): lax.ppermute(advanced[-1], 'tm', [(i, i + 1) for i in range(groups - 1)])]
    pallas_call x2 -> x3, Pallas kernels: 8.14 us -> 8.17 us  [call(): pl.pallas_call(functools.partial(kernel, chunks), out_shape=[jax.ShapeDty...]
  transfers between devices with their start and end apart: 5 -> 5, of which waited for: 2 -> 2; matrix products, arithmetic and copies ran while one was open for 2% -> 2% of each run, Pallas kernels for 20% -> 21%
where the time goes in v13:
time: 39.4 us; the launch traced here: 39.1 us
  waiting for transfers between devices  17.9 us (45%)
  Pallas kernels  9.03 us (23%)
  starting transfers between devices  8.55 us (22%)
  other arithmetic  1.75 us (4%)
  local copies, waits for them, and re-layouts  1.12 us (3%)
  between operations  0.75 us (2%)
    ppermute x1, waiting for transfers between devices, on_device(): lax.ppermute(advanced[-1], 'tm', [(i, i + 1) for i in range(groups - 1)])  12.2 us
    pallas_call x3, Pallas kernels, call(): pl.pallas_call(functools.partial(kernel, chunks), out_shape=[jax.ShapeDty...  8.17 us
    ppermute x2, waiting for transfers between devices, exchange(): return lax.ppermute(edges, both, route(shift, 1))  5.68 us
    all_to_all x1, starting transfers between devices, on_device(): lax.all_to_all(packed, 'tm', split_axis=0, concat_axis=0, axis_index_grou...  4.03 us
    ppermute x1, starting transfers between devices, on_device(): lax.ppermute(advanced[-1], 'tm', [(i, i + 1) for i in range(groups - 1)])  2.31 us
    ppermute x2, starting transfers between devices, exchange(): return lax.ppermute(edges, both, route(shift, 1))  2.16 us
    squeeze x1, local copies, waits for them, and re-layouts, on_device(): c_points[k]  1.05 us
    concatenate x1, other arithmetic, on_device(): coarse = jnp.concatenate([coarse[split:], coarse[:split]], axis=0)  0.92 us
  transfers between devices with their start and end apart: 5, of which 2 were waited for; matrix products, arithmetic and copies ran while one was open for 2% of the time, Pallas kernels for 21%

profile of v13, /device:TPU:16, one launch (start us, length us, event | category | flops | bytes accessed | tf_op | source)
XLA Modules:
  0.0 39.1 jit_solution(3451734285805619711)
XLA Ops:
  0.6 1.1 %slice_bitcast_fusion = (f32[3,32,512]{2,1,0:T(8,128)S(1)}, f32[3,32,512]{2,1,0:T(8,128)S(1)}) fusion(f32[2,3,32,512]{3,2,1,0:T(8,128)} %refs_0_.3), kind=kLoop, calls=%fused_computation.5 | loop fusion | bytes 786432 | tf_op jit(solution)/shard_map/squeeze | solution.py:303
  1.7 0.0 copy-start
  1.8 1.6 %collective-permute-start.2 = (f32[2,3,16,512]{3,2,1,0:T(8,128)S(1)}, f32[2,3,16,512]{3,2,1,0:T(8,128)S(1)}, u32[]{:S(2)}, u32[]{:S(2)}) collective-permute-start(f32[2,3,16,512]{3,2,1,0:T(8,128)S(1)} %pad_maximum_fusion.3), channel_id=1, source_target_pairs={{0,1},{1,0},{2,3},{3,2},{4,5},{5,4},{6,7},{7,6},{8,9},{9,8},{10,11... | collective-permute-start | bytes 589832 | tf_op jit(solution)/shard_map/ppermute | solution.py:276
  3.3 0.6 %collective-permute-start = (f32[2,3,16,512]{3,2,1,0:T(8,128)S(1)}, f32[2,3,16,512]{3,2,1,0:T(8,128)S(1)}, u32[]{:S(2)}, u32[]{:S(2)}) collective-permute-start(f32[2,3,16,512]{3,2,1,0:T(8,128)S(1)} %pad_maximum_fusion.2), channel_id=1, source_target_pairs={{0,1},{1,0},{2,3},{3,2},{4,5},{5,4},{6,7},{7,6},{8,9},{9,8},{10,11... | collective-permute-start | bytes 589832 | tf_op jit(solution)/shard_map/ppermute | solution.py:276
  3.9 5.7 %collective-permute-done.2.refs_1_ = f32[2,3,16,512]{3,2,1,0:T(8,128)S(1)} collective-permute-done((f32[2,3,16,512]{3,2,1,0:T(8,128)S(1)}, f32[2,3,16,512]{3,2,1,0:T(8,128)S(1)}, u32[]{:S(2)}, u32[]{:S(2)}) %collective-permute-start.2) | collective-permute-done | bytes 196640 | tf_op jit(solution)/shard_map/ppermute | solution.py:276
  9.6 0.0 copy-done
  9.6 2.1 %shard_map.31 = (f32[3,32,512]{2,1,0:T(8,128)S(1)}, f32[3,8,4,8,128]{4,3,2,1,0:T(8,128)S(1)}) custom-call(f32[2,3,32,512]{3,2,1,0:T(8,128)S(1)} %copy-done, f32[2,3,16,512]{3,2,1,0:T(8,128)S(1)} %collective-permute-done.2.refs_1_), custom_call_target="tpu_custom_call" | custom-call | flops 11796480 | bytes 393216 | tf_op jit(solution)/shard_map/pallas_call | solution.py:214
  11.7 0.1 collective-permute-start.3
  11.8 2.0 %shard_map.32.refs_2_ = f32[3,32,512]{2,1,0:T(8,128)S(1)} custom-call(f32[3,8,4,8,128]{4,3,2,1,0:T(8,128)S(1)} %get-tuple-element.8.carried), custom_call_target="tpu_custom_call" | custom-call | flops 11796480 | bytes 393216 | tf_op jit(solution)/shard_map/pallas_call | solution.py:214
  13.8 0.0 collective-permute-done.refs_1_
  13.8 4.1 %shard_map.30 = (f32[3,32,512]{2,1,0:T(8,128)S(1)}, f32[3,32,512]{2,1,0:T(8,128)S(1)}) custom-call(f32[2,3,32,512]{3,2,1,0:T(8,128)S(1)} %copy-done, f32[2,3,16,512]{3,2,1,0:T(8,128)S(1)} %collective-permute-done.refs_1_), custom_call_target="tpu_custom_call" | custom-call | flops 23592960 | bytes 786432 | tf_op jit(solution)/shard_map/pallas_call | solution.py:214
  17.9 0.0 collective-permute-done.3.refs_1_
  17.9 0.9 %shard_map.33 = f32[32,3,1,2,512]{4,3,2,1,0:T(2,128)} custom-call(f32[3,32,512]{2,1,0:T(8,128)S(1)} %get-tuple-element.6.refs_0_, f32[3,32,512]{2,1,0:T(8,128)S(1)} %collective-permute-done.3.refs_1_, f32[3,32,512]{2,1,0:T(8,128)S(1)} %shard_map.32.refs_2_, f32[3,32,512]{2,1,0:T(8,128)S(1)} %get-tuple-element.9.refs_3_), custom_call_target="tpu_custom_call" | custom-call | flops 98304 | bytes 1179648 | tf_op jit(solution)/shard_map/pallas_call | solution.py:289
  18.8 4.0 %all-to-all-start = ((f32[32,3,1,2,512]{4,3,2,1,0:T(2,128)}), f32[32,3,1,2,512]{4,3,2,1,0:T(2,128)S(1)}, u32[]{:S(2)}, u32[]{:S(2)}) async-start(f32[32,3,1,2,512]{4,3,2,1,0:T(2,128)} %shard_map.33), calls=%async_computation | async-start | bytes 786432 | tf_op jit(solution)/shard_map/all_to_all | solution.py:311
  22.8 2.3 %collective-permute-start.1 = (f32[3,32,512]{2,1,0:T(8,128)S(1)}, f32[3,32,512]{2,1,0:T(8,128)S(1)}, u32[]{:S(2)}, u32[]{:S(2)}) collective-permute-start(f32[3,32,512]{2,1,0:T(8,128)S(1)} %get-tuple-element.6.refs_0_), channel_id=1, source_target_pairs={{0,2},{2,4},{4,6},{6,8},{8,10},{10,12},{12,14},{14,16},{16,18},{18... | collective-permute-start | bytes 589832 | tf_op jit(solution)/shard_map/ppermute | solution.py:316
  25.1 12.2 %collective-permute-done.1 = f32[3,32,512]{2,1,0:T(8,128)S(1)} collective-permute-done((f32[3,32,512]{2,1,0:T(8,128)S(1)}, f32[3,32,512]{2,1,0:T(8,128)S(1)}, u32[]{:S(2)}, u32[]{:S(2)}) %collective-permute-start.1) | collective-permute-done | bytes 196640 | tf_op jit(solution)/shard_map/ppermute | solution.py:316
  37.4 0.8 %pad_maximum_fusion = f32[2,3,32,512]{3,2,1,0:T(8,128)} fusion(f32[1,3,32,512]{3,2,1,0:T(8,128)S(1)} %bitcast.17, f32[1,3,32,512]{3,2,1,0:T(8,128)S(1)} %select_bitcast_fusion), kind=kLoop, calls=%fused_computation | loop fusion | flops 98304 | bytes 786432 | tf_op jit(solution)/shard_map/stack | solution.py:318
  38.2 0.0 all-to-all-done
  38.2 0.9 %pad_maximum_fusion.1 = f32[32,3,1,2,512]{4,3,2,1,0:T(2,128)} fusion(f32[15,3,1,2,512]{4,3,2,1,0:T(2,128)S(1)} %slice.38, f32[17,3,1,2,512]{4,3,2,1,0:T(2,128)S(1)} %slice.37), kind=kLoop, calls=%fused_computation.1 | loop fusion | flops 98304 | bytes 786432 | tf_op jit(solution)/shard_map/concatenate | solution.py:315
  (6 shorter events, 0.1 us)
Async XLA Ops:
  1.7 7.9 %copy-start = (f32[2,3,32,512]{3,2,1,0:T(8,128)S(1)}, f32[2,3,32,512]{3,2,1,0:T(8,128)}, u32[]{:S(2)}) copy-start(f32[2,3,32,512]{3,2,1,0:T(8,128)} %refs_0_.3) | copy-start | bytes 1179652
  1.8 7.9 %collective-permute-start.2 = (f32[2,3,16,512]{3,2,1,0:T(8,128)S(1)}, f32[2,3,16,512]{3,2,1,0:T(8,128)S(1)}, u32[]{:S(2)}, u32[]{:S(2)}) collective-permute-start(f32[2,3,16,512]{3,2,1,0:T(8,128)S(1)} %pad_maximum_fusion.3), channel_id=1, source_target_pairs={{0,1},{1,0},{2,3},{3,2},{4,5},{5,4},{6,7},{7,6},{8,9},{9,8},{10,11... | collective-permute-start | bytes 589832 | tf_op jit(solution)/shard_map/ppermute | solution.py:276
  3.3 10.5 %collective-permute-start = (f32[2,3,16,512]{3,2,1,0:T(8,128)S(1)}, f32[2,3,16,512]{3,2,1,0:T(8,128)S(1)}, u32[]{:S(2)}, u32[]{:S(2)}) collective-permute-start(f32[2,3,16,512]{3,2,1,0:T(8,128)S(1)} %pad_maximum_fusion.2), channel_id=1, source_target_pairs={{0,1},{1,0},{2,3},{3,2},{4,5},{5,4},{6,7},{7,6},{8,9},{9,8},{10,11... | collective-permute-start | bytes 589832 | tf_op jit(solution)/shard_map/ppermute | solution.py:276
  11.7 6.2 %collective-permute-start.3 = (f32[3,32,512]{2,1,0:T(8,128)S(1)}, f32[3,32,512]{2,1,0:T(8,128)S(1)}, u32[]{:S(2)}, u32[]{:S(2)}) collective-permute-start(f32[3,32,512]{2,1,0:T(8,128)S(1)} %get-tuple-element.7), channel_id=1, source_target_pairs={{0,30},{1,31},{2,0},{3,1},{4,2},{5,3},{6,4},{7,5},{8,6},{9,7},{10,... | collective-permute-start | bytes 589832 | tf_op jit(solution)/shard_map/ppermute | solution.py:308
  18.8 19.4 %all-to-all-start = ((f32[32,3,1,2,512]{4,3,2,1,0:T(2,128)}), f32[32,3,1,2,512]{4,3,2,1,0:T(2,128)S(1)}, u32[]{:S(2)}, u32[]{:S(2)}) async-start(f32[32,3,1,2,512]{4,3,2,1,0:T(2,128)} %shard_map.33), calls=%async_computation | async-start | bytes 786432 | tf_op jit(solution)/shard_map/all_to_all | solution.py:311
  22.8 14.6 %collective-permute-start.1 = (f32[3,32,512]{2,1,0:T(8,128)S(1)}, f32[3,32,512]{2,1,0:T(8,128)S(1)}, u32[]{:S(2)}, u32[]{:S(2)}) collective-permute-start(f32[3,32,512]{2,1,0:T(8,128)S(1)} %get-tuple-element.6.refs_0_), channel_id=1, source_target_pairs={{0,2},{2,4},{4,6},{6,8},{8,10},{10,12},{12,14},{14,16},{16,18},{18... | collective-permute-start | bytes 589832 | tf_op jit(solution)/shard_map/ppermute | solution.py:316

commit v14 on v13

--- a/solution.py
+++ b/solution.py
@@ -161,6 +161,20 @@
     wide.take(ext, 2 * FACTOR, rows, put(pushed))
 
 
+def cut_kernel(points, own, *refs):
+    outs, sems = refs[:-1], refs[-1]
+    rows, width = own.shape[2], 2 * FACTOR
+    copies = []
+    for k in range(points):
+        for side, start in enumerate((rows - width, 0)):
+            part = own.at[k, :, pl.ds(start, width), :]
+            copies.append(pltpu.make_async_copy(part, outs[k].at[side], sems.at[k, side]))
+    for copy in copies:
+        copy.start()
+    for copy in copies:
+        copy.wait()
+
+
 def head_kernel(chunks, point, own, halo, advanced, carried, ext, state, held):
     rows = own.shape[2]
     wide = Rows(rows + 4 * FACTOR, chunks)
@@ -257,8 +271,16 @@
     return call(finish_kernel, [shape], 1, rows, columns, (carried,))[0]
 
 
-def edges_of(block, width):
-    return jnp.stack([block[..., -width:, :], block[..., :width, :]])
+def cut(c_points):
+    points, fields, _, columns = c_points.shape
+    edges = jax.ShapeDtypeStruct((2, fields, 2 * FACTOR, columns), jnp.float32)
+    return pl.pallas_call(
+        functools.partial(cut_kernel, points),
+        out_shape=[edges] * points,
+        in_specs=[pl.BlockSpec(memory_space=pltpu.HBM)],
+        out_specs=[VMEM] * points,
+        scratch_shapes=[pltpu.SemaphoreType.DMA((points, 2))],
+    )(c_points)
 
 
 def route(shift, move):
@@ -300,7 +322,7 @@
 def on_device(c_points):
     points = c_points.shape[0]
     groups = lax.axis_size("tm")
-    halos = [exchange(edges_of(c_points[k], 2 * FACTOR), 0) for k in range(points)]
+    halos = [exchange(edges, 0) for edges in cut(c_points)]
     first, carried = head(0, c_points, halos[0])
     ends = [(first, finish(carried, first.shape))]
     ends += [chain(k, c_points, halos[k]) for k in range(1, points)]
@@ -314,6 +336,7 @@
     split = (groups - groups // 2) * points - 1
     coarse = jnp.concatenate([coarse[split:], coarse[:split]], axis=0)
     incoming = lax.ppermute(advanced[-1], "tm", [(i, i + 1) for i in range(groups - 1)])
+    coarse, incoming = lax.optimization_barrier((coarse, incoming))
     opening = jnp.where(lax.axis_index("tm") == 0, c_points[0], incoming)
     return (jnp.stack([opening, *advanced[:-1]]), coarse)
 

time: 39.4 us -> 39.6 us (level)
  the two profiles are of different devices: /device:TPU:16 before, /device:TPU:0 now
where the time goes in v14:
time: 39.6 us; the launch traced here: 39.4 us
  waiting for transfers between devices  13.7 us (35%)
  starting transfers between devices  12.3 us (31%)
  Pallas kernels  10.9 us (28%)
  other arithmetic  1.72 us (4%)
  between operations  0.72 us (2%)
    pallas_call x3, Pallas kernels, call(): pl.pallas_call(functools.partial(kernel, chunks), out_shape=[jax.ShapeDty...  8.16 us
    all_to_all x1, waiting for transfers between devices, on_device(): lax.all_to_all(packed, 'tm', split_axis=0, concat_axis=0, axis_index_grou...  7.86 us
    ppermute x2, waiting for transfers between devices, exchange(): return lax.ppermute(edges, both, route(shift, 1))  5.86 us
    all_to_all x1, starting transfers between devices, on_device(): lax.all_to_all(packed, 'tm', split_axis=0, concat_axis=0, axis_index_grou...  4.56 us
    ppermute x2, starting transfers between devices, exchange(): return lax.ppermute(edges, both, route(shift, 1))  3.08 us
    ppermute x1, starting transfers between devices, on_device(): next_first = lax.ppermute(advanced[0], ('tm', 'space'), route(-1, 0))  2.6 us
    ppermute x1, starting transfers between devices, on_device(): lax.ppermute(advanced[-1], 'tm', [(i, i + 1) for i in range(groups - 1)])  2.05 us
    pallas_call x1, Pallas kernels, cut(): pl.pallas_call(functools.partial(cut_kernel, points), out_shape=[edges] *...  1.86 us
  transfers between devices with their start and end apart: 5, of which 2 were waited for; matrix products, arithmetic and copies ran while one was open for 2% of the time, Pallas kernels for 21%

profile of v14, /device:TPU:0, one launch (start us, length us, event | category | flops | bytes accessed | tf_op | source)
XLA Modules:
  0.0 39.4 jit_solution(2468792139990046913)
XLA Ops:
  0.6 0.0 copy-start
  0.6 1.9 %shard_map.30 = (f32[2,3,16,512]{3,2,1,0:T(8,128)}, f32[2,3,16,512]{3,2,1,0:T(8,128)}) custom-call(f32[2,3,32,512]{3,2,1,0:T(8,128)} %refs_0_.3), custom_call_target="tpu_custom_call" | custom-call | tf_op jit(solution)/shard_map/pallas_call | solution.py:277
  2.5 3.0 %collective-permute-start.1 = (f32[2,3,16,512]{3,2,1,0:T(8,128)}, f32[2,3,16,512]{3,2,1,0:T(8,128)S(1)}, u32[]{:S(2)}, u32[]{:S(2)}) collective-permute-start(f32[2,3,16,512]{3,2,1,0:T(8,128)} %get-tuple-element.12), channel_id=1, source_target_pairs={{0,1},{1,0},{2,3},{3,2},{4,5},{5,4},{6,7},{7,6},{8,9},{9,8},{10,11... | collective-permute-start | bytes 589832 | tf_op jit(solution)/shard_map/ppermute | solution.py:298
  5.5 0.1 collective-permute-start
  5.6 5.9 %collective-permute-done.1.refs_1_ = f32[2,3,16,512]{3,2,1,0:T(8,128)S(1)} collective-permute-done((f32[2,3,16,512]{3,2,1,0:T(8,128)}, f32[2,3,16,512]{3,2,1,0:T(8,128)S(1)}, u32[]{:S(2)}, u32[]{:S(2)}) %collective-permute-start.1) | collective-permute-done | bytes 196640 | tf_op jit(solution)/shard_map/ppermute | solution.py:298
  11.4 0.0 copy-done
  11.5 2.1 %shard_map.32 = (f32[3,32,512]{2,1,0:T(8,128)S(1)}, f32[3,8,4,8,128]{4,3,2,1,0:T(8,128)S(1)}) custom-call(f32[2,3,32,512]{3,2,1,0:T(8,128)S(1)} %copy-done, f32[2,3,16,512]{3,2,1,0:T(8,128)S(1)} %collective-permute-done.1.refs_1_), custom_call_target="tpu_custom_call" | custom-call | flops 11796480 | bytes 393216 | tf_op jit(solution)/shard_map/pallas_call | solution.py:228
  13.5 2.6 %collective-permute-start.2 = (f32[3,32,512]{2,1,0:T(8,128)S(1)}, f32[3,32,512]{2,1,0:T(8,128)S(1)}, u32[]{:S(2)}, u32[]{:S(2)}) collective-permute-start(f32[3,32,512]{2,1,0:T(8,128)S(1)} %get-tuple-element.13), channel_id=1, source_target_pairs={{0,30},{1,31},{2,0},{3,1},{4,2},{5,3},{6,4},{7,5},{8,6},{9,7},{10,... | collective-permute-start | bytes 589832 | tf_op jit(solution)/shard_map/ppermute | solution.py:330
  16.1 2.0 %shard_map.33.refs_2_ = f32[3,32,512]{2,1,0:T(8,128)S(1)} custom-call(f32[3,8,4,8,128]{4,3,2,1,0:T(8,128)S(1)} %get-tuple-element.14.carried), custom_call_target="tpu_custom_call" | custom-call | flops 11796480 | bytes 393216 | tf_op jit(solution)/shard_map/pallas_call | solution.py:228
  18.2 0.0 collective-permute-done.refs_1_
  18.2 4.1 %shard_map.31 = (f32[3,32,512]{2,1,0:T(8,128)S(1)}, f32[3,32,512]{2,1,0:T(8,128)S(1)}) custom-call(f32[2,3,32,512]{3,2,1,0:T(8,128)S(1)} %copy-done, f32[2,3,16,512]{3,2,1,0:T(8,128)S(1)} %collective-permute-done.refs_1_), custom_call_target="tpu_custom_call" | custom-call | flops 23592960 | bytes 786432 | tf_op jit(solution)/shard_map/pallas_call | solution.py:228
  22.3 0.0 collective-permute-done.2.refs_1_
  22.3 0.9 %shard_map.34 = f32[32,3,1,2,512]{4,3,2,1,0:T(2,128)} custom-call(f32[3,32,512]{2,1,0:T(8,128)S(1)} %get-tuple-element.11.refs_0_, f32[3,32,512]{2,1,0:T(8,128)S(1)} %collective-permute-done.2.refs_1_, f32[3,32,512]{2,1,0:T(8,128)S(1)} %shard_map.33.refs_2_, f32[3,32,512]{2,1,0:T(8,128)S(1)} %get-tuple-element.15.refs_3_), custom_call_target="tpu_custom_call" | custom-call | flops 98304 | bytes 1179648 | tf_op jit(solution)/shard_map/pallas_call | solution.py:311
  23.1 4.6 %all-to-all-start = ((f32[32,3,1,2,512]{4,3,2,1,0:T(2,128)}), f32[32,3,1,2,512]{4,3,2,1,0:T(2,128)S(1)}, u32[]{:S(2)}, u32[]{:S(2)}) async-start(f32[32,3,1,2,512]{4,3,2,1,0:T(2,128)} %shard_map.34), calls=%async_computation | async-start | bytes 786432 | tf_op jit(solution)/shard_map/all_to_all | solution.py:333
  27.7 2.1 %collective-permute-start.3 = (f32[3,32,512]{2,1,0:T(8,128)S(1)}, f32[3,32,512]{2,1,0:T(8,128)S(1)}, u32[]{:S(2)}, u32[]{:S(2)}) collective-permute-start(f32[3,32,512]{2,1,0:T(8,128)S(1)} %get-tuple-element.11.refs_0_), channel_id=1, source_target_pairs={{0,2},{2,4},{4,6},{6,8},{8,10},{10,12},{12,14},{14,16},{16,18},{18... | collective-permute-start | bytes 589832 | tf_op jit(solution)/shard_map/ppermute | solution.py:338
  29.8 7.9 %all-to-all-done = f32[32,3,1,2,512]{4,3,2,1,0:T(2,128)S(1)} async-done(((f32[32,3,1,2,512]{4,3,2,1,0:T(2,128)}), f32[32,3,1,2,512]{4,3,2,1,0:T(2,128)S(1)}, u32[]{:S(2)}, u32[]{:S(2)}) %all-to-all-start) | async-done | bytes 393248 | tf_op jit(solution)/shard_map/all_to_all | solution.py:333
  37.7 0.9 %pad_maximum_fusion = f32[32,3,1,2,512]{4,3,2,1,0:T(2,128)} fusion(f32[15,3,1,2,512]{4,3,2,1,0:T(2,128)S(1)} %slice.13, f32[17,3,1,2,512]{4,3,2,1,0:T(2,128)S(1)} %slice.12), kind=kLoop, calls=%fused_computation | loop fusion | flops 98304 | bytes 786432 | tf_op jit(solution)/shard_map/concatenate | solution.py:337
  38.6 0.0 collective-permute-done.3
  38.6 0.8 %pad_maximum_fusion.1 = f32[2,3,32,512]{3,2,1,0:T(8,128)} fusion(f32[1,3,32,512]{3,2,1,0:T(8,128)S(1)} %bitcast.7, f32[1,3,32,512]{3,2,1,0:T(8,128)S(1)} %fusion), kind=kLoop, calls=%fused_computation.1 | loop fusion | flops 98304 | bytes 786432 | tf_op jit(solution)/shard_map/stack | solution.py:341
  (3 shorter events, 0.1 us)
Async XLA Ops:
  0.6 10.8 %copy-start = (f32[2,3,32,512]{3,2,1,0:T(8,128)S(1)}, f32[2,3,32,512]{3,2,1,0:T(8,128)}, u32[]{:S(2)}) copy-start(f32[2,3,32,512]{3,2,1,0:T(8,128)} %refs_0_.3) | copy-start | bytes 1179652
  2.5 8.9 %collective-permute-start.1 = (f32[2,3,16,512]{3,2,1,0:T(8,128)}, f32[2,3,16,512]{3,2,1,0:T(8,128)S(1)}, u32[]{:S(2)}, u32[]{:S(2)}) collective-permute-start(f32[2,3,16,512]{3,2,1,0:T(8,128)} %get-tuple-element.12), channel_id=1, source_target_pairs={{0,1},{1,0},{2,3},{3,2},{4,5},{5,4},{6,7},{7,6},{8,9},{9,8},{10,11... | collective-permute-start | bytes 589832 | tf_op jit(solution)/shard_map/ppermute | solution.py:298
  5.5 12.7 %collective-permute-start = (f32[2,3,16,512]{3,2,1,0:T(8,128)}, f32[2,3,16,512]{3,2,1,0:T(8,128)S(1)}, u32[]{:S(2)}, u32[]{:S(2)}) collective-permute-start(f32[2,3,16,512]{3,2,1,0:T(8,128)} %get-tuple-element.10), channel_id=1, source_target_pairs={{0,1},{1,0},{2,3},{3,2},{4,5},{5,4},{6,7},{7,6},{8,9},{9,8},{10,11... | collective-permute-start | bytes 589832 | tf_op jit(solution)/shard_map/ppermute | solution.py:298
  13.5 8.7 %collective-permute-start.2 = (f32[3,32,512]{2,1,0:T(8,128)S(1)}, f32[3,32,512]{2,1,0:T(8,128)S(1)}, u32[]{:S(2)}, u32[]{:S(2)}) collective-permute-start(f32[3,32,512]{2,1,0:T(8,128)S(1)} %get-tuple-element.13), channel_id=1, source_target_pairs={{0,30},{1,31},{2,0},{3,1},{4,2},{5,3},{6,4},{7,5},{8,6},{9,7},{10,... | collective-permute-start | bytes 589832 | tf_op jit(solution)/shard_map/ppermute | solution.py:330
  23.1 14.5 %all-to-all-start = ((f32[32,3,1,2,512]{4,3,2,1,0:T(2,128)}), f32[32,3,1,2,512]{4,3,2,1,0:T(2,128)S(1)}, u32[]{:S(2)}, u32[]{:S(2)}) async-start(f32[32,3,1,2,512]{4,3,2,1,0:T(2,128)} %shard_map.34), calls=%async_computation | async-start | bytes 786432 | tf_op jit(solution)/shard_map/all_to_all | solution.py:333
  27.7 10.9 %collective-permute-start.3 = (f32[3,32,512]{2,1,0:T(8,128)S(1)}, f32[3,32,512]{2,1,0:T(8,128)S(1)}, u32[]{:S(2)}, u32[]{:S(2)}) collective-permute-start(f32[3,32,512]{2,1,0:T(8,128)S(1)} %get-tuple-element.11.refs_0_), channel_id=1, source_target_pairs={{0,2},{2,4},{4,6},{6,8},{8,10},{10,12},{12,14},{14,16},{16,18},{18... | collective-permute-start | bytes 589832 | tf_op jit(solution)/shard_map/ppermute | solution.py:338

commit v15 on v12

--- a/solution.py
+++ b/solution.py
@@ -117,13 +117,13 @@
             value = ext.at[f, c][pl.ds(i, SUB, stride=self.pitch), :]
             state[0, f, i, c] = value if f == 0 else MOMENTUM * value
 
-    def store(self, ext, state, steps):
-        shrink = 0.25**steps
+    def store(self, ext, state):
+        shrink = 0.25**FACTOR
         for f, c, i in self.cells():
             value = state[0, f, i, c] * (shrink if f == 0 else shrink / MOMENTUM)
             ext.at[f, c][pl.ds(i, SUB, stride=self.pitch), :] = value
 
-    def propagate(self, state, held, steps):
+    def propagate(self, state, held):
         depth = self.depth
 
         def two(_, factor):
@@ -132,7 +132,7 @@
             step(state.at[1], state.at[0], held, 1 % depth, depth, self.chunks, factor)
             return factor * 0.25
 
-        lax.fori_loop(0, FACTOR // 2, two, jnp.float32(PRESSURE * 0.25**steps))
+        lax.fori_loop(0, FACTOR // 2, two, jnp.float32(PRESSURE))
 
     def take(self, ext, start, count, use):
         for at, place, length in self.pieces(start, count):
@@ -148,17 +148,39 @@
     return use
 
 
-def chain_kernel(chunks, point, own, halo, advanced, pushed, ext, state, held):
-    rows = own.shape[2]
+def first_half(chunks, block, halo, middle, ext, state, held):
+    rows = block.shape[1]
     wide = Rows(rows + 4 * FACTOR, chunks)
-    wide.fill(ext, [halo.at[0], own.at[point], halo.at[1]])
+    wide.fill(ext, [halo.at[0], block, halo.at[1]])
     wide.load(ext, state)
-    wide.propagate(state, held, 0)
-    wide.store(ext, state, FACTOR)
-    wide.take(ext, 2 * FACTOR, rows, put(advanced))
-    wide.propagate(state, held, FACTOR)
-    wide.store(ext, state, 2 * FACTOR)
-    wide.take(ext, 2 * FACTOR, rows, put(pushed))
+    wide.propagate(state, held)
+    wide.store(ext, state)
+    wide.take(ext, FACTOR, rows + 2 * FACTOR, put(middle))
+
+
+def second_half(chunks, middle, pushed, ext, state, held):
+    rows = pushed.shape[1]
+    narrow = Rows(rows + 2 * FACTOR, chunks)
+    narrow.fill(ext, [middle])
+    narrow.load(ext, state)
+    narrow.propagate(state, held)
+    narrow.store(ext, state)
+    narrow.take(ext, FACTOR, rows, put(pushed))
+
+
+def chain_kernel(chunks, point, own, halo, advanced, pushed, middle, *scratch):
+    first_half(chunks, own.at[point], halo, middle, *scratch)
+    advanced[...] = middle[:, FACTOR : FACTOR + own.shape[2], :]
+    second_half(chunks, middle, pushed, *scratch)
+
+
+def head_kernel(chunks, point, own, halo, advanced, middle, *scratch):
+    first_half(chunks, own.at[point], halo, middle, *scratch)
+    advanced[...] = middle[:, FACTOR : FACTOR + own.shape[2], :]
+
+
+def finish_kernel(chunks, middle, pushed, *scratch):
+    second_half(chunks, middle, pushed, *scratch)
 
 
 def pack_kernel(points, groups, *refs):
@@ -177,13 +199,13 @@
         part = slice(g * share, (g + 1) * share)
         for k in range(points):
             for f in range(3):
-                packed[(groups - 1 - g) * points + k, f, 0] = difference[k, f, part, :]
+                packed[(g - groups // 2) % groups * points + k, f, 0] = difference[k, f, part, :]
 
 
 VMEM = pl.BlockSpec(memory_space=pltpu.VMEM)
 
 
-def call(kernel, shapes, work, rows, columns, operands):
+def call(kernel, shapes, work, rows, columns, operands, extra=()):
     chunks = columns // LANES
     extended = rows + 4 * FACTOR
     cost = pl.CostEstimate(
@@ -197,6 +219,7 @@
         in_specs=[VMEM] * len(operands),
         out_specs=[VMEM] * len(shapes),
         scratch_shapes=[
+            *extra,
             pltpu.VMEM((3, chunks, extended + SUB, LANES), jnp.float32),
             pltpu.VMEM((2, 3, extended // SUB, chunks, SUB, LANES), jnp.float32),
             pltpu.VMEM((3, chunks, SUB, LANES), jnp.float32),
@@ -208,15 +231,32 @@
 
 def chain(point, c_points, halo):
     _, fields, rows, columns = c_points.shape
-    shape = (fields, rows, columns)
     return call(
         lambda chunks, *refs: chain_kernel(chunks, point, *refs),
-        [shape, shape],
+        [(fields, rows, columns)] * 2,
         2,
         rows,
         columns,
         (c_points, halo),
-    )
+        extra=[pltpu.VMEM((fields, rows + 2 * FACTOR, columns), jnp.float32)],
+    )
+
+
+def head(point, c_points, halo):
+    _, fields, rows, columns = c_points.shape
+    return call(
+        lambda chunks, *refs: head_kernel(chunks, point, *refs),
+        [(fields, rows, columns), (fields, rows + 2 * FACTOR, columns)],
+        1,
+        rows,
+        columns,
+        (c_points, halo),
+    )
+
+
+def finish(middle, shape):
+    _, rows, columns = shape
+    return call(finish_kernel, [shape], 1, rows, columns, (middle,))[0]
 
 
 def edges_of(block, width):
@@ -263,16 +303,20 @@
     points = c_points.shape[0]
     groups = lax.axis_size("tm")
     halos = [exchange(edges_of(c_points[k], 2 * FACTOR), 0) for k in range(points)]
-    advanced, pushed = zip(*[chain(k, c_points, halos[k]) for k in range(points)])
+    first, middle = head(0, c_points, halos[0])
+    ends = [(first, finish(middle, first.shape))]
+    ends += [chain(k, c_points, halos[k]) for k in range(1, points)]
+    advanced, pushed = zip(*ends)
     next_first = lax.ppermute(advanced[0], ("tm", "space"), route(-1, 0))
     packed = pack([*advanced[1:], next_first], pushed, groups)
-    members = [list(reversed(range(groups)))]
+    members = [[(groups // 2 + g) % groups for g in range(groups)]]
     coarse = lax.all_to_all(
         packed, "tm", split_axis=0, concat_axis=0, axis_index_groups=members, tiled=True
     )
-    coarse = coarse.reshape(groups, points, *coarse.shape[1:])[::-1].reshape(coarse.shape)
-    coarse = jnp.concatenate([coarse[-1:], coarse[:-1]], axis=0)
+    split = (groups - groups // 2) * points - 1
+    coarse = jnp.concatenate([coarse[split:], coarse[:split]], axis=0)
     incoming = lax.ppermute(advanced[-1], "tm", [(i, i + 1) for i in range(groups - 1)])
+    coarse, incoming = lax.optimization_barrier((coarse, incoming))
     opening = jnp.where(lax.axis_index("tm") == 0, c_points[0], incoming)
     return (jnp.stack([opening, *advanced[:-1]]), coarse)
 

time: 41 us -> 38.2 us (0.932)
  the two profiles are of different devices: /device:TPU:16 before, /device:TPU:0 now
where the time goes in v15:
time: 38.2 us; the launch traced here: 38 us
  waiting for transfers between devices  13.5 us (35%)
  starting transfers between devices  12.3 us (32%)
  Pallas kernels  8.57 us (22%)
  other arithmetic  1.75 us (5%)
  local copies, waits for them, and re-layouts  1.12 us (3%)
  between operations  0.74 us (2%)
    all_to_all x1, waiting for transfers between devices, on_device(): lax.all_to_all(packed, 'tm', split_axis=0, concat_axis=0, axis_index_grou...  7.86 us
    pallas_call x3, Pallas kernels, call(): pl.pallas_call(functools.partial(kernel, chunks), out_shape=[jax.ShapeDty...  7.7 us
    ppermute x2, waiting for transfers between devices, exchange(): return lax.ppermute(edges, both, route(shift, 1))  5.63 us
    all_to_all x1, starting transfers between devices, on_device(): lax.all_to_all(packed, 'tm', split_axis=0, concat_axis=0, axis_index_grou...  4.56 us
    ppermute x2, starting transfers between devices, exchange(): return lax.ppermute(edges, both, route(shift, 1))  3.09 us
    ppermute x1, starting transfers between devices, on_device(): next_first = lax.ppermute(advanced[0], ('tm', 'space'), route(-1, 0))  2.6 us
    ppermute x1, starting transfers between devices, on_device(): lax.ppermute(advanced[-1], 'tm', [(i, i + 1) for i in range(groups - 1)])  2.05 us
    squeeze x1, local copies, waits for them, and re-layouts, on_device(): c_points[k]  1.05 us
  transfers between devices with their start and end apart: 5, of which 2 were waited for; matrix products, arithmetic and copies ran while one was open for 3% of the time, Pallas kernels for 20%

profile of v15, /device:TPU:0, one launch (start us, length us, event | category | flops | bytes accessed | tf_op | source)
XLA Modules:
  0.0 38.0 jit_solution(12480686240072376972)
XLA Ops:
  0.6 1.1 %slice_bitcast_fusion = (f32[3,32,512]{2,1,0:T(8,128)S(1)}, f32[3,32,512]{2,1,0:T(8,128)S(1)}) fusion(f32[2,3,32,512]{3,2,1,0:T(8,128)} %refs_0_.3), kind=kLoop, calls=%fused_computation.5 | loop fusion | bytes 786432 | tf_op jit(solution)/shard_map/squeeze | solution.py:305
  1.7 0.0 copy-start
  1.8 3.0 %collective-permute-start.1 = (f32[2,3,16,512]{3,2,1,0:T(8,128)S(1)}, f32[2,3,16,512]{3,2,1,0:T(8,128)S(1)}, u32[]{:S(2)}, u32[]{:S(2)}) collective-permute-start(f32[2,3,16,512]{3,2,1,0:T(8,128)S(1)} %pad_maximum_fusion.3), channel_id=1, source_target_pairs={{0,1},{1,0},{2,3},{3,2},{4,5},{5,4},{6,7},{7,6},{8,9},{9,8},{10,11... | collective-permute-start | bytes 589832 | tf_op jit(solution)/shard_map/ppermute | solution.py:278
  4.8 0.1 collective-permute-start
  4.9 5.6 %collective-permute-done.1.refs_1_ = f32[2,3,16,512]{3,2,1,0:T(8,128)S(1)} collective-permute-done((f32[2,3,16,512]{3,2,1,0:T(8,128)S(1)}, f32[2,3,16,512]{3,2,1,0:T(8,128)S(1)}, u32[]{:S(2)}, u32[]{:S(2)}) %collective-permute-start.1) | collective-permute-done | bytes 196640 | tf_op jit(solution)/shard_map/ppermute | solution.py:278
  10.5 0.0 copy-done
  10.5 2.1 %shard_map.31 = (f32[3,32,512]{2,1,0:T(8,128)S(1)}, f32[3,48,512]{2,1,0:T(8,128)S(1)}) custom-call(f32[2,3,32,512]{3,2,1,0:T(8,128)S(1)} %copy-done, f32[2,3,16,512]{3,2,1,0:T(8,128)S(1)} %collective-permute-done.1.refs_1_), custom_call_target="tpu_custom_call" | custom-call | flops 11796480 | bytes 393216 | tf_op jit(solution)/shard_map/pallas_call | solution.py:216
  12.6 2.6 %collective-permute-start.2 = (f32[3,32,512]{2,1,0:T(8,128)S(1)}, f32[3,32,512]{2,1,0:T(8,128)S(1)}, u32[]{:S(2)}, u32[]{:S(2)}) collective-permute-start(f32[3,32,512]{2,1,0:T(8,128)S(1)} %get-tuple-element.9), channel_id=1, source_target_pairs={{0,30},{1,31},{2,0},{3,1},{4,2},{5,3},{6,4},{7,5},{8,6},{9,7},{10,... | collective-permute-start | bytes 589832 | tf_op jit(solution)/shard_map/ppermute | solution.py:310
  15.2 1.8 %shard_map.32.refs_2_ = f32[3,32,512]{2,1,0:T(8,128)S(1)} custom-call(f32[3,48,512]{2,1,0:T(8,128)S(1)} %get-tuple-element.10.middle), custom_call_target="tpu_custom_call" | custom-call | flops 11796480 | bytes 393216 | tf_op jit(solution)/shard_map/pallas_call | solution.py:216
  17.0 0.0 collective-permute-done.refs_1_
  17.0 3.9 %shard_map.30 = (f32[3,32,512]{2,1,0:T(8,128)S(1)}, f32[3,32,512]{2,1,0:T(8,128)S(1)}) custom-call(f32[2,3,32,512]{3,2,1,0:T(8,128)S(1)} %copy-done, f32[2,3,16,512]{3,2,1,0:T(8,128)S(1)} %collective-permute-done.refs_1_), custom_call_target="tpu_custom_call" | custom-call | flops 23592960 | bytes 786432 | tf_op jit(solution)/shard_map/pallas_call | solution.py:216
  20.8 0.0 collective-permute-done.2.refs_1_
  20.8 0.9 %shard_map.33 = f32[32,3,1,2,512]{4,3,2,1,0:T(2,128)} custom-call(f32[3,32,512]{2,1,0:T(8,128)S(1)} %get-tuple-element.8.refs_0_, f32[3,32,512]{2,1,0:T(8,128)S(1)} %collective-permute-done.2.refs_1_, f32[3,32,512]{2,1,0:T(8,128)S(1)} %shard_map.32.refs_2_, f32[3,32,512]{2,1,0:T(8,128)S(1)} %get-tuple-element.11.refs_3_), custom_call_target="tpu_custom_call" | custom-call | flops 98304 | bytes 1179648 | tf_op jit(solution)/shard_map/pallas_call | solution.py:291
  21.7 4.6 %all-to-all-start = ((f32[32,3,1,2,512]{4,3,2,1,0:T(2,128)}), f32[32,3,1,2,512]{4,3,2,1,0:T(2,128)S(1)}, u32[]{:S(2)}, u32[]{:S(2)}) async-start(f32[32,3,1,2,512]{4,3,2,1,0:T(2,128)} %shard_map.33), calls=%async_computation | async-start | bytes 786432 | tf_op jit(solution)/shard_map/all_to_all | solution.py:313
  26.3 2.1 %collective-permute-start.3 = (f32[3,32,512]{2,1,0:T(8,128)S(1)}, f32[3,32,512]{2,1,0:T(8,128)S(1)}, u32[]{:S(2)}, u32[]{:S(2)}) collective-permute-start(f32[3,32,512]{2,1,0:T(8,128)S(1)} %get-tuple-element.8.refs_0_), channel_id=1, source_target_pairs={{0,2},{2,4},{4,6},{6,8},{8,10},{10,12},{12,14},{14,16},{16,18},{18... | collective-permute-start | bytes 589832 | tf_op jit(solution)/shard_map/ppermute | solution.py:318
  28.3 7.9 %all-to-all-done = f32[32,3,1,2,512]{4,3,2,1,0:T(2,128)S(1)} async-done(((f32[32,3,1,2,512]{4,3,2,1,0:T(2,128)}), f32[32,3,1,2,512]{4,3,2,1,0:T(2,128)S(1)}, u32[]{:S(2)}, u32[]{:S(2)}) %all-to-all-start) | async-done | bytes 393248 | tf_op jit(solution)/shard_map/all_to_all | solution.py:313
  36.2 0.9 %pad_maximum_fusion = f32[32,3,1,2,512]{4,3,2,1,0:T(2,128)} fusion(f32[15,3,1,2,512]{4,3,2,1,0:T(2,128)S(1)} %slice.38, f32[17,3,1,2,512]{4,3,2,1,0:T(2,128)S(1)} %slice.37), kind=kLoop, calls=%fused_computation | loop fusion | flops 98304 | bytes 786432 | tf_op jit(solution)/shard_map/concatenate | solution.py:317
  37.2 0.0 collective-permute-done.3
  37.2 0.8 %pad_maximum_fusion.1 = f32[2,3,32,512]{3,2,1,0:T(8,128)} fusion(f32[1,3,32,512]{3,2,1,0:T(8,128)S(1)} %bitcast.17, f32[1,3,32,512]{3,2,1,0:T(8,128)S(1)} %select_bitcast_fusion), kind=kLoop, calls=%fused_computation.1 | loop fusion | flops 98304 | bytes 786432 | tf_op jit(solution)/shard_map/stack | solution.py:321
  (6 shorter events, 0.1 us)
Async XLA Ops:
  1.7 8.8 %copy-start = (f32[2,3,32,512]{3,2,1,0:T(8,128)S(1)}, f32[2,3,32,512]{3,2,1,0:T(8,128)}, u32[]{:S(2)}) copy-start(f32[2,3,32,512]{3,2,1,0:T(8,128)} %refs_0_.3) | copy-start | bytes 1179652
  1.8 8.7 %collective-permute-start.1 = (f32[2,3,16,512]{3,2,1,0:T(8,128)S(1)}, f32[2,3,16,512]{3,2,1,0:T(8,128)S(1)}, u32[]{:S(2)}, u32[]{:S(2)}) collective-permute-start(f32[2,3,16,512]{3,2,1,0:T(8,128)S(1)} %pad_maximum_fusion.3), channel_id=1, source_target_pairs={{0,1},{1,0},{2,3},{3,2},{4,5},{5,4},{6,7},{7,6},{8,9},{9,8},{10,11... | collective-permute-start | bytes 589832 | tf_op jit(solution)/shard_map/ppermute | solution.py:278
  4.8 12.2 %collective-permute-start = (f32[2,3,16,512]{3,2,1,0:T(8,128)S(1)}, f32[2,3,16,512]{3,2,1,0:T(8,128)S(1)}, u32[]{:S(2)}, u32[]{:S(2)}) collective-permute-start(f32[2,3,16,512]{3,2,1,0:T(8,128)S(1)} %pad_maximum_fusion.2), channel_id=1, source_target_pairs={{0,1},{1,0},{2,3},{3,2},{4,5},{5,4},{6,7},{7,6},{8,9},{9,8},{10,11... | collective-permute-start | bytes 589832 | tf_op jit(solution)/shard_map/ppermute | solution.py:278
  12.6 8.3 %collective-permute-start.2 = (f32[3,32,512]{2,1,0:T(8,128)S(1)}, f32[3,32,512]{2,1,0:T(8,128)S(1)}, u32[]{:S(2)}, u32[]{:S(2)}) collective-permute-start(f32[3,32,512]{2,1,0:T(8,128)S(1)} %get-tuple-element.9), channel_id=1, source_target_pairs={{0,30},{1,31},{2,0},{3,1},{4,2},{5,3},{6,4},{7,5},{8,6},{9,7},{10,... | collective-permute-start | bytes 589832 | tf_op jit(solution)/shard_map/ppermute | solution.py:310
  21.7 14.5 %all-to-all-start = ((f32[32,3,1,2,512]{4,3,2,1,0:T(2,128)}), f32[32,3,1,2,512]{4,3,2,1,0:T(2,128)S(1)}, u32[]{:S(2)}, u32[]{:S(2)}) async-start(f32[32,3,1,2,512]{4,3,2,1,0:T(2,128)} %shard_map.33), calls=%async_computation | async-start | bytes 786432 | tf_op jit(solution)/shard_map/all_to_all | solution.py:313
  26.3 10.9 %collective-permute-start.3 = (f32[3,32,512]{2,1,0:T(8,128)S(1)}, f32[3,32,512]{2,1,0:T(8,128)S(1)}, u32[]{:S(2)}, u32[]{:S(2)}) collective-permute-start(f32[3,32,512]{2,1,0:T(8,128)S(1)} %get-tuple-element.8.refs_0_), channel_id=1, source_target_pairs={{0,2},{2,4},{4,6},{6,8},{8,10},{10,12},{12,14},{14,16},{16,18},{18... | collective-permute-start | bytes 589832 | tf_op jit(solution)/shard_map/ppermute | solution.py:318

commit v16 on v15

--- a/solution.py
+++ b/solution.py
@@ -183,6 +183,16 @@
     second_half(chunks, middle, pushed, *scratch)
 
 
+def half_kernel(chunks, block, halo, advanced, *scratch):
+    rows = block.shape[1]
+    narrow = Rows(rows + 2 * FACTOR, chunks)
+    narrow.fill(scratch[0], [halo.at[0], block, halo.at[1]])
+    narrow.load(*scratch[:2])
+    narrow.propagate(*scratch[1:])
+    narrow.store(*scratch[:2])
+    narrow.take(scratch[0], FACTOR, rows, put(advanced))
+
+
 def pack_kernel(points, groups, *refs):
     following, pushed, (packed, difference) = refs[:points], refs[points:-2], refs[-2:]
     rows = difference.shape[2]
@@ -259,6 +269,10 @@
     return call(finish_kernel, [shape], 1, rows, columns, (middle,))[0]
 
 
+def half(block, halo):
+    return call(half_kernel, [block.shape], 1, *block.shape[1:], (block, halo))[0]
+
+
 def edges_of(block, width):
     return jnp.stack([block[..., -width:, :], block[..., :width, :]])
 
@@ -303,11 +317,15 @@
     points = c_points.shape[0]
     groups = lax.axis_size("tm")
     halos = [exchange(edges_of(c_points[k], 2 * FACTOR), 0) for k in range(points)]
+    behind = lax.ppermute(c_points[-1], "tm", [(i, i + 1) for i in range(groups - 1)])
+    halos[0], behind = lax.optimization_barrier((halos[0], behind))
+    behind_halo = exchange(edges_of(behind, FACTOR), 0)
     first, middle = head(0, c_points, halos[0])
     ends = [(first, finish(middle, first.shape))]
     ends += [chain(k, c_points, halos[k]) for k in range(1, points)]
     advanced, pushed = zip(*ends)
     next_first = lax.ppermute(advanced[0], ("tm", "space"), route(-1, 0))
+    next_first, behind_halo = lax.optimization_barrier((next_first, behind_halo))
     packed = pack([*advanced[1:], next_first], pushed, groups)
     members = [[(groups // 2 + g) % groups for g in range(groups)]]
     coarse = lax.all_to_all(
@@ -315,9 +333,8 @@
     )
     split = (groups - groups // 2) * points - 1
     coarse = jnp.concatenate([coarse[split:], coarse[:split]], axis=0)
-    incoming = lax.ppermute(advanced[-1], "tm", [(i, i + 1) for i in range(groups - 1)])
-    coarse, incoming = lax.optimization_barrier((coarse, incoming))
-    opening = jnp.where(lax.axis_index("tm") == 0, c_points[0], incoming)
+    behind, behind_halo, _ = lax.optimization_barrier((behind, behind_halo, packed))
+    opening = jnp.where(lax.axis_index("tm") == 0, c_points[0], half(behind, behind_halo))
     return (jnp.stack([opening, *advanced[:-1]]), coarse)
 
 

time: 38.2 us -> 39.1 us (1.024)
  waiting for transfers between devices: 13.5 us -> 10.4 us
  starting transfers between devices: 12.3 us -> 14.5 us
  Pallas kernels: 8.57 us -> 10.3 us
    ppermute x2 -> x3, waiting for transfers between devices: 5.63 us -> 3.05 us  [exchange(): return lax.ppermute(edges, both, route(shift, 1))]
    ppermute x2 -> x3, starting transfers between devices: 3.09 us -> 4.93 us  [exchange(): return lax.ppermute(edges, both, route(shift, 1))]
    pallas_call x3 -> x4, Pallas kernels: 7.7 us -> 9.48 us  [call(): pl.pallas_call(functools.partial(kernel, chunks), out_shape=[jax.ShapeDty...]
    ppermute x1, starting transfers between devices: 2.6 us -> 3.43 us  [on_device(): next_first = lax.ppermute(advanced[0], ('tm', 'space'), route(-1, 0))]
    ppermute x1, starting transfers between devices: 2.05 us -> 1.46 us  [on_device(): lax.ppermute(c_points[-1], 'tm', [(i, i + 1) for i in range(groups - 1)])]
    all_to_all x1, waiting for transfers between devices: 7.86 us -> 7.32 us  [on_device(): lax.all_to_all(packed, 'tm', split_axis=0, concat_axis=0, axis_index_grou...]
  transfers between devices with their start and end apart: 5 -> 6, of which waited for: 2 -> 2; matrix products, arithmetic and copies ran while one was open for 3% -> 2% of each run, Pallas kernels for 20% -> 24%
where the time goes in v16:
time: 39.1 us; the launch traced here: 38.8 us
  starting transfers between devices  14.5 us (37%)
  waiting for transfers between devices  10.4 us (27%)
  Pallas kernels  10.3 us (26%)
  other arithmetic  1.76 us (5%)
  local copies, waits for them, and re-layouts  1.13 us (3%)
  between operations  0.76 us (2%)
    pallas_call x4, Pallas kernels, call(): pl.pallas_call(functools.partial(kernel, chunks), out_shape=[jax.ShapeDty...  9.48 us
    all_to_all x1, waiting for transfers between devices, on_device(): lax.all_to_all(packed, 'tm', split_axis=0, concat_axis=0, axis_index_grou...  7.32 us
    ppermute x3, starting transfers between devices, exchange(): return lax.ppermute(edges, both, route(shift, 1))  4.93 us
    all_to_all x1, starting transfers between devices, on_device(): lax.all_to_all(packed, 'tm', split_axis=0, concat_axis=0, axis_index_grou...  4.64 us
    ppermute x1, starting transfers between devices, on_device(): next_first = lax.ppermute(advanced[0], ('tm', 'space'), route(-1, 0))  3.43 us
    ppermute x3, waiting for transfers between devices, exchange(): return lax.ppermute(edges, both, route(shift, 1))  3.05 us
    ppermute x1, starting transfers between devices, on_device(): lax.ppermute(c_points[-1], 'tm', [(i, i + 1) for i in range(groups - 1)])  1.46 us
    squeeze x1, local copies, waits for them, and re-layouts, on_device(): c_points[-1]  1.05 us
  transfers between devices with their start and end apart: 6, of which 2 were waited for; matrix products, arithmetic and copies ran while one was open for 2% of the time, Pallas kernels for 24%

profile of v16, /device:TPU:0, one launch (start us, length us, event | category | flops | bytes accessed | tf_op | source)
XLA Modules:
  0.0 38.8 jit_solution(386613000145158145)
XLA Ops:
  0.6 1.1 %slice_bitcast_fusion = (f32[3,32,512]{2,1,0:T(8,128)S(1)}, f32[3,32,512]{2,1,0:T(8,128)S(1)}) fusion(f32[2,3,32,512]{3,2,1,0:T(8,128)} %refs_0_.3), kind=kLoop, calls=%fused_computation.5 | loop fusion | bytes 786432 | tf_op jit(solution)/shard_map/squeeze | solution.py:320
  1.7 0.0 copy-start
  1.8 3.0 %collective-permute-start = (f32[2,3,16,512]{3,2,1,0:T(8,128)S(1)}, f32[2,3,16,512]{3,2,1,0:T(8,128)S(1)}, u32[]{:S(2)}, u32[]{:S(2)}) collective-permute-start(f32[2,3,16,512]{3,2,1,0:T(8,128)S(1)} %pad_maximum_fusion.2), channel_id=1, source_target_pairs={{0,1},{1,0},{2,3},{3,2},{4,5},{5,4},{6,7},{7,6},{8,9},{9,8},{10,11... | collective-permute-start | bytes 589832 | tf_op jit(solution)/shard_map/ppermute | solution.py:292
  4.8 1.5 %collective-permute-start.1 = (f32[3,32,512]{2,1,0:T(8,128)S(1)}, f32[3,32,512]{2,1,0:T(8,128)S(1)}, u32[]{:S(2)}, u32[]{:S(2)}) collective-permute-start(f32[3,32,512]{2,1,0:T(8,128)S(1)} %get-tuple-element.22), channel_id=1, source_target_pairs={{0,2},{2,4},{4,6},{6,8},{8,10},{10,12},{12,14},{14,16},{16,18},{18... | collective-permute-start | bytes 589832 | tf_op jit(solution)/shard_map/ppermute | solution.py:320
  6.3 0.4 collective-permute-start.4
  6.6 3.0 %collective-permute-done.refs_1_ = f32[2,3,16,512]{3,2,1,0:T(8,128)S(1)} collective-permute-done((f32[2,3,16,512]{3,2,1,0:T(8,128)S(1)}, f32[2,3,16,512]{3,2,1,0:T(8,128)S(1)}, u32[]{:S(2)}, u32[]{:S(2)}) %collective-permute-start) | collective-permute-done | bytes 196640 | tf_op jit(solution)/shard_map/ppermute | solution.py:292
  9.7 0.0 collective-permute-done.1.block
  9.7 0.0 copy-done
  9.7 2.1 %shard_map.30 = (f32[3,32,512]{2,1,0:T(8,128)S(1)}, f32[3,48,512]{2,1,0:T(8,128)S(1)}) custom-call(f32[2,3,32,512]{3,2,1,0:T(8,128)S(1)} %copy-done, f32[2,3,16,512]{3,2,1,0:T(8,128)S(1)} %collective-permute-done.refs_1_), custom_call_target="tpu_custom_call" | custom-call | flops 11796480 | bytes 393216 | tf_op jit(solution)/shard_map/pallas_call | solution.py:226
  11.8 3.4 %collective-permute-start.2 = (f32[3,32,512]{2,1,0:T(8,128)S(1)}, f32[3,32,512]{2,1,0:T(8,128)S(1)}, u32[]{:S(2)}, u32[]{:S(2)}) collective-permute-start(f32[3,32,512]{2,1,0:T(8,128)S(1)} %get-tuple-element.14), channel_id=1, source_target_pairs={{0,30},{1,31},{2,0},{3,1},{4,2},{5,3},{6,4},{7,5},{8,6},{9,7},{10,... | collective-permute-start | bytes 589832 | tf_op jit(solution)/shard_map/ppermute | solution.py:327
  15.2 1.6 %collective-permute-start.3 = (f32[2,3,8,512]{3,2,1,0:T(8,128)S(1)}, f32[2,3,8,512]{3,2,1,0:T(8,128)S(1)}, u32[]{:S(2)}, u32[]{:S(2)}) collective-permute-start(f32[2,3,8,512]{3,2,1,0:T(8,128)S(1)} %pad_maximum_fusion.4), channel_id=1, source_target_pairs={{0,1},{1,0},{2,3},{3,2},{4,5},{5,4},{6,7},{7,6},{8,9},{9,8},{10,11... | collective-permute-start | bytes 294920 | tf_op jit(solution)/shard_map/ppermute | solution.py:292
  16.8 1.8 %shard_map.32.refs_2_ = f32[3,32,512]{2,1,0:T(8,128)S(1)} custom-call(f32[3,48,512]{2,1,0:T(8,128)S(1)} %get-tuple-element.18.middle), custom_call_target="tpu_custom_call" | custom-call | flops 11796480 | bytes 393216 | tf_op jit(solution)/shard_map/pallas_call | solution.py:226
  18.5 0.0 collective-permute-done.4.refs_1_
  18.6 3.9 %shard_map.31 = (f32[3,32,512]{2,1,0:T(8,128)S(1)}, f32[3,32,512]{2,1,0:T(8,128)S(1)}) custom-call(f32[2,3,32,512]{3,2,1,0:T(8,128)S(1)} %copy-done, f32[2,3,16,512]{3,2,1,0:T(8,128)S(1)} %collective-permute-done.4.refs_1_), custom_call_target="tpu_custom_call" | custom-call | flops 23592960 | bytes 786432 | tf_op jit(solution)/shard_map/pallas_call | solution.py:226
  22.4 0.0 collective-permute-done.3.halo
  22.4 0.0 collective-permute-done.2.refs_1_
  22.4 0.9 %shard_map.33 = f32[32,3,1,2,512]{4,3,2,1,0:T(2,128)} custom-call(f32[3,32,512]{2,1,0:T(8,128)S(1)} %get-tuple-element.16.refs_0_, f32[3,32,512]{2,1,0:T(8,128)S(1)} %collective-permute-done.2.refs_1_, f32[3,32,512]{2,1,0:T(8,128)S(1)} %shard_map.32.refs_2_, f32[3,32,512]{2,1,0:T(8,128)S(1)} %get-tuple-element.19.refs_3_), custom_call_target="tpu_custom_call" | custom-call | flops 98304 | bytes 1179648 | tf_op jit(solution)/shard_map/pallas_call | solution.py:305
  23.3 4.6 %all-to-all-start = ((f32[32,3,1,2,512]{4,3,2,1,0:T(2,128)}), f32[32,3,1,2,512]{4,3,2,1,0:T(2,128)S(1)}, u32[]{:S(2)}, u32[]{:S(2)}) async-start(f32[32,3,1,2,512]{4,3,2,1,0:T(2,128)} %shard_map.33), calls=%async_computation | async-start | bytes 786432 | tf_op jit(solution)/shard_map/all_to_all | solution.py:331
  27.9 1.8 %shard_map.34 = f32[3,32,512]{2,1,0:T(8,128)S(1)} custom-call(f32[3,32,512]{2,1,0:T(8,128)S(1)} %collective-permute-done.1.block, f32[2,3,8,512]{3,2,1,0:T(8,128)S(1)} %collective-permute-done.3.halo), custom_call_target="tpu_custom_call" | custom-call | flops 11796480 | bytes 393216 | tf_op jit(solution)/shard_map/pallas_call | solution.py:226
  29.8 0.8 %pad_maximum_fusion = f32[2,3,32,512]{3,2,1,0:T(8,128)} fusion(f32[1,3,32,512]{3,2,1,0:T(8,128)S(1)} %bitcast.21, f32[1,3,32,512]{3,2,1,0:T(8,128)S(1)} %select_bitcast_fusion), kind=kLoop, calls=%fused_computation | loop fusion | flops 98304 | bytes 786432 | tf_op jit(solution)/shard_map/stack | solution.py:338
  30.5 7.3 %all-to-all-done = f32[32,3,1,2,512]{4,3,2,1,0:T(2,128)S(1)} async-done(((f32[32,3,1,2,512]{4,3,2,1,0:T(2,128)}), f32[32,3,1,2,512]{4,3,2,1,0:T(2,128)S(1)}, u32[]{:S(2)}, u32[]{:S(2)}) %all-to-all-start) | async-done | bytes 393248 | tf_op jit(solution)/shard_map/all_to_all | solution.py:331
  37.9 0.9 %pad_maximum_fusion.1 = f32[32,3,1,2,512]{4,3,2,1,0:T(2,128)} fusion(f32[15,3,1,2,512]{4,3,2,1,0:T(2,128)S(1)} %slice.47, f32[17,3,1,2,512]{4,3,2,1,0:T(2,128)S(1)} %slice.46), kind=kLoop, calls=%fused_computation.1 | loop fusion | flops 98304 | bytes 786432 | tf_op jit(solution)/shard_map/concatenate | solution.py:335
  (8 shorter events, 0.1 us)
Async XLA Ops:
  1.7 7.9 %copy-start = (f32[2,3,32,512]{3,2,1,0:T(8,128)S(1)}, f32[2,3,32,512]{3,2,1,0:T(8,128)}, u32[]{:S(2)}) copy-start(f32[2,3,32,512]{3,2,1,0:T(8,128)} %refs_0_.3) | copy-start | bytes 1179652
  1.8 7.9 %collective-permute-start = (f32[2,3,16,512]{3,2,1,0:T(8,128)S(1)}, f32[2,3,16,512]{3,2,1,0:T(8,128)S(1)}, u32[]{:S(2)}, u32[]{:S(2)}) collective-permute-start(f32[2,3,16,512]{3,2,1,0:T(8,128)S(1)} %pad_maximum_fusion.2), channel_id=1, source_target_pairs={{0,1},{1,0},{2,3},{3,2},{4,5},{5,4},{6,7},{7,6},{8,9},{9,8},{10,11... | collective-permute-start | bytes 589832 | tf_op jit(solution)/shard_map/ppermute | solution.py:292
  4.8 4.9 %collective-permute-start.1 = (f32[3,32,512]{2,1,0:T(8,128)S(1)}, f32[3,32,512]{2,1,0:T(8,128)S(1)}, u32[]{:S(2)}, u32[]{:S(2)}) collective-permute-start(f32[3,32,512]{2,1,0:T(8,128)S(1)} %get-tuple-element.22), channel_id=1, source_target_pairs={{0,2},{2,4},{4,6},{6,8},{8,10},{10,12},{12,14},{14,16},{16,18},{18... | collective-permute-start | bytes 589832 | tf_op jit(solution)/shard_map/ppermute | solution.py:320
  6.3 12.3 %collective-permute-start.4 = (f32[2,3,16,512]{3,2,1,0:T(8,128)S(1)}, f32[2,3,16,512]{3,2,1,0:T(8,128)S(1)}, u32[]{:S(2)}, u32[]{:S(2)}) collective-permute-start(f32[2,3,16,512]{3,2,1,0:T(8,128)S(1)} %pad_maximum_fusion.3), channel_id=1, source_target_pairs={{0,1},{1,0},{2,3},{3,2},{4,5},{5,4},{6,7},{7,6},{8,9},{9,8},{10,11... | collective-permute-start | bytes 589832 | tf_op jit(solution)/shard_map/ppermute | solution.py:292
  11.8 10.7 %collective-permute-start.2 = (f32[3,32,512]{2,1,0:T(8,128)S(1)}, f32[3,32,512]{2,1,0:T(8,128)S(1)}, u32[]{:S(2)}, u32[]{:S(2)}) collective-permute-start(f32[3,32,512]{2,1,0:T(8,128)S(1)} %get-tuple-element.14), channel_id=1, source_target_pairs={{0,30},{1,31},{2,0},{3,1},{4,2},{5,3},{6,4},{7,5},{8,6},{9,7},{10,... | collective-permute-start | bytes 589832 | tf_op jit(solution)/shard_map/ppermute | solution.py:327
  15.2 7.2 %collective-permute-start.3 = (f32[2,3,8,512]{3,2,1,0:T(8,128)S(1)}, f32[2,3,8,512]{3,2,1,0:T(8,128)S(1)}, u32[]{:S(2)}, u32[]{:S(2)}) collective-permute-start(f32[2,3,8,512]{3,2,1,0:T(8,128)S(1)} %pad_maximum_fusion.4), channel_id=1, source_target_pairs={{0,1},{1,0},{2,3},{3,2},{4,5},{5,4},{6,7},{7,6},{8,9},{9,8},{10,11... | collective-permute-start | bytes 294920 | tf_op jit(solution)/shard_map/ppermute | solution.py:292
  23.3 14.6 %all-to-all-start = ((f32[32,3,1,2,512]{4,3,2,1,0:T(2,128)}), f32[32,3,1,2,512]{4,3,2,1,0:T(2,128)S(1)}, u32[]{:S(2)}, u32[]{:S(2)}) async-start(f32[32,3,1,2,512]{4,3,2,1,0:T(2,128)} %shard_map.33), calls=%async_computation | async-start | bytes 786432 | tf_op jit(solution)/shard_map/all_to_all | solution.py:331

commit v17 on v15

--- a/solution.py
+++ b/solution.py
@@ -126,13 +126,9 @@
     def propagate(self, state, held):
         depth = self.depth
 
-        def two(_, factor):
-            step(state.at[0], state.at[1], held, 0, depth, self.chunks, factor)
-            factor = factor * 0.25
-            step(state.at[1], state.at[0], held, 1 % depth, depth, self.chunks, factor)
-            return factor * 0.25
-
-        lax.fori_loop(0, FACTOR // 2, two, jnp.float32(PRESSURE))
+        for n in range(FACTOR):
+            now, then = state.at[n % 2], state.at[(n + 1) % 2]
+            step(now, then, held, n % depth, depth, self.chunks, PRESSURE * 0.25**n)
 
     def take(self, ext, start, count, use):
         for at, place, length in self.pieces(start, count):
@@ -313,12 +309,14 @@
     coarse = lax.all_to_all(
         packed, "tm", split_axis=0, concat_axis=0, axis_index_groups=members, tiled=True
     )
-    split = (groups - groups // 2) * points - 1
-    coarse = jnp.concatenate([coarse[split:], coarse[:split]], axis=0)
     incoming = lax.ppermute(advanced[-1], "tm", [(i, i + 1) for i in range(groups - 1)])
+    updated, _ = lax.optimization_barrier((jnp.stack([c_points[0], *advanced[:-1]]), packed))
     coarse, incoming = lax.optimization_barrier((coarse, incoming))
     opening = jnp.where(lax.axis_index("tm") == 0, c_points[0], incoming)
-    return (jnp.stack([opening, *advanced[:-1]]), coarse)
+    updated = lax.dynamic_update_slice(updated, opening[None], (0, 0, 0, 0))
+    updated, coarse = lax.optimization_barrier((updated, coarse))
+    split = (groups - groups // 2) * points - 1
+    return (updated, jnp.concatenate([coarse[split:], coarse[:split]], axis=0))
 
 
 def solution(mesh):

time: 38.2 us -> 37.4 us (0.979)
  the two profiles are of different devices: /device:TPU:0 before, /device:TPU:16 now
where the time goes in v17:
time: 37.4 us; the launch traced here: 37.1 us
  waiting for transfers between devices  17.9 us (48%)
  starting transfers between devices  8.95 us (24%)
  Pallas kernels  7.37 us (20%)
  local copies, waits for them, and re-layouts  1.14 us (3%)
  other arithmetic  1 us (3%)
  between operations  0.77 us (2%)
    ppermute x1, waiting for transfers between devices, on_device(): lax.ppermute(advanced[-1], 'tm', [(i, i + 1) for i in range(groups - 1)])  12.2 us
    pallas_call x3, Pallas kernels, call(): pl.pallas_call(functools.partial(kernel, chunks), out_shape=[jax.ShapeDty...  6.5 us
    ppermute x2, waiting for transfers between devices, exchange(): return lax.ppermute(edges, both, route(shift, 1))  5.68 us
    all_to_all x1, starting transfers between devices, on_device(): lax.all_to_all(packed, 'tm', split_axis=0, concat_axis=0, axis_index_grou...  4.43 us
    ppermute x1, starting transfers between devices, on_device(): lax.ppermute(advanced[-1], 'tm', [(i, i + 1) for i in range(groups - 1)])  2.31 us
    ppermute x2, starting transfers between devices, exchange(): return lax.ppermute(edges, both, route(shift, 1))  2.16 us
    squeeze x1, local copies, waits for them, and re-layouts, on_device(): c_points[k]  1.07 us
    concatenate x1, other arithmetic, on_device(): return (updated, jnp.concatenate([coarse[split:], coarse[:split]], axis=0))  0.92 us
  transfers between devices with their start and end apart: 5, of which 2 were waited for; matrix products, arithmetic and copies ran while one was open for 0% of the time, Pallas kernels for 18%

profile of v17, /device:TPU:16, one launch (start us, length us, event | category | flops | bytes accessed | tf_op | source)
XLA Modules:
  0.0 37.1 jit_solution(5581861656290984212)
XLA Ops:
  0.6 1.1 %slice_bitcast_fusion = (f32[3,32,512]{2,1,0:T(8,128)S(1)}, f32[3,32,512]{2,1,0:T(8,128)S(1)}, f32[1,3,32,512]{3,2,1,0:T(8,128)S(1)}) fusion(f32[2,3,32,512]{3,2,1,0:T(8,128)} %refs_0_.3), kind=kLoop, calls=%fused_computation.5 | loop fusion | bytes 983040 | tf_op jit(solution)/shard_map/squeeze | solution.py:301
  1.7 0.0 copy-start
  1.8 1.6 %collective-permute-start = (f32[2,3,16,512]{3,2,1,0:T(8,128)S(1)}, f32[2,3,16,512]{3,2,1,0:T(8,128)S(1)}, u32[]{:S(2)}, u32[]{:S(2)}) collective-permute-start(f32[2,3,16,512]{3,2,1,0:T(8,128)S(1)} %pad_maximum_fusion.2), channel_id=1, source_target_pairs={{0,1},{1,0},{2,3},{3,2},{4,5},{5,4},{6,7},{7,6},{8,9},{9,8},{10,11... | collective-permute-start | bytes 589832 | tf_op jit(solution)/shard_map/ppermute | solution.py:274
  3.4 0.6 %collective-permute-start.1 = (f32[2,3,16,512]{3,2,1,0:T(8,128)S(1)}, f32[2,3,16,512]{3,2,1,0:T(8,128)S(1)}, u32[]{:S(2)}, u32[]{:S(2)}) collective-permute-start(f32[2,3,16,512]{3,2,1,0:T(8,128)S(1)} %pad_maximum_fusion.3), channel_id=1, source_target_pairs={{0,1},{1,0},{2,3},{3,2},{4,5},{5,4},{6,7},{7,6},{8,9},{9,8},{10,11... | collective-permute-start | bytes 589832 | tf_op jit(solution)/shard_map/ppermute | solution.py:274
  4.0 5.7 %collective-permute-done.refs_1_ = f32[2,3,16,512]{3,2,1,0:T(8,128)S(1)} collective-permute-done((f32[2,3,16,512]{3,2,1,0:T(8,128)S(1)}, f32[2,3,16,512]{3,2,1,0:T(8,128)S(1)}, u32[]{:S(2)}, u32[]{:S(2)}) %collective-permute-start) | collective-permute-done | bytes 196640 | tf_op jit(solution)/shard_map/ppermute | solution.py:274
  9.6 0.0 copy-done
  9.6 1.8 %shard_map.30 = (f32[3,32,512]{2,1,0:T(8,128)S(1)}, f32[3,48,512]{2,1,0:T(8,128)S(1)}) custom-call(f32[2,3,32,512]{3,2,1,0:T(8,128)S(1)} %copy-done, f32[2,3,16,512]{3,2,1,0:T(8,128)S(1)} %collective-permute-done.refs_1_), custom_call_target="tpu_custom_call" | custom-call | flops 11796480 | bytes 393216 | tf_op jit(solution)/shard_map/pallas_call | solution.py:212
  11.5 0.1 collective-permute-start.2
  11.6 1.4 %shard_map.32.refs_2_ = f32[3,32,512]{2,1,0:T(8,128)S(1)} custom-call(f32[3,48,512]{2,1,0:T(8,128)S(1)} %get-tuple-element.13.middle), custom_call_target="tpu_custom_call" | custom-call | flops 11796480 | bytes 393216 | tf_op jit(solution)/shard_map/pallas_call | solution.py:212
  13.0 0.0 collective-permute-done.1.refs_1_
  13.0 3.3 %shard_map.31 = (f32[3,32,512]{2,1,0:T(8,128)S(1)}, f32[3,32,512]{2,1,0:T(8,128)S(1)}) custom-call(f32[2,3,32,512]{3,2,1,0:T(8,128)S(1)} %copy-done, f32[2,3,16,512]{3,2,1,0:T(8,128)S(1)} %collective-permute-done.1.refs_1_), custom_call_target="tpu_custom_call" | custom-call | flops 23592960 | bytes 786432 | tf_op jit(solution)/shard_map/pallas_call | solution.py:212
  16.2 0.0 collective-permute-done.2.refs_1_
  16.2 0.9 %shard_map.33 = f32[32,3,1,2,512]{4,3,2,1,0:T(2,128)} custom-call(f32[3,32,512]{2,1,0:T(8,128)S(1)} %get-tuple-element.12.refs_0_, f32[3,32,512]{2,1,0:T(8,128)S(1)} %collective-permute-done.2.refs_1_, f32[3,32,512]{2,1,0:T(8,128)S(1)} %shard_map.32.refs_2_, f32[3,32,512]{2,1,0:T(8,128)S(1)} %get-tuple-element.14.refs_3_), custom_call_target="tpu_custom_call" | custom-call | flops 98304 | bytes 1179648 | tf_op jit(solution)/shard_map/pallas_call | solution.py:287
  17.1 4.4 %all-to-all-start = ((f32[32,3,1,2,512]{4,3,2,1,0:T(2,128)}), f32[32,3,1,2,512]{4,3,2,1,0:T(2,128)S(1)}, u32[]{:S(2)}, u32[]{:S(2)}) async-start(f32[32,3,1,2,512]{4,3,2,1,0:T(2,128)} %shard_map.33), calls=%async_computation | async-start | bytes 786432 | tf_op jit(solution)/shard_map/all_to_all | solution.py:309
  21.5 2.3 %collective-permute-start.3 = (f32[3,32,512]{2,1,0:T(8,128)S(1)}, f32[3,32,512]{2,1,0:T(8,128)S(1)}, u32[]{:S(2)}, u32[]{:S(2)}) collective-permute-start(f32[3,32,512]{2,1,0:T(8,128)S(1)} %get-tuple-element.12.refs_0_), channel_id=1, source_target_pairs={{0,2},{2,4},{4,6},{6,8},{8,10},{10,12},{12,14},{14,16},{16,18},{18... | collective-permute-start | bytes 589832 | tf_op jit(solution)/shard_map/ppermute | solution.py:312
  23.9 12.2 %collective-permute-done.3 = f32[3,32,512]{2,1,0:T(8,128)S(1)} collective-permute-done((f32[3,32,512]{2,1,0:T(8,128)S(1)}, f32[3,32,512]{2,1,0:T(8,128)S(1)}, u32[]{:S(2)}, u32[]{:S(2)}) %collective-permute-start.3) | collective-permute-done | bytes 196640 | tf_op jit(solution)/shard_map/ppermute | solution.py:312
  36.1 0.0 all-to-all-done
  36.1 0.0 copy-start.1
  36.2 0.9 %pad_maximum_fusion.1 = f32[32,3,1,2,512]{4,3,2,1,0:T(2,128)} fusion(f32[15,3,1,2,512]{4,3,2,1,0:T(2,128)S(1)} %slice.33, f32[17,3,1,2,512]{4,3,2,1,0:T(2,128)S(1)} %slice.32), kind=kLoop, calls=%fused_computation.1 | loop fusion | flops 98304 | bytes 786432 | tf_op jit(solution)/shard_map/concatenate | solution.py:319
  37.1 0.0 copy-done.1
  (7 shorter events, 0.1 us)
Async XLA Ops:
  1.7 7.9 %copy-start = (f32[2,3,32,512]{3,2,1,0:T(8,128)S(1)}, f32[2,3,32,512]{3,2,1,0:T(8,128)}, u32[]{:S(2)}) copy-start(f32[2,3,32,512]{3,2,1,0:T(8,128)} %refs_0_.3) | copy-start | bytes 1179652
  1.8 7.9 %collective-permute-start = (f32[2,3,16,512]{3,2,1,0:T(8,128)S(1)}, f32[2,3,16,512]{3,2,1,0:T(8,128)S(1)}, u32[]{:S(2)}, u32[]{:S(2)}) collective-permute-start(f32[2,3,16,512]{3,2,1,0:T(8,128)S(1)} %pad_maximum_fusion.2), channel_id=1, source_target_pairs={{0,1},{1,0},{2,3},{3,2},{4,5},{5,4},{6,7},{7,6},{8,9},{9,8},{10,11... | collective-permute-start | bytes 589832 | tf_op jit(solution)/shard_map/ppermute | solution.py:274
  3.4 9.6 %collective-permute-start.1 = (f32[2,3,16,512]{3,2,1,0:T(8,128)S(1)}, f32[2,3,16,512]{3,2,1,0:T(8,128)S(1)}, u32[]{:S(2)}, u32[]{:S(2)}) collective-permute-start(f32[2,3,16,512]{3,2,1,0:T(8,128)S(1)} %pad_maximum_fusion.3), channel_id=1, source_target_pairs={{0,1},{1,0},{2,3},{3,2},{4,5},{5,4},{6,7},{7,6},{8,9},{9,8},{10,11... | collective-permute-start | bytes 589832 | tf_op jit(solution)/shard_map/ppermute | solution.py:274
  11.5 4.8 %collective-permute-start.2 = (f32[3,32,512]{2,1,0:T(8,128)S(1)}, f32[3,32,512]{2,1,0:T(8,128)S(1)}, u32[]{:S(2)}, u32[]{:S(2)}) collective-permute-start(f32[3,32,512]{2,1,0:T(8,128)S(1)} %get-tuple-element.11), channel_id=1, source_target_pairs={{0,30},{1,31},{2,0},{3,1},{4,2},{5,3},{6,4},{7,5},{8,6},{9,7},{10,... | collective-permute-start | bytes 589832 | tf_op jit(solution)/shard_map/ppermute | solution.py:306
  17.1 19.0 %all-to-all-start = ((f32[32,3,1,2,512]{4,3,2,1,0:T(2,128)}), f32[32,3,1,2,512]{4,3,2,1,0:T(2,128)S(1)}, u32[]{:S(2)}, u32[]{:S(2)}) async-start(f32[32,3,1,2,512]{4,3,2,1,0:T(2,128)} %shard_map.33), calls=%async_computation | async-start | bytes 786432 | tf_op jit(solution)/shard_map/all_to_all | solution.py:309
  21.5 14.6 %collective-permute-start.3 = (f32[3,32,512]{2,1,0:T(8,128)S(1)}, f32[3,32,512]{2,1,0:T(8,128)S(1)}, u32[]{:S(2)}, u32[]{:S(2)}) collective-permute-start(f32[3,32,512]{2,1,0:T(8,128)S(1)} %get-tuple-element.12.refs_0_), channel_id=1, source_target_pairs={{0,2},{2,4},{4,6},{6,8},{8,10},{10,12},{12,14},{14,16},{16,18},{18... | collective-permute-start | bytes 589832 | tf_op jit(solution)/shard_map/ppermute | solution.py:312
  36.1 1.0 %copy-start.1 = (f32[2,3,32,512]{3,2,1,0:T(8,128)}, f32[2,3,32,512]{3,2,1,0:T(8,128)S(1)}, u32[]{:S(2)}) copy-start(f32[2,3,32,512]{3,2,1,0:T(8,128)S(1)} %bitcast_dynamic-update-slice_fusion) | copy-start | bytes 1179652

commit v18 on v17

--- a/solution.py
+++ b/solution.py
@@ -164,9 +164,22 @@
     narrow.take(ext, FACTOR, rows, put(pushed))
 
 
-def chain_kernel(chunks, point, own, halo, advanced, pushed, middle, *scratch):
+def lay_out(groups, difference, place):
+    share = difference.shape[1] // groups
+    for g in range(groups):
+        part = slice(g * share, (g + 1) * share)
+        for f in range(3):
+            place((g - groups // 2) % groups)[f, 0] = difference[f, part, :]
+
+
+def chain_kernel(
+    chunks, point, groups, own, halo, before, advanced, pushed, packed, middle, difference, *scratch
+):
+    rows = own.shape[2]
     first_half(chunks, own.at[point], halo, middle, *scratch)
-    advanced[...] = middle[:, FACTOR : FACTOR + own.shape[2], :]
+    advanced[...] = middle[:, FACTOR : FACTOR + rows, :]
+    difference[...] = before[...] - middle[:, FACTOR : FACTOR + rows, :]
+    lay_out(groups, difference, lambda n: packed.at[n])
     second_half(chunks, middle, pushed, *scratch)
 
 
@@ -179,23 +192,18 @@
     second_half(chunks, middle, pushed, *scratch)
 
 
-def pack_kernel(points, groups, *refs):
-    following, pushed, (packed, difference) = refs[:points], refs[points:-2], refs[-2:]
-    rows = difference.shape[2]
-    share = rows // groups
-    for k in range(points):
-        difference[k] = pushed[k][...] - following[k][...]
+def pack_kernel(points, groups, following, pushed, *refs):
+    ready, (packed, difference) = refs[: points - 1], refs[points - 1 :]
+    for k in range(points - 1):
+        for n in range(groups):
+            packed[n * points + k] = ready[k][n]
+    difference[...] = pushed[...] - following[...]
 
     @pl.when(lax.axis_index("tm") == groups - 1)
     def _():
-        first = following[points - 1]
-        difference[points - 1] = first[...] - first[...]
-
-    for g in range(groups):
-        part = slice(g * share, (g + 1) * share)
-        for k in range(points):
-            for f in range(3):
-                packed[(g - groups // 2) % groups * points + k, f, 0] = difference[k, f, part, :]
+        difference[...] = following[...] - following[...]
+
+    lay_out(groups, difference, lambda n: packed.at[n * points + points - 1])
 
 
 VMEM = pl.BlockSpec(memory_space=pltpu.VMEM)
@@ -225,16 +233,20 @@
     )(*operands)
 
 
-def chain(point, c_points, halo):
+def chain(point, c_points, halo, before, groups):
     _, fields, rows, columns = c_points.shape
+    shape = (fields, rows, columns)
     return call(
-        lambda chunks, *refs: chain_kernel(chunks, point, *refs),
-        [(fields, rows, columns)] * 2,
+        lambda chunks, *refs: chain_kernel(chunks, point, groups, *refs),
+        [shape, shape, (groups, fields, 1, rows // groups, columns)],
         2,
         rows,
         columns,
-        (c_points, halo),
-        extra=[pltpu.VMEM((fields, rows + 2 * FACTOR, columns), jnp.float32)],
+        (c_points, halo, before),
+        extra=[
+            pltpu.VMEM((fields, rows + 2 * FACTOR, columns), jnp.float32),
+            pltpu.VMEM(shape, jnp.float32),
+        ],
     )
 
 
@@ -280,19 +292,19 @@
     )
 
 
-def pack(following, pushed, groups):
-    points, (fields, rows, columns) = len(pushed), pushed[0].shape
+def pack(following, pushed, ready, groups):
+    points, (fields, rows, columns) = len(ready) + 1, pushed.shape
     packet = (groups * points, fields, 1, rows // groups, columns)
     size = points * fields * rows * columns
     return pl.pallas_call(
         functools.partial(pack_kernel, points, groups),
         out_shape=jax.ShapeDtypeStruct(packet, jnp.float32),
-        in_specs=[VMEM] * (2 * points),
+        in_specs=[VMEM] * (points + 1),
         out_specs=VMEM,
-        scratch_shapes=[pltpu.VMEM((points, fields, rows, columns), jnp.float32)],
+        scratch_shapes=[pltpu.VMEM((fields, rows, columns), jnp.float32)],
         compiler_params=pltpu.CompilerParams(vmem_limit_bytes=24 * 2**20),
         cost_estimate=pl.CostEstimate(flops=size, bytes_accessed=12 * size, transcendentals=0),
-    )(*following, *pushed)
+    )(following, pushed, *ready)
 
 
 def on_device(c_points):
@@ -300,11 +312,13 @@
     groups = lax.axis_size("tm")
     halos = [exchange(edges_of(c_points[k], 2 * FACTOR), 0) for k in range(points)]
     first, middle = head(0, c_points, halos[0])
-    ends = [(first, finish(middle, first.shape))]
-    ends += [chain(k, c_points, halos[k]) for k in range(1, points)]
-    advanced, pushed = zip(*ends)
+    advanced, pushed, ready = [first], finish(middle, first.shape), []
+    for k in range(1, points):
+        now, pushed, part = chain(k, c_points, halos[k], pushed, groups)
+        advanced.append(now)
+        ready.append(part)
     next_first = lax.ppermute(advanced[0], ("tm", "space"), route(-1, 0))
-    packed = pack([*advanced[1:], next_first], pushed, groups)
+    packed = pack(next_first, pushed, ready, groups)
     members = [[(groups // 2 + g) % groups for g in range(groups)]]
     coarse = lax.all_to_all(
         packed, "tm", split_axis=0, concat_axis=0, axis_index_groups=members, tiled=True

time: 37.4 us -> 37.3 us (level)
  no operation moved by 1% of the time
where the time goes in v18:
time: 37.3 us; the launch traced here: 37.1 us
  waiting for transfers between devices  17.9 us (48%)
  starting transfers between devices  8.9 us (24%)
  Pallas kernels  7.38 us (20%)
  local copies, waits for them, and re-layouts  1.14 us (3%)
  other arithmetic  1 us (3%)
  between operations  0.77 us (2%)
    ppermute x1, waiting for transfers between devices, on_device(): lax.ppermute(advanced[-1], 'tm', [(i, i + 1) for i in range(groups - 1)])  12.2 us
    pallas_call x3, Pallas kernels, call(): pl.pallas_call(functools.partial(kernel, chunks), out_shape=[jax.ShapeDty...  6.56 us
    ppermute x2, waiting for transfers between devices, exchange(): return lax.ppermute(edges, both, route(shift, 1))  5.68 us
    all_to_all x1, starting transfers between devices, on_device(): lax.all_to_all(packed, 'tm', split_axis=0, concat_axis=0, axis_index_grou...  4.38 us
    ppermute x1, starting transfers between devices, on_device(): lax.ppermute(advanced[-1], 'tm', [(i, i + 1) for i in range(groups - 1)])  2.31 us
    ppermute x2, starting transfers between devices, exchange(): return lax.ppermute(edges, both, route(shift, 1))  2.16 us
    squeeze x1, local copies, waits for them, and re-layouts, on_device(): c_points[k]  1.07 us
    concatenate x1, other arithmetic, on_device(): return (updated, jnp.concatenate([coarse[split:], coarse[:split]], axis=0))  0.92 us
  transfers between devices with their start and end apart: 5, of which 2 were waited for; matrix products, arithmetic and copies ran while one was open for 0% of the time, Pallas kernels for 18%

profile of v18, /device:TPU:16, one launch (start us, length us, event | category | flops | bytes accessed | tf_op | source)
XLA Modules:
  0.0 37.1 jit_solution(13066117762793767274)
XLA Ops:
  0.6 1.1 %slice_bitcast_fusion = (f32[3,32,512]{2,1,0:T(8,128)S(1)}, f32[3,32,512]{2,1,0:T(8,128)S(1)}, f32[1,3,32,512]{3,2,1,0:T(8,128)S(1)}) fusion(f32[2,3,32,512]{3,2,1,0:T(8,128)} %refs_0_.3), kind=kLoop, calls=%fused_computation.5 | loop fusion | bytes 983040 | tf_op jit(solution)/shard_map/squeeze | solution.py:313
  1.7 0.0 copy-start
  1.8 1.6 %collective-permute-start = (f32[2,3,16,512]{3,2,1,0:T(8,128)S(1)}, f32[2,3,16,512]{3,2,1,0:T(8,128)S(1)}, u32[]{:S(2)}, u32[]{:S(2)}) collective-permute-start(f32[2,3,16,512]{3,2,1,0:T(8,128)S(1)} %pad_maximum_fusion.2), channel_id=1, source_target_pairs={{0,1},{1,0},{2,3},{3,2},{4,5},{5,4},{6,7},{7,6},{8,9},{9,8},{10,11... | collective-permute-start | bytes 589832 | tf_op jit(solution)/shard_map/ppermute | solution.py:286
  3.4 0.6 %collective-permute-start.2 = (f32[2,3,16,512]{3,2,1,0:T(8,128)S(1)}, f32[2,3,16,512]{3,2,1,0:T(8,128)S(1)}, u32[]{:S(2)}, u32[]{:S(2)}) collective-permute-start(f32[2,3,16,512]{3,2,1,0:T(8,128)S(1)} %pad_maximum_fusion.3), channel_id=1, source_target_pairs={{0,1},{1,0},{2,3},{3,2},{4,5},{5,4},{6,7},{7,6},{8,9},{9,8},{10,11... | collective-permute-start | bytes 589832 | tf_op jit(solution)/shard_map/ppermute | solution.py:286
  4.0 5.7 %collective-permute-done.refs_1_ = f32[2,3,16,512]{3,2,1,0:T(8,128)S(1)} collective-permute-done((f32[2,3,16,512]{3,2,1,0:T(8,128)S(1)}, f32[2,3,16,512]{3,2,1,0:T(8,128)S(1)}, u32[]{:S(2)}, u32[]{:S(2)}) %collective-permute-start) | collective-permute-done | bytes 196640 | tf_op jit(solution)/shard_map/ppermute | solution.py:286
  9.6 0.0 copy-done
  9.6 1.8 %shard_map.30 = (f32[3,32,512]{2,1,0:T(8,128)S(1)}, f32[3,48,512]{2,1,0:T(8,128)S(1)}) custom-call(f32[2,3,32,512]{3,2,1,0:T(8,128)S(1)} %copy-done, f32[2,3,16,512]{3,2,1,0:T(8,128)S(1)} %collective-permute-done.refs_1_), custom_call_target="tpu_custom_call" | custom-call | flops 11796480 | bytes 393216 | tf_op jit(solution)/shard_map/pallas_call | solution.py:220
  11.5 0.1 collective-permute-start.1
  11.6 1.4 %shard_map.31.refs_2_ = f32[3,32,512]{2,1,0:T(8,128)S(1)} custom-call(f32[3,48,512]{2,1,0:T(8,128)S(1)} %get-tuple-element.13.middle), custom_call_target="tpu_custom_call" | custom-call | flops 11796480 | bytes 393216 | tf_op jit(solution)/shard_map/pallas_call | solution.py:220
  13.0 0.0 collective-permute-done.2.refs_1_
  13.0 3.3 %shard_map.32 = (f32[3,32,512]{2,1,0:T(8,128)S(1)}, f32[3,32,512]{2,1,0:T(8,128)S(1)}, f32[16,3,1,2,512]{4,3,2,1,0:T(2,128)S(1)}) custom-call(f32[2,3,32,512]{3,2,1,0:T(8,128)S(1)} %copy-done, f32[2,3,16,512]{3,2,1,0:T(8,128)S(1)} %collective-permute-done.2.refs_1_, f32[3,32,512]{2,1,0:T(8,128)S(1)} %shard_map.31.refs_2_), custom_call_target="tpu_custom_call" | custom-call | flops 23592960 | bytes 786432 | tf_op jit(solution)/shard_map/pallas_call | solution.py:220
  16.3 0.0 collective-permute-done.1.following
  16.3 0.8 %shard_map.33 = f32[32,3,1,2,512]{4,3,2,1,0:T(2,128)} custom-call(f32[3,32,512]{2,1,0:T(8,128)S(1)} %collective-permute-done.1.following, f32[3,32,512]{2,1,0:T(8,128)S(1)} %get-tuple-element.14.pushed, f32[16,3,1,2,512]{4,3,2,1,0:T(2,128)S(1)} %get-tuple-element.15.refs_0_), custom_call_target="tpu_custom_call" | custom-call | flops 98304 | bytes 1179648 | tf_op jit(solution)/shard_map/pallas_call | solution.py:299
  17.1 4.4 %all-to-all-start = ((f32[32,3,1,2,512]{4,3,2,1,0:T(2,128)}), f32[32,3,1,2,512]{4,3,2,1,0:T(2,128)S(1)}, u32[]{:S(2)}, u32[]{:S(2)}) async-start(f32[32,3,1,2,512]{4,3,2,1,0:T(2,128)} %shard_map.33), calls=%async_computation | async-start | bytes 786432 | tf_op jit(solution)/shard_map/all_to_all | solution.py:323
  21.5 2.3 %collective-permute-start.3 = (f32[3,32,512]{2,1,0:T(8,128)S(1)}, f32[3,32,512]{2,1,0:T(8,128)S(1)}, u32[]{:S(2)}, u32[]{:S(2)}) collective-permute-start(f32[3,32,512]{2,1,0:T(8,128)S(1)} %get-tuple-element.17), channel_id=1, source_target_pairs={{0,2},{2,4},{4,6},{6,8},{8,10},{10,12},{12,14},{14,16},{16,18},{18... | collective-permute-start | bytes 589832 | tf_op jit(solution)/shard_map/ppermute | solution.py:326
  23.9 12.2 %collective-permute-done.3 = f32[3,32,512]{2,1,0:T(8,128)S(1)} collective-permute-done((f32[3,32,512]{2,1,0:T(8,128)S(1)}, f32[3,32,512]{2,1,0:T(8,128)S(1)}, u32[]{:S(2)}, u32[]{:S(2)}) %collective-permute-start.3) | collective-permute-done | bytes 196640 | tf_op jit(solution)/shard_map/ppermute | solution.py:326
  36.1 0.0 all-to-all-done
  36.1 0.0 copy-start.1
  36.2 0.9 %pad_maximum_fusion.1 = f32[32,3,1,2,512]{4,3,2,1,0:T(2,128)} fusion(f32[15,3,1,2,512]{4,3,2,1,0:T(2,128)S(1)} %slice.33, f32[17,3,1,2,512]{4,3,2,1,0:T(2,128)S(1)} %slice.32), kind=kLoop, calls=%fused_computation.1 | loop fusion | flops 98304 | bytes 786432 | tf_op jit(solution)/shard_map/concatenate | solution.py:333
  37.1 0.0 copy-done.1
  (7 shorter events, 0.1 us)
Async XLA Ops:
  1.7 7.9 %copy-start = (f32[2,3,32,512]{3,2,1,0:T(8,128)S(1)}, f32[2,3,32,512]{3,2,1,0:T(8,128)}, u32[]{:S(2)}) copy-start(f32[2,3,32,512]{3,2,1,0:T(8,128)} %refs_0_.3) | copy-start | bytes 1179652
  1.8 7.9 %collective-permute-start = (f32[2,3,16,512]{3,2,1,0:T(8,128)S(1)}, f32[2,3,16,512]{3,2,1,0:T(8,128)S(1)}, u32[]{:S(2)}, u32[]{:S(2)}) collective-permute-start(f32[2,3,16,512]{3,2,1,0:T(8,128)S(1)} %pad_maximum_fusion.2), channel_id=1, source_target_pairs={{0,1},{1,0},{2,3},{3,2},{4,5},{5,4},{6,7},{7,6},{8,9},{9,8},{10,11... | collective-permute-start | bytes 589832 | tf_op jit(solution)/shard_map/ppermute | solution.py:286
  3.4 9.6 %collective-permute-start.2 = (f32[2,3,16,512]{3,2,1,0:T(8,128)S(1)}, f32[2,3,16,512]{3,2,1,0:T(8,128)S(1)}, u32[]{:S(2)}, u32[]{:S(2)}) collective-permute-start(f32[2,3,16,512]{3,2,1,0:T(8,128)S(1)} %pad_maximum_fusion.3), channel_id=1, source_target_pairs={{0,1},{1,0},{2,3},{3,2},{4,5},{5,4},{6,7},{7,6},{8,9},{9,8},{10,11... | collective-permute-start | bytes 589832 | tf_op jit(solution)/shard_map/ppermute | solution.py:286
  11.5 4.8 %collective-permute-start.1 = (f32[3,32,512]{2,1,0:T(8,128)S(1)}, f32[3,32,512]{2,1,0:T(8,128)S(1)}, u32[]{:S(2)}, u32[]{:S(2)}) collective-permute-start(f32[3,32,512]{2,1,0:T(8,128)S(1)} %get-tuple-element.12), channel_id=1, source_target_pairs={{0,30},{1,31},{2,0},{3,1},{4,2},{5,3},{6,4},{7,5},{8,6},{9,7},{10,... | collective-permute-start | bytes 589832 | tf_op jit(solution)/shard_map/ppermute | solution.py:320
  17.1 19.0 %all-to-all-start = ((f32[32,3,1,2,512]{4,3,2,1,0:T(2,128)}), f32[32,3,1,2,512]{4,3,2,1,0:T(2,128)S(1)}, u32[]{:S(2)}, u32[]{:S(2)}) async-start(f32[32,3,1,2,512]{4,3,2,1,0:T(2,128)} %shard_map.33), calls=%async_computation | async-start | bytes 786432 | tf_op jit(solution)/shard_map/all_to_all | solution.py:323
  21.5 14.6 %collective-permute-start.3 = (f32[3,32,512]{2,1,0:T(8,128)S(1)}, f32[3,32,512]{2,1,0:T(8,128)S(1)}, u32[]{:S(2)}, u32[]{:S(2)}) collective-permute-start(f32[3,32,512]{2,1,0:T(8,128)S(1)} %get-tuple-element.17), channel_id=1, source_target_pairs={{0,2},{2,4},{4,6},{6,8},{8,10},{10,12},{12,14},{14,16},{16,18},{18... | collective-permute-start | bytes 589832 | tf_op jit(solution)/shard_map/ppermute | solution.py:326
  36.1 1.0 %copy-start.1 = (f32[2,3,32,512]{3,2,1,0:T(8,128)}, f32[2,3,32,512]{3,2,1,0:T(8,128)S(1)}, u32[]{:S(2)}) copy-start(f32[2,3,32,512]{3,2,1,0:T(8,128)S(1)} %bitcast_dynamic-update-slice_fusion) | copy-start | bytes 1179652

commit v19 on v18

--- a/solution.py
+++ b/solution.py
@@ -164,12 +164,21 @@
     narrow.take(ext, FACTOR, rows, put(pushed))
 
 
+def stride_of(groups):
+    return groups // 4 if groups % 4 == 0 else 1
+
+
+def listed(g, groups):
+    turn, rest = divmod((g - groups // 2) % groups, stride_of(groups))
+    return rest * (groups // stride_of(groups)) + turn
+
+
 def lay_out(groups, difference, place):
     share = difference.shape[1] // groups
     for g in range(groups):
         part = slice(g * share, (g + 1) * share)
         for f in range(3):
-            place((g - groups // 2) % groups)[f, 0] = difference[f, part, :]
+            place(listed(g, groups))[f, 0] = difference[f, part, :]
 
 
 def chain_kernel(
@@ -319,7 +328,7 @@
         ready.append(part)
     next_first = lax.ppermute(advanced[0], ("tm", "space"), route(-1, 0))
     packed = pack(next_first, pushed, ready, groups)
-    members = [[(groups // 2 + g) % groups for g in range(groups)]]
+    members = [sorted(range(groups), key=lambda g: listed(g, groups))]
     coarse = lax.all_to_all(
         packed, "tm", split_axis=0, concat_axis=0, axis_index_groups=members, tiled=True
     )
@@ -329,6 +338,9 @@
     opening = jnp.where(lax.axis_index("tm") == 0, c_points[0], incoming)
     updated = lax.dynamic_update_slice(updated, opening[None], (0, 0, 0, 0))
     updated, coarse = lax.optimization_barrier((updated, coarse))
+    shape = coarse.shape
+    steps = coarse.reshape(stride_of(groups), -1, points, *shape[1:])
+    coarse = jnp.swapaxes(steps, 0, 1).reshape(shape)
     split = (groups - groups // 2) * points - 1
     return (updated, jnp.concatenate([coarse[split:], coarse[:split]], axis=0))
 

time: 37.3 us -> 38.1 us (1.021)
  local copies, waits for them, and re-layouts: 1.14 us -> 1.87 us
    unnamed x4, local copies, waits for them, and re-layouts: 0.01 us -> 0.71 us
  transfers between devices with their start and end apart: 5 -> 5, of which waited for: 2 -> 2; matrix products, arithmetic and copies ran while one was open for 0% -> 0% of each run, Pallas kernels for 18% -> 17%
where the time goes in v19:
time: 38.1 us; the launch traced here: 37.8 us
  waiting for transfers between devices  17.9 us (47%)
  starting transfers between devices  8.9 us (23%)
  Pallas kernels  7.38 us (19%)
  local copies, waits for them, and re-layouts  1.87 us (5%)
  other arithmetic  1 us (3%)
  between operations  0.77 us (2%)
    ppermute x1, waiting for transfers between devices, on_device(): lax.ppermute(advanced[-1], 'tm', [(i, i + 1) for i in range(groups - 1)])  12.2 us
    pallas_call x3, Pallas kernels, call(): pl.pallas_call(functools.partial(kernel, chunks), out_shape=[jax.ShapeDty...  6.56 us
    ppermute x2, waiting for transfers between devices, exchange(): return lax.ppermute(edges, both, route(shift, 1))  5.68 us
    all_to_all x1, starting transfers between devices, on_device(): lax.all_to_all(packed, 'tm', split_axis=0, concat_axis=0, axis_index_grou...  4.38 us
    ppermute x1, starting transfers between devices, on_device(): lax.ppermute(advanced[-1], 'tm', [(i, i + 1) for i in range(groups - 1)])  2.31 us
    ppermute x2, starting transfers between devices, exchange(): return lax.ppermute(edges, both, route(shift, 1))  2.16 us
    squeeze x1, local copies, waits for them, and re-layouts, on_device(): c_points[k]  1.07 us
    concatenate x1, other arithmetic, on_device(): return (updated, jnp.concatenate([coarse[split:], coarse[:split]], axis=0))  0.92 us
  transfers between devices with their start and end apart: 5, of which 2 were waited for; matrix products, arithmetic and copies ran while one was open for 0% of the time, Pallas kernels for 17%

profile of v19, /device:TPU:16, one launch (start us, length us, event | category | flops | bytes accessed | tf_op | source)
XLA Modules:
  0.0 37.8 jit_solution(14729366836793864035)
XLA Ops:
  0.6 1.1 %slice_bitcast_fusion = (f32[3,32,512]{2,1,0:T(8,128)S(1)}, f32[3,32,512]{2,1,0:T(8,128)S(1)}, f32[1,3,32,512]{3,2,1,0:T(8,128)S(1)}) fusion(f32[2,3,32,512]{3,2,1,0:T(8,128)} %refs_0_.3), kind=kLoop, calls=%fused_computation.5 | loop fusion | bytes 983040 | tf_op jit(solution)/shard_map/squeeze | solution.py:322
  1.7 0.0 copy-start
  1.8 1.6 %collective-permute-start = (f32[2,3,16,512]{3,2,1,0:T(8,128)S(1)}, f32[2,3,16,512]{3,2,1,0:T(8,128)S(1)}, u32[]{:S(2)}, u32[]{:S(2)}) collective-permute-start(f32[2,3,16,512]{3,2,1,0:T(8,128)S(1)} %pad_maximum_fusion.2), channel_id=1, source_target_pairs={{0,1},{1,0},{2,3},{3,2},{4,5},{5,4},{6,7},{7,6},{8,9},{9,8},{10,11... | collective-permute-start | bytes 589832 | tf_op jit(solution)/shard_map/ppermute | solution.py:295
  3.4 0.6 %collective-permute-start.2 = (f32[2,3,16,512]{3,2,1,0:T(8,128)S(1)}, f32[2,3,16,512]{3,2,1,0:T(8,128)S(1)}, u32[]{:S(2)}, u32[]{:S(2)}) collective-permute-start(f32[2,3,16,512]{3,2,1,0:T(8,128)S(1)} %pad_maximum_fusion.3), channel_id=1, source_target_pairs={{0,1},{1,0},{2,3},{3,2},{4,5},{5,4},{6,7},{7,6},{8,9},{9,8},{10,11... | collective-permute-start | bytes 589832 | tf_op jit(solution)/shard_map/ppermute | solution.py:295
  4.0 5.7 %collective-permute-done.refs_1_ = f32[2,3,16,512]{3,2,1,0:T(8,128)S(1)} collective-permute-done((f32[2,3,16,512]{3,2,1,0:T(8,128)S(1)}, f32[2,3,16,512]{3,2,1,0:T(8,128)S(1)}, u32[]{:S(2)}, u32[]{:S(2)}) %collective-permute-start) | collective-permute-done | bytes 196640 | tf_op jit(solution)/shard_map/ppermute | solution.py:295
  9.6 0.0 copy-done
  9.6 1.8 %shard_map.30 = (f32[3,32,512]{2,1,0:T(8,128)S(1)}, f32[3,48,512]{2,1,0:T(8,128)S(1)}) custom-call(f32[2,3,32,512]{3,2,1,0:T(8,128)S(1)} %copy-done, f32[2,3,16,512]{3,2,1,0:T(8,128)S(1)} %collective-permute-done.refs_1_), custom_call_target="tpu_custom_call" | custom-call | flops 11796480 | bytes 393216 | tf_op jit(solution)/shard_map/pallas_call | solution.py:229
  11.5 0.1 collective-permute-start.1
  11.6 1.4 %shard_map.31.refs_2_ = f32[3,32,512]{2,1,0:T(8,128)S(1)} custom-call(f32[3,48,512]{2,1,0:T(8,128)S(1)} %get-tuple-element.13.middle), custom_call_target="tpu_custom_call" | custom-call | flops 11796480 | bytes 393216 | tf_op jit(solution)/shard_map/pallas_call | solution.py:229
  13.0 0.0 collective-permute-done.2.refs_1_
  13.0 3.3 %shard_map.32 = (f32[3,32,512]{2,1,0:T(8,128)S(1)}, f32[3,32,512]{2,1,0:T(8,128)S(1)}, f32[16,3,1,2,512]{4,3,2,1,0:T(2,128)S(1)}) custom-call(f32[2,3,32,512]{3,2,1,0:T(8,128)S(1)} %copy-done, f32[2,3,16,512]{3,2,1,0:T(8,128)S(1)} %collective-permute-done.2.refs_1_, f32[3,32,512]{2,1,0:T(8,128)S(1)} %shard_map.31.refs_2_), custom_call_target="tpu_custom_call" | custom-call | flops 23592960 | bytes 786432 | tf_op jit(solution)/shard_map/pallas_call | solution.py:229
  16.3 0.0 collective-permute-done.1.following
  16.3 0.8 %shard_map.33 = f32[32,3,1,2,512]{4,3,2,1,0:T(2,128)} custom-call(f32[3,32,512]{2,1,0:T(8,128)S(1)} %collective-permute-done.1.following, f32[3,32,512]{2,1,0:T(8,128)S(1)} %get-tuple-element.14.pushed, f32[16,3,1,2,512]{4,3,2,1,0:T(2,128)S(1)} %get-tuple-element.15.refs_0_), custom_call_target="tpu_custom_call" | custom-call | flops 98304 | bytes 1179648 | tf_op jit(solution)/shard_map/pallas_call | solution.py:308
  17.1 4.4 %all-to-all-start = ((f32[32,3,1,2,512]{4,3,2,1,0:T(2,128)}), f32[32,3,1,2,512]{4,3,2,1,0:T(2,128)S(1)}, u32[]{:S(2)}, u32[]{:S(2)}) async-start(f32[32,3,1,2,512]{4,3,2,1,0:T(2,128)} %shard_map.33), calls=%async_computation | async-start | bytes 786432 | tf_op jit(solution)/shard_map/all_to_all | solution.py:332
  21.5 2.3 %collective-permute-start.3 = (f32[3,32,512]{2,1,0:T(8,128)S(1)}, f32[3,32,512]{2,1,0:T(8,128)S(1)}, u32[]{:S(2)}, u32[]{:S(2)}) collective-permute-start(f32[3,32,512]{2,1,0:T(8,128)S(1)} %get-tuple-element.17), channel_id=1, source_target_pairs={{0,2},{2,4},{4,6},{6,8},{8,10},{10,12},{12,14},{14,16},{16,18},{18... | collective-permute-start | bytes 589832 | tf_op jit(solution)/shard_map/ppermute | solution.py:335
  23.9 12.2 %collective-permute-done.3 = f32[3,32,512]{2,1,0:T(8,128)S(1)} collective-permute-done((f32[3,32,512]{2,1,0:T(8,128)S(1)}, f32[3,32,512]{2,1,0:T(8,128)S(1)}, u32[]{:S(2)}, u32[]{:S(2)}) %collective-permute-start.3) | collective-permute-done | bytes 196640 | tf_op jit(solution)/shard_map/ppermute | solution.py:335
  36.1 0.0 all-to-all-done
  36.1 0.0 copy-start.1
  36.2 0.7 %copy-done.1 = f32[2,3,32,512]{3,2,1,0:T(8,128)} copy-done((f32[2,3,32,512]{3,2,1,0:T(8,128)}, f32[2,3,32,512]{3,2,1,0:T(8,128)S(1)}, u32[]{:S(2)}) %copy-start.1) | copy-done | bytes 393240
  36.9 0.9 %pad_maximum_fusion.1 = f32[32,3,1,2,512]{4,3,2,1,0:T(2,128)} fusion(f32[15,3,1,2,512]{4,3,2,1,0:T(2,128)S(1)} %slice.39, f32[17,3,1,2,512]{4,3,2,1,0:T(2,128)S(1)} %slice.38), kind=kLoop, calls=%fused_computation.1 | loop fusion | flops 98304 | bytes 786432 | tf_op jit(solution)/shard_map/concatenate | solution.py:345
  (8 shorter events, 0.2 us)
Async XLA Ops:
  1.7 7.9 %copy-start = (f32[2,3,32,512]{3,2,1,0:T(8,128)S(1)}, f32[2,3,32,512]{3,2,1,0:T(8,128)}, u32[]{:S(2)}) copy-start(f32[2,3,32,512]{3,2,1,0:T(8,128)} %refs_0_.3) | copy-start | bytes 1179652
  1.8 7.9 %collective-permute-start = (f32[2,3,16,512]{3,2,1,0:T(8,128)S(1)}, f32[2,3,16,512]{3,2,1,0:T(8,128)S(1)}, u32[]{:S(2)}, u32[]{:S(2)}) collective-permute-start(f32[2,3,16,512]{3,2,1,0:T(8,128)S(1)} %pad_maximum_fusion.2), channel_id=1, source_target_pairs={{0,1},{1,0},{2,3},{3,2},{4,5},{5,4},{6,7},{7,6},{8,9},{9,8},{10,11... | collective-permute-start | bytes 589832 | tf_op jit(solution)/shard_map/ppermute | solution.py:295
  3.4 9.6 %collective-permute-start.2 = (f32[2,3,16,512]{3,2,1,0:T(8,128)S(1)}, f32[2,3,16,512]{3,2,1,0:T(8,128)S(1)}, u32[]{:S(2)}, u32[]{:S(2)}) collective-permute-start(f32[2,3,16,512]{3,2,1,0:T(8,128)S(1)} %pad_maximum_fusion.3), channel_id=1, source_target_pairs={{0,1},{1,0},{2,3},{3,2},{4,5},{5,4},{6,7},{7,6},{8,9},{9,8},{10,11... | collective-permute-start | bytes 589832 | tf_op jit(solution)/shard_map/ppermute | solution.py:295
  11.5 4.8 %collective-permute-start.1 = (f32[3,32,512]{2,1,0:T(8,128)S(1)}, f32[3,32,512]{2,1,0:T(8,128)S(1)}, u32[]{:S(2)}, u32[]{:S(2)}) collective-permute-start(f32[3,32,512]{2,1,0:T(8,128)S(1)} %get-tuple-element.12), channel_id=1, source_target_pairs={{0,30},{1,31},{2,0},{3,1},{4,2},{5,3},{6,4},{7,5},{8,6},{9,7},{10,... | collective-permute-start | bytes 589832 | tf_op jit(solution)/shard_map/ppermute | solution.py:329
  17.1 18.9 %all-to-all-start = ((f32[32,3,1,2,512]{4,3,2,1,0:T(2,128)}), f32[32,3,1,2,512]{4,3,2,1,0:T(2,128)S(1)}, u32[]{:S(2)}, u32[]{:S(2)}) async-start(f32[32,3,1,2,512]{4,3,2,1,0:T(2,128)} %shard_map.33), calls=%async_computation | async-start | bytes 786432 | tf_op jit(solution)/shard_map/all_to_all | solution.py:332
  21.5 14.6 %collective-permute-start.3 = (f32[3,32,512]{2,1,0:T(8,128)S(1)}, f32[3,32,512]{2,1,0:T(8,128)S(1)}, u32[]{:S(2)}, u32[]{:S(2)}) collective-permute-start(f32[3,32,512]{2,1,0:T(8,128)S(1)} %get-tuple-element.17), channel_id=1, source_target_pairs={{0,2},{2,4},{4,6},{6,8},{8,10},{10,12},{12,14},{14,16},{16,18},{18... | collective-permute-start | bytes 589832 | tf_op jit(solution)/shard_map/ppermute | solution.py:335
  36.1 0.7 %copy-start.1 = (f32[2,3,32,512]{3,2,1,0:T(8,128)}, f32[2,3,32,512]{3,2,1,0:T(8,128)S(1)}, u32[]{:S(2)}) copy-start(f32[2,3,32,512]{3,2,1,0:T(8,128)S(1)} %bitcast_dynamic-update-slice_fusion) | copy-start | bytes 1179652

commit v20 on v18

--- a/solution.py
+++ b/solution.py
@@ -224,7 +224,7 @@
         out_specs=[VMEM] * len(shapes),
         scratch_shapes=[
             *extra,
-            pltpu.VMEM((3, chunks, extended + SUB, LANES), jnp.float32),
+            pltpu.VMEM((3, chunks, extended + extended // SUB + SUB, LANES), jnp.float32),
             pltpu.VMEM((2, 3, extended // SUB, chunks, SUB, LANES), jnp.float32),
             pltpu.VMEM((3, chunks, SUB, LANES), jnp.float32),
         ],

time: 37.3 us -> 37.3 us (level)
  no operation moved by 1% of the time
where the time goes in v20:
time: 37.3 us; the launch traced here: 37.1 us
  waiting for transfers between devices  17.9 us (48%)
  starting transfers between devices  8.9 us (24%)
  Pallas kernels  7.37 us (20%)
  local copies, waits for them, and re-layouts  1.14 us (3%)
  other arithmetic  1 us (3%)
  between operations  0.77 us (2%)
    ppermute x1, waiting for transfers between devices, on_device(): lax.ppermute(advanced[-1], 'tm', [(i, i + 1) for i in range(groups - 1)])  12.2 us
    pallas_call x3, Pallas kernels, call(): pl.pallas_call(functools.partial(kernel, chunks), out_shape=[jax.ShapeDty...  6.55 us
    ppermute x2, waiting for transfers between devices, exchange(): return lax.ppermute(edges, both, route(shift, 1))  5.68 us
    all_to_all x1, starting transfers between devices, on_device(): lax.all_to_all(packed, 'tm', split_axis=0, concat_axis=0, axis_index_grou...  4.38 us
    ppermute x1, starting transfers between devices, on_device(): lax.ppermute(advanced[-1], 'tm', [(i, i + 1) for i in range(groups - 1)])  2.31 us
    ppermute x2, starting transfers between devices, exchange(): return lax.ppermute(edges, both, route(shift, 1))  2.16 us
    squeeze x1, local copies, waits for them, and re-layouts, on_device(): c_points[k]  1.07 us
    concatenate x1, other arithmetic, on_device(): return (updated, jnp.concatenate([coarse[split:], coarse[:split]], axis=0))  0.92 us
  transfers between devices with their start and end apart: 5, of which 2 were waited for; matrix products, arithmetic and copies ran while one was open for 0% of the time, Pallas kernels for 18%

profile of v20, /device:TPU:16, one launch (start us, length us, event | category | flops | bytes accessed | tf_op | source)
XLA Modules:
  0.0 37.1 jit_solution(3439729713328403227)
XLA Ops:
  0.6 1.1 %slice_bitcast_fusion = (f32[3,32,512]{2,1,0:T(8,128)S(1)}, f32[3,32,512]{2,1,0:T(8,128)S(1)}, f32[1,3,32,512]{3,2,1,0:T(8,128)S(1)}) fusion(f32[2,3,32,512]{3,2,1,0:T(8,128)} %refs_0_.3), kind=kLoop, calls=%fused_computation.5 | loop fusion | bytes 983040 | tf_op jit(solution)/shard_map/squeeze | solution.py:313
  1.7 0.0 copy-start
  1.8 1.6 %collective-permute-start = (f32[2,3,16,512]{3,2,1,0:T(8,128)S(1)}, f32[2,3,16,512]{3,2,1,0:T(8,128)S(1)}, u32[]{:S(2)}, u32[]{:S(2)}) collective-permute-start(f32[2,3,16,512]{3,2,1,0:T(8,128)S(1)} %pad_maximum_fusion.2), channel_id=1, source_target_pairs={{0,1},{1,0},{2,3},{3,2},{4,5},{5,4},{6,7},{7,6},{8,9},{9,8},{10,11... | collective-permute-start | bytes 589832 | tf_op jit(solution)/shard_map/ppermute | solution.py:286
  3.4 0.6 %collective-permute-start.2 = (f32[2,3,16,512]{3,2,1,0:T(8,128)S(1)}, f32[2,3,16,512]{3,2,1,0:T(8,128)S(1)}, u32[]{:S(2)}, u32[]{:S(2)}) collective-permute-start(f32[2,3,16,512]{3,2,1,0:T(8,128)S(1)} %pad_maximum_fusion.3), channel_id=1, source_target_pairs={{0,1},{1,0},{2,3},{3,2},{4,5},{5,4},{6,7},{7,6},{8,9},{9,8},{10,11... | collective-permute-start | bytes 589832 | tf_op jit(solution)/shard_map/ppermute | solution.py:286
  4.0 5.7 %collective-permute-done.refs_1_ = f32[2,3,16,512]{3,2,1,0:T(8,128)S(1)} collective-permute-done((f32[2,3,16,512]{3,2,1,0:T(8,128)S(1)}, f32[2,3,16,512]{3,2,1,0:T(8,128)S(1)}, u32[]{:S(2)}, u32[]{:S(2)}) %collective-permute-start) | collective-permute-done | bytes 196640 | tf_op jit(solution)/shard_map/ppermute | solution.py:286
  9.6 0.0 copy-done
  9.6 1.8 %shard_map.30 = (f32[3,32,512]{2,1,0:T(8,128)S(1)}, f32[3,48,512]{2,1,0:T(8,128)S(1)}) custom-call(f32[2,3,32,512]{3,2,1,0:T(8,128)S(1)} %copy-done, f32[2,3,16,512]{3,2,1,0:T(8,128)S(1)} %collective-permute-done.refs_1_), custom_call_target="tpu_custom_call" | custom-call | flops 11796480 | bytes 393216 | tf_op jit(solution)/shard_map/pallas_call | solution.py:220
  11.5 0.1 collective-permute-start.1
  11.5 1.4 %shard_map.31.refs_2_ = f32[3,32,512]{2,1,0:T(8,128)S(1)} custom-call(f32[3,48,512]{2,1,0:T(8,128)S(1)} %get-tuple-element.13.middle), custom_call_target="tpu_custom_call" | custom-call | flops 11796480 | bytes 393216 | tf_op jit(solution)/shard_map/pallas_call | solution.py:220
  13.0 0.0 collective-permute-done.2.refs_1_
  13.0 3.3 %shard_map.32 = (f32[3,32,512]{2,1,0:T(8,128)S(1)}, f32[3,32,512]{2,1,0:T(8,128)S(1)}, f32[16,3,1,2,512]{4,3,2,1,0:T(2,128)S(1)}) custom-call(f32[2,3,32,512]{3,2,1,0:T(8,128)S(1)} %copy-done, f32[2,3,16,512]{3,2,1,0:T(8,128)S(1)} %collective-permute-done.2.refs_1_, f32[3,32,512]{2,1,0:T(8,128)S(1)} %shard_map.31.refs_2_), custom_call_target="tpu_custom_call" | custom-call | flops 23592960 | bytes 786432 | tf_op jit(solution)/shard_map/pallas_call | solution.py:220
  16.3 0.0 collective-permute-done.1.following
  16.3 0.8 %shard_map.33 = f32[32,3,1,2,512]{4,3,2,1,0:T(2,128)} custom-call(f32[3,32,512]{2,1,0:T(8,128)S(1)} %collective-permute-done.1.following, f32[3,32,512]{2,1,0:T(8,128)S(1)} %get-tuple-element.14.pushed, f32[16,3,1,2,512]{4,3,2,1,0:T(2,128)S(1)} %get-tuple-element.15.refs_0_), custom_call_target="tpu_custom_call" | custom-call | flops 98304 | bytes 1179648 | tf_op jit(solution)/shard_map/pallas_call | solution.py:299
  17.1 4.4 %all-to-all-start = ((f32[32,3,1,2,512]{4,3,2,1,0:T(2,128)}), f32[32,3,1,2,512]{4,3,2,1,0:T(2,128)S(1)}, u32[]{:S(2)}, u32[]{:S(2)}) async-start(f32[32,3,1,2,512]{4,3,2,1,0:T(2,128)} %shard_map.33), calls=%async_computation | async-start | bytes 786432 | tf_op jit(solution)/shard_map/all_to_all | solution.py:323
  21.5 2.3 %collective-permute-start.3 = (f32[3,32,512]{2,1,0:T(8,128)S(1)}, f32[3,32,512]{2,1,0:T(8,128)S(1)}, u32[]{:S(2)}, u32[]{:S(2)}) collective-permute-start(f32[3,32,512]{2,1,0:T(8,128)S(1)} %get-tuple-element.17), channel_id=1, source_target_pairs={{0,2},{2,4},{4,6},{6,8},{8,10},{10,12},{12,14},{14,16},{16,18},{18... | collective-permute-start | bytes 589832 | tf_op jit(solution)/shard_map/ppermute | solution.py:326
  23.9 12.2 %collective-permute-done.3 = f32[3,32,512]{2,1,0:T(8,128)S(1)} collective-permute-done((f32[3,32,512]{2,1,0:T(8,128)S(1)}, f32[3,32,512]{2,1,0:T(8,128)S(1)}, u32[]{:S(2)}, u32[]{:S(2)}) %collective-permute-start.3) | collective-permute-done | bytes 196640 | tf_op jit(solution)/shard_map/ppermute | solution.py:326
  36.1 0.0 all-to-all-done
  36.1 0.0 copy-start.1
  36.2 0.9 %pad_maximum_fusion.1 = f32[32,3,1,2,512]{4,3,2,1,0:T(2,128)} fusion(f32[15,3,1,2,512]{4,3,2,1,0:T(2,128)S(1)} %slice.33, f32[17,3,1,2,512]{4,3,2,1,0:T(2,128)S(1)} %slice.32), kind=kLoop, calls=%fused_computation.1 | loop fusion | flops 98304 | bytes 786432 | tf_op jit(solution)/shard_map/concatenate | solution.py:333
  37.1 0.0 copy-done.1
  (7 shorter events, 0.1 us)
Async XLA Ops:
  1.7 7.9 %copy-start = (f32[2,3,32,512]{3,2,1,0:T(8,128)S(1)}, f32[2,3,32,512]{3,2,1,0:T(8,128)}, u32[]{:S(2)}) copy-start(f32[2,3,32,512]{3,2,1,0:T(8,128)} %refs_0_.3) | copy-start | bytes 1179652
  1.8 7.9 %collective-permute-start = (f32[2,3,16,512]{3,2,1,0:T(8,128)S(1)}, f32[2,3,16,512]{3,2,1,0:T(8,128)S(1)}, u32[]{:S(2)}, u32[]{:S(2)}) collective-permute-start(f32[2,3,16,512]{3,2,1,0:T(8,128)S(1)} %pad_maximum_fusion.2), channel_id=1, source_target_pairs={{0,1},{1,0},{2,3},{3,2},{4,5},{5,4},{6,7},{7,6},{8,9},{9,8},{10,11... | collective-permute-start | bytes 589832 | tf_op jit(solution)/shard_map/ppermute | solution.py:286
  3.4 9.6 %collective-permute-start.2 = (f32[2,3,16,512]{3,2,1,0:T(8,128)S(1)}, f32[2,3,16,512]{3,2,1,0:T(8,128)S(1)}, u32[]{:S(2)}, u32[]{:S(2)}) collective-permute-start(f32[2,3,16,512]{3,2,1,0:T(8,128)S(1)} %pad_maximum_fusion.3), channel_id=1, source_target_pairs={{0,1},{1,0},{2,3},{3,2},{4,5},{5,4},{6,7},{7,6},{8,9},{9,8},{10,11... | collective-permute-start | bytes 589832 | tf_op jit(solution)/shard_map/ppermute | solution.py:286
  11.5 4.8 %collective-permute-start.1 = (f32[3,32,512]{2,1,0:T(8,128)S(1)}, f32[3,32,512]{2,1,0:T(8,128)S(1)}, u32[]{:S(2)}, u32[]{:S(2)}) collective-permute-start(f32[3,32,512]{2,1,0:T(8,128)S(1)} %get-tuple-element.12), channel_id=1, source_target_pairs={{0,30},{1,31},{2,0},{3,1},{4,2},{5,3},{6,4},{7,5},{8,6},{9,7},{10,... | collective-permute-start | bytes 589832 | tf_op jit(solution)/shard_map/ppermute | solution.py:320
  17.1 19.0 %all-to-all-start = ((f32[32,3,1,2,512]{4,3,2,1,0:T(2,128)}), f32[32,3,1,2,512]{4,3,2,1,0:T(2,128)S(1)}, u32[]{:S(2)}, u32[]{:S(2)}) async-start(f32[32,3,1,2,512]{4,3,2,1,0:T(2,128)} %shard_map.33), calls=%async_computation | async-start | bytes 786432 | tf_op jit(solution)/shard_map/all_to_all | solution.py:323
  21.5 14.6 %collective-permute-start.3 = (f32[3,32,512]{2,1,0:T(8,128)S(1)}, f32[3,32,512]{2,1,0:T(8,128)S(1)}, u32[]{:S(2)}, u32[]{:S(2)}) collective-permute-start(f32[3,32,512]{2,1,0:T(8,128)S(1)} %get-tuple-element.17), channel_id=1, source_target_pairs={{0,2},{2,4},{4,6},{6,8},{8,10},{10,12},{12,14},{14,16},{16,18},{18... | collective-permute-start | bytes 589832 | tf_op jit(solution)/shard_map/ppermute | solution.py:326
  36.1 1.0 %copy-start.1 = (f32[2,3,32,512]{3,2,1,0:T(8,128)}, f32[2,3,32,512]{3,2,1,0:T(8,128)S(1)}, u32[]{:S(2)}) copy-start(f32[2,3,32,512]{3,2,1,0:T(8,128)S(1)} %bitcast_dynamic-update-slice_fusion) | copy-start | bytes 1179652
